TPU v7x, 128 devices: a whole 4x4x4 slice. The times are simulated.
128 devices in a mesh: grp: 8 (over y_hi, x), seq: 16 (over y_lo, z, core).
Axes of the slice: x: 4, y: 4 (y_hi: 2, y_lo: 2; y = y_hi * 2 + y_lo), z: 4, core: 2. Of those that a mesh axis runs over, the one named last changes fastest.
Arguments:
- tokens: bfloat16 [2, 8192, 2048], P(None, ('grp', 'seq')), may hold values from -6 to 6
- segment_ids: int32 [2, 8192], P(None, 'grp'), may hold values from -1 to 32, as said below
- w_qkv: bfloat16 [2048, 1920], P(('grp', 'seq')), may hold values from -0.125 to 0.125
- w_out: bfloat16 [1280, 2048], P(None, ('grp', 'seq')), may hold values from -1.5 to 1.5
- w_gate_up: bfloat16 [2048, 10240], P(('grp', 'seq')), may hold values from -0.125 to 0.125
- w_down: bfloat16 [5120, 2048], P(('grp', 'seq')), may hold values from -0.078125 to 0.078125
- attn_gain: bfloat16 [2048], P(('grp', 'seq')), may hold values from 0.5 to 1.5
- ffn_gain: bfloat16 [2048], P(('grp', 'seq')), may hold values from 0.5 to 1.5
- query_gain: bfloat16 [64], replicated, may hold values from 0.25 to 1.75
- key_gain: bfloat16 [64], replicated, may hold values from 0.25 to 1.75
- out_grad: bfloat16 [2, 8192, 2048], P(None, ('grp', 'seq')), may hold values from -6 to 6
Outputs:
- mixed: bfloat16 [2, 8192, 2048], P(None, ('grp', 'seq'))
- input_grad: float32 [2, 8192, 2048], P(None, ('grp', 'seq'))
- w_qkv_grad: float32 [2048, 1920], P(('grp', 'seq'))
- w_out_grad: float32 [1280, 2048], P(None, ('grp', 'seq'))
- w_gate_up_grad: float32 [2048, 10240], P(('grp', 'seq'))
- w_down_grad: float32 [5120, 2048], P(('grp', 'seq'))
- attn_gain_grad: float32 [2048], P(('grp', 'seq'))
- ffn_gain_grad: float32 [2048], P(('grp', 'seq'))
- query_gain_grad: float32 [64], replicated
- key_gain_grad: float32 [64], replicated
Inputs may be any that keep to these rules, and one draw needn't show every extreme that they name: `segment_ids`: in each sequence the numbers never fall, start at 0 and rise by one at each new document, up to at most 32, where the remaining documents share the last number; padding (-1) fills a tail of one or more tokens. In each group one of the 2 sequences holds a document that begins within the first 64 tokens and ends within the last 64.
All inputs are finite; a program needn't handle non-finite values.
Results may differ from a plain program's by a relative error of at most 0.02.
Values may be sent and summed in bfloat16 or wider, within the bound.
A program may use at most 384 MiB of HBM per device.

v0:
```python
import jax
import jax.numpy as jnp
from jax import lax
from jax.sharding import PartitionSpec as P

Q_HEADS = 20
KV_HEADS = 5


EPS = 1e-06


def rms_scale(values):
    return lax.rsqrt(jnp.mean(values * values, axis=-1, keepdims=True) + EPS)


def rotate(values):
    half = values.shape[-1] // 2
    return jnp.concatenate([-values[..., half:], values[..., :half]], axis=-1)


def rotate_back(values):
    half = values.shape[-1] // 2
    return jnp.concatenate([values[..., half:], -values[..., :half]], axis=-1)


def norm_back(upstream, normed, scale, gain):
    scaled = upstream * gain
    inner = jnp.mean(scaled * normed, axis=-1, keepdims=True)
    return scale * (scaled - normed * inner)


def contract_last(left, right):
    return lax.dot_general(
        left, right, (((1,), (1,)), ((), ())), preferred_element_type=jnp.float32
    )


def contract_rows(left, right):
    return lax.dot_general(
        left, right, (((0,), (0,)), ((), ())), preferred_element_type=jnp.float32
    )


def rope_tables(positions, head_size):
    half = head_size // 2
    inverse = 10000.0 ** (-jnp.arange(half, dtype=jnp.float32) / half)
    angles = positions[:, None] * inverse[None, :]
    angles = jnp.concatenate([angles, angles], axis=1)
    return (jnp.cos(angles)[:, None, :], jnp.sin(angles)[:, None, :])


def attention_scores(grouped, keys, allowed, factor):
    scores = (
        jnp.einsum("tgjd,sgd->gjts", grouped, keys, preferred_element_type=jnp.float32) * factor
    )
    return jnp.where(allowed[None, None], scores, -1e30)


def layer_pass(weights, head_gains, hidden_in, seg_row, cotangent, start):
    w_qkv, w_out, w_gate_up, w_down, attn_gain, ffn_gain = weights
    query_gain, key_gain = head_gains
    gain_one = attn_gain.astype(jnp.float32)
    gain_two = ffn_gain.astype(jnp.float32)
    tok_rows = hidden_in.shape[0]
    head_size = query_gain.shape[0]
    query_dim = Q_HEADS * head_size
    key_dim = KV_HEADS * head_size
    groups = Q_HEADS // KV_HEADS
    factor = head_size ** (-0.5)
    seq_len = seg_row.shape[0]
    hidden = hidden_in.astype(jnp.float32)
    scale_one = rms_scale(hidden)
    norm_one = hidden * scale_one
    normed = (norm_one * gain_one).astype(jnp.bfloat16)
    packed = jnp.dot(normed, w_qkv, preferred_element_type=jnp.float32)
    query_raw = packed[:, :query_dim].reshape(tok_rows, Q_HEADS, head_size)
    key_raw = packed[:, query_dim : query_dim + key_dim].reshape(tok_rows, KV_HEADS, head_size)
    value_raw = packed[:, query_dim + key_dim :]
    query_scale = rms_scale(query_raw)
    query_norm = query_raw * query_scale
    key_scale = rms_scale(key_raw)
    key_norm = key_raw * key_scale
    query_head = query_norm * query_gain
    key_head = key_norm * key_gain
    positions = (start + jnp.arange(tok_rows)).astype(jnp.float32)
    cosine, sine = rope_tables(positions, head_size)
    queries = (query_head * cosine + rotate(query_head) * sine).astype(jnp.bfloat16)
    keys_local = (key_head * cosine + rotate(key_head) * sine).astype(jnp.bfloat16)
    kv_local = jnp.concatenate(
        [keys_local.reshape(tok_rows, key_dim), value_raw.astype(jnp.bfloat16)], axis=1
    )
    kv_whole = lax.all_gather(kv_local, "seq", axis=0, tiled=True)
    keys = kv_whole[:, :key_dim].reshape(seq_len, KV_HEADS, head_size)
    values = kv_whole[:, key_dim:].reshape(seq_len, KV_HEADS, head_size)
    grouped = queries.reshape(tok_rows, KV_HEADS, groups, head_size)
    query_ids = lax.dynamic_slice_in_dim(seg_row, start, tok_rows)
    query_pos = start + jnp.arange(tok_rows)
    key_pos = jnp.arange(seq_len)
    allowed = (
        (key_pos[None, :] <= query_pos[:, None])
        & (seg_row[None, :] == query_ids[:, None])
        & (query_ids[:, None] >= 0)
    )
    allowed = allowed | (key_pos[None, :] == query_pos[:, None])
    scores = attention_scores(grouped, keys, allowed, factor)
    peak = jnp.max(scores, axis=-1, keepdims=True)
    raised = jnp.exp(scores - peak)
    row_total = jnp.sum(raised, axis=-1, keepdims=True)
    log_total = peak + jnp.log(row_total)
    probs = (raised / row_total).astype(jnp.bfloat16)
    attended = jnp.einsum("gjts,sgd->tgjd", probs, values, preferred_element_type=jnp.float32)
    attended = attended.reshape(tok_rows, query_dim).astype(jnp.bfloat16)
    resid = hidden + jnp.dot(attended, w_out, preferred_element_type=jnp.float32)
    scale_two = rms_scale(resid)
    norm_two = resid * scale_two
    normed_ffn = (norm_two * gain_two).astype(jnp.bfloat16)
    gate_up = jnp.dot(normed_ffn, w_gate_up, preferred_element_type=jnp.float32)
    width = gate_up.shape[1] // 2
    gate = gate_up[:, :width]
    upper = gate_up[:, width:]
    sigmoid_gate = jax.nn.sigmoid(gate)
    active = gate * sigmoid_gate
    inner = (active * upper).astype(jnp.bfloat16)
    result = (resid + jnp.dot(inner, w_down, preferred_element_type=jnp.float32)).astype(
        jnp.bfloat16
    )
    upstream = cotangent.astype(jnp.float32)
    d_inner = contract_last(cotangent, w_down)
    d_gate = d_inner * upper * sigmoid_gate * (1.0 + gate * (1.0 - sigmoid_gate))
    d_upper = d_inner * active
    d_gate_up = jnp.concatenate([d_gate, d_upper], axis=1).astype(jnp.bfloat16)
    d_normed_ffn = contract_last(d_gate_up, w_gate_up)
    ffn_term = jnp.sum(d_normed_ffn * norm_two, axis=0)
    d_resid = upstream + norm_back(d_normed_ffn, norm_two, scale_two, gain_two)
    resid_low = d_resid.astype(jnp.bfloat16)
    d_attended = contract_last(resid_low, w_out).astype(jnp.bfloat16)
    d_attended = d_attended.reshape(tok_rows, KV_HEADS, groups, head_size)
    again = jnp.exp(scores - log_total)
    again_low = again.astype(jnp.bfloat16)
    d_probs = jnp.einsum("tgjd,sgd->gjts", d_attended, values, preferred_element_type=jnp.float32)
    d_values = jnp.einsum(
        "gjts,tgjd->sgd", again_low, d_attended, preferred_element_type=jnp.float32
    )
    row_inner = jnp.sum(again * d_probs, axis=-1, keepdims=True)
    d_scores = (again * (d_probs - row_inner)).astype(jnp.bfloat16)
    d_queries = (
        jnp.einsum("gjts,sgd->tgjd", d_scores, keys, preferred_element_type=jnp.float32) * factor
    )
    d_keys = (
        jnp.einsum("gjts,tgjd->sgd", d_scores, grouped, preferred_element_type=jnp.float32) * factor
    )
    kv_terms = jnp.concatenate(
        [d_keys.reshape(seq_len, key_dim), d_values.reshape(seq_len, key_dim)], axis=1
    )
    kv_grads = lax.psum_scatter(
        kv_terms.astype(jnp.bfloat16), "seq", scatter_dimension=0, tiled=True
    ).astype(jnp.float32)
    key_grad = kv_grads[:, :key_dim].reshape(tok_rows, KV_HEADS, head_size)
    value_grad = kv_grads[:, key_dim:]
    query_grad = d_queries.reshape(tok_rows, Q_HEADS, head_size)
    d_query_head = query_grad * cosine + rotate_back(query_grad * sine)
    d_key_head = key_grad * cosine + rotate_back(key_grad * sine)
    query_term = jnp.sum(d_query_head * query_norm, axis=(0, 1))
    key_term = jnp.sum(d_key_head * key_norm, axis=(0, 1))
    d_query_raw = norm_back(d_query_head, query_norm, query_scale, query_gain)
    d_key_raw = norm_back(d_key_head, key_norm, key_scale, key_gain)
    d_packed = jnp.concatenate(
        [
            d_query_raw.reshape(tok_rows, query_dim),
            d_key_raw.reshape(tok_rows, key_dim),
            value_grad,
        ],
        axis=1,
    ).astype(jnp.bfloat16)
    d_normed = contract_last(d_packed, w_qkv)
    attn_term = jnp.sum(d_normed * norm_one, axis=0)
    input_grad = d_resid + norm_back(d_normed, norm_one, scale_one, gain_one)
    kept_rows = (normed, d_packed, attended, resid_low, normed_ffn, d_gate_up, inner, cotangent)
    return (result, input_grad, kept_rows, (attn_term, ffn_term, query_term, key_term))


def per_device(
    tokens,
    segment_ids,
    w_qkv,
    w_out,
    w_gate_up,
    w_down,
    attn_gain,
    ffn_gain,
    query_gain,
    key_gain,
    out_grad,
):
    local = (w_qkv, w_out, w_gate_up, w_down, attn_gain, ffn_gain)
    head_gains = (query_gain.astype(jnp.float32), key_gain.astype(jnp.float32))
    tok_rows = tokens.shape[1]
    start = lax.axis_index("seq") * tok_rows
    results = []
    input_grads = []
    kept_all = []
    gain_terms = []
    for micro_index in range(tokens.shape[0]):
        weights = (
            lax.all_gather(local[0], ("grp", "seq"), axis=0, tiled=True),
            lax.all_gather(local[1], ("grp", "seq"), axis=1, tiled=True),
            lax.all_gather(local[2], ("grp", "seq"), axis=0, tiled=True),
            lax.all_gather(local[3], ("grp", "seq"), axis=0, tiled=True),
            lax.all_gather(local[4], ("grp", "seq"), axis=0, tiled=True),
            lax.all_gather(local[5], ("grp", "seq"), axis=0, tiled=True),
        )
        result, input_grad, kept_rows, terms = layer_pass(
            weights,
            head_gains,
            tokens[micro_index],
            segment_ids[micro_index],
            out_grad[micro_index],
            start,
        )
        results.append(result)
        input_grads.append(input_grad)
        kept_all.append(kept_rows)
        gain_terms.append(terms)
    stacked = [jnp.concatenate([entry[slot] for entry in kept_all], axis=0) for slot in range(8)]
    grad_qkv = contract_rows(stacked[0], stacked[1])
    grad_out = contract_rows(stacked[2], stacked[3])
    grad_gate_up = contract_rows(stacked[4], stacked[5])
    grad_down = contract_rows(stacked[6], stacked[7])
    term_sums = [gain_terms[0][slot] for slot in range(4)]
    for entry in gain_terms[1:]:
        term_sums = [term_sums[slot] + entry[slot] for slot in range(4)]
    owned = (
        lax.psum_scatter(grad_qkv, ("grp", "seq"), scatter_dimension=0, tiled=True),
        lax.psum_scatter(grad_out, ("grp", "seq"), scatter_dimension=1, tiled=True),
        lax.psum_scatter(grad_gate_up, ("grp", "seq"), scatter_dimension=0, tiled=True),
        lax.psum_scatter(grad_down, ("grp", "seq"), scatter_dimension=0, tiled=True),
        lax.psum_scatter(term_sums[0], ("grp", "seq"), scatter_dimension=0, tiled=True),
        lax.psum_scatter(term_sums[1], ("grp", "seq"), scatter_dimension=0, tiled=True),
    )
    head_sums = lax.psum((term_sums[2], term_sums[3]), ("grp", "seq"))
    return (
        jnp.stack(results),
        jnp.stack(input_grads),
        owned[0],
        owned[1],
        owned[2],
        owned[3],
        owned[4],
        owned[5],
        head_sums[0],
        head_sums[1],
    )


def solution(mesh):
    return jax.shard_map(
        per_device,
        mesh=mesh,
        in_specs=(
            P(None, ("grp", "seq"), None),
            P(None, "grp"),
            P(("grp", "seq"), None),
            P(None, ("grp", "seq")),
            P(("grp", "seq"), None),
            P(("grp", "seq"), None),
            P(("grp", "seq")),
            P(("grp", "seq")),
            P(),
            P(),
            P(None, ("grp", "seq"), None),
        ),
        out_specs=(
            P(None, ("grp", "seq"), None),
            P(None, ("grp", "seq"), None),
            P(("grp", "seq"), None),
            P(None, ("grp", "seq")),
            P(("grp", "seq"), None),
            P(("grp", "seq"), None),
            P(("grp", "seq")),
            P(("grp", "seq")),
            P(),
            P(),
        ),
        check_vma=False,
    )
```

profile of v0, /device:TPU:1, one launch (start us, length us, event | category | flops | bytes accessed | tf_op | source)
XLA Modules:
  0.0 3972.1 jit_solution(3133596446840242995)
XLA Ops:
  9.7 68.9 %all-reduce.5 = (bf16[2048]{0:T(1024)(128)(2,1)S(1)}, bf16[2048]{0:T(1024)(128)(2,1)S(1)}) all-reduce(bf16[2048]{0:T(1024)(128)(2,1)S(1)} %dynamic-update-slice, bf16[2048]{0:T(1024)(128)(2,1)S(1)} %dynamic-update-slice.1), channel_id=1, replica_groups=mesh['grp'=8,'seq'=16] {'grp','seq'}, use_global_device_ids=true, to_apply=%add | all-reduce | flops 4096 | bytes 16384
  84.0 131.4 %all-gather.7.cloned.1.call-done = bf16[2048,1920]{1,0:T(8,128)(2,1)} async-done(((bf16[16,1920]{1,0:T(8,128)(2,1)}), bf16[2048,1920]{1,0:T(8,128)(2,1)}) %all-gather.7.cloned.1.call-update) | async-done | bytes 7864336 | tf_op jit(solution)/shard_map/all_gather | solution.py:206
  232.8 23.8 all-gather.17.cloned.1.call-done
  261.9 30.0 all-gather.9.cloned.1.call-done
  301.6 191.4 %all-gather.11.cloned.1.call-done = bf16[1280,2048]{0,1:T(8,128)(2,1)} async-done(((bf16[1280,16]{0,1:T(8,128)(2,1)}), bf16[1280,2048]{0,1:T(8,128)(2,1)}) %all-gather.11.cloned.1.call-update) | async-done | bytes 5242896 | tf_op jit(solution)/shard_map/all_gather | solution.py:207
  504.9 238.8 %all-gather.13.cloned.1.call-done = bf16[2048,10240]{1,0:T(8,128)(2,1)} async-done(((bf16[16,10240]{1,0:T(8,128)(2,1)}), bf16[2048,10240]{1,0:T(8,128)(2,1)}) %all-gather.13.cloned.1.call-update) | async-done | bytes 41943056 | tf_op jit(solution)/shard_map/all_gather | solution.py:208
  743.7 18.3 fusion.143
  762.0 18.7 fusion.141
  780.7 185.1 %all-gather.15.cloned.1.call-done = bf16[5120,2048]{1,0:T(8,128)(2,1)} async-done(((bf16[40,2048]{1,0:T(8,128)(2,1)}), bf16[5120,2048]{1,0:T(8,128)(2,1)}) %all-gather.15.cloned.1.call-update) | async-done | bytes 20971536 | tf_op jit(solution)/shard_map/all_gather | solution.py:209
  965.8 12.4 multiply_convert_fusion.1
  978.2 12.1 multiply_convert_fusion.3
  990.3 18.4 fusion.46
  1008.7 20.8 multiply_reduce_fusion.6
  1129.6 42.7 %reduce-scatter.9.cloned.1.call-done = bf16[64,640]{1,0:T(8,128)(2,1)} async-done(((bf16[1024,640]{1,0:T(8,128)(2,1)}), bf16[64,640]{1,0:T(8,128)(2,1)}) %reduce-scatter.9.cloned.1.call-update) | async-done | bytes 81936 | tf_op jit(solution)/shard_map/reduce_scatter | solution.py:156
  1175.6 7.7 fusion.90
  1184.7 16.3 fusion.54
  1202.1 30.7 fusion.14
  1233.9 9.1 fusion.28
  1242.9 9.1 fusion.29
  1266.5 69.0 %all-reduce.4 = (f32[2048]{0:T(1024)S(1)}, f32[2048]{0:T(1024)S(1)}, f32[64]{0:T(128)}, f32[64]{0:T(128)}) all-reduce(f32[2048]{0:T(1024)S(1)} %add.258, f32[2048]{0:T(1024)S(1)} %add.259, f32[64]{0:T(128)S(1)} %add.260, f32[64]{0:T(128)S(1)} %add.261), channel_id=8, replica_groups=mesh['grp'=8,'seq'=16] {'grp','seq'}, use_global_device_ids=true, to_apply=%region_30.31.clone | all-reduce | flops 4224 | bytes 33792
  1340.6 483.9 %reduce-scatter.13.cloned.1.call-done = f32[1280,16]{0,1:T(8,128)} async-done(((f32[1280,2048]{0,1:T(8,128)}), f32[1280,16]{0,1:T(8,128)}) %reduce-scatter.13.cloned.1.call-update) | async-done | bytes 81936 | tf_op jit(solution)/shard_map/reduce_scatter | solution.py:235
  1824.4 660.8 %reduce-scatter.11.cloned.1.call-done = f32[16,1920]{1,0:T(8,128)} async-done(((f32[2048,1920]{1,0:T(8,128)}), f32[16,1920]{1,0:T(8,128)}) %reduce-scatter.11.cloned.1.call-update) | async-done | bytes 122896 | tf_op jit(solution)/shard_map/reduce_scatter | solution.py:234
  2485.3 703.2 %reduce-scatter.17.cloned.1.call-done = f32[40,2048]{1,0:T(8,128)} async-done(((f32[5120,2048]{1,0:T(8,128)}), f32[40,2048]{1,0:T(8,128)}) %reduce-scatter.17.cloned.1.call-update) | async-done | bytes 327696 | tf_op jit(solution)/shard_map/reduce_scatter | solution.py:237
  3188.4 776.6 %reduce-scatter.15.cloned.1.call-done = f32[16,10240]{1,0:T(8,128)} async-done(((f32[2048,10240]{1,0:T(8,128)}), f32[16,10240]{1,0:T(8,128)}) %reduce-scatter.15.cloned.1.call-update) | async-done | bytes 655376 | tf_op jit(solution)/shard_map/reduce_scatter | solution.py:236
  (445 shorter events, 176.6 us)
Async XLA Ops:
  7.2 208.3 %all-gather.7.cloned.1.call-start = ((), (), s32[]{:S(2)}) async-start(), calls=%async_computation.6 | async-start | bytes 7925760 | tf_op jit(solution)/shard_map/all_gather | solution.py:206
  7.9 248.8 %all-gather.17.cloned.1.call-start = ((), (), s32[]{:S(2)}) async-start(), calls=%async_computation.11 | async-start | bytes 1392640 | tf_op jit(solution)/shard_map/all_gather | solution.py:93
  79.2 143.5 %copy-start.100 = (f32[64]{0:T(128)}, f32[64]{0:T(128)S(1)}, u32[]{:S(2)}) copy-start(f32[64]{0:T(128)S(1)} %convert_element_type.142) | copy-start | bytes 772
  224.3 67.7 %all-gather.9.cloned.1.call-start = ((), (), s32[]{:S(2)}) async-start(), calls=%async_computation.7 | async-start | bytes 1392640 | tf_op jit(solution)/shard_map/all_gather | solution.py:93
  225.2 267.8 %all-gather.11.cloned.1.call-start = ((), (), s32[]{:S(2)}) async-start(), calls=%async_computation.8 | async-start | bytes 5283840 | tf_op jit(solution)/shard_map/all_gather | solution.py:207
  225.7 518.0 %all-gather.13.cloned.1.call-start = ((), (), s32[]{:S(2)}) async-start(), calls=%async_computation.9 | async-start | bytes 42270720 | tf_op jit(solution)/shard_map/all_gather | solution.py:208
  226.3 739.5 %all-gather.15.cloned.1.call-start = ((), (), s32[]{:S(2)}) async-start(), calls=%async_computation.10 | async-start | bytes 21135360 | tf_op jit(solution)/shard_map/all_gather | solution.py:209
  226.9 901.6 %reduce-scatter.7.cloned.1.call-start = ((), (), s32[]{:S(2)}) async-start(), calls=%async_computation.12 | async-start | bytes 1392640 | tf_op jit(solution)/shard_map/reduce_scatter | solution.py:156
  227.2 802.4 %copy-start.66 = (f32[2048]{0:T(1024)}, f32[2048]{0:T(1024)S(1)}, u32[]{:S(2)}) copy-start(f32[2048]{0:T(1024)S(1)} %convert_element_type.151) | copy-start | bytes 24580
  261.9 235.4 %copy-start.23 = (bf16[1024,320]{0,1:T(8,128)(2,1)}, bf16[1024,320]{0,1:T(8,128)(2,1)S(1)}, u32[]{:S(2)}) copy-start(bf16[1024,320]{0,1:T(8,128)(2,1)S(1)} %copy.280) | copy-start | bytes 1966084
  299.7 193.3 %copy-start.10 = (bf16[2,64,2048]{2,1,0:T(8,128)(2,1)S(1)}, bf16[2,64,2048]{2,1,0:T(8,128)(2,1)}, u32[]{:S(2)}) copy-start(bf16[2,64,2048]{2,1,0:T(8,128)(2,1)} %param.11) | copy-start | bytes 1572868
  301.5 196.8 %copy-start.52 = (bf16[5,64,4,64]{3,1,2,0:T(8,128)(2,1)}, bf16[5,64,4,64]{3,1,2,0:T(8,128)(2,1)S(1)}, u32[]{:S(2)}) copy-start(bf16[5,64,4,64]{3,1,2,0:T(8,128)(2,1)S(1)} %fusion.61) | copy-start | bytes 491524
  301.6 195.7 %copy-start.68 = (pred[64,1024]{1,0:T(8,128)(4,1)S(1)}, pred[64,1024]{1,0:T(8,128)(4,1)}, u32[]{:S(2)}) copy-start(pred[64,1024]{1,0:T(8,128)(4,1)} %get-tuple-element.106) | copy-start | bytes 196612
  497.3 532.3 %copy-start.94 = (f32[64]{0:T(128)}, f32[64]{0:T(128)S(1)}, u32[]{:S(2)}) copy-start(f32[64]{0:T(128)S(1)} %add_rsqrt_fusion.6) | copy-start | bytes 772
  504.7 524.9 %copy-start.6 = (f32[64,2048]{1,0:T(8,128)}, f32[64,2048]{1,0:T(8,128)S(1)}, u32[]{:S(2)}) copy-start(f32[64,2048]{1,0:T(8,128)S(1)} %get-tuple-element.116) | copy-start | bytes 1572868
  504.7 524.9 %copy-start.96 = (f32[64]{0:T(128)}, f32[64]{0:T(128)S(1)}, u32[]{:S(2)}) copy-start(f32[64]{0:T(128)S(1)} %add_rsqrt_fusion.4) | copy-start | bytes 772
  504.9 257.1 %copy-start.37 = (bf16[64,2048]{1,0:T(8,128)(2,1)}, bf16[64,2048]{1,0:T(8,128)(2,1)S(1)}, u32[]{:S(2)}) copy-start(bf16[64,2048]{1,0:T(8,128)(2,1)S(1)} %get-tuple-element.100) | copy-start | bytes 786436
  504.9 257.1 %copy-start.35 = (bf16[64,2048]{1,0:T(8,128)(2,1)}, bf16[64,2048]{1,0:T(8,128)(2,1)S(1)}, u32[]{:S(2)}) copy-start(bf16[64,2048]{1,0:T(8,128)(2,1)S(1)} %get-tuple-element.99) | copy-start | bytes 786436
  762.0 203.8 %copy-start.8 = (bf16[2,64,2048]{2,1,0:T(8,128)(2,1)S(1)}, bf16[2,64,2048]{2,1,0:T(8,128)(2,1)}, u32[]{:S(2)}) copy-start(bf16[2,64,2048]{2,1,0:T(8,128)(2,1)} %param.21) | copy-start | bytes 1572868
  1051.9 120.4 %reduce-scatter.9.cloned.1.call-start = ((), (), s32[]{:S(2)}) async-start(), calls=%async_computation.13 | async-start | bytes 1392640 | tf_op jit(solution)/shard_map/reduce_scatter | solution.py:156
  1071.1 753.4 %reduce-scatter.13.cloned.1.call-start = ((), (), s32[]{:S(2)}) async-start(), calls=%async_computation.15 | async-start | bytes 10567680 | tf_op jit(solution)/shard_map/reduce_scatter | solution.py:235
  1077.8 1407.5 %reduce-scatter.11.cloned.1.call-start = ((), (), s32[]{:S(2)}) async-start(), calls=%async_computation.14 | async-start | bytes 15851520 | tf_op jit(solution)/shard_map/reduce_scatter | solution.py:234
  1183.3 2005.1 %reduce-scatter.17.cloned.1.call-start = ((), (), s32[]{:S(2)}) async-start(), calls=%async_computation.17 | async-start | bytes 42270720 | tf_op jit(solution)/shard_map/reduce_scatter | solution.py:237
  1201.1 2763.9 %reduce-scatter.15.cloned.1.call-start = ((), (), s32[]{:S(2)}) async-start(), calls=%async_computation.16 | async-start | bytes 84541440 | tf_op jit(solution)/shard_map/reduce_scatter | solution.py:236
  (104 other events, 2814.7 us)
Sparse Core Ops, SparseCore 0:
  9.7 205.6 all-gather.6
  224.4 32.2 all-gather.16
  259.0 32.9 all-gather.8
  293.5 199.4 all-gather.10
  494.5 249.1 all-gather.12
  745.3 220.4 all-gather.14
  1052.1 57.3 reduce-scatter.6
  1111.9 60.3 reduce-scatter.8
  1175.3 649.0 reduce-scatter.12
  1827.2 657.9 reduce-scatter.10
  2488.4 700.0 reduce-scatter.16
  3191.4 773.5 reduce-scatter.14
where the time goes:
time: 3980 us; the launch traced here: 3970 us
  waiting for transfers between devices  3470 us (87%)
  matrix products  243 us (6%)
  blocking collectives  138 us (3%)
  local copies, waits for them, and re-layouts  63.4 us (2%)
  other arithmetic  40.4 us (1%)
    reduce_scatter x1, waiting for transfers between devices, per_device(): lax.psum_scatter(grad_gate_up, ('grp', 'seq'), scatter_dimension=0, tiled...  777 us
    reduce_scatter x1, waiting for transfers between devices, per_device(): lax.psum_scatter(grad_down, ('grp', 'seq'), scatter_dimension=0, tiled=True)  703 us
    reduce_scatter x1, waiting for transfers between devices, per_device(): lax.psum_scatter(grad_qkv, ('grp', 'seq'), scatter_dimension=0, tiled=True)  661 us
    reduce_scatter x1, waiting for transfers between devices, per_device(): lax.psum_scatter(grad_out, ('grp', 'seq'), scatter_dimension=1, tiled=True)  484 us
    all_gather x1, waiting for transfers between devices, per_device(): lax.all_gather(local[2], ('grp', 'seq'), axis=0, tiled=True)  239 us
    all_gather x1, waiting for transfers between devices, per_device(): lax.all_gather(local[1], ('grp', 'seq'), axis=1, tiled=True)  191 us
    all_gather x1, waiting for transfers between devices, per_device(): lax.all_gather(local[3], ('grp', 'seq'), axis=0, tiled=True)  185 us
    unnamed x2, blocking collectives  138 us
  transfers between devices with their start and end apart: 12, of which 11 were waited for; matrix products, arithmetic and copies ran while one was open for 6% of the time, Pallas kernels for 0%

commit v1 on v0

v1 whole, which is shorter than its diff:
```python
import jax
import jax.numpy as jnp
from jax import lax
from jax.experimental import pallas as pl
from jax.experimental.pallas import tpu as pltpu
from jax.sharding import PartitionSpec as P

Q_HEADS = 20
KV_HEADS = 5
GROUP = 4
HEAD = 64
D = 2048
FF = 5120
QD = 1280
KD = 320
QKV = 1920
SEQ = 1024
MICRO = 2
ROWS = 64
TOK = 128
FS = 640
EPS = 1e-06
MESH = pl.DeviceIdType.MESH
F32 = jnp.float32
BF16 = jnp.bfloat16
ANY = pl.BlockSpec(memory_space=pl.ANY)


class Place:
    def __init__(self):
        g = lax.axis_index("grp")
        s = lax.axis_index("seq")
        self.g, self.s = g, s
        self.yh, self.x = g // 4, g % 4
        self.yl, self.z, self.c = s // 8, (s // 2) % 4, s % 2
        self.y = self.yh * 2 + self.yl

    def at(self, x=None, y=None, z=None, c=None):
        x = self.x if x is None else x
        y = self.y if y is None else y
        z = self.z if z is None else z
        c = self.c if c is None else c
        return ((y // 2) * 4 + x, (y % 2) * 8 + z * 2 + c)

    def step(self, axis, k):
        if axis == "x":
            return self.at(x=(self.x + k) % 4)
        if axis == "y":
            return self.at(y=(self.y + k) % 4)
        if axis == "z":
            return self.at(z=(self.z + k) % 4)
        return self.at(c=1 - self.c)

    def pos(self, axis, k):
        return (getattr(self, axis) + k) % 4


class Links:
    def __init__(self, send_sems, recv_sems):
        self.send_sems, self.recv_sems = send_sems, recv_sems
        self.used = 0
        self.sent = []

    def send(self, src, dst, to):
        i = self.used
        self.used += 1
        copy = pltpu.make_async_remote_copy(
            src_ref=src,
            dst_ref=dst,
            send_sem=self.send_sems.at[i],
            recv_sem=self.recv_sems.at[i],
            device_id=to,
            device_id_type=MESH,
        )
        copy.start()
        self.sent.append(copy)
        return copy

    def local(self, src, dst):
        i = self.used
        self.used += 1
        copy = pltpu.make_async_copy(src, dst, self.recv_sems.at[i])
        copy.start()
        return copy

    def drain(self):
        for copy in self.sent:
            copy.wait_send()


def greet(partners):
    barrier = pltpu.get_barrier_semaphore()
    for to in partners:
        pl.semaphore_signal(barrier, inc=1, device_id=to, device_id_type=MESH)
    pl.semaphore_wait(barrier, len(partners))


def any_call(body, name, cid, n_in, outs, scratch, sems, vmem=48 << 20):
    return pl.pallas_call(
        body,
        out_shape=outs,
        in_specs=[ANY] * n_in,
        out_specs=[ANY] * len(outs),
        name=name,
        scratch_shapes=list(scratch)
        + [pltpu.SemaphoreType.DMA((sems,)), pltpu.SemaphoreType.DMA((sems,))],
        compiler_params=pltpu.CompilerParams(
            collective_id=cid, has_side_effects=True, vmem_limit_bytes=vmem
        ),
    )


def sds(shape, dtype):
    return jax.ShapeDtypeStruct(shape, dtype)


def slab_target(p):
    to = p.at(x=p.z, y=p.c * 2 + p.yl, z=p.g // 2, c=p.g % 2)
    return to


def slab_source(p):
    m = p.z * 2 + p.c
    return p.at(x=m % 4, y=(m // 4) * 2 + p.yl, z=p.x, c=p.yh)


def same(p, to):
    return (to[0] == p.g) & (to[1] == p.s)


def greet_plane(p, partners, slab_to, slab_from, own_slab):
    barrier = pltpu.get_barrier_semaphore()
    for to in partners:
        pl.semaphore_signal(barrier, inc=1, device_id=to, device_id_type=MESH)

    @pl.when(jnp.logical_not(own_slab))
    def _():
        pl.semaphore_signal(barrier, inc=1, device_id=slab_to, device_id_type=MESH)
        pl.semaphore_signal(barrier, inc=1, device_id=slab_from, device_id_type=MESH)
        pl.semaphore_wait(barrier, len(partners) + 2)

    @pl.when(own_slab)
    def _():
        pl.semaphore_wait(barrier, len(partners))


def slab_copy(src, dst, ssem, rsem, i, to):
    return pltpu.make_async_remote_copy(
        src_ref=src,
        dst_ref=dst,
        send_sem=ssem.at[i],
        recv_sem=rsem.at[i],
        device_id=to,
        device_id_type=MESH,
    )


def gather_body(wq, wo, wg, wd, og, WQ, WO, WG, WD, OG, ssem, rsem):
    p = Place()
    k = Links(ssem, rsem)
    m = p.z * 2 + p.c
    partners = [p.step(a, j) for a in "xyz" for j in (1, 2, 3)]
    partners += [p.at(z=(p.z + j) % 4, c=1 - p.c) for j in range(4)]
    slab_to, slab_from = slab_target(p), slab_source(p)
    own_slab = same(p, slab_to)
    greet_plane(p, partners, slab_to, slab_from, own_slab)

    yh, x, yl, z, c = p.yh, p.x, p.yl, p.z, p.c
    local = [
        k.local(wq, WQ.at[yh, x, yl, z, c]),
        k.local(wo, WO.at[yh, x, yl, z, c]),
        k.local(og, OG.at[z, c]),
    ]
    pieces = []
    for dz in range(4):
        for dc in range(2):
            zz, cc = (z + dz) % 4, (c + dc) % 2
            mm = zz * 2 + cc
            for half in range(2):
                src = wg.at[:, pl.ds(pl.multiple_of(half * FF + mm * FS, 128), FS)]
                dst = WG.at[yh, x, yl, m, :, pl.ds(half * FS, FS)]
                if dz == 0 and dc == 0:
                    local.append(k.local(src, dst))
                else:
                    pieces.append(k.send(src, dst, p.at(z=zz, c=cc)))
    slab_dst = WD.at[yl, z, c]
    i = k.used
    k.used += 1

    @pl.when(own_slab)
    def _():
        pltpu.make_async_copy(wd, slab_dst, rsem.at[i]).start()

    slab = slab_copy(wd, slab_dst, ssem, rsem, i, slab_to)

    @pl.when(jnp.logical_not(own_slab))
    def _():
        slab.start()

    def wq_a(*at):
        return WQ.at[(*at, slice(None), pl.ds(0, 1024))]

    def wq_b(*at):
        return WQ.at[(*at, slice(None), pl.ds(1024, 1024))]

    def wo_(*at):
        return WO.at[(*at, slice(None), slice(None))]

    every = slice(None)
    first = []
    for j in (1, 2, 3):
        first.append(k.send(wq.at[:, pl.ds(0, 1024)], wq_a(yh, x, yl, z, c), p.step("y", j)))
        first.append(k.send(wq.at[:, pl.ds(1024, 1024)], wq_b(yh, x, yl, z, c), p.step("z", j)))
        first.append(k.send(wo, wo_(yh, x, yl, z, c), p.step("x", j)))
    rows = [k.send(og, OG.at[z, c], p.step("z", j)) for j in (1, 2, 3)]
    rows_core = k.send(og, OG.at[z, c], p.step("c", 1))

    for copy in local:
        copy.wait()
    for copy in pieces:
        copy.wait_recv()

    @pl.when(own_slab)
    def _():
        pltpu.make_async_copy(wd, slab_dst, rsem.at[i]).wait()

    @pl.when(jnp.logical_not(own_slab))
    def _():
        slab.wait_recv()

    lo, hi = pl.ds(0, FS), pl.ds(FS, FS)
    dlo, dhi = pl.ds(0, 512), pl.ds(512, 512)
    mine_lo = WG.at[yh, x, yl, :, :, lo]
    mine_hi = WG.at[yh, x, yl, :, :, hi]
    slab_lo = WD.at[yl, x, yh, :, dlo]
    slab_hi = WD.at[yl, x, yh, :, dhi]
    plane = []
    for j in (1, 2, 3):
        plane.append(k.send(mine_lo, mine_lo, p.step("x", j)))
        plane.append(k.send(mine_hi, mine_hi, p.step("y", j)))
        plane.append(k.send(slab_lo, slab_lo, p.step("x", j)))
        plane.append(k.send(slab_hi, slab_hi, p.step("y", j)))

    for copy in first:
        copy.wait_recv()
    second = []
    for j in (1, 2, 3):
        src = wq_a(every, x, every, z, c)
        second.append(k.send(src, src, p.step("z", j)))
        src = wq_b(yh, x, yl, every, c)
        second.append(k.send(src, src, p.step("x", j)))
        src = wo_(yh, every, yl, z, c)
        second.append(k.send(src, src, p.step("y", j)))

    for copy in plane:
        copy.wait_recv()
    plane2 = []
    for j in (1, 2, 3):
        src = WG.at[yh, :, yl, :, :, lo]
        plane2.append(k.send(src, src, p.step("y", j)))
        src = WG.at[:, x, :, :, :, hi]
        plane2.append(k.send(src, src, p.step("x", j)))
        src = WD.at[yl, :, yh, :, dlo]
        plane2.append(k.send(src, src, p.step("y", j)))
        src = WD.at[:, x, :, :, dhi]
        plane2.append(k.send(src, src, p.step("x", j)))

    for copy in second:
        copy.wait_recv()
    third = []
    for j in (1, 2, 3):
        src = wq_a(every, x, every, every, c)
        third.append((k.send(src, src, p.step("x", j)), wq_a(every, p.pos("x", -j), every, every, c)))
        src = wq_b(yh, every, yl, every, c)
        yy = p.pos("y", -j)
        third.append(
            (k.send(src, src, p.step("y", j)), wq_b(yy // 2, every, yy % 2, every, c))
        )
        src = wo_(every, every, every, z, c)
        third.append((k.send(src, src, p.step("z", j)), wo_(every, every, every, p.pos("z", -j), c)))
    last = []
    for src in (wq_a(every, x, every, every, c), wq_b(yh, every, yl, every, c), wo_(every, every, every, z, c)):
        last.append(k.send(src, src, p.step("c", 1)))
    for j, copy in zip((1, 2, 3), rows):
        copy.wait_recv()
        src = OG.at[p.pos("z", -j), c]
        last.append(k.send(src, src, p.step("c", 1)))
    for copy, src in third:
        copy.wait_recv()
        last.append(k.send(src, src, p.step("c", 1)))
    for copy in plane2 + last + [rows_core]:
        copy.wait_recv()
    k.drain()

    @pl.when(jnp.logical_not(own_slab))
    def _():
        slab.wait_send()


def gather_weights(wq, wo, wg, wd, og):
    outs = [
        sds((2, 4, 2, 4, 2, 16, 2048), BF16),
        sds((2, 4, 2, 4, 2, 16, QD), BF16),
        sds((2, 4, 2, 8, 16, 2 * FS), BF16),
        sds((2, 4, 2, 80, 1024), BF16),
        sds((4, 2, TOK, D), BF16),
    ]
    return any_call(gather_body, "gather_weights", 0, 5, outs, [], 100)(wq, wo, wg, wd, og)


def kv_gather_body(kv, KV, ssem, rsem):
    p = Place()
    k = Links(ssem, rsem)
    yl, z, c = p.yl, p.z, p.c
    partner = p.at(y=p.yh * 2 + 1 - yl)
    greet([p.step("z", j) for j in (1, 2, 3)] + [partner, p.step("c", 1)])
    own = k.local(kv, KV.at[:, yl, z, c])
    across = k.send(kv, KV.at[:, yl, z, c], partner)
    ring = [k.send(kv, KV.at[:, yl, z, c], p.step("z", j)) for j in (1, 2, 3)]
    across.wait_recv()
    src = KV.at[:, 1 - yl, z, c]
    ring += [k.send(src, src, p.step("z", j)) for j in (1, 2, 3)]
    own.wait()
    for copy in ring:
        copy.wait_recv()
    src = KV.at[:, :, :, c]
    core = k.send(src, src, p.step("c", 1))
    core.wait_recv()
    k.drain()


def kv_gather(kv):
    outs = [sds((2, 2, 4, 2, ROWS, 2 * KD), BF16)]
    return any_call(kv_gather_body, "kv_gather", 1, 1, outs, [], 10)(kv)[0]


def kv_reduce_body(part, out, own, r0, s0, r1, s1, r2, res, ssem, rsem):
    p = Place()
    k = Links(ssem, rsem)
    yl, z, c = p.yl, p.z, p.c
    partner = p.at(y=p.yh * 2 + 1 - yl)
    greet([p.step("z", j) for j in (1, 2, 3)] + [partner, p.step("c", 1)])
    core = k.send(part.at[:, :, :, 1 - c], r0, p.step("c", 1))
    mine = k.local(part.at[:, :, :, c], own)
    mine.wait()
    core.wait_recv()

    @pl.loop(0, 4)
    def _(zz):
        for a in range(2):
            for b in range(2):
                s0[a, b, zz] = (own[a, b, zz].astype(F32) + r0[a, b, zz].astype(F32)).astype(BF16)

    ring = []
    for j in (1, 2, 3):
        zz = p.pos("z", j)
        ring.append(k.send(s0.at[:, :, zz], r1.at[j - 1], p.step("z", j)))
    for copy in ring:
        copy.wait_recv()
    for a in range(2):
        for b in range(2):
            total = s0[a, b, z].astype(F32)
            for j in range(3):
                total = total + r1[j, a, b].astype(F32)
            s1[a, b] = total.astype(BF16)
    across = k.send(s1.at[:, 1 - yl], r2, partner)
    across.wait_recv()
    for a in range(2):
        res[a] = s1[a, yl].astype(F32) + r2[a].astype(F32)
    done = k.local(res, out)
    done.wait()
    k.drain()


def kv_reduce(part):
    w = 2 * KD
    scratch = [
        pltpu.VMEM((2, 2, 4, ROWS, w), BF16),
        pltpu.VMEM((2, 2, 4, ROWS, w), BF16),
        pltpu.VMEM((2, 2, 4, ROWS, w), BF16),
        pltpu.VMEM((3, 2, 2, ROWS, w), BF16),
        pltpu.VMEM((2, 2, ROWS, w), BF16),
        pltpu.VMEM((2, ROWS, w), BF16),
        pltpu.VMEM((2, ROWS, w), F32),
    ]
    outs = [sds((2, ROWS, w), F32)]
    return any_call(kv_reduce_body, "kv_reduce", 2, 1, outs, scratch, 10)(part)[0]


def row_gather_body(rows, ALL, ssem, rsem):
    p = Place()
    k = Links(ssem, rsem)
    z, c = p.z, p.c
    greet([p.step("z", j) for j in (1, 2, 3)] + [p.step("c", 1)])
    own = k.local(rows, ALL.at[z, c])
    ring = [k.send(rows, ALL.at[z, c], p.step("z", j)) for j in (1, 2, 3)]
    core = [k.send(rows, ALL.at[z, c], p.step("c", 1))]
    for j, copy in zip((1, 2, 3), ring):
        copy.wait_recv()
        src = ALL.at[p.pos("z", -j), c]
        core.append(k.send(src, src, p.step("c", 1)))
    own.wait()
    for copy in core:
        copy.wait_recv()
    k.drain()


def row_gather(rows):
    outs = [sds((4, 2, TOK, D), BF16)]
    return any_call(row_gather_body, "row_gather", 3, 1, outs, [], 10)(rows)[0]


def row_reduce(p, k, part, own, r0, s0, r1, res):
    z, c = p.z, p.c
    core = k.send(part.at[:, 1 - c], r0, p.step("c", 1))
    mine = k.local(part.at[:, c], own)
    yield
    mine.wait()
    core.wait_recv()

    @pl.loop(0, 4)
    def _(zz):
        @pl.loop(0, TOK, step=32)
        def _(t):
            at = pl.ds(pl.multiple_of(t, 32), 32)
            s0[zz, at] = (own[zz, at].astype(F32) + r0[zz, at].astype(F32)).astype(BF16)

    ring = [k.send(s0.at[p.pos("z", j)], r1.at[j - 1], p.step("z", j)) for j in (1, 2, 3)]
    yield
    for copy in ring:
        copy.wait_recv()

    @pl.loop(0, TOK, step=32)
    def _(t):
        at = pl.ds(pl.multiple_of(t, 32), 32)
        total = s0[z, at].astype(F32)
        for j in range(3):
            total = total + r1[j, at].astype(F32)
        res[at] = total


def row_scratch():
    return [
        pltpu.VMEM((4, TOK, D), BF16),
        pltpu.VMEM((4, TOK, D), BF16),
        pltpu.VMEM((4, TOK, D), BF16),
        pltpu.VMEM((3, TOK, D), BF16),
        pltpu.VMEM((TOK, D), F32),
    ]


def row_reduce_body(part, out, own, r0, s0, r1, res, ssem, rsem):
    p = Place()
    k = Links(ssem, rsem)
    greet([p.step("z", j) for j in (1, 2, 3)] + [p.step("c", 1)])
    for _ in row_reduce(p, k, part, own, r0, s0, r1, res):
        pass
    done = k.local(res, out)
    done.wait()
    k.drain()


def row_reduce_call(part):
    outs = [sds((TOK, D), F32)]
    return any_call(row_reduce_body, "row_reduce", 4, 1, outs, row_scratch(), 10)(part)[0]


def pair_body(n, *refs):
    ins, outs = refs[:n], refs[n : 2 * n]
    ssem, rsem = refs[2 * n :]
    p = Place()
    k = Links(ssem, rsem)
    greet([p.step("c", 1)])
    copies = [k.send(i, o.at[1], p.step("c", 1)) for i, o in zip(ins, outs)]
    local = [k.local(i, o.at[0]) for i, o in zip(ins, outs)]
    for copy in local:
        copy.wait()
    for copy in copies:
        copy.wait_recv()
    k.drain()


def pair_exchange(*arrays):
    n = len(arrays)
    outs = [sds((2, *a.shape), a.dtype) for a in arrays]

    def body(*refs):
        pair_body(n, *refs)

    return any_call(body, "pair_exchange", 5, n, outs, [], 2 * n)(*arrays)


def add_blocks(dst, own, recv, chunk):
    lead, rows = dst.shape[:-2], dst.shape[-2]
    count = 1
    for n in lead:
        count *= n

    @pl.loop(0, count)
    def _(i):
        at = []
        rest = i
        for n in reversed(lead):
            at.insert(0, rest % n)
            rest = rest // n

        @pl.loop(0, rows, step=chunk)
        def _(t):
            here = (*at, pl.ds(pl.multiple_of(t, chunk), chunk))
            total = own[here].astype(F32)
            for j in range(3):
                total = total + recv[(j, *here)].astype(F32)
            dst[here] = total.astype(dst.dtype)


def staged_reduce(p, k, src, stages, scr, chunk):
    own = scr[0]
    cur = src
    for n, (axis, pick) in enumerate(stages):
        recv, total = scr[1 + 2 * n], scr[2 + 2 * n]
        if n == 0:
            mine = k.local(pick(src, p.pos(axis, 0)), own)
        ring = [k.send(pick(cur, p.pos(axis, j)), recv.at[j - 1], p.step(axis, j)) for j in (1, 2, 3)]
        yield
        if n == 0:
            mine.wait()
        for copy in ring:
            copy.wait_recv()
        add_blocks(total, own if n == 0 else pick(cur, p.pos(axis, 0)), recv, chunk)
        cur = total


def staged_scratch(shapes):
    out = [pltpu.VMEM(shapes[0], BF16)]
    for n, shape in enumerate(shapes):
        out.append(pltpu.VMEM((3, *shape), BF16))
        out.append(pltpu.VMEM(shape, F32 if n == len(shapes) - 1 else BF16))
    return out


EVERY = slice(None)


def cols_at(start, size):
    return pl.ds(start, size)


def wg_stages(half):
    cols = pl.ds(half * FS, FS)
    if half == 0:
        return [
            ("y", lambda r, i: r.at[i // 2, :, i % 2, :, cols]),
            ("x", lambda r, i: r.at[i]),
        ]
    return [
        ("x", lambda r, i: r.at[:, i, :, :, cols]),
        ("y", lambda r, i: r.at[i // 2, i % 2]),
    ]


def wd_stages(half):
    cols = pl.ds(half * 512, 512)
    if half == 0:
        return [
            ("y", lambda r, i: r.at[i % 2, :, i // 2, :, cols]),
            ("x", lambda r, i: r.at[i]),
        ]
    return [
        ("x", lambda r, i: r.at[:, i, :, :, cols]),
        ("y", lambda r, i: r.at[i % 2, i // 2]),
    ]


def q_stages(half):
    cols = pl.ds(half * 512, 512)
    if half == 0:
        return [
            ("x", lambda r, i: r.at[:, i, :, :, :, cols]),
            ("z", lambda r, i: r.at[:, :, i]),
            ("y", lambda r, i: r.at[i // 2, i % 2]),
        ]
    return [
        ("y", lambda r, i: r.at[i // 2, :, i % 2, :, :, cols]),
        ("x", lambda r, i: r.at[i]),
        ("z", lambda r, i: r.at[i]),
    ]


def o_stages():
    return [
        ("z", lambda r, i: r.at[:, :, :, i]),
        ("y", lambda r, i: r.at[i // 2, :, i % 2]),
        ("x", lambda r, i: r.at[i]),
    ]


GRAD_SHAPES = [
    [(4, 128, FS), (128, FS)],
    [(2, 2, 128, FS), (128, FS)],
    [(4, 80, 512), (80, 512)],
    [(2, 2, 80, 512), (80, 512)],
    [(2, 2, 4, 32, 512), (2, 2, 32, 512), (32, 512)],
    [(4, 4, 32, 512), (4, 32, 512), (32, 512)],
    [(2, 4, 2, 32, 640), (4, 32, 640), (32, 640)],
]


def small_reduce(p, k, part, vec, recv):
    mine = k.local(part, vec.at[0])
    mine.wait()
    for n, axis in enumerate("xyzc"):
        steps = (1,) if axis == "c" else (1, 2, 3)
        ring = [k.send(vec.at[n], recv.at[n, j - 1], p.step(axis, j)) for j in steps]
        yield
        for copy in ring:
            copy.wait_recv()
        total = vec[n]
        for j in range(len(steps)):
            total = total + recv[n, j]
        vec[n + 1] = total


def grads_body(*refs):
    dwg, dwd, dq, do, dmix, small, GWG, GWD, GQ, GO, MIX, SMALL = refs[:12]
    scr = list(refs[12:])
    parts = []
    for shapes in GRAD_SHAPES:
        n = 1 + 2 * len(shapes)
        parts.append(scr[:n])
        scr = scr[n:]
    mix, (vec, recv), (ssem, rsem) = scr[:5], scr[5:7], scr[7:9]
    p = Place()
    k = Links(ssem, rsem)
    yh, x, yl, z, c = p.yh, p.x, p.yl, p.z, p.c
    m = z * 2 + c
    partners = [p.step(a, j) for a in "xyz" for j in (1, 2, 3)]
    partners += [p.at(z=(z + j) % 4, c=1 - c) for j in range(4)]
    slab_to, slab_from = slab_target(p), slab_source(p)
    own_slab = same(p, slab_to)
    greet_plane(p, partners, slab_to, slab_from, own_slab)

    chunk = 16
    gens = [
        staged_reduce(p, k, dwg, wg_stages(0), parts[0], chunk),
        staged_reduce(p, k, dwg, wg_stages(1), parts[1], chunk),
        staged_reduce(p, k, dwd, wd_stages(0), parts[2], chunk),
        staged_reduce(p, k, dwd, wd_stages(1), parts[3], chunk),
        row_reduce(p, k, dmix, *mix),
        staged_reduce(p, k, do, o_stages(), parts[6], chunk),
        staged_reduce(p, k, dq, q_stages(0), parts[4], chunk),
        staged_reduce(p, k, dq, q_stages(1), parts[5], chunk),
        small_reduce(p, k, small, vec, recv),
    ]
    alive = list(gens)
    while alive:
        alive = [g for g in alive if next(g, alive) is not alive]

    last, local = [], []
    for half in range(2):
        total = parts[half][-1]
        cols = pl.ds(pl.multiple_of(half * FF + m * FS, 128), FS)
        for dz in range(4):
            for dc in range(2):
                zz, cc = (z + dz) % 4, (c + dc) % 2
                src = total.at[pl.ds(pl.multiple_of((zz * 2 + cc) * 16, 16), 16)]
                if dz == 0 and dc == 0:
                    local.append(k.local(src, GWG.at[:, cols]))
                else:
                    last.append(k.send(src, GWG.at[:, cols], p.at(z=zz, c=cc)))
    slabs = []
    for half in range(2):
        i = k.used
        k.used += 1
        src, dst = parts[2 + half][-1], GWD.at[:, pl.ds(half * 512, 512)]
        slabs.append((src, dst, i))

        @pl.when(own_slab)
        def _(src=src, dst=dst, i=i):
            pltpu.make_async_copy(src, dst, rsem.at[i]).start()

        @pl.when(jnp.logical_not(own_slab))
        def _(src=src, dst=dst, i=i):
            slab_copy(src, dst, ssem, rsem, i, slab_from).start()

    for total, dst in (
        (parts[4][-1], GQ.at[c, :, pl.ds(0, 512)]),
        (parts[5][-1], GQ.at[c, :, pl.ds(512, 512)]),
        (parts[6][-1], GO.at[c]),
    ):
        mine = total.at[pl.ds(pl.multiple_of(c * 16, 16), 16)]
        other = total.at[pl.ds(pl.multiple_of((1 - c) * 16, 16), 16)]
        local.append(k.local(mine, dst))
        last.append(k.send(other, dst, p.step("c", 1)))
    local.append(k.local(mix[-1], MIX))
    local.append(k.local(vec.at[4], SMALL))
    for copy in local:
        copy.wait()
    for copy in last:
        copy.wait_recv()
    for src, dst, i in slabs:

        @pl.when(own_slab)
        def _(src=src, dst=dst, i=i):
            pltpu.make_async_copy(src, dst, rsem.at[i]).wait()

        @pl.when(jnp.logical_not(own_slab))
        def _(src=src, dst=dst, i=i):
            slab_copy(src, dst, ssem, rsem, i, slab_from).wait()

    k.drain()


def reduce_grads(dwg, dwd, dq, do, dmix, small):
    outs = [
        sds((16, 2 * FF), F32),
        sds((80, 1024), F32),
        sds((2, 16, 1024), F32),
        sds((2, 16, 640), F32),
        sds((TOK, D), F32),
        sds((40, 128), F32),
    ]
    scratch = []
    for shapes in GRAD_SHAPES:
        scratch += staged_scratch(shapes)
    scratch += row_scratch()
    scratch += [pltpu.VMEM((5, 40, 128), F32), pltpu.VMEM((4, 3, 40, 128), F32)]
    return any_call(grads_body, "reduce_grads", 6, 6, outs, scratch, 110, 56 << 20)(
        dwg, dwd, dq, do, dmix, small
    )


def rms_scale(values):
    return lax.rsqrt(jnp.mean(values * values, axis=-1, keepdims=True) + EPS)


def rotate(values):
    half = values.shape[-1] // 2
    return jnp.concatenate([-values[..., half:], values[..., :half]], axis=-1)


def rotate_back(values):
    half = values.shape[-1] // 2
    return jnp.concatenate([values[..., half:], -values[..., :half]], axis=-1)


def norm_back(upstream, normed, scale, gain):
    scaled = upstream * gain
    inner = jnp.mean(scaled * normed, axis=-1, keepdims=True)
    return scale * (scaled - normed * inner)


def dot(left, right):
    return jnp.dot(left, right, preferred_element_type=F32)


def dot_last(left, right):
    return lax.dot_general(left, right, (((1,), (1,)), ((), ())), preferred_element_type=F32)


def dot_rows(left, right):
    return lax.dot_general(left, right, (((0,), (0,)), ((), ())), preferred_element_type=F32)


def rope_tables(positions):
    half = HEAD // 2
    inverse = 10000.0 ** (-jnp.arange(half, dtype=F32) / half)
    angles = positions[:, None] * inverse[None, :]
    angles = jnp.concatenate([angles, angles], axis=1)
    return (jnp.cos(angles)[:, None, :], jnp.sin(angles)[:, None, :])


def per_device(
    tokens,
    segment_ids,
    w_qkv,
    w_out,
    w_gate_up,
    w_down,
    attn_gain,
    ffn_gain,
    query_gain,
    key_gain,
    out_grad,
):
    s = lax.axis_index("seq")
    g = lax.axis_index("grp")
    c = s % 2
    start = s * ROWS
    query_gain = query_gain.astype(F32)
    key_gain = key_gain.astype(F32)
    gains = jnp.stack([attn_gain, ffn_gain], axis=1)
    wq_in = jnp.concatenate([w_qkv, jnp.pad(gains, ((0, 0), (0, 126)))], axis=1)
    og_in = out_grad.reshape(TOK, D)
    WQ, WO, WG, WD, OG = gather_weights(
        wq_in, w_out.T, w_gate_up, w_down.reshape(80, 1024), og_in
    )
    WQ = WQ.reshape(D, 2048)
    WO = WO.reshape(D, QD)
    WG = WG.reshape(D, 2 * FS)
    WD = WD.reshape(FS, D)
    OG = OG.reshape(8 * TOK, D)
    gain_one = WQ[:, QKV].astype(F32)
    gain_two = WQ[:, QKV + 1].astype(F32)

    hidden = tokens.reshape(TOK, D).astype(F32)
    scale_one = rms_scale(hidden)
    norm_one = hidden * scale_one
    normed = (norm_one * gain_one).astype(BF16)
    packed = dot(normed, WQ)
    query_raw = packed[:, :QD].reshape(TOK, Q_HEADS, HEAD)
    key_raw = packed[:, QD : QD + KD].reshape(TOK, KV_HEADS, HEAD)
    value_raw = packed[:, QD + KD : QKV]
    query_scale = rms_scale(query_raw)
    query_norm = query_raw * query_scale
    key_scale = rms_scale(key_raw)
    key_norm = key_raw * key_scale
    query_head = query_norm * query_gain
    key_head = key_norm * key_gain
    positions = (start + jnp.arange(ROWS)).astype(F32)
    positions = jnp.concatenate([positions] * MICRO)
    cosine, sine = rope_tables(positions)
    queries = (query_head * cosine + rotate(query_head) * sine).astype(BF16)
    keys_local = (key_head * cosine + rotate(key_head) * sine).astype(BF16)
    kv_local = jnp.concatenate([keys_local.reshape(TOK, KD), value_raw.astype(BF16)], axis=1)
    kv = kv_gather(kv_local.reshape(MICRO, ROWS, 2 * KD)).reshape(MICRO, SEQ, 2 * KD)
    keys = kv[:, :, :KD].reshape(MICRO, SEQ, KV_HEADS, HEAD)
    values = kv[:, :, KD:].reshape(MICRO, SEQ, KV_HEADS, HEAD)
    grouped = queries.reshape(MICRO, ROWS, KV_HEADS, GROUP, HEAD)
    query_ids = lax.dynamic_slice_in_dim(segment_ids, start, ROWS, axis=1)
    query_pos = start + jnp.arange(ROWS)
    key_pos = jnp.arange(SEQ)
    allowed = (
        (key_pos[None, None, :] <= query_pos[None, :, None])
        & (segment_ids[:, None, :] == query_ids[:, :, None])
        & (query_ids[:, :, None] >= 0)
    )
    allowed = allowed | (key_pos[None, None, :] == query_pos[None, :, None])
    factor = HEAD ** (-0.5)
    scores = (
        jnp.einsum("mtgjd,msgd->mgjts", grouped, keys, preferred_element_type=F32) * factor
    )
    scores = jnp.where(allowed[:, None, None], scores, -1e30)
    peak = jnp.max(scores, axis=-1, keepdims=True)
    raised = jnp.exp(scores - peak)
    row_total = jnp.sum(raised, axis=-1, keepdims=True)
    log_total = peak + jnp.log(row_total)
    probs = (raised / row_total).astype(BF16)
    attended = jnp.einsum("mgjts,msgd->mtgjd", probs, values, preferred_element_type=F32)
    attended = attended.reshape(TOK, QD).astype(BF16)
    resid = hidden + dot_last(attended, WO)
    scale_two = rms_scale(resid)
    norm_two = resid * scale_two
    normed_ffn = (norm_two * gain_two).astype(BF16)

    rows = row_gather(normed_ffn).reshape(8 * TOK, D)
    gate_up = dot(rows, WG)
    gate = gate_up[:, :FS]
    upper = gate_up[:, FS:]
    sigmoid_gate = jax.nn.sigmoid(gate)
    active = gate * sigmoid_gate
    inner = (active * upper).astype(BF16)
    mixed_part = dot(inner, WD).astype(BF16)
    d_inner = dot_last(OG, WD)
    d_gate = d_inner * upper * sigmoid_gate * (1.0 + gate * (1.0 - sigmoid_gate))
    d_upper = d_inner * active
    d_gate_up = jnp.concatenate([d_gate, d_upper], axis=1).astype(BF16)
    d_rows_part = dot_last(d_gate_up, WG).astype(BF16)
    grad_gate_up = dot_rows(rows, d_gate_up).astype(BF16)
    grad_down = dot_rows(inner, OG).astype(BF16)

    d_normed_ffn = row_reduce_call(d_rows_part.reshape(4, 2, TOK, D))
    upstream = og_in.astype(F32)
    ffn_term = jnp.sum(d_normed_ffn * norm_two, axis=0)
    d_resid = upstream + norm_back(d_normed_ffn, norm_two, scale_two, gain_two)
    resid_low = d_resid.astype(BF16)
    d_attended = dot(resid_low, WO).astype(BF16)
    d_attended = d_attended.reshape(MICRO, ROWS, KV_HEADS, GROUP, HEAD)
    again = jnp.exp(scores - log_total)
    again_low = again.astype(BF16)
    d_probs = jnp.einsum("mtgjd,msgd->mgjts", d_attended, values, preferred_element_type=F32)
    d_values = jnp.einsum("mgjts,mtgjd->msgd", again_low, d_attended, preferred_element_type=F32)
    row_inner = jnp.sum(again * d_probs, axis=-1, keepdims=True)
    d_scores = (again * (d_probs - row_inner)).astype(BF16)
    d_queries = (
        jnp.einsum("mgjts,msgd->mtgjd", d_scores, keys, preferred_element_type=F32) * factor
    )
    d_keys = (
        jnp.einsum("mgjts,mtgjd->msgd", d_scores, grouped, preferred_element_type=F32) * factor
    )
    kv_terms = jnp.concatenate(
        [d_keys.reshape(MICRO, SEQ, KD), d_values.reshape(MICRO, SEQ, KD)], axis=2
    ).astype(BF16)
    kv_grads = kv_reduce(kv_terms.reshape(MICRO, 2, 4, 2, ROWS, 2 * KD)).reshape(TOK, 2 * KD)
    key_grad = kv_grads[:, :KD].reshape(TOK, KV_HEADS, HEAD)
    value_grad = kv_grads[:, KD:]
    query_grad = d_queries.reshape(TOK, Q_HEADS, HEAD)
    d_query_head = query_grad * cosine + rotate_back(query_grad * sine)
    d_key_head = key_grad * cosine + rotate_back(key_grad * sine)
    query_term = jnp.sum(d_query_head * query_norm, axis=(0, 1))
    key_term = jnp.sum(d_key_head * key_norm, axis=(0, 1))
    d_query_raw = norm_back(d_query_head, query_norm, query_scale, query_gain)
    d_key_raw = norm_back(d_key_head, key_norm, key_scale, key_gain)
    d_packed = jnp.concatenate(
        [d_query_raw.reshape(TOK, QD), d_key_raw.reshape(TOK, KD), value_grad], axis=1
    ).astype(BF16)
    d_normed = dot_last(d_packed, WQ[:, :QKV])
    attn_term = jnp.sum(d_normed * norm_one, axis=0)
    input_grad = d_resid + norm_back(d_normed, norm_one, scale_one, gain_one)

    pair = pair_exchange(normed, d_packed, attended, resid_low)
    normed_2, packed_2, attended_2, low_2 = [a.reshape(2 * TOK, -1) for a in pair]
    packed_cols = lax.dynamic_slice_in_dim(packed_2, c * 896, 1024, axis=1)
    attended_cols = lax.dynamic_slice_in_dim(attended_2, c * 640, 640, axis=1)
    grad_q = dot_rows(normed_2, packed_cols).astype(BF16)
    grad_o = dot_rows(low_2, attended_cols).astype(BF16)

    small = jnp.concatenate(
        [
            attn_term.reshape(16, 128),
            ffn_term.reshape(16, 128),
            jnp.pad(jnp.concatenate([query_term, key_term]).reshape(1, 128), ((0, 7), (0, 0))),
        ],
        axis=0,
    )
    gwg, gwd, gq, go, mix, sums = reduce_grads(
        grad_gate_up.reshape(2, 4, 2, 128, 2 * FS),
        grad_down.reshape(2, 4, 2, 80, 1024),
        grad_q.reshape(2, 4, 2, 4, 32, 1024),
        grad_o.reshape(2, 4, 2, 4, 32, 640),
        mixed_part.reshape(4, 2, TOK, D),
        small,
    )
    result = (resid + mix).astype(BF16)
    w_qkv_grad = jnp.concatenate([gq[0], gq[1][:, 128:]], axis=1)
    w_out_grad = jnp.concatenate([go[0], go[1]], axis=1).T
    at = (g * 16 + s) * 16
    attn_sum = lax.dynamic_slice_in_dim(sums[:16].reshape(D), at, 16)
    ffn_sum = lax.dynamic_slice_in_dim(sums[16:32].reshape(D), at, 16)
    return (
        result.reshape(MICRO, ROWS, D),
        input_grad.reshape(MICRO, ROWS, D),
        w_qkv_grad,
        w_out_grad,
        gwg,
        gwd.reshape(40, D),
        attn_sum,
        ffn_sum,
        sums[32, :HEAD],
        sums[32, HEAD:],
    )


def solution(mesh):
    return jax.shard_map(
        per_device,
        mesh=mesh,
        in_specs=(
            P(None, ("grp", "seq"), None),
            P(None, "grp"),
            P(("grp", "seq"), None),
            P(None, ("grp", "seq")),
            P(("grp", "seq"), None),
            P(("grp", "seq"), None),
            P(("grp", "seq")),
            P(("grp", "seq")),
            P(),
            P(),
            P(None, ("grp", "seq"), None),
        ),
        out_specs=(
            P(None, ("grp", "seq"), None),
            P(None, ("grp", "seq"), None),
            P(("grp", "seq"), None),
            P(None, ("grp", "seq")),
            P(("grp", "seq"), None),
            P(("grp", "seq"), None),
            P(("grp", "seq")),
            P(("grp", "seq")),
            P(),
            P(),
        ),
        check_vma=False,
    )
```

time: 3980 us -> 629 us (0.16)
  waiting for transfers between devices: 3470 us -> 0 us
  Pallas kernels: 0 us -> 360 us
  blocking collectives: 138 us -> 0 us
  matrix products: 243 us -> 107 us
  local copies, waits for them, and re-layouts: 63.4 us -> 117 us
    reduce_scatter x6 -> x0, waiting for transfers between devices: 2670 us -> none  [the longest x1 777 us: per_device(): lax.psum_scatter(grad_gate_up, ('grp', 'seq'), scatter_dimension=0, tiled...]
    all_gather x6 -> x0, waiting for transfers between devices: 801 us -> none  [the longest x1 239 us: per_device(): lax.all_gather(local[2], ('grp', 'seq'), axis=0, tiled=True)]
    pallas_call x0 -> x7, Pallas kernels: none -> 360 us  [the longest x1 125 us: reduce_grads(): any_call(grads_body, 'reduce_grads', 6, 6, outs, scratch, 110, 56 << 20)]
    unnamed x2 -> x0, blocking collectives: 138 us -> none
    dot_general x32 -> x18, matrix products: 243 us -> 107 us  [the longest x4 31.1 us: dot_last(): lax.dot_general(left, right, (((1,), (1,)), ((), ())), preferred_element_...]
  transfers between devices with their start and end apart: 12 -> 0, of which waited for: 11 -> 0; matrix products, arithmetic and copies ran while one was open for 6% -> 0% of each run, Pallas kernels for 0% -> 0%
where the time goes in v1:
time: 629 us; the launch traced here: 623 us
  Pallas kernels  360 us (57%)
  local copies, waits for them, and re-layouts  117 us (19%)
  matrix products  107 us (17%)
  other arithmetic  36.9 us (6%)
    pallas_call x1, Pallas kernels, reduce_grads(): any_call(grads_body, 'reduce_grads', 6, 6, outs, scratch, 110, 56 << 20)  125 us
    pallas_call x1, Pallas kernels, gather_weights(): any_call(gather_body, 'gather_weights', 0, 5, outs, [], 100)  113 us
    pallas_call x1, Pallas kernels, row_reduce_call(): any_call(row_reduce_body, 'row_reduce', 4, 1, outs, row_scratch(), 10)(part)  31.7 us
    dot_general x4, matrix products, dot_last(): lax.dot_general(left, right, (((1,), (1,)), ((), ())), preferred_element_...  31.1 us
    pallas_call x1, Pallas kernels, row_gather(): return any_call(row_gather_body, 'row_gather', 3, 1, outs, [], 10)(rows)[0]  29.6 us
    pallas_call x1, Pallas kernels, kv_gather(): return any_call(kv_gather_body, 'kv_gather', 1, 1, outs, [], 10)(kv)[0]  29.2 us
    pallas_call x1, Pallas kernels, kv_reduce(): any_call(kv_reduce_body, 'kv_reduce', 2, 1, outs, scratch, 10)(part)[0]  26.9 us
    concatenate x4, local copies, waits for them, and re-layouts, per_device(): jnp.concatenate([d_keys.reshape(MICRO, SEQ, KD), d_values.reshape(MICRO,...  24.9 us

profile of v1, /device:TPU:1, one launch (start us, length us, event | category | flops | bytes accessed | tf_op | source)
XLA Modules:
  0.0 623.2 jit_solution(7697824480217137607)
XLA Ops:
  6.0 113.3 %gather_weights.1 = (bf16[2,4,2,4,2,16,2048]{6,5,4,3,2,1,0:T(8,128)(2,1)}, bf16[2,4,2,4,2,16,1280]{6,5,4,3,2,1,0:T(8,128)(2,1)}, bf16[2,4,2,8,16,1280]{5,4,3,2,1...) custom-call(bf16[16,2048]{1,0:T(8,128)(2,1)S(1)} %fusion.27.wq, ...), custom_call_target="tpu_custom_call" | custom-call | tf_op jit(solution)/shard_map/gather_weights/pallas_call | solution.py:308
  124.2 4.7 fusion.45
  133.2 29.2 %kv_gather.1 = bf16[2,2,4,2,64,640]{5,4,3,2,1,0:T(8,128)(2,1)S(1)} custom-call(bf16[2,64,640]{2,1,0:T(8,128)(2,1)S(1)} %pad_maximum_fusion.5.kv), custom_call_target="tpu_custom_call" | custom-call | tf_op jit(solution)/shard_map/kv_gather/pallas_call | solution.py:334
  200.7 6.9 %fusion.23 = bf16[2,64,5,4,64]{1,4,3,2,0:T(8,128)(2,1)} fusion(bf16[2,1024,5,64,1]{1,3,4,2,0:T(8,128)(2,1)} %bitcast.226, f32[2,5,4,64]{3,2,1,0:T(4,128)S(1)} %fusion.3, f32[2,5,4,64]{3,2,1,0:T(4,128)S(1)} %get-tuple-element.85, f32[2,5,1024,64,4]{2,3,4,1,0:T(8,128)} %copy-done.11, pred[2,64,1024]{2,1,0:T(8,128)(4,1)S(1)} %and_or_fusion), kind=kOutput, calls=%fused_computation.45 | convolution fusion | flops 348815360 | bytes 12275712 | tf_op jit(solution)/shard_map/mgjts,msgd->mtgjd/dot_general | solution.py:848
  211.3 5.3 multiply_reduce_fusion.6
  219.5 29.6 %row_gather.1 = bf16[4,2,128,2048]{3,2,1,0:T(8,128)(2,1)S(1)} custom-call(bf16[128,2048]{1,0:T(8,128)(2,1)S(1)} %multiply_convert_fusion.4.rows), custom_call_target="tpu_custom_call" | custom-call | tf_op jit(solution)/shard_map/row_gather/pallas_call | solution.py:410
  249.1 10.6 %fusion.46 = f32[1024,1280]{0,1:T(8,128)} fusion(bf16[1024,2048]{1,0:T(8,128)(2,1)S(1)} %bitcast.199, bf16[2048,1280]{1,0:T(8,128)(2,1)} %bitcast.257), kind=kOutput, calls=%fused_computation.146 | convolution fusion | flops 5368709120 | bytes 14680064 | tf_op jit(solution)/shard_map/dot_general | solution.py:753
  262.6 9.5 %multiply_convert_fusion.2 = (bf16[1024,640]{0,1:T(8,128)(2,1)S(1)}, bf16[1024,640]{0,1:T(8,128)(2,1)S(1)}, bf16[1024,640]{0,1:T(8,128)(2,1)}) fusion(f32[1024,1280]{0,1:T(8,128)} %fusion.46, bf16[1024,2048]{1,0:T(8,128)(2,1)} %bitcast.259, bf16[640,2048]{1,0:T(8,128)(2,1)} %reshape.447), kind=kOutput, calls=%fused_computation.30 | convolution fusion | flops 2694184960 | bytes 15990784 | tf_op jit(solution)/shard_map/dot_general | solution.py:757
  272.1 9.4 %convolution_convert_fusion.3 = bf16[1024,2048]{1,0:T(8,128)(2,1)S(1)} fusion(bf16[2048,1280]{1,0:T(8,128)(2,1)} %bitcast.258, bf16[1024,640]{0,1:T(8,128)(2,1)S(1)} %get-tuple-element.51, bf16[1024,640]{0,1:T(8,128)(2,1)S(1)} %get-tuple-element.50), kind=kOutput, calls=%fused_computation.20 | convolution fusion | flops 5376049152 | bytes 12058624 | tf_op jit(solution)/shard_map/dot_general | solution.py:757
  281.5 31.7 %row_reduce.1 = f32[128,2048]{1,0:T(8,128)S(1)} custom-call(bf16[4,2,128,2048]{3,2,1,0:T(8,128)(2,1)S(1)} %bitcast.198), custom_call_target="tpu_custom_call" | custom-call | tf_op jit(solution)/shard_map/row_reduce/pallas_call | solution.py:465
  318.7 7.2 %fusion = (f32[2,5,4,64]{3,2,1,0:T(4,128)S(1)}, f32[2,5,1024,64,4]{2,3,4,1,0:T(8,128)S(1)}) fusion(f32[2,5,4,64]{3,2,1,0:T(4,128)S(1)} %log_add_fusion, f32[2,5,1024,64,4]{2,3,4,1,0:T(8,128)} %copy-done.11, pred[2,64,1024]{2,1,0:T(8,128)(4,1)S(1)} %copy-done.27, bf16[2,1024,5,64,1]{1,3,4,2,0:T(8,128)(2,1)} %bitcast.227, bf16[2,64,5,4,64]{1,4,3,2,0:T(8,128)(2,1)} %copy.175), kind=kOutput, calls=%fused_computation.2 | convolution fusion | flops 348648960 | bytes 22761472 | tf_op jit(solution)/shard_map/mtgjd,msgd->mgjts/dot_general | solution.py:880
  333.6 6.2 concatenate.108
  339.8 6.3 %copy.176 = bf16[2,2,4,2,64,320]{5,4,3,2,1,0:T(8,128)(2,1)} copy(bf16[2,2,4,2,64,320]{4,3,2,1,5,0:T(2,128)(2,1)} %concatenate.108) | data formatting | bytes 2621440 | tf_op jit(solution)/shard_map/concatenate | solution.py:890
  346.1 7.8 %fusion.16 = bf16[2,1024,5,64]{1,3,2,0:T(8,128)(2,1)} fusion(bf16[2,64,5,4,64]{1,4,3,2,0:T(8,128)(2,1)S(1)} %copy-done.29, f32[2,5,4,64]{3,2,1,0:T(4,128)S(1)} %log_add_fusion, f32[2,5,1024,64,4]{2,3,4,1,0:T(8,128)} %copy-done.11, pred[2,64,1024]{2,1,0:T(8,128)(4,1)S(1)} %copy-done.27), kind=kOutput, calls=%fused_computation.35 | convolution fusion | flops 346685440 | bytes 12265472 | tf_op jit(solution)/shard_map/mgjts,mtgjd->msgd/dot_general | solution.py:881
  354.0 6.1 concatenate.109
  360.1 6.3 %copy.177 = bf16[2,2,4,2,64,320]{5,4,3,2,1,0:T(8,128)(2,1)} copy(bf16[2,2,4,2,64,320]{4,3,2,1,5,0:T(2,128)(2,1)} %concatenate.109) | data formatting | bytes 2621440 | tf_op jit(solution)/shard_map/concatenate | solution.py:890
  369.4 26.9 %kv_reduce.1 = f32[2,64,640]{2,1,0:T(8,128)S(1)} custom-call(bf16[2,2,4,2,64,640]{5,4,3,2,1,0:T(8,128)(2,1)S(1)} %pad_maximum_fusion.1.part), custom_call_target="tpu_custom_call" | custom-call | tf_op jit(solution)/shard_map/kv_reduce/pallas_call | solution.py:387
  404.7 6.6 %broadcast_multiply_fusion = (f32[2,64,5,4,64]{1,4,3,2,0:T(8,128)S(1)}, f32[2,64,5,4,64]{1,4,3,2,0:T(8,128)}) fusion(bf16[2,1024,5,64,1]{1,3,4,2,0:T(8,128)(2,1)} %bitcast.221, bf16[2,5,4,64,1024]{4,3,2,1,0:T(8,128)(2,1)} %copy-done.12), kind=kOutput, calls=%fused_computation.61 | convolution fusion | flops 335708160 | bytes 7864320 | tf_op jit(solution)/shard_map/mgjts,msgd->mtgjd/dot_general | solution.py:885
  442.8 7.0 %multiply_reduce_fusion.2 = (f32[128]{0:T(128)S(1)}, f32[2048]{0:T(1024)S(1)}, bf16[128,2048]{1,0:T(8,128)(2,1)S(1)}, f32[128,2048]{1,0:T(8,128)}) fusion(bf16[2,64,2048]{2,1,0:T(8,128)(2,1)S(1)} %copy-done.20, f32[2048]{0:T(1024)S(1)} %bitcast.253, f32[128]{0:T(128)S(1)} %rsqrt.45, bf16[128,1920]{1,0:T(8,128)(2,1)S(1)} %concatenate.113.refs_1_, ...), kind=kOutput, calls=%fused_computation.48 | convolution fusion | flops 1008990080 | bytes 10470400 | tf_op jit(solution)/shard_map/dot_general | solution.py:757
  461.6 4.8 convolution_convert_fusion.2
  466.5 7.4 %convolution_convert_fusion = bf16[2048,1280]{1,0:T(8,128)(2,1)} fusion(bf16[1024,2048]{1,0:T(8,128)(2,1)S(1)} %bitcast.200, bf16[1024,640]{0,1:T(8,128)(2,1)S(1)} %copy-done.70, bf16[1024,640]{0,1:T(8,128)(2,1)S(1)} %copy-done.68), kind=kOutput, calls=%fused_computation.13 | convolution fusion | flops 5376573440 | bytes 12058624 | tf_op jit(solution)/shard_map/dot_general | solution.py:761
  473.9 5.2 convolution_convert_fusion.1
  483.2 5.1 reshape.450.refs_1_
  488.3 125.0 %reduce_grads.1 = (f32[16,10240]{1,0:T(8,128)}, f32[80,1024]{1,0:T(8,128)}, f32[2,16,1024]{2,1,0:T(8,128)}, f32[2,16,640]{2,1,0:T(8,128)}, f32[128,2048]{1,0:T(8,128)}, /*index=5*/f32[40,128]{1,0:T(8,128)}) custom-call(bf16[2,4,2,128,1280]{4,3,2,1,0:T(8,128)(2,1)} %bitcast.225, bf16[2,4,2,80,1024]{4,3,2,1,0:T(8,128)(2,1)} %reshape.450.refs_1_, ...), custom_call_target="tpu_custom_call" | custom-call | tf_op jit(solution)/shard_map/reduce_grads/pallas_call | solution.py:727
  (290 shorter events, 143.1 us)
Async XLA Ops:
  6.0 117.7 %copy-start.18 = (bf16[2,64,2048]{2,1,0:T(8,128)(2,1)S(1)}, bf16[2,64,2048]{2,1,0:T(8,128)(2,1)}, u32[]{:S(2)}) copy-start(bf16[2,64,2048]{2,1,0:T(8,128)(2,1)} %param.11) | copy-start | bytes 1572868
  130.0 32.4 %copy-start.24 = (f32[128,320]{0,1:T(8,128)}, f32[128,320]{0,1:T(8,128)S(1)}, u32[]{:S(2)}) copy-start(f32[128,320]{0,1:T(8,128)S(1)} %copy.192) | copy-start | bytes 491524
  131.7 33.1 %copy-start.30 = (f32[128,320]{1,0:T(8,128)}, f32[128,320]{1,0:T(8,128)S(1)}, u32[]{:S(2)}) copy-start(f32[128,320]{1,0:T(8,128)S(1)} %copy.149) | copy-start | bytes 491524
  131.9 32.9 %copy-start.32 = (f32[128,320]{1,0:T(8,128)}, f32[128,320]{1,0:T(8,128)S(1)}, u32[]{:S(2)}) copy-start(f32[128,320]{1,0:T(8,128)S(1)} %copy.150) | copy-start | bytes 491524
  170.7 9.7 %copy-start.42 = (f32[128,20]{0,1:T(8,128)}, f32[128,20]{0,1:T(8,128)S(1)}, u32[]{:S(2)}) copy-start(f32[128,20]{0,1:T(8,128)S(1)} %add_rsqrt_fusion) | copy-start | bytes 30724
  170.8 14.8 %copy-start.54 = (f32[64]{0:T(128)}, f32[64]{0:T(128)S(1)}, u32[]{:S(2)}) copy-start(f32[64]{0:T(128)S(1)} %convert_element_type.128) | copy-start | bytes 772
  188.2 12.4 %copy-start.26 = (pred[2,64,1024]{2,1,0:T(8,128)(4,1)}, pred[2,64,1024]{2,1,0:T(8,128)(4,1)S(1)}, u32[]{:S(2)}) copy-start(pred[2,64,1024]{2,1,0:T(8,128)(4,1)S(1)} %and_or_fusion) | copy-start | bytes 393220
  216.6 97.6 %copy-start.52 = (f32[128]{0:T(128)}, f32[128]{0:T(128)S(1)}, u32[]{:S(2)}) copy-start(f32[128]{0:T(128)S(1)} %add_rsqrt_fusion.3) | copy-start | bytes 1540
  249.1 10.6 %copy-start.2 = (bf16[4,2,128,2048]{3,2,1,0:T(8,128)(2,1)}, bf16[4,2,128,2048]{3,2,1,0:T(8,128)(2,1)S(1)}, u32[]{:S(2)}) copy-start(bf16[4,2,128,2048]{3,2,1,0:T(8,128)(2,1)S(1)} %row_gather.1) | copy-start | bytes 12582916
  262.6 51.9 %slice-start.3 = ((s8[5242880]{0:T(1024)(128)(4,1)}), s8[4194304]{0:T(1024)(128)(4,1)S(1)}, s32[]{:S(2)}) async-start(s8[5242880]{0:T(1024)(128)(4,1)} %bitcast.217), calls=%async_computation.3 | async-start | bytes 8388608
  272.1 9.4 %copy-start.69 = (bf16[1024,640]{0,1:T(8,128)(2,1)}, bf16[1024,640]{0,1:T(8,128)(2,1)S(1)}, u32[]{:S(2)}) copy-start(bf16[1024,640]{0,1:T(8,128)(2,1)S(1)} %get-tuple-element.51) | copy-start | bytes 3932164
  272.1 42.4 %slice-start.4 = ((s8[5242880]{0:T(1024)(128)(4,1)}), s8[1048576]{0:T(1024)(128)(4,1)S(1)}, s32[]{:S(2)}) async-start(s8[5242880]{0:T(1024)(128)(4,1)} %bitcast.217), calls=%async_computation.4 | async-start | bytes 2097152
  281.5 31.8 %copy-start.13 = (f32[128,2048]{1,0:T(8,128)S(1)}, f32[128,2048]{1,0:T(8,128)}, u32[]{:S(2)}) copy-start(f32[128,2048]{1,0:T(8,128)} %get-tuple-element.88) | copy-start | bytes 3145732
  281.5 32.6 %copy-start.1 = (bf16[2,64,2048]{2,1,0:T(8,128)(2,1)S(1)}, bf16[2,64,2048]{2,1,0:T(8,128)(2,1)}, u32[]{:S(2)}) copy-start(bf16[2,64,2048]{2,1,0:T(8,128)(2,1)} %param.21) | copy-start | bytes 1572868
  369.3 28.7 %copy-start.39 = (f32[128,64]{0,1:T(8,128)S(1)}, f32[128,64]{0,1:T(8,128)}, u32[]{:S(2)}) copy-start(f32[128,64]{0,1:T(8,128)} %copy-done.38) | copy-start | bytes 98308
  369.3 28.7 %copy-start.25 = (f32[128,320]{0,1:T(8,128)S(1)}, f32[128,320]{0,1:T(8,128)}, u32[]{:S(2)}) copy-start(f32[128,320]{0,1:T(8,128)} %copy-done.24) | copy-start | bytes 491524
  369.3 28.7 %copy-start.37 = (f32[128,64]{0,1:T(8,128)S(1)}, f32[128,64]{0,1:T(8,128)}, u32[]{:S(2)}) copy-start(f32[128,64]{0,1:T(8,128)} %copy-done.36) | copy-start | bytes 98308
  369.3 33.5 %copy-start.31 = (f32[128,320]{1,0:T(8,128)S(1)}, f32[128,320]{1,0:T(8,128)}, u32[]{:S(2)}) copy-start(f32[128,320]{1,0:T(8,128)} %copy-done.30) | copy-start | bytes 491524
  369.3 33.5 %copy-start.33 = (f32[128,320]{1,0:T(8,128)S(1)}, f32[128,320]{1,0:T(8,128)}, u32[]{:S(2)}) copy-start(f32[128,320]{1,0:T(8,128)} %copy-done.32) | copy-start | bytes 491524
  488.3 128.1 %copy-start.14 = (f32[128,2048]{1,0:T(8,128)S(1)}, f32[128,2048]{1,0:T(8,128)}, u32[]{:S(2)}) copy-start(f32[128,2048]{1,0:T(8,128)} %get-tuple-element.88) | copy-start | bytes 3145732
  488.3 128.1 %copy-start.21 = (bf16[2,64,2048]{2,1,0:T(8,128)(2,1)S(1)}, bf16[2,64,2048]{2,1,0:T(8,128)(2,1)}, u32[]{:S(2)}) copy-start(bf16[2,64,2048]{2,1,0:T(8,128)(2,1)} %param.11) | copy-start | bytes 1572868
  488.3 128.1 %copy-start.34 = (f32[128,2048]{1,0:T(8,128)S(1)}, f32[128,2048]{1,0:T(8,128)}, u32[]{:S(2)}) copy-start(f32[128,2048]{1,0:T(8,128)} %get-tuple-element.93) | copy-start | bytes 3145732
  488.3 128.1 %copy-start.53 = (f32[128]{0:T(128)S(1)}, f32[128]{0:T(128)}, u32[]{:S(2)}) copy-start(f32[128]{0:T(128)} %copy-done.52) | copy-start | bytes 1540
  488.3 128.1 %copy-start.59 = (f32[128]{0:T(128)S(1)}, f32[128]{0:T(128)}, u32[]{:S(2)}) copy-start(f32[128]{0:T(128)} %copy-done.58) | copy-start | bytes 1540
  (52 other events, 228.5 us)

commit v2 on v1

v2 whole, which is shorter than its diff:
```python
import jax
import jax.numpy as jnp
from jax import lax
from jax.experimental import pallas as pl
from jax.experimental.pallas import tpu as pltpu
from jax.sharding import PartitionSpec as P

Q_HEADS = 20
KV_HEADS = 5
GROUP = 4
HEAD = 64
D = 2048
FF = 5120
QD = 1280
KD = 320
QKV = 1920
SEQ = 1024
MICRO = 2
ROWS = 64
TOK = 128
FS = 640
EPS = 1e-06
MESH = pl.DeviceIdType.MESH
F32 = jnp.float32
BF16 = jnp.bfloat16
ANY = pl.BlockSpec(memory_space=pl.ANY)


class Place:
    def __init__(self):
        g = lax.axis_index("grp")
        s = lax.axis_index("seq")
        self.g, self.s = g, s
        self.yh, self.x = g // 4, g % 4
        self.yl, self.z, self.c = s // 8, (s // 2) % 4, s % 2
        self.y = self.yh * 2 + self.yl

    def at(self, x=None, y=None, z=None, c=None):
        x = self.x if x is None else x
        y = self.y if y is None else y
        z = self.z if z is None else z
        c = self.c if c is None else c
        return ((y // 2) * 4 + x, (y % 2) * 8 + z * 2 + c)

    def step(self, axis, k):
        if axis == "x":
            return self.at(x=(self.x + k) % 4)
        if axis == "y":
            return self.at(y=(self.y + k) % 4)
        if axis == "z":
            return self.at(z=(self.z + k) % 4)
        return self.at(c=1 - self.c)

    def pos(self, axis, k):
        return (getattr(self, axis) + k) % 4


class Links:
    def __init__(self, send_sems, recv_sems):
        self.send_sems, self.recv_sems = send_sems, recv_sems
        self.used = 0
        self.sent = []

    def send(self, src, dst, to):
        i = self.used
        self.used += 1
        copy = pltpu.make_async_remote_copy(
            src_ref=src,
            dst_ref=dst,
            send_sem=self.send_sems.at[i],
            recv_sem=self.recv_sems.at[i],
            device_id=to,
            device_id_type=MESH,
        )
        copy.start()
        self.sent.append(copy)
        return copy

    def local(self, src, dst):
        i = self.used
        self.used += 1
        copy = pltpu.make_async_copy(src, dst, self.recv_sems.at[i])
        copy.start()
        return copy

    def drain(self):
        for copy in self.sent:
            copy.wait_send()


def greet(partners):
    barrier = pltpu.get_barrier_semaphore()
    for to in partners:
        pl.semaphore_signal(barrier, inc=1, device_id=to, device_id_type=MESH)
    pl.semaphore_wait(barrier, len(partners))


def any_call(body, name, cid, n_in, outs, scratch, sems, vmem=48 << 20):
    return pl.pallas_call(
        body,
        out_shape=outs,
        in_specs=[ANY] * n_in,
        out_specs=[ANY] * len(outs),
        name=name,
        scratch_shapes=list(scratch)
        + [pltpu.SemaphoreType.DMA((sems,)), pltpu.SemaphoreType.DMA((sems,))],
        compiler_params=pltpu.CompilerParams(
            collective_id=cid, has_side_effects=True, vmem_limit_bytes=vmem
        ),
    )


def sds(shape, dtype):
    return jax.ShapeDtypeStruct(shape, dtype)


def rms_scale(values):
    return lax.rsqrt(jnp.mean(values * values, axis=-1, keepdims=True) + EPS)


def norm_back(upstream, normed, scale, gain):
    scaled = upstream * gain
    inner = jnp.mean(scaled * normed, axis=-1, keepdims=True)
    return scale * (scaled - normed * inner)


def dot(left, right):
    return jnp.dot(left, right, preferred_element_type=F32)


def dot_last(left, right):
    return lax.dot_general(left, right, (((1,), (1,)), ((), ())), preferred_element_type=F32)


def dot_rows(left, right):
    return lax.dot_general(left, right, (((0,), (0,)), ((), ())), preferred_element_type=F32)


def slab_target(p):
    to = p.at(x=p.z, y=p.c * 2 + p.yl, z=p.g // 2, c=p.g % 2)
    return to


def slab_source(p):
    m = p.z * 2 + p.c
    return p.at(x=m % 4, y=(m // 4) * 2 + p.yl, z=p.x, c=p.yh)


def same(p, to):
    return (to[0] == p.g) & (to[1] == p.s)


def greet_plane(p, partners, slab_to, slab_from, own_slab):
    barrier = pltpu.get_barrier_semaphore()
    for to in partners:
        pl.semaphore_signal(barrier, inc=1, device_id=to, device_id_type=MESH)

    @pl.when(jnp.logical_not(own_slab))
    def _():
        pl.semaphore_signal(barrier, inc=1, device_id=slab_to, device_id_type=MESH)
        pl.semaphore_signal(barrier, inc=1, device_id=slab_from, device_id_type=MESH)
        pl.semaphore_wait(barrier, len(partners) + 2)

    @pl.when(own_slab)
    def _():
        pl.semaphore_wait(barrier, len(partners))


def slab_copy(src, dst, ssem, rsem, i, to):
    return pltpu.make_async_remote_copy(
        src_ref=src,
        dst_ref=dst,
        send_sem=ssem.at[i],
        recv_sem=rsem.at[i],
        device_id=to,
        device_id_type=MESH,
    )


def row_reduce(p, k, part, own, r0, s0, r1, res):
    z, c = p.z, p.c
    core = k.send(part.at[:, 1 - c], r0, p.step("c", 1))
    mine = k.local(part.at[:, c], own)
    yield
    mine.wait()
    core.wait_recv()

    @pl.loop(0, 4)
    def _(zz):
        @pl.loop(0, TOK, step=32)
        def _(t):
            at = pl.ds(pl.multiple_of(t, 32), 32)
            s0[zz, at] = (own[zz, at].astype(F32) + r0[zz, at].astype(F32)).astype(BF16)

    ring = [k.send(s0.at[p.pos("z", j)], r1.at[j - 1], p.step("z", j)) for j in (1, 2, 3)]
    yield
    for copy in ring:
        copy.wait_recv()

    @pl.loop(0, TOK, step=32)
    def _(t):
        at = pl.ds(pl.multiple_of(t, 32), 32)
        total = s0[z, at].astype(F32)
        for j in range(3):
            total = total + r1[j, at].astype(F32)
        res[at] = total


def row_scratch():
    return [
        pltpu.VMEM((4, TOK, D), BF16),
        pltpu.VMEM((4, TOK, D), BF16),
        pltpu.VMEM((4, TOK, D), BF16),
        pltpu.VMEM((3, TOK, D), BF16),
        pltpu.VMEM((TOK, D), F32),
    ]


def pair_body(n, *refs):
    ins, outs = refs[:n], refs[n : 2 * n]
    ssem, rsem = refs[2 * n :]
    p = Place()
    k = Links(ssem, rsem)
    greet([p.step("c", 1)])
    copies = [k.send(i, o.at[1], p.step("c", 1)) for i, o in zip(ins, outs)]
    local = [k.local(i, o.at[0]) for i, o in zip(ins, outs)]
    for copy in local:
        copy.wait()
    for copy in copies:
        copy.wait_recv()
    k.drain()


def pair_exchange(*arrays):
    n = len(arrays)
    outs = [sds((2, *a.shape), a.dtype) for a in arrays]

    def body(*refs):
        pair_body(n, *refs)

    return any_call(body, "pair_exchange", 5, n, outs, [], 2 * n)(*arrays)


def add_blocks(dst, own, recv, chunk):
    lead, rows = dst.shape[:-2], dst.shape[-2]
    count = 1
    for n in lead:
        count *= n

    @pl.loop(0, count)
    def _(i):
        at = []
        rest = i
        for n in reversed(lead):
            at.insert(0, rest % n)
            rest = rest // n

        @pl.loop(0, rows, step=chunk)
        def _(t):
            here = (*at, pl.ds(pl.multiple_of(t, chunk), chunk))
            total = own[here].astype(F32)
            for j in range(3):
                total = total + recv[(j, *here)].astype(F32)
            dst[here] = total.astype(dst.dtype)


def staged_reduce(p, k, src, stages, scr, chunk):
    own = scr[0]
    cur = src
    for n, (axis, pick) in enumerate(stages):
        recv, total = scr[1 + 2 * n], scr[2 + 2 * n]
        if n == 0:
            mine = k.local(pick(src, p.pos(axis, 0)), own)
        ring = [k.send(pick(cur, p.pos(axis, j)), recv.at[j - 1], p.step(axis, j)) for j in (1, 2, 3)]
        yield
        if n == 0:
            mine.wait()
        for copy in ring:
            copy.wait_recv()
        add_blocks(total, own if n == 0 else pick(cur, p.pos(axis, 0)), recv, chunk)
        cur = total


def staged_scratch(shapes):
    out = [pltpu.VMEM(shapes[0], BF16)]
    for n, shape in enumerate(shapes):
        out.append(pltpu.VMEM((3, *shape), BF16))
        out.append(pltpu.VMEM(shape, F32 if n == len(shapes) - 1 else BF16))
    return out


EVERY = slice(None)


def wg_stages(half):
    cols = pl.ds(half * FS, FS)
    if half == 0:
        return [
            ("y", lambda r, i: r.at[i // 2, :, i % 2, :, cols]),
            ("x", lambda r, i: r.at[i]),
        ]
    return [
        ("x", lambda r, i: r.at[:, i, :, :, cols]),
        ("y", lambda r, i: r.at[i // 2, i % 2]),
    ]


def wd_stages(half):
    cols = pl.ds(half * 512, 512)
    if half == 0:
        return [
            ("y", lambda r, i: r.at[i % 2, :, i // 2, :, cols]),
            ("x", lambda r, i: r.at[i]),
        ]
    return [
        ("x", lambda r, i: r.at[:, i, :, :, cols]),
        ("y", lambda r, i: r.at[i % 2, i // 2]),
    ]


def q_stages(half):
    cols = pl.ds(half * 512, 512)
    if half == 0:
        return [
            ("x", lambda r, i: r.at[:, i, :, :, :, cols]),
            ("z", lambda r, i: r.at[:, :, i]),
            ("y", lambda r, i: r.at[i // 2, i % 2]),
        ]
    return [
        ("y", lambda r, i: r.at[i // 2, :, i % 2, :, :, cols]),
        ("x", lambda r, i: r.at[i]),
        ("z", lambda r, i: r.at[i]),
    ]


def o_stages():
    return [
        ("z", lambda r, i: r.at[:, :, :, i]),
        ("y", lambda r, i: r.at[i // 2, :, i % 2]),
        ("x", lambda r, i: r.at[i]),
    ]


GRAD_SHAPES = [
    [(4, 128, FS), (128, FS)],
    [(2, 2, 128, FS), (128, FS)],
    [(4, 80, 512), (80, 512)],
    [(2, 2, 80, 512), (80, 512)],
    [(2, 2, 4, 32, 512), (2, 2, 32, 512), (32, 512)],
    [(4, 4, 32, 512), (4, 32, 512), (32, 512)],
    [(2, 4, 2, 32, 640), (4, 32, 640), (32, 640)],
]


def small_reduce(p, k, part, vec, recv):
    mine = k.local(part, vec.at[0])
    mine.wait()
    for n, axis in enumerate("xyzc"):
        steps = (1,) if axis == "c" else (1, 2, 3)
        ring = [k.send(vec.at[n], recv.at[n, j - 1], p.step(axis, j)) for j in steps]
        yield
        for copy in ring:
            copy.wait_recv()
        total = vec[n]
        for j in range(len(steps)):
            total = total + recv[n, j]
        vec[n + 1] = total


def grads_body(*refs):
    dwg, dwd, dq, do, dmix, small, GWG, GWD, GQ, GO, MIX, SMALL = refs[:12]
    scr = list(refs[12:])
    parts = []
    for shapes in GRAD_SHAPES:
        n = 1 + 2 * len(shapes)
        parts.append(scr[:n])
        scr = scr[n:]
    mix, (vec, recv), (ssem, rsem) = scr[:5], scr[5:7], scr[7:9]
    p = Place()
    k = Links(ssem, rsem)
    yh, x, yl, z, c = p.yh, p.x, p.yl, p.z, p.c
    m = z * 2 + c
    partners = [p.step(a, j) for a in "xyz" for j in (1, 2, 3)]
    partners += [p.at(z=(z + j) % 4, c=1 - c) for j in range(4)]
    slab_to, slab_from = slab_target(p), slab_source(p)
    own_slab = same(p, slab_to)
    greet_plane(p, partners, slab_to, slab_from, own_slab)

    chunk = 16
    gens = [
        staged_reduce(p, k, dwg, wg_stages(0), parts[0], chunk),
        staged_reduce(p, k, dwg, wg_stages(1), parts[1], chunk),
        staged_reduce(p, k, dwd, wd_stages(0), parts[2], chunk),
        staged_reduce(p, k, dwd, wd_stages(1), parts[3], chunk),
        row_reduce(p, k, dmix, *mix),
        staged_reduce(p, k, do, o_stages(), parts[6], chunk),
        staged_reduce(p, k, dq, q_stages(0), parts[4], chunk),
        staged_reduce(p, k, dq, q_stages(1), parts[5], chunk),
        small_reduce(p, k, small, vec, recv),
    ]
    alive = list(gens)
    while alive:
        alive = [g for g in alive if next(g, alive) is not alive]

    last, local = [], []
    for half in range(2):
        total = parts[half][-1]
        cols = pl.ds(pl.multiple_of(half * FF + m * FS, 128), FS)
        for dz in range(4):
            for dc in range(2):
                zz, cc = (z + dz) % 4, (c + dc) % 2
                src = total.at[pl.ds(pl.multiple_of((zz * 2 + cc) * 16, 16), 16)]
                if dz == 0 and dc == 0:
                    local.append(k.local(src, GWG.at[:, cols]))
                else:
                    last.append(k.send(src, GWG.at[:, cols], p.at(z=zz, c=cc)))
    slabs = []
    for half in range(2):
        i = k.used
        k.used += 1
        src, dst = parts[2 + half][-1], GWD.at[:, pl.ds(half * 512, 512)]
        slabs.append((src, dst, i))

        @pl.when(own_slab)
        def _(src=src, dst=dst, i=i):
            pltpu.make_async_copy(src, dst, rsem.at[i]).start()

        @pl.when(jnp.logical_not(own_slab))
        def _(src=src, dst=dst, i=i):
            slab_copy(src, dst, ssem, rsem, i, slab_from).start()

    for total, dst in (
        (parts[4][-1], GQ.at[c, :, pl.ds(0, 512)]),
        (parts[5][-1], GQ.at[c, :, pl.ds(512, 512)]),
        (parts[6][-1], GO.at[c]),
    ):
        mine = total.at[pl.ds(pl.multiple_of(c * 16, 16), 16)]
        other = total.at[pl.ds(pl.multiple_of((1 - c) * 16, 16), 16)]
        local.append(k.local(mine, dst))
        last.append(k.send(other, dst, p.step("c", 1)))
    local.append(k.local(mix[-1], MIX))
    local.append(k.local(vec.at[4], SMALL))
    for copy in local:
        copy.wait()
    for copy in last:
        copy.wait_recv()
    for src, dst, i in slabs:

        @pl.when(own_slab)
        def _(src=src, dst=dst, i=i):
            pltpu.make_async_copy(src, dst, rsem.at[i]).wait()

        @pl.when(jnp.logical_not(own_slab))
        def _(src=src, dst=dst, i=i):
            slab_copy(src, dst, ssem, rsem, i, slab_from).wait()

    k.drain()


def reduce_grads(dwg, dwd, dq, do, dmix, small):
    outs = [
        sds((16, 2 * FF), F32),
        sds((80, 1024), F32),
        sds((2, 16, 1024), F32),
        sds((2, 16, 640), F32),
        sds((TOK, D), F32),
        sds((40, 128), F32),
    ]
    scratch = []
    for shapes in GRAD_SHAPES:
        scratch += staged_scratch(shapes)
    scratch += row_scratch()
    scratch += [pltpu.VMEM((5, 40, 128), F32), pltpu.VMEM((4, 3, 40, 128), F32)]
    return any_call(grads_body, "reduce_grads", 6, 6, outs, scratch, 110, 56 << 20)(
        dwg, dwd, dq, do, dmix, small
    )


def swap(a, b):
    left = lax.broadcasted_iota(jnp.int32, a.shape, 1) < ROWS
    return jnp.where(left, a, pltpu.roll(b, ROWS, 1)), jnp.where(left, pltpu.roll(a, ROWS, 1), b)


def head_scale(v):
    return lax.rsqrt(jnp.mean(v * v, axis=-2, keepdims=True) + EPS)


def half_turn(v):
    half = HEAD // 2
    return jnp.concatenate([-v[..., half:, :], v[..., :half, :]], axis=-2)


def half_back(v):
    half = HEAD // 2
    return jnp.concatenate([v[..., half:, :], -v[..., :half, :]], axis=-2)


def low(v):
    return v.astype(BF16).astype(F32)


def query_units(packed_t, g, cos, sin, gain):
    raw = packed_t[pl.ds(pl.multiple_of(g * 256, 256), 256)].reshape(GROUP, HEAD, TOK)
    head = raw * head_scale(raw) * gain
    turned = low(head * cos + half_turn(head) * sin) * (HEAD ** -0.5)
    a0, a1 = swap(turned[0], turned[1])
    b0, b1 = swap(turned[2], turned[3])
    none = jnp.zeros((HEAD, 256), F32)
    return [
        jnp.concatenate([jnp.concatenate([a, b], axis=1), none], axis=0) for a, b in ((a0, b0), (a1, b1))
    ]


def fill_bias(bias, segc, segq, start):
    @pl.loop(0, SEQ, step=128)
    def _(t):
        at = pl.ds(pl.multiple_of(t, 128), 128)
        key = lax.broadcasted_iota(jnp.int32, (128, 256), 0) + t
        query = lax.broadcasted_iota(jnp.int32, (128, 256), 1) % ROWS + start
        for m in range(MICRO):
            ok = (key <= query) & (segc[at, m : m + 1] == segq[m : m + 1, :])
            ok = ok | (key == query)
            bias[m, at] = jnp.where(ok, 3e38, -1e30)


def unit_kv(KV, m, g):
    cols = pl.ds(pl.multiple_of(g * 128, 128), 128)
    return KV[m, :, :, :, :, cols].reshape(SEQ, 128)


def front_body(*refs):
    (x_ref, wq, wo, wg, wd, og, segc, segq, cos_ref, sin_ref, qgain, kgain) = refs[:12]
    (WQ, WO, WG, WD, OG, RG, KV, pt_out, lse_out, att_out, resid_out, normed_out, gains_out) = refs[12:25]
    (wqs, wos, kvl, kvs, bias, qts, ots, n2, ssem, rsem) = refs[25:]
    p = Place()
    k = Links(ssem, rsem)
    yh, x, yl, z, c = p.yh, p.x, p.yl, p.z, p.c
    m = z * 2 + c
    yl_partner = p.at(y=p.yh * 2 + 1 - yl)
    partners = [p.step(a, j) for a in "xyz" for j in (1, 2, 3)]
    partners += [p.at(z=(z + j) % 4, c=1 - c) for j in range(4)]
    slab_to, slab_from = slab_target(p), slab_source(p)
    own_slab = same(p, slab_to)
    greet_plane(p, partners, slab_to, slab_from, own_slab)

    def wq_a(*at):
        return wqs.at[(*at, EVERY, pl.ds(0, 1024))]

    def wq_b(*at):
        return wqs.at[(*at, EVERY, pl.ds(1024, 1024))]

    def wo_(*at):
        return wos.at[(*at, EVERY, EVERY)]

    own_wq = k.local(wq, wqs.at[yh, x, yl, z, c])
    own_wo = k.local(wo, wos.at[yh, x, yl, z, c])
    q1, o1 = [], []
    for j in (1, 2, 3):
        q1.append(k.send(wq.at[:, pl.ds(0, 1024)], wq_a(yh, x, yl, z, c), p.step("y", j)))
        q1.append(k.send(wq.at[:, pl.ds(1024, 1024)], wq_b(yh, x, yl, z, c), p.step("z", j)))
    for j in (1, 2, 3):
        o1.append(k.send(wo, wo_(yh, x, yl, z, c), p.step("x", j)))
    pieces, own_pieces = [], []
    for dz in range(4):
        for dc in range(2):
            zz, cc = (z + dz) % 4, (c + dc) % 2
            mm = zz * 2 + cc
            for half in range(2):
                src = wg.at[:, pl.ds(pl.multiple_of(half * FF + mm * FS, 128), FS)]
                dst = WG.at[yh, x, yl, m, :, pl.ds(half * FS, FS)]
                if dz == 0 and dc == 0:
                    own_pieces.append(k.local(src, dst))
                else:
                    pieces.append(k.send(src, dst, p.at(z=zz, c=cc)))
    slab_dst = WD.at[yl, z, c]
    i = k.used
    k.used += 1
    slab = slab_copy(wd, slab_dst, ssem, rsem, i, slab_to)

    @pl.when(own_slab)
    def _():
        pltpu.make_async_copy(wd, slab_dst, rsem.at[i]).start()

    @pl.when(jnp.logical_not(own_slab))
    def _():
        slab.start()

    fill_bias(bias, segc, segq, p.s * ROWS)

    own_wq.wait()
    own_wo.wait()
    for copy in q1:
        copy.wait_recv()
    q2 = []
    for j in (1, 2, 3):
        src = wq_a(EVERY, x, EVERY, z, c)
        q2.append(k.send(src, src, p.step("z", j)))
        src = wq_b(yh, x, yl, EVERY, c)
        q2.append(k.send(src, src, p.step("x", j)))
    for copy in o1:
        copy.wait_recv()
    o2 = []
    for j in (1, 2, 3):
        src = wo_(yh, EVERY, yl, z, c)
        o2.append(k.send(src, src, p.step("y", j)))
    for copy in q2:
        copy.wait_recv()
    q3 = []
    for j in (1, 2, 3):
        src = wq_a(EVERY, x, EVERY, EVERY, c)
        q3.append((k.send(src, src, p.step("x", j)), wq_a(EVERY, p.pos("x", -j), EVERY, EVERY, c)))
        src = wq_b(yh, EVERY, yl, EVERY, c)
        yy = p.pos("y", -j)
        q3.append((k.send(src, src, p.step("y", j)), wq_b(yy // 2, EVERY, yy % 2, EVERY, c)))
    qc = []
    for src in (wq_a(EVERY, x, EVERY, EVERY, c), wq_b(yh, EVERY, yl, EVERY, c)):
        qc.append(k.send(src, src, p.step("c", 1)))
    for copy in o2:
        copy.wait_recv()
    o3 = []
    for j in (1, 2, 3):
        src = wo_(EVERY, EVERY, EVERY, z, c)
        o3.append((k.send(src, src, p.step("z", j)), wo_(EVERY, EVERY, EVERY, p.pos("z", -j), c)))
    oc = [k.send(wo_(EVERY, EVERY, EVERY, z, c), wo_(EVERY, EVERY, EVERY, z, c), p.step("c", 1))]

    for copy in own_pieces:
        copy.wait()
    for copy in pieces:
        copy.wait_recv()

    @pl.when(own_slab)
    def _():
        pltpu.make_async_copy(wd, slab_dst, rsem.at[i]).wait()

    @pl.when(jnp.logical_not(own_slab))
    def _():
        slab.wait_recv()

    for copy, src in q3:
        copy.wait_recv()
        qc.append(k.send(src, src, p.step("c", 1)))
    lo, hi = pl.ds(0, FS), pl.ds(FS, FS)
    dlo, dhi = pl.ds(0, 512), pl.ds(512, 512)
    plane = []
    for j in (1, 2, 3):
        for src, axis in (
            (WG.at[yh, x, yl, :, :, lo], "x"),
            (WG.at[yh, x, yl, :, :, hi], "y"),
            (WD.at[yl, x, yh, :, dlo], "x"),
            (WD.at[yl, x, yh, :, dhi], "y"),
        ):
            plane.append(k.send(src, src, p.step(axis, j)))
    for copy in qc:
        copy.wait_recv()
    keep_wq = k.local(wqs, WQ)

    pick = jnp.where(
        lax.broadcasted_iota(jnp.int32, (8, 128), 0) == lax.broadcasted_iota(jnp.int32, (8, 128), 1), 1.0, 0.0
    ).astype(BF16)
    gain_cols = wqs[:, :, :, :, :, :, pl.ds(QKV, 128)].reshape(D, 128)
    gains_out[...] = dot_last(pick, gain_cols)
    hidden = x_ref[...].astype(F32)
    normed = (hidden * rms_scale(hidden) * gains_out[0:1, :]).astype(BF16)
    normed_out[...] = normed

    @pl.loop(0, 8)
    def _(t):
        cols = pl.ds(pl.multiple_of(t * 256, 256), 256)
        w = wqs[:, :, :, :, :, :, cols].reshape(D, 256)
        pt_out[cols] = dot(normed_out[...], w).T

    cos, sin = cos_ref[...], sin_ref[...]

    @pl.loop(0, KV_HEADS)
    def _(g):
        raw = pt_out[pl.ds(pl.multiple_of(QD + g * HEAD, HEAD), HEAD)]
        head = raw * head_scale(raw) * kgain[...]
        key = head * cos + half_turn(head) * sin
        value = pt_out[pl.ds(pl.multiple_of(QD + KD + g * HEAD, HEAD), HEAD)]
        both = jnp.concatenate([key, value], axis=0).T.astype(BF16)
        cols = pl.ds(pl.multiple_of(g * 128, 128), 128)
        for mm in range(MICRO):
            kvl[mm, :, cols] = both[mm * ROWS : (mm + 1) * ROWS]

    own_kv = k.local(kvl, kvs.at[:, yl, z, c])
    across = k.send(kvl, kvs.at[:, yl, z, c], yl_partner)
    ring = [k.send(kvl, kvs.at[:, yl, z, c], p.step("z", j)) for j in (1, 2, 3)]

    @pl.loop(0, KV_HEADS)
    def _(g):
        for mm, unit in enumerate(query_units(pt_out, g, cos, sin, qgain[...])):
            qts[g, mm] = unit.astype(BF16)

    for copy in plane:
        copy.wait_recv()
    across.wait_recv()
    src = kvs.at[:, 1 - yl, z, c]
    ring += [k.send(src, src, p.step("z", j)) for j in (1, 2, 3)]
    plane2 = []
    for j in (1, 2, 3):
        for src, axis in (
            (WG.at[yh, :, yl, :, :, lo], "y"),
            (WG.at[:, x, :, :, :, hi], "x"),
            (WD.at[yl, :, yh, :, dlo], "y"),
            (WD.at[:, x, :, :, dhi], "x"),
        ):
            plane2.append(k.send(src, src, p.step(axis, j)))
    own_kv.wait()
    for copy in ring:
        copy.wait_recv()
    src = kvs.at[:, :, :, c]
    kvc = k.send(src, src, p.step("c", 1))
    for copy, src in o3:
        copy.wait_recv()
        oc.append(k.send(src, src, p.step("c", 1)))
    own_og = k.local(og, OG.at[z, c])
    rows = [k.send(og, OG.at[z, c], p.step("z", j)) for j in (1, 2, 3)]
    last = [k.send(og, OG.at[z, c], p.step("c", 1))]
    kvc.wait_recv()
    keep_kv = k.local(kvs, KV)

    @pl.loop(0, 2 * KV_HEADS)
    def _(u):
        g, mm = u // 2, u % 2
        kv = unit_kv(kvs, mm, g)
        score = jnp.minimum(dot(kv, qts[g, mm]), bias[mm])
        peak = jnp.max(score, axis=0, keepdims=True)
        raised = jnp.exp(score - peak)
        total = jnp.sum(raised, axis=0, keepdims=True)
        probs = (raised * (1.0 / total)).astype(BF16)
        ots[g, mm] = dot_rows(kv, probs)[HEAD:]
        lse_out[u] = jnp.broadcast_to(peak + jnp.log(total), (8, 256))

    for g in range(KV_HEADS):
        for t in range(2):
            cols = slice(t * 128, (t + 1) * 128)
            a, b = swap(ots[g, 0, :, cols], ots[g, 1, :, cols])
            at = (g * GROUP + 2 * t) * HEAD
            att_out[:, at : at + 128] = jnp.concatenate([a, b], axis=0).T.astype(BF16)

    for copy in oc:
        copy.wait_recv()
    keep_wo = k.local(wos, WO)

    @pl.loop(0, 8)
    def _(t):
        w = wos[t // 4, t % 4].reshape(256, QD)
        cols = pl.ds(pl.multiple_of(t * 256, 256), 256)
        resid_out[:, cols] = x_ref[:, cols].astype(F32) + dot_last(att_out[...], w)

    resid = resid_out[...]
    n2[...] = (resid * rms_scale(resid) * gains_out[1:2, :]).astype(BF16)
    own_n2 = k.local(n2, RG.at[z, c])
    ring2 = [k.send(n2, RG.at[z, c], p.step("z", j)) for j in (1, 2, 3)]
    last.append(k.send(n2, RG.at[z, c], p.step("c", 1)))
    for j, copy in zip((1, 2, 3), rows):
        copy.wait_recv()
        src = OG.at[p.pos("z", -j), c]
        last.append(k.send(src, src, p.step("c", 1)))
    for j, copy in zip((1, 2, 3), ring2):
        copy.wait_recv()
        src = RG.at[p.pos("z", -j), c]
        last.append(k.send(src, src, p.step("c", 1)))
    for copy in plane2 + last:
        copy.wait_recv()
    for copy in (keep_wq, keep_kv, keep_wo, own_og, own_n2):
        copy.wait()
    k.drain()

    @pl.when(jnp.logical_not(own_slab))
    def _():
        slab.wait_send()


VMEM = pl.BlockSpec(memory_space=pltpu.VMEM)


def front(x, wq, wo, wg, wd, og, segc, segq, cos, sin, qgain, kgain):
    hbm = [
        sds((2, 4, 2, 4, 2, 16, 2048), BF16),
        sds((2, 4, 2, 4, 2, 16, QD), BF16),
        sds((2, 4, 2, 8, 16, 2 * FS), BF16),
        sds((2, 4, 2, 80, 1024), BF16),
        sds((4, 2, TOK, D), BF16),
        sds((4, 2, TOK, D), BF16),
        sds((2, 2, 4, 2, ROWS, 2 * KD), BF16),
    ]
    vmem = [
        sds((2048, TOK), F32),
        sds((2 * KV_HEADS, 8, 256), F32),
        sds((TOK, QD), BF16),
        sds((TOK, D), F32),
        sds((TOK, D), BF16),
        sds((8, D), F32),
    ]
    scratch = [
        pltpu.VMEM((2, 4, 2, 4, 2, 16, 2048), BF16),
        pltpu.VMEM((2, 4, 2, 4, 2, 16, QD), BF16),
        pltpu.VMEM((2, ROWS, 2 * KD), BF16),
        pltpu.VMEM((2, 2, 4, 2, ROWS, 2 * KD), BF16),
        pltpu.VMEM((2, SEQ, 256), F32),
        pltpu.VMEM((KV_HEADS, 2, 128, 256), BF16),
        pltpu.VMEM((KV_HEADS, 2, HEAD, 256), F32),
        pltpu.VMEM((TOK, D), BF16),
        pltpu.SemaphoreType.DMA((120,)),
        pltpu.SemaphoreType.DMA((120,)),
    ]
    return pl.pallas_call(
        front_body,
        out_shape=hbm + vmem,
        in_specs=[VMEM] + [ANY] * 5 + [VMEM] * 6,
        out_specs=[ANY] * len(hbm) + [VMEM] * len(vmem),
        scratch_shapes=scratch,
        name="front",
        compiler_params=pltpu.CompilerParams(
            collective_id=0, has_side_effects=True, vmem_limit_bytes=56 << 20
        ),
    )(x, wq, wo, wg, wd, og, segc, segq, cos, sin, qgain, kgain)


def back_body(*refs):
    (part, x_ref, og_ref, resid_ref, gains, WQ, WO, KV, pt, lse, segc, segq, cos_ref, sin_ref, qgain, kgain) = refs[:16]
    (in_grad, dp_out, low_out, rows_out, heads_out) = refs[16:21]
    (rown, rr0, rs0, rr1, rres) = refs[21:26]
    (wqs, wos, kvs, bias, qts, qns, dts, dns, dqt, dpt, datt, dres, kpart) = refs[26:39]
    (k0, ks0, k1, ks1, k2, kres, ssem, rsem) = refs[39:]
    p = Place()
    k = Links(ssem, rsem)
    yl, z, c = p.yl, p.z, p.c
    yl_partner = p.at(y=p.yh * 2 + 1 - yl)
    greet([p.step("z", j) for j in (1, 2, 3)] + [yl_partner, p.step("c", 1)])
    get_wo = k.local(WO, wos)
    get_kv = k.local(KV, kvs)
    get_wq = k.local(WQ, wqs)
    steps = row_reduce(p, k, part, rown, rr0, rs0, rr1, rres)
    next(steps)
    fill_bias(bias, segc, segq, p.s * ROWS)
    next(steps)
    cos, sin = cos_ref[...], sin_ref[...]

    @pl.loop(0, KV_HEADS)
    def _(g):
        for mm, unit in enumerate(query_units(pt, g, cos, sin, qgain[...])):
            qts[g, mm] = unit.astype(BF16)
            qns[g, mm] = unit.T.astype(BF16)

    next(steps, None)
    resid = resid_ref[...]
    scale_two = rms_scale(resid)
    norm_two = resid * scale_two
    d_normed = rres[...]
    rows_out[1:2, :] = jnp.sum(d_normed * norm_two, axis=0, keepdims=True)
    d_resid = og_ref[...].astype(F32) + norm_back(d_normed, norm_two, scale_two, gains[1:2, :])
    dres[...] = d_resid
    low_out[...] = d_resid.astype(BF16)
    get_wo.wait()

    @pl.loop(0, 5)
    def _(t):
        cols = pl.ds(pl.multiple_of(t * 256, 256), 256)
        w = wos[:, :, :, :, :, :, cols].reshape(D, 256)
        datt[:, cols] = low(dot(low_out[...], w))

    for g in range(KV_HEADS):
        tiles = []
        for t in range(2):
            at = (g * GROUP + 2 * t) * HEAD
            both = datt[:, at : at + 128].T
            tiles.append(swap(both[:HEAD], both[HEAD:]))
        for mm in range(MICRO):
            none = jnp.zeros((HEAD, 256), F32)
            unit = jnp.concatenate([none, jnp.concatenate([tiles[0][mm], tiles[1][mm]], axis=1)], axis=0)
            dts[g, mm] = unit.astype(BF16)
            dns[g, mm] = unit.T.astype(BF16)
    get_kv.wait()

    @pl.loop(0, 2 * KV_HEADS)
    def _(u):
        g, mm = u // 2, u % 2
        kv = unit_kv(kvs, mm, g)
        score = jnp.minimum(dot(kv, qts[g, mm]), bias[mm])
        again = jnp.exp(score - lse[u, 0:1, :])
        d_probs = dot(kv, dts[g, mm])
        inner = jnp.sum(again * d_probs, axis=0, keepdims=True)
        d_scores = (again * (d_probs - inner)).astype(BF16)
        d_kv = dot(d_scores, qns[g, mm]) + dot(again.astype(BF16), dns[g, mm])
        cols = pl.ds(pl.multiple_of(g * 128, 128), 128)
        kpart[mm, :, :, :, :, cols] = d_kv.astype(BF16).reshape(2, 4, 2, ROWS, 128)
        dqt[g, mm] = dot_rows(kv, d_scores)[:HEAD] * (HEAD ** -0.5)

    core = k.send(kpart.at[:, :, :, 1 - c], k0, p.step("c", 1))
    core.wait_recv()

    @pl.loop(0, 4)
    def _(zz):
        for a in range(2):
            for b in range(2):
                ks0[a, b, zz] = (kpart[a, b, zz, c].astype(F32) + k0[a, b, zz].astype(F32)).astype(BF16)

    ring = [k.send(ks0.at[:, :, p.pos("z", j)], k1.at[j - 1], p.step("z", j)) for j in (1, 2, 3)]

    query_sum = jnp.zeros((HEAD, TOK), F32)
    for g in range(KV_HEADS):
        heads = []
        for t in range(2):
            cols = slice(t * 128, (t + 1) * 128)
            heads += list(swap(dqt[g, 0, :, cols], dqt[g, 1, :, cols]))
        for h in range(GROUP):
            at = (g * GROUP + h) * HEAD
            d_raw, term = head_back(pt[at : at + HEAD], heads[h], cos, sin, qgain[...])
            query_sum = query_sum + term
            dpt[at : at + HEAD] = d_raw
    heads_out[0] = query_sum

    for copy in ring:
        copy.wait_recv()
    for a in range(2):
        for b in range(2):
            total = ks0[a, b, z].astype(F32)
            for j in range(3):
                total = total + k1[j, a, b].astype(F32)
            ks1[a, b] = total.astype(BF16)
    across = k.send(ks1.at[:, 1 - yl], k2, yl_partner)
    across.wait_recv()
    for a in range(2):
        kres[pl.ds(a * ROWS, ROWS)] = ks1[a, yl].astype(F32) + k2[a].astype(F32)
    key_sum = jnp.zeros((HEAD, TOK), F32)
    for g in range(KV_HEADS):
        both = kres[:, g * 128 : (g + 1) * 128].T
        at = QD + g * HEAD
        d_raw, term = head_back(pt[at : at + HEAD], both[:HEAD], cos, sin, kgain[...])
        key_sum = key_sum + term
        dpt[at : at + HEAD] = d_raw
        dpt[at + KD : at + KD + HEAD] = both[HEAD:]
    heads_out[1] = key_sum
    for t in range(15):
        dp_out[:, t * 128 : (t + 1) * 128] = dpt[t * 128 : (t + 1) * 128].T.astype(BF16)
    get_wq.wait()

    @pl.loop(0, 8)
    def _(t):
        w = wqs[t // 4, t % 4].reshape(256, 2048)[:, :QKV]
        cols = pl.ds(pl.multiple_of(t * 256, 256), 256)
        in_grad[:, cols] = dot_last(dp_out[...], w)

    hidden = x_ref[...].astype(F32)
    scale_one = rms_scale(hidden)
    norm_one = hidden * scale_one
    d_normed = in_grad[...]
    rows_out[0:1, :] = jnp.sum(d_normed * norm_one, axis=0, keepdims=True)
    in_grad[...] = dres[...] + norm_back(d_normed, norm_one, scale_one, gains[0:1, :])
    k.drain()


def head_back(raw, grad, cos, sin, gain):
    scale = head_scale(raw)
    normed = raw * scale
    d_head = grad * cos + half_back(grad * sin)
    scaled = d_head * gain
    inner = jnp.mean(scaled * normed, axis=0, keepdims=True)
    return scale * (scaled - normed * inner), d_head * normed


def back(part, x, og, resid, gains, WQ, WO, KV, pt, lse, segc, segq, cos, sin, qgain, kgain):
    outs = [
        sds((TOK, D), F32),
        sds((TOK, QKV), BF16),
        sds((TOK, D), BF16),
        sds((8, D), F32),
        sds((2, HEAD, TOK), F32),
    ]
    w = 2 * KD
    scratch = row_scratch() + [
        pltpu.VMEM((2, 4, 2, 4, 2, 16, 2048), BF16),
        pltpu.VMEM((2, 4, 2, 4, 2, 16, QD), BF16),
        pltpu.VMEM((2, 2, 4, 2, ROWS, w), BF16),
        pltpu.VMEM((2, SEQ, 256), F32),
        pltpu.VMEM((KV_HEADS, 2, 128, 256), BF16),
        pltpu.VMEM((KV_HEADS, 2, 256, 128), BF16),
        pltpu.VMEM((KV_HEADS, 2, 128, 256), BF16),
        pltpu.VMEM((KV_HEADS, 2, 256, 128), BF16),
        pltpu.VMEM((KV_HEADS, 2, HEAD, 256), F32),
        pltpu.VMEM((QKV, TOK), F32),
        pltpu.VMEM((TOK, QD), F32),
        pltpu.VMEM((TOK, D), F32),
        pltpu.VMEM((2, 2, 4, 2, ROWS, w), BF16),
        pltpu.VMEM((2, 2, 4, ROWS, w), BF16),
        pltpu.VMEM((2, 2, 4, ROWS, w), BF16),
        pltpu.VMEM((3, 2, 2, ROWS, w), BF16),
        pltpu.VMEM((2, 2, ROWS, w), BF16),
        pltpu.VMEM((2, ROWS, w), BF16),
        pltpu.VMEM((TOK, w), F32),
        pltpu.SemaphoreType.DMA((20,)),
        pltpu.SemaphoreType.DMA((20,)),
    ]
    return pl.pallas_call(
        back_body,
        out_shape=outs,
        in_specs=[ANY] + [VMEM] * 4 + [ANY] * 3 + [VMEM] * 8,
        out_specs=[VMEM] * len(outs),
        scratch_shapes=scratch,
        name="back",
        compiler_params=pltpu.CompilerParams(
            collective_id=4, has_side_effects=True, vmem_limit_bytes=56 << 20
        ),
    )(part, x, og, resid, gains, WQ, WO, KV, pt, lse, segc, segq, cos, sin, qgain, kgain)


def rope_tables(start):
    half = HEAD // 2
    inverse = 10000.0 ** (-jnp.arange(half, dtype=F32) / half)
    positions = (start + jnp.arange(TOK) % ROWS).astype(F32)
    angles = inverse[:, None] * positions[None, :]
    angles = jnp.concatenate([angles, angles], axis=0)
    return jnp.cos(angles), jnp.sin(angles)


def per_device(
    tokens,
    segment_ids,
    w_qkv,
    w_out,
    w_gate_up,
    w_down,
    attn_gain,
    ffn_gain,
    query_gain,
    key_gain,
    out_grad,
):
    s = lax.axis_index("seq")
    g = lax.axis_index("grp")
    c = s % 2
    start = s * ROWS
    qgain = query_gain.astype(F32)[:, None]
    kgain = key_gain.astype(F32)[:, None]
    gains = jnp.stack([attn_gain, ffn_gain], axis=1)
    wq_in = jnp.concatenate([w_qkv, jnp.pad(gains, ((0, 0), (0, 126)))], axis=1)
    og_in = out_grad.reshape(TOK, D)
    x_in = tokens.reshape(TOK, D)
    segc = segment_ids.T
    query_ids = lax.dynamic_slice_in_dim(segment_ids, start, ROWS, axis=1)
    segq = jnp.tile(jnp.where(query_ids >= 0, query_ids, -2), (1, GROUP))
    cos, sin = rope_tables(start)
    (WQ, WO, WG, WD, OG, RG, KV, pt, lse, attended, resid, normed, gain_rows) = front(
        x_in, wq_in, w_out.T, w_gate_up, w_down.reshape(80, 1024), og_in,
        segc, segq, cos, sin, qgain, kgain,
    )
    WG = WG.reshape(D, 2 * FS)
    WD = WD.reshape(FS, D)
    OG = OG.reshape(8 * TOK, D)
    rows = RG.reshape(8 * TOK, D)

    gate_up = dot(rows, WG)
    gate = gate_up[:, :FS]
    upper = gate_up[:, FS:]
    sigmoid_gate = jax.nn.sigmoid(gate)
    active = gate * sigmoid_gate
    inner = (active * upper).astype(BF16)
    mixed_part = dot(inner, WD).astype(BF16)
    d_inner = dot_last(OG, WD)
    d_gate = d_inner * upper * sigmoid_gate * (1.0 + gate * (1.0 - sigmoid_gate))
    d_upper = d_inner * active
    d_gate_up = jnp.concatenate([d_gate, d_upper], axis=1).astype(BF16)
    d_rows_part = dot_last(d_gate_up, WG).astype(BF16)
    grad_gate_up = dot_rows(rows, d_gate_up).astype(BF16)
    grad_down = dot_rows(inner, OG).astype(BF16)

    input_grad, d_packed, resid_low, terms, head_terms = back(
        d_rows_part.reshape(4, 2, TOK, D), x_in, og_in, resid, gain_rows, WQ, WO, KV, pt, lse,
        segc, segq, cos, sin, qgain, kgain,
    )

    pair = pair_exchange(normed, d_packed, attended, resid_low)
    normed_2, packed_2, attended_2, low_2 = [a.reshape(2 * TOK, -1) for a in pair]
    packed_cols = lax.dynamic_slice_in_dim(packed_2, c * 896, 1024, axis=1)
    attended_cols = lax.dynamic_slice_in_dim(attended_2, c * 640, 640, axis=1)
    grad_q = dot_rows(normed_2, packed_cols).astype(BF16)
    grad_o = dot_rows(low_2, attended_cols).astype(BF16)

    head_sums = jnp.sum(head_terms, axis=2).reshape(1, 128)
    small = jnp.concatenate(
        [terms[:2].reshape(32, 128), jnp.pad(head_sums, ((0, 7), (0, 0)))], axis=0
    )
    gwg, gwd, gq, go, mix, sums = reduce_grads(
        grad_gate_up.reshape(2, 4, 2, 128, 2 * FS),
        grad_down.reshape(2, 4, 2, 80, 1024),
        grad_q.reshape(2, 4, 2, 4, 32, 1024),
        grad_o.reshape(2, 4, 2, 4, 32, 640),
        mixed_part.reshape(4, 2, TOK, D),
        small,
    )
    result = (resid + mix).astype(BF16)
    w_qkv_grad = jnp.concatenate([gq[0], gq[1][:, 128:]], axis=1)
    w_out_grad = jnp.concatenate([go[0], go[1]], axis=1).T
    at = (g * 16 + s) * 16
    attn_sum = lax.dynamic_slice_in_dim(sums[:16].reshape(D), at, 16)
    ffn_sum = lax.dynamic_slice_in_dim(sums[16:32].reshape(D), at, 16)
    return (
        result.reshape(MICRO, ROWS, D),
        input_grad.reshape(MICRO, ROWS, D),
        w_qkv_grad,
        w_out_grad,
        gwg,
        gwd.reshape(40, D),
        attn_sum,
        ffn_sum,
        sums[32, :HEAD],
        sums[32, HEAD:],
    )


def solution(mesh):
    return jax.shard_map(
        per_device,
        mesh=mesh,
        in_specs=(
            P(None, ("grp", "seq"), None),
            P(None, "grp"),
            P(("grp", "seq"), None),
            P(None, ("grp", "seq")),
            P(("grp", "seq"), None),
            P(("grp", "seq"), None),
            P(("grp", "seq")),
            P(("grp", "seq")),
            P(),
            P(),
            P(None, ("grp", "seq"), None),
        ),
        out_specs=(
            P(None, ("grp", "seq"), None),
            P(None, ("grp", "seq"), None),
            P(("grp", "seq"), None),
            P(None, ("grp", "seq")),
            P(("grp", "seq"), None),
            P(("grp", "seq"), None),
            P(("grp", "seq")),
            P(("grp", "seq")),
            P(),
            P(),
        ),
        check_vma=False,
    )
```

time: 629 us -> 425 us (0.68)
  local copies, waits for them, and re-layouts: 117 us -> 20.2 us
  matrix products: 107 us -> 55.2 us
  other arithmetic: 36.9 us -> 10.1 us
  Pallas kernels: 360 us -> 338 us
    concatenate x15 -> x0, local copies, waits for them, and re-layouts: 44.2 us -> none  [the longest x4 24.9 us: per_device(): jnp.concatenate([d_keys.reshape(MICRO, SEQ, KD), d_values.reshape(MICRO,...]
    dot_general x6 -> x0, matrix products: 33.9 us -> none  [the longest x1 7.81 us: per_device(): jnp.einsum('mgjts,mtgjd->msgd', again_low, d_attended, preferred_element_...]
    pallas_call x5 -> x2, Pallas kernels: 231 us -> 215 us  [the longest x1 133 us: front(): pl.pallas_call(front_body, out_shape=hbm + vmem, in_specs=[VMEM] + [ANY]...]
    unnamed x156 -> x31, local copies, waits for them, and re-layouts: 19.5 us -> 4.4 us
    slice x10 -> x1, local copies, waits for them, and re-layouts: 14.3 us -> 0.85 us  [per_device(): terms[:2].reshape(32, 128)]
    dot_general x4 -> x2, matrix products: 31.1 us -> 18.6 us  [dot_last(): lax.dot_general(left, right, (((1,), (1,)), ((), ())), preferred_element_...]
    reshape x6 -> x2, local copies, waits for them, and re-layouts: 11.6 us -> 0.1 us  [the longest x1 0.08 us: per_device(): head_sums = jnp.sum(head_terms, axis=2).reshape(1, 128)]
    mul x20 -> x0, local copies, waits for them, and re-layouts: 10.1 us -> none  [the longest x2 4.56 us: per_device(): jnp.einsum('mgjts,msgd->mtgjd', d_scores, keys, preferred_element_type=F32)]
where the time goes in v2:
time: 425 us; the launch traced here: 424 us
  Pallas kernels  338 us (80%)
  matrix products  55.2 us (13%)
  local copies, waits for them, and re-layouts  20.2 us (5%)
  other arithmetic  10.1 us (2%)
    pallas_call x1, Pallas kernels, front(): pl.pallas_call(front_body, out_shape=hbm + vmem, in_specs=[VMEM] + [ANY]...  133 us
    pallas_call x1, Pallas kernels, reduce_grads(): any_call(grads_body, 'reduce_grads', 6, 6, outs, scratch, 110, 56 << 20)  118 us
    pallas_call x1, Pallas kernels, back(): pl.pallas_call(back_body, out_shape=outs, in_specs=[ANY] + [VMEM] * 4 + [...  82.3 us
    dot_general x4, matrix products, dot_rows(): lax.dot_general(left, right, (((0,), (0,)), ((), ())), preferred_element_...  19.7 us
    dot_general x2, matrix products, dot_last(): lax.dot_general(left, right, (((1,), (1,)), ((), ())), preferred_element_...  18.6 us
    dot_general x2, matrix products, dot(): return jnp.dot(left, right, preferred_element_type=F32)  16.9 us

profile of v2, /device:TPU:1, one launch (start us, length us, event | category | flops | bytes accessed | tf_op | source)
XLA Modules:
  0.0 424.3 jit_solution(15902573810137961608)
XLA Ops:
  2.9 1.7 copy.31
  7.3 1.6 reshape.114.refs_4_
  9.7 1.5 fusion.4.refs_1_
  11.2 133.2 %front.1 = (bf16[2,4,2,4,2,16,2048]{6,5,4,3,2,1,0:T(8,128)(2,1)}, bf16[2,4,2,4,2,16,1280]{6,5,4,3,2,1,0:T(8,128)(2,1)}, bf16[2,4,2,8,16,1280]{5,4,3,2,1,0:T(8,12...) custom-call(bf16[128,2048]{1,0:T(8,128)(2,1)} %bitcast.69, ...), custom_call_target="tpu_custom_call" | custom-call | tf_op jit(solution)/shard_map/front/pallas_call | solution.py:808
  144.4 10.4 %fusion.13 = f32[1024,1280]{0,1:T(8,128)} fusion(bf16[1024,2048]{1,0:T(8,128)(2,1)} %bitcast.78, bf16[2048,1280]{1,0:T(8,128)(2,1)} %bitcast.76), kind=kOutput, calls=%fused_computation.46 | convolution fusion | flops 5368709120 | bytes 14680064 | tf_op jit(solution)/shard_map/dot_general | solution.py:128
  154.8 3.7 reshape.118
  158.5 7.9 %multiply_convert_fusion.2 = (bf16[1024,640]{0,1:T(8,128)(2,1)S(1)}, bf16[1024,640]{0,1:T(8,128)(2,1)S(1)}, bf16[1024,640]{0,1:T(8,128)(2,1)}) fusion(f32[1024,1280]{0,1:T(8,128)} %fusion.13, bf16[1024,2048]{1,0:T(8,128)(2,1)} %bitcast.80, bf16[640,2048]{1,0:T(8,128)(2,1)S(1)} %reshape.118), kind=kOutput, calls=%fused_computation.9 | convolution fusion | flops 2694184960 | bytes 15990784 | tf_op jit(solution)/shard_map/dot_general | solution.py:132
  166.4 10.7 %convolution_convert_fusion.3 = bf16[1024,2048]{1,0:T(8,128)(2,1)} fusion(bf16[2048,1280]{1,0:T(8,128)(2,1)} %bitcast.77, bf16[1024,640]{0,1:T(8,128)(2,1)S(1)} %get-tuple-element.67, bf16[1024,640]{0,1:T(8,128)(2,1)S(1)} %get-tuple-element.66), kind=kOutput, calls=%fused_computation.3 | convolution fusion | flops 5376049152 | bytes 12058624 | tf_op jit(solution)/shard_map/dot_general | solution.py:132
  177.1 82.3 %back.1 = (f32[128,2048]{1,0:T(8,128)}, bf16[128,1920]{1,0:T(8,128)(2,1)}, bf16[128,2048]{1,0:T(8,128)(2,1)}, f32[8,2048]{1,0:T(8,128)}, f32[2,64,128]{2,1,0:T(8,128)}) custom-call(bf16[4,2,128,2048]{3,2,1,0:T(8,128)(2,1)} %bitcast.68, bf16[128,2048]{1,0:T(8,128)(2,1)} %bitcast.70, bf16[128,2048]{1,0:T(8,128)(2,1)} %bitcast.72, ...), custom_call_target="tpu_custom_call" | custom-call | tf_op jit(solution)/shard_map/back/pallas_call | solution.py:996
  259.4 0.8 slice.38
  260.3 0.9 reduce_sum.9
  261.9 6.5 %convolution_convert_fusion.1 = bf16[1024,2048]{1,0:T(8,128)(2,1)} fusion(bf16[1024,640]{0,1:T(8,128)(2,1)} %get-tuple-element.68, bf16[640,2048]{1,0:T(8,128)(2,1)S(1)} %reshape.118), kind=kOutput, calls=%fused_computation.1 | convolution fusion | flops 2686451712 | bytes 8126464 | tf_op jit(solution)/shard_map/dot_general | solution.py:128
  268.5 4.6 %pair_exchange.1 = (bf16[2,128,2048]{2,1,0:T(8,128)(2,1)S(1)}, bf16[2,128,1920]{2,1,0:T(8,128)(2,1)S(1)}, bf16[2,128,1280]{2,1,0:T(8,128)(2,1)S(1)}, bf16[2,128,2048]{2,1,0:T(8,128)(2,1)S(1)}) custom-call(bf16[128,2048]{1,0:T(8,128)(2,1)S(1)} %copy-done, bf16[128,1920]{1,0:T(8,128)(2,1)S(1)} %copy-done.2, bf16[128,1280]{1,0:T(8,128)(2,1)S(1)} %copy-done.3, ...), custom_call_target="tpu_custom_call" | custom-call | tf_op jit(solution)/shard_map/pair_exchange/pallas_call | solution.py:241
  273.9 3.5 convolution_convert_fusion.4
  277.4 3.4 convolution_convert_fusion.2
  280.8 3.1 convolution_convert_fusion.5
  283.9 2.9 reshape.121.refs_1_
  286.8 9.8 %convolution_convert_fusion = bf16[2048,1280]{1,0:T(8,128)(2,1)} fusion(bf16[1024,2048]{1,0:T(8,128)(2,1)} %bitcast.79, bf16[1024,640]{0,1:T(8,128)(2,1)} %copy-done.13, bf16[1024,640]{0,1:T(8,128)(2,1)} %copy-done.12), kind=kOutput, calls=%fused_computation | convolution fusion | flops 5376573440 | bytes 12058624 | tf_op jit(solution)/shard_map/dot_general | solution.py:136
  296.6 117.9 %reduce_grads.1 = (f32[16,10240]{1,0:T(8,128)}, f32[80,1024]{1,0:T(8,128)}, f32[2,16,1024]{2,1,0:T(8,128)}, f32[2,16,640]{2,1,0:T(8,128)}, f32[128,2048]{1,0:T(8,128)}, /*index=5*/f32[40,128]{1,0:T(8,128)}) custom-call(bf16[2,4,2,128,1280]{4,3,2,1,0:T(8,128)(2,1)} %bitcast.64, bf16[2,4,2,80,1024]{4,3,2,1,0:T(8,128)(2,1)} %reshape.121.refs_1_, ...), custom_call_target="tpu_custom_call" | custom-call | tf_op jit(solution)/shard_map/reduce_grads/pallas_call | solution.py:474
  414.6 0.9 slice_bitcast_fusion.3
  416.1 0.9 slice_bitcast_fusion.1
  417.7 2.2 add_convert_fusion
  422.5 1.0 copy.41
  423.5 0.8 copy.42
  (52 shorter events, 11.2 us)
Async XLA Ops:
  166.4 10.7 %copy-start.12 = (bf16[1024,640]{0,1:T(8,128)(2,1)}, bf16[1024,640]{0,1:T(8,128)(2,1)S(1)}, u32[]{:S(2)}) copy-start(bf16[1024,640]{0,1:T(8,128)(2,1)S(1)} %get-tuple-element.66) | copy-start | bytes 3932164
  166.4 10.7 %copy-start.13 = (bf16[1024,640]{0,1:T(8,128)(2,1)}, bf16[1024,640]{0,1:T(8,128)(2,1)S(1)}, u32[]{:S(2)}) copy-start(bf16[1024,640]{0,1:T(8,128)(2,1)S(1)} %get-tuple-element.67) | copy-start | bytes 3932164
  261.9 6.5 %copy-start = (bf16[128,2048]{1,0:T(8,128)(2,1)S(1)}, bf16[128,2048]{1,0:T(8,128)(2,1)}, u32[]{:S(2)}) copy-start(bf16[128,2048]{1,0:T(8,128)(2,1)} %get-tuple-element.43.refs_0_) | copy-start | bytes 1572868
  261.9 6.5 %copy-start.1 = (bf16[128,2048]{1,0:T(8,128)(2,1)S(1)}, bf16[128,2048]{1,0:T(8,128)(2,1)}, u32[]{:S(2)}) copy-start(bf16[128,2048]{1,0:T(8,128)(2,1)} %get-tuple-element.52.refs_3_) | copy-start | bytes 1572868
  261.9 6.5 %copy-start.2 = (bf16[128,1920]{1,0:T(8,128)(2,1)S(1)}, bf16[128,1920]{1,0:T(8,128)(2,1)}, u32[]{:S(2)}) copy-start(bf16[128,1920]{1,0:T(8,128)(2,1)} %get-tuple-element.50.refs_1_) | copy-start | bytes 1474564
  261.9 6.5 %copy-start.3 = (bf16[128,1280]{1,0:T(8,128)(2,1)S(1)}, bf16[128,1280]{1,0:T(8,128)(2,1)}, u32[]{:S(2)}) copy-start(bf16[128,1280]{1,0:T(8,128)(2,1)} %get-tuple-element.51.refs_2_) | copy-start | bytes 983044
  273.1 0.8 copy-start.4
  277.4 3.4 copy-start.10
  277.4 3.4 copy-start.11
  296.6 121.1 %copy-start.5 = (f32[128,2048]{1,0:T(8,128)S(1)}, f32[128,2048]{1,0:T(8,128)}, u32[]{:S(2)}) copy-start(f32[128,2048]{1,0:T(8,128)} %get-tuple-element.38.refs_3_) | copy-start | bytes 3145732
  414.5 5.3 %copy-start.8 = (f32[80,1024]{1,0:T(8,128)S(1)}, f32[80,1024]{1,0:T(8,128)}, u32[]{:S(2)}) copy-start(f32[80,1024]{1,0:T(8,128)} %get-tuple-element.64) | copy-start | bytes 983044
  414.6 6.2 %copy-start.9 = (f32[40,128]{1,0:T(8,128)S(1)}, f32[40,128]{1,0:T(8,128)}, u32[]{:S(2)}) copy-start(f32[40,128]{1,0:T(8,128)} %get-tuple-element.65) | copy-start | bytes 61444
  414.6 7.9 %copy-start.6 = (f32[128,2048]{1,0:T(8,128)S(1)}, f32[128,2048]{1,0:T(8,128)}, u32[]{:S(2)}) copy-start(f32[128,2048]{1,0:T(8,128)} %get-tuple-element.60) | copy-start | bytes 3145732
  417.7 5.8 %copy-start.7 = (f32[16,10240]{1,0:T(8,128)S(1)}, f32[16,10240]{1,0:T(8,128)}, u32[]{:S(2)}) copy-start(f32[16,10240]{1,0:T(8,128)} %get-tuple-element.93) | copy-start | bytes 1966084

commit v3 on v2

--- a/solution.py
+++ b/solution.py
@@ -95,21 +95,6 @@
     pl.semaphore_wait(barrier, len(partners))
 
 
-def any_call(body, name, cid, n_in, outs, scratch, sems, vmem=48 << 20):
-    return pl.pallas_call(
-        body,
-        out_shape=outs,
-        in_specs=[ANY] * n_in,
-        out_specs=[ANY] * len(outs),
-        name=name,
-        scratch_shapes=list(scratch)
-        + [pltpu.SemaphoreType.DMA((sems,)), pltpu.SemaphoreType.DMA((sems,))],
-        compiler_params=pltpu.CompilerParams(
-            collective_id=cid, has_side_effects=True, vmem_limit_bytes=vmem
-        ),
-    )
-
-
 def sds(shape, dtype):
     return jax.ShapeDtypeStruct(shape, dtype)
 
@@ -177,70 +162,6 @@
     )
 
 
-def row_reduce(p, k, part, own, r0, s0, r1, res):
-    z, c = p.z, p.c
-    core = k.send(part.at[:, 1 - c], r0, p.step("c", 1))
-    mine = k.local(part.at[:, c], own)
-    yield
-    mine.wait()
-    core.wait_recv()
-
-    @pl.loop(0, 4)
-    def _(zz):
-        @pl.loop(0, TOK, step=32)
-        def _(t):
-            at = pl.ds(pl.multiple_of(t, 32), 32)
-            s0[zz, at] = (own[zz, at].astype(F32) + r0[zz, at].astype(F32)).astype(BF16)
-
-    ring = [k.send(s0.at[p.pos("z", j)], r1.at[j - 1], p.step("z", j)) for j in (1, 2, 3)]
-    yield
-    for copy in ring:
-        copy.wait_recv()
-
-    @pl.loop(0, TOK, step=32)
-    def _(t):
-        at = pl.ds(pl.multiple_of(t, 32), 32)
-        total = s0[z, at].astype(F32)
-        for j in range(3):
-            total = total + r1[j, at].astype(F32)
-        res[at] = total
-
-
-def row_scratch():
-    return [
-        pltpu.VMEM((4, TOK, D), BF16),
-        pltpu.VMEM((4, TOK, D), BF16),
-        pltpu.VMEM((4, TOK, D), BF16),
-        pltpu.VMEM((3, TOK, D), BF16),
-        pltpu.VMEM((TOK, D), F32),
-    ]
-
-
-def pair_body(n, *refs):
-    ins, outs = refs[:n], refs[n : 2 * n]
-    ssem, rsem = refs[2 * n :]
-    p = Place()
-    k = Links(ssem, rsem)
-    greet([p.step("c", 1)])
-    copies = [k.send(i, o.at[1], p.step("c", 1)) for i, o in zip(ins, outs)]
-    local = [k.local(i, o.at[0]) for i, o in zip(ins, outs)]
-    for copy in local:
-        copy.wait()
-    for copy in copies:
-        copy.wait_recv()
-    k.drain()
-
-
-def pair_exchange(*arrays):
-    n = len(arrays)
-    outs = [sds((2, *a.shape), a.dtype) for a in arrays]
-
-    def body(*refs):
-        pair_body(n, *refs)
-
-    return any_call(body, "pair_exchange", 5, n, outs, [], 2 * n)(*arrays)
-
-
 def add_blocks(dst, own, recv, chunk):
     lead, rows = dst.shape[:-2], dst.shape[-2]
     count = 1
@@ -268,7 +189,7 @@
     own = scr[0]
     cur = src
     for n, (axis, pick) in enumerate(stages):
-        recv, total = scr[1 + 2 * n], scr[2 + 2 * n]
+        recv = scr[1] if n == 0 else scr[2 * n]
         if n == 0:
             mine = k.local(pick(src, p.pos(axis, 0)), own)
         ring = [k.send(pick(cur, p.pos(axis, j)), recv.at[j - 1], p.step(axis, j)) for j in (1, 2, 3)]
@@ -277,15 +198,16 @@
             mine.wait()
         for copy in ring:
             copy.wait_recv()
+        total = own if n == 0 else scr[2 * n + 1]
         add_blocks(total, own if n == 0 else pick(cur, p.pos(axis, 0)), recv, chunk)
         cur = total
 
 
 def staged_scratch(shapes):
-    out = [pltpu.VMEM(shapes[0], BF16)]
-    for n, shape in enumerate(shapes):
+    out = [pltpu.VMEM(shapes[0], BF16), pltpu.VMEM((3, *shapes[0]), BF16)]
+    for n, shape in enumerate(shapes[1:]):
         out.append(pltpu.VMEM((3, *shape), BF16))
-        out.append(pltpu.VMEM(shape, F32 if n == len(shapes) - 1 else BF16))
+        out.append(pltpu.VMEM(shape, F32 if n == len(shapes) - 2 else BF16))
     return out
 
 
@@ -318,18 +240,24 @@
     ]
 
 
-def q_stages(half):
-    cols = pl.ds(half * 512, 512)
-    if half == 0:
+def q_stages(part):
+    cols = pl.ds((0, 384, 768)[part], (384, 384, 256)[part])
+    if part == 0:
         return [
             ("x", lambda r, i: r.at[:, i, :, :, :, cols]),
             ("z", lambda r, i: r.at[:, :, i]),
             ("y", lambda r, i: r.at[i // 2, i % 2]),
         ]
+    if part == 1:
+        return [
+            ("y", lambda r, i: r.at[i // 2, :, i % 2, :, :, cols]),
+            ("x", lambda r, i: r.at[i]),
+            ("z", lambda r, i: r.at[i]),
+        ]
     return [
-        ("y", lambda r, i: r.at[i // 2, :, i % 2, :, :, cols]),
+        ("z", lambda r, i: r.at[:, :, :, i, :, cols]),
+        ("y", lambda r, i: r.at[i // 2, :, i % 2]),
         ("x", lambda r, i: r.at[i]),
-        ("z", lambda r, i: r.at[i]),
     ]
 
 
@@ -341,14 +269,17 @@
     ]
 
 
-GRAD_SHAPES = [
+PLANE_SHAPES = [
     [(4, 128, FS), (128, FS)],
     [(2, 2, 128, FS), (128, FS)],
     [(4, 80, 512), (80, 512)],
     [(2, 2, 80, 512), (80, 512)],
-    [(2, 2, 4, 32, 512), (2, 2, 32, 512), (32, 512)],
-    [(4, 4, 32, 512), (4, 32, 512), (32, 512)],
-    [(2, 4, 2, 32, 640), (4, 32, 640), (32, 640)],
+]
+O_SHAPES = [(2, 4, 2, 32, 640), (4, 32, 640), (32, 640)]
+Q_SHAPES = [
+    [(2, 2, 4, 32, 384), (2, 2, 32, 384), (32, 384)],
+    [(4, 4, 32, 384), (4, 32, 384), (32, 384)],
+    [(2, 4, 2, 32, 256), (4, 32, 256), (32, 256)],
 ]
 
 
@@ -367,115 +298,6 @@
         vec[n + 1] = total
 
 
-def grads_body(*refs):
-    dwg, dwd, dq, do, dmix, small, GWG, GWD, GQ, GO, MIX, SMALL = refs[:12]
-    scr = list(refs[12:])
-    parts = []
-    for shapes in GRAD_SHAPES:
-        n = 1 + 2 * len(shapes)
-        parts.append(scr[:n])
-        scr = scr[n:]
-    mix, (vec, recv), (ssem, rsem) = scr[:5], scr[5:7], scr[7:9]
-    p = Place()
-    k = Links(ssem, rsem)
-    yh, x, yl, z, c = p.yh, p.x, p.yl, p.z, p.c
-    m = z * 2 + c
-    partners = [p.step(a, j) for a in "xyz" for j in (1, 2, 3)]
-    partners += [p.at(z=(z + j) % 4, c=1 - c) for j in range(4)]
-    slab_to, slab_from = slab_target(p), slab_source(p)
-    own_slab = same(p, slab_to)
-    greet_plane(p, partners, slab_to, slab_from, own_slab)
-
-    chunk = 16
-    gens = [
-        staged_reduce(p, k, dwg, wg_stages(0), parts[0], chunk),
-        staged_reduce(p, k, dwg, wg_stages(1), parts[1], chunk),
-        staged_reduce(p, k, dwd, wd_stages(0), parts[2], chunk),
-        staged_reduce(p, k, dwd, wd_stages(1), parts[3], chunk),
-        row_reduce(p, k, dmix, *mix),
-        staged_reduce(p, k, do, o_stages(), parts[6], chunk),
-        staged_reduce(p, k, dq, q_stages(0), parts[4], chunk),
-        staged_reduce(p, k, dq, q_stages(1), parts[5], chunk),
-        small_reduce(p, k, small, vec, recv),
-    ]
-    alive = list(gens)
-    while alive:
-        alive = [g for g in alive if next(g, alive) is not alive]
-
-    last, local = [], []
-    for half in range(2):
-        total = parts[half][-1]
-        cols = pl.ds(pl.multiple_of(half * FF + m * FS, 128), FS)
-        for dz in range(4):
-            for dc in range(2):
-                zz, cc = (z + dz) % 4, (c + dc) % 2
-                src = total.at[pl.ds(pl.multiple_of((zz * 2 + cc) * 16, 16), 16)]
-                if dz == 0 and dc == 0:
-                    local.append(k.local(src, GWG.at[:, cols]))
-                else:
-                    last.append(k.send(src, GWG.at[:, cols], p.at(z=zz, c=cc)))
-    slabs = []
-    for half in range(2):
-        i = k.used
-        k.used += 1
-        src, dst = parts[2 + half][-1], GWD.at[:, pl.ds(half * 512, 512)]
-        slabs.append((src, dst, i))
-
-        @pl.when(own_slab)
-        def _(src=src, dst=dst, i=i):
-            pltpu.make_async_copy(src, dst, rsem.at[i]).start()
-
-        @pl.when(jnp.logical_not(own_slab))
-        def _(src=src, dst=dst, i=i):
-            slab_copy(src, dst, ssem, rsem, i, slab_from).start()
-
-    for total, dst in (
-        (parts[4][-1], GQ.at[c, :, pl.ds(0, 512)]),
-        (parts[5][-1], GQ.at[c, :, pl.ds(512, 512)]),
-        (parts[6][-1], GO.at[c]),
-    ):
-        mine = total.at[pl.ds(pl.multiple_of(c * 16, 16), 16)]
-        other = total.at[pl.ds(pl.multiple_of((1 - c) * 16, 16), 16)]
-        local.append(k.local(mine, dst))
-        last.append(k.send(other, dst, p.step("c", 1)))
-    local.append(k.local(mix[-1], MIX))
-    local.append(k.local(vec.at[4], SMALL))
-    for copy in local:
-        copy.wait()
-    for copy in last:
-        copy.wait_recv()
-    for src, dst, i in slabs:
-
-        @pl.when(own_slab)
-        def _(src=src, dst=dst, i=i):
-            pltpu.make_async_copy(src, dst, rsem.at[i]).wait()
-
-        @pl.when(jnp.logical_not(own_slab))
-        def _(src=src, dst=dst, i=i):
-            slab_copy(src, dst, ssem, rsem, i, slab_from).wait()
-
-    k.drain()
-
-
-def reduce_grads(dwg, dwd, dq, do, dmix, small):
-    outs = [
-        sds((16, 2 * FF), F32),
-        sds((80, 1024), F32),
-        sds((2, 16, 1024), F32),
-        sds((2, 16, 640), F32),
-        sds((TOK, D), F32),
-        sds((40, 128), F32),
-    ]
-    scratch = []
-    for shapes in GRAD_SHAPES:
-        scratch += staged_scratch(shapes)
-    scratch += row_scratch()
-    scratch += [pltpu.VMEM((5, 40, 128), F32), pltpu.VMEM((4, 3, 40, 128), F32)]
-    return any_call(grads_body, "reduce_grads", 6, 6, outs, scratch, 110, 56 << 20)(
-        dwg, dwd, dq, do, dmix, small
-    )
-
-
 def swap(a, b):
     left = lax.broadcasted_iota(jnp.int32, a.shape, 1) < ROWS
     return jnp.where(left, a, pltpu.roll(b, ROWS, 1)), jnp.where(left, pltpu.roll(a, ROWS, 1), b)
@@ -530,8 +352,8 @@
 
 def front_body(*refs):
     (x_ref, wq, wo, wg, wd, og, segc, segq, cos_ref, sin_ref, qgain, kgain) = refs[:12]
-    (WQ, WO, WG, WD, OG, RG, KV, pt_out, lse_out, att_out, resid_out, normed_out, gains_out) = refs[12:25]
-    (wqs, wos, kvl, kvs, bias, qts, ots, n2, ssem, rsem) = refs[25:]
+    (WQ, WO, WG, WD, OG, KV, pt_out, lse_out, att_out, resid_out, normed_out, gains_out, n2_out) = refs[12:25]
+    (wqs, wos, kvl, kvs, bias, qts, ots, ssem, rsem) = refs[25:]
     p = Place()
     k = Links(ssem, rsem)
     yh, x, yl, z, c = p.yh, p.x, p.yl, p.z, p.c
@@ -749,21 +571,14 @@
         resid_out[:, cols] = x_ref[:, cols].astype(F32) + dot_last(att_out[...], w)
 
     resid = resid_out[...]
-    n2[...] = (resid * rms_scale(resid) * gains_out[1:2, :]).astype(BF16)
-    own_n2 = k.local(n2, RG.at[z, c])
-    ring2 = [k.send(n2, RG.at[z, c], p.step("z", j)) for j in (1, 2, 3)]
-    last.append(k.send(n2, RG.at[z, c], p.step("c", 1)))
+    n2_out[...] = (resid * rms_scale(resid) * gains_out[1:2, :]).astype(BF16)
     for j, copy in zip((1, 2, 3), rows):
         copy.wait_recv()
         src = OG.at[p.pos("z", -j), c]
         last.append(k.send(src, src, p.step("c", 1)))
-    for j, copy in zip((1, 2, 3), ring2):
-        copy.wait_recv()
-        src = RG.at[p.pos("z", -j), c]
-        last.append(k.send(src, src, p.step("c", 1)))
     for copy in plane2 + last:
         copy.wait_recv()
-    for copy in (keep_wq, keep_kv, keep_wo, own_og, own_n2):
+    for copy in (keep_wq, keep_kv, keep_wo, own_og):
         copy.wait()
     k.drain()
 
@@ -782,7 +597,6 @@
         sds((2, 4, 2, 8, 16, 2 * FS), BF16),
         sds((2, 4, 2, 80, 1024), BF16),
         sds((4, 2, TOK, D), BF16),
-        sds((4, 2, TOK, D), BF16),
         sds((2, 2, 4, 2, ROWS, 2 * KD), BF16),
     ]
     vmem = [
@@ -792,6 +606,7 @@
         sds((TOK, D), F32),
         sds((TOK, D), BF16),
         sds((8, D), F32),
+        sds((TOK, D), BF16),
     ]
     scratch = [
         pltpu.VMEM((2, 4, 2, 4, 2, 16, 2048), BF16),
@@ -801,7 +616,6 @@
         pltpu.VMEM((2, SEQ, 256), F32),
         pltpu.VMEM((KV_HEADS, 2, 128, 256), BF16),
         pltpu.VMEM((KV_HEADS, 2, HEAD, 256), F32),
-        pltpu.VMEM((TOK, D), BF16),
         pltpu.SemaphoreType.DMA((120,)),
         pltpu.SemaphoreType.DMA((120,)),
     ]
@@ -818,24 +632,231 @@
     )(x, wq, wo, wg, wd, og, segc, segq, cos, sin, qgain, kgain)
 
 
+def ffn_body(n2, OG, WG, WD, d_out, mix_out, dwg_out, dwd_out, *scr):
+    (rows, ogs, wgs, wd80, wds, dgu, inn, din, part, mixs, r0, s0, r1, dwg, dwd32, dwd, ssem, rsem, lsem) = scr
+    p = Place()
+    z, c = p.z, p.c
+    sib = p.step("c", 1)
+    greet([p.step("z", j) for j in (1, 2, 3)] + [sib])
+
+    def remote(src, dst, i, to):
+        return pltpu.make_async_remote_copy(
+            src_ref=src,
+            dst_ref=dst,
+            send_sem=ssem.at[i],
+            recv_sem=rsem.at[i],
+            device_id=to,
+            device_id_type=MESH,
+        )
+
+    def local(src, dst, i):
+        copy = pltpu.make_async_copy(src, dst, lsem.at[i])
+        copy.start()
+        return copy
+
+    sent = []
+    for j in (1, 2, 3):
+        copy = remote(n2, rows.at[z, c], j, p.step("z", j))
+        copy.start()
+        sent.append(copy)
+    remote(n2, rows.at[z, c], 4, sib).start()
+    own = local(n2, rows.at[z, c], 0)
+    get_wd = local(WD, wd80, 1)
+    get_wg = local(WG, wgs, 2)
+    get_og = local(OG, ogs, 3)
+    get_wd.wait()
+
+    @pl.loop(0, 8)
+    def _(i):
+        yl, x = i // 4, i % 4
+        a, b = wd80[yl, x, 0].astype(F32), wd80[yl, x, 1].astype(F32)
+        at = pl.ds(pl.multiple_of(i * 80, 80), 80)
+        wds[at, :1024] = jnp.concatenate([a[:40], b[:40]], axis=0).astype(BF16)
+        wds[at, 1024:] = jnp.concatenate([a[40:], b[40:]], axis=0).astype(BF16)
+
+    own.wait()
+    get_wg.wait()
+    get_og.wait()
+
+    @pl.loop(0, 4)
+    def _(j):
+        o = jnp.where(j == 2, 3, jnp.where(j == 3, 2, j))
+        zz = (z + o) % 4
+        at = pl.ds(pl.multiple_of(zz * 256, 256), 256)
+
+        @pl.when(o > 0)
+        def _():
+            remote(n2, rows.at[zz, c], (4 - o) % 4, sib).wait_recv()
+            remote(rows.at[zz, c], rows.at[zz, c], 4 + o, sib).start()
+
+        remote(rows.at[zz, c], rows.at[zz, 1 - c], 4 + o, sib).wait_recv()
+        r = rows[zz].reshape(256, D)
+        din[...] = dot_last(ogs[zz].reshape(256, D), wds[...])
+        for t in range(5):
+            lo, hi = slice(t * 128, (t + 1) * 128), slice(FS + t * 128, FS + (t + 1) * 128)
+            w = jnp.concatenate(
+                [wgs[:, :, :, :, :, lo].reshape(D, 128), wgs[:, :, :, :, :, hi].reshape(D, 128)], axis=1
+            )
+            both = dot(r, w)
+            gate, upper = both[:, :128], both[:, 128:]
+            sig = jax.nn.sigmoid(gate)
+            active = gate * sig
+            d_inner = din[:, lo]
+            inn[at, lo] = (active * upper).astype(BF16)
+            dgu[at, lo] = (d_inner * upper * sig * (1.0 + gate * (1.0 - sig))).astype(BF16)
+            dgu[at, hi] = (d_inner * active).astype(BF16)
+
+        @pl.loop(0, 8)
+        def _(t):
+            w = wgs[t // 4, t % 4].reshape(256, 2 * FS)
+            cols = pl.ds(pl.multiple_of(t * 256, 256), 256)
+            part[zz, :, :, cols] = dot_last(dgu[at], w).astype(BF16).reshape(2, TOK, 256)
+
+        remote(part.at[zz, 1 - c], r0.at[zz], 8 + o, sib).start()
+
+        @pl.loop(0, 4)
+        def _(t):
+            cols = pl.ds(pl.multiple_of(t * 512, 512), 512)
+            mixs[zz, :, :, cols] = dot(inn[at], wds[:, cols]).astype(BF16).reshape(2, TOK, 512)
+
+        remote(part.at[zz, 1 - c], r0.at[zz], 8 + o, sib).wait_recv()
+
+        @pl.loop(0, TOK, step=16)
+        def _(t):
+            here = pl.ds(pl.multiple_of(t, 16), 16)
+            s0[zz, here] = (part[zz, c, here].astype(F32) + r0[zz, here].astype(F32)).astype(BF16)
+
+        @pl.when(o > 0)
+        def _():
+            remote(s0.at[zz], r1.at[o - 1], 12 + o, p.at(z=zz)).start()
+
+    out_mix = local(mixs, mix_out, 4)
+
+    @pl.loop(0, 8)
+    def _(t):
+        cols = pl.ds(pl.multiple_of(t * 256, 256), 256)
+        left = rows[:, :, :, cols].reshape(8 * TOK, 256)
+        dwg[t // 4, t % 4] = dot_rows(left, dgu[...]).astype(BF16).reshape(2, TOK, 2 * FS)
+
+    out_wg = local(dwg, dwg_out, 5)
+
+    @pl.loop(0, 5)
+    def _(t):
+        units = pl.ds(pl.multiple_of(t * 128, 128), 128)
+        dwd32[units] = dot_rows(inn[:, units], ogs[...].reshape(8 * TOK, D))
+
+    @pl.loop(0, 8)
+    def _(i):
+        yl, x = i // 4, i % 4
+        at = pl.ds(pl.multiple_of(i * 80, 80), 80)
+        lo, hi = dwd32[at, :1024], dwd32[at, 1024:]
+        dwd[yl, x, 0] = jnp.concatenate([lo[:40], hi[:40]], axis=0).astype(BF16)
+        dwd[yl, x, 1] = jnp.concatenate([lo[40:], hi[40:]], axis=0).astype(BF16)
+
+    out_wd = local(dwd, dwd_out, 6)
+    for o in (1, 2, 3):
+        remote(s0.at[0], r1.at[o - 1], 12 + o, sib).wait_recv()
+
+    @pl.loop(0, TOK, step=16)
+    def _(t):
+        here = pl.ds(pl.multiple_of(t, 16), 16)
+        total = s0[z, here].astype(F32)
+        for j in range(3):
+            total = total + r1[j, here].astype(F32)
+        d_out[here] = total
+
+    for copy in sent:
+        copy.wait_send()
+    for o in range(4):
+        remote(rows.at[0, 0], rows.at[0, 0], 4 + o, sib).wait_send()
+        remote(part.at[0, 0], r0.at[0], 8 + o, sib).wait_send()
+    for o in (1, 2, 3):
+        remote(s0.at[0], r1.at[o - 1], 12 + o, sib).wait_send()
+    for copy in (out_mix, out_wg, out_wd):
+        copy.wait()
+
+
+def ffn(n2, OG, WG, WD):
+    outs = [
+        sds((TOK, D), F32),
+        sds((4, 2, TOK, D), BF16),
+        sds((2, 4, 2, TOK, 2 * FS), BF16),
+        sds((2, 4, 2, 80, 1024), BF16),
+    ]
+    scratch = [
+        pltpu.VMEM((4, 2, TOK, D), BF16),
+        pltpu.VMEM((4, 2, TOK, D), BF16),
+        pltpu.VMEM((2, 4, 2, 8, 16, 2 * FS), BF16),
+        pltpu.VMEM((2, 4, 2, 80, 1024), BF16),
+        pltpu.VMEM((FS, D), BF16),
+        pltpu.VMEM((8 * TOK, 2 * FS), BF16),
+        pltpu.VMEM((8 * TOK, FS), BF16),
+        pltpu.VMEM((256, FS), F32),
+        pltpu.VMEM((4, 2, TOK, D), BF16),
+        pltpu.VMEM((4, 2, TOK, D), BF16),
+        pltpu.VMEM((4, TOK, D), BF16),
+        pltpu.VMEM((4, TOK, D), BF16),
+        pltpu.VMEM((3, TOK, D), BF16),
+        pltpu.VMEM((2, 4, 2, TOK, 2 * FS), BF16),
+        pltpu.VMEM((FS, D), F32),
+        pltpu.VMEM((2, 4, 2, 80, 1024), BF16),
+        pltpu.SemaphoreType.DMA((16,)),
+        pltpu.SemaphoreType.DMA((16,)),
+        pltpu.SemaphoreType.DMA((7,)),
+    ]
+    return pl.pallas_call(
+        ffn_body,
+        out_shape=outs,
+        in_specs=[VMEM] + [ANY] * 3,
+        out_specs=[VMEM] + [ANY] * 3,
+        scratch_shapes=scratch,
+        name="ffn",
+        compiler_params=pltpu.CompilerParams(
+            collective_id=1, has_side_effects=True, vmem_limit_bytes=60 << 20
+        ),
+    )(n2, OG, WG, WD)
+
+
 def back_body(*refs):
-    (part, x_ref, og_ref, resid_ref, gains, WQ, WO, KV, pt, lse, segc, segq, cos_ref, sin_ref, qgain, kgain) = refs[:16]
-    (in_grad, dp_out, low_out, rows_out, heads_out) = refs[16:21]
-    (rown, rr0, rs0, rr1, rres) = refs[21:26]
-    (wqs, wos, kvs, bias, qts, qns, dts, dns, dqt, dpt, datt, dres, kpart) = refs[26:39]
-    (k0, ks0, k1, ks1, k2, kres, ssem, rsem) = refs[39:]
+    (dn_ref, x_ref, og_ref, resid_ref, gains, att_ref, pt, lse, segc, segq, cos_ref, sin_ref, qgain, kgain) = refs[:14]
+    (WQ, WO, KV, mix_part, dwg, dwd) = refs[14:20]
+    (in_grad, dp_out, rows_out, heads_out, mixed_out, GWG, GWD, GO) = refs[20:28]
+    (wos, kvs, bias, qts, qns, dts, dns, dqt, dpt, datt, dres, kpart) = refs[28:40]
+    (k0, k1, ks1, k2, kres, wq2, low2, att2, do) = refs[40:49]
+    scr = list(refs[49:])
+    parts = []
+    for shapes in PLANE_SHAPES + [O_SHAPES]:
+        n = 2 * len(shapes)
+        parts.append(scr[:n])
+        scr = scr[n:]
+    mix, (ssem, rsem) = scr[:3], scr[3:]
     p = Place()
     k = Links(ssem, rsem)
     yl, z, c = p.yl, p.z, p.c
+    m = z * 2 + c
+    sib = p.step("c", 1)
     yl_partner = p.at(y=p.yh * 2 + 1 - yl)
-    greet([p.step("z", j) for j in (1, 2, 3)] + [yl_partner, p.step("c", 1)])
+    partners = [p.step(a, j) for a in "xyz" for j in (1, 2, 3)]
+    partners += [p.at(z=(z + j) % 4, c=1 - c) for j in range(4)]
+    slab_to, slab_from = slab_target(p), slab_source(p)
+    own_slab = same(p, slab_to)
+    greet_plane(p, partners, slab_to, slab_from, own_slab)
     get_wo = k.local(WO, wos)
     get_kv = k.local(KV, kvs)
-    get_wq = k.local(WQ, wqs)
-    steps = row_reduce(p, k, part, rown, rr0, rs0, rr1, rres)
-    next(steps)
+    plane = [
+        staged_reduce(p, k, dwg, wg_stages(0), parts[0], 16),
+        staged_reduce(p, k, dwg, wg_stages(1), parts[1], 16),
+        staged_reduce(p, k, dwd, wd_stages(0), parts[2], 16),
+        staged_reduce(p, k, dwd, wd_stages(1), parts[3], 16),
+    ]
+    for step in plane:
+        next(step)
+    mixing = mix_reduce(p, k, mix_part, mix, resid_ref, mixed_out)
+    next(mixing)
+    own_att = k.local(att_ref, att2.at[0])
+    pair_att = k.send(att_ref, att2.at[1], sib)
     fill_bias(bias, segc, segq, p.s * ROWS)
-    next(steps)
+    next(mixing)
     cos, sin = cos_ref[...], sin_ref[...]
 
     @pl.loop(0, KV_HEADS)
@@ -844,22 +865,22 @@
             qts[g, mm] = unit.astype(BF16)
             qns[g, mm] = unit.T.astype(BF16)
 
-    next(steps, None)
     resid = resid_ref[...]
     scale_two = rms_scale(resid)
     norm_two = resid * scale_two
-    d_normed = rres[...]
+    d_normed = dn_ref[...]
     rows_out[1:2, :] = jnp.sum(d_normed * norm_two, axis=0, keepdims=True)
     d_resid = og_ref[...].astype(F32) + norm_back(d_normed, norm_two, scale_two, gains[1:2, :])
     dres[...] = d_resid
-    low_out[...] = d_resid.astype(BF16)
+    low2[0] = d_resid.astype(BF16)
+    pair_low = k.send(low2.at[0], low2.at[1], sib)
     get_wo.wait()
 
     @pl.loop(0, 5)
     def _(t):
         cols = pl.ds(pl.multiple_of(t * 256, 256), 256)
         w = wos[:, :, :, :, :, :, cols].reshape(D, 256)
-        datt[:, cols] = low(dot(low_out[...], w))
+        datt[:, cols] = low(dot(low2[0], w))
 
     for g in range(KV_HEADS):
         tiles = []
@@ -895,9 +916,24 @@
     def _(zz):
         for a in range(2):
             for b in range(2):
-                ks0[a, b, zz] = (kpart[a, b, zz, c].astype(F32) + k0[a, b, zz].astype(F32)).astype(BF16)
-
-    ring = [k.send(ks0.at[:, :, p.pos("z", j)], k1.at[j - 1], p.step("z", j)) for j in (1, 2, 3)]
+                k0[a, b, zz] = (kpart[a, b, zz, c].astype(F32) + k0[a, b, zz].astype(F32)).astype(BF16)
+
+    ring = [k.send(k0.at[:, :, p.pos("z", j)], k1.at[j - 1], p.step("z", j)) for j in (1, 2, 3)]
+
+    own_att.wait()
+    pair_att.wait_recv()
+    pair_low.wait_recv()
+    att_cols = pl.ds(pl.multiple_of(c * 640, 128), 640)
+
+    @pl.loop(0, 8)
+    def _(t):
+        cols = pl.ds(pl.multiple_of(t * 256, 256), 256)
+        left = low2[:, :, cols].reshape(2 * TOK, 256)
+        right = att2[:, :, att_cols].reshape(2 * TOK, 640)
+        do[t // 4, t % 4] = dot_rows(left, right).astype(BF16).reshape(2, 4, 32, 640)
+
+    outward = staged_reduce(p, k, do, o_stages(), parts[4], 16)
+    next(outward)
 
     query_sum = jnp.zeros((HEAD, TOK), F32)
     for g in range(KV_HEADS):
@@ -916,7 +952,7 @@
         copy.wait_recv()
     for a in range(2):
         for b in range(2):
-            total = ks0[a, b, z].astype(F32)
+            total = k0[a, b, z].astype(F32)
             for j in range(3):
                 total = total + k1[j, a, b].astype(F32)
             ks1[a, b] = total.astype(BF16)
@@ -933,23 +969,107 @@
         dpt[at : at + HEAD] = d_raw
         dpt[at + KD : at + KD + HEAD] = both[HEAD:]
     heads_out[1] = key_sum
+    get_wq = [k.local(WQ.at[0, 0], wq2.at[0])]
     for t in range(15):
         dp_out[:, t * 128 : (t + 1) * 128] = dpt[t * 128 : (t + 1) * 128].T.astype(BF16)
-    get_wq.wait()
-
-    @pl.loop(0, 8)
-    def _(t):
-        w = wqs[t // 4, t % 4].reshape(256, 2048)[:, :QKV]
-        cols = pl.ds(pl.multiple_of(t * 256, 256), 256)
-        in_grad[:, cols] = dot_last(dp_out[...], w)
-
+    for step in plane:
+        next(step)
+    for t in range(8):
+        if t < 7:
+            get_wq.append(k.local(WQ.at[(t + 1) // 4, (t + 1) % 4], wq2.at[(t + 1) % 2]))
+        get_wq[t].wait()
+        w = wq2[t % 2].reshape(256, 2048)[:, :QKV]
+        in_grad[:, t * 256 : (t + 1) * 256] = dot_last(dp_out[...], w)
+    next(outward)
     hidden = x_ref[...].astype(F32)
     scale_one = rms_scale(hidden)
     norm_one = hidden * scale_one
     d_normed = in_grad[...]
     rows_out[0:1, :] = jnp.sum(d_normed * norm_one, axis=0, keepdims=True)
     in_grad[...] = dres[...] + norm_back(d_normed, norm_one, scale_one, gains[0:1, :])
+    next(mixing, None)
+    next(outward)
+    for step in plane:
+        next(step, None)
+
+    last, local = [], []
+    for half in range(2):
+        total = parts[half][-1]
+        cols = pl.ds(pl.multiple_of(half * FF + m * FS, 128), FS)
+        for dz in range(4):
+            for dc in range(2):
+                zz, cc = (z + dz) % 4, (c + dc) % 2
+                src = total.at[pl.ds(pl.multiple_of((zz * 2 + cc) * 16, 16), 16)]
+                if dz == 0 and dc == 0:
+                    local.append(k.local(src, GWG.at[:, cols]))
+                else:
+                    last.append(k.send(src, GWG.at[:, cols], p.at(z=zz, c=cc)))
+    slabs = []
+    for half in range(2):
+        i = k.used
+        k.used += 1
+        src, dst = parts[2 + half][-1], GWD.at[:, pl.ds(half * 512, 512)]
+        slabs.append((src, dst, i))
+
+        @pl.when(own_slab)
+        def _(src=src, dst=dst, i=i):
+            pltpu.make_async_copy(src, dst, rsem.at[i]).start()
+
+        @pl.when(jnp.logical_not(own_slab))
+        def _(src=src, dst=dst, i=i):
+            slab_copy(src, dst, ssem, rsem, i, slab_from).start()
+
+    next(outward, None)
+    total = parts[4][-1]
+    mine = total.at[pl.ds(pl.multiple_of(c * 16, 16), 16)]
+    other = total.at[pl.ds(pl.multiple_of((1 - c) * 16, 16), 16)]
+    local.append(k.local(mine, GO.at[c]))
+    last.append(k.send(other, GO.at[c], sib))
+    for copy in local:
+        copy.wait()
+    for copy in last:
+        copy.wait_recv()
+    for src, dst, i in slabs:
+
+        @pl.when(own_slab)
+        def _(src=src, dst=dst, i=i):
+            pltpu.make_async_copy(src, dst, rsem.at[i]).wait()
+
+        @pl.when(jnp.logical_not(own_slab))
+        def _(src=src, dst=dst, i=i):
+            slab_copy(src, dst, ssem, rsem, i, slab_from).wait()
+
     k.drain()
+
+
+def mix_reduce(p, k, part, scr, resid, out):
+    own, r0, r1 = scr
+    z, c = p.z, p.c
+    core = k.send(part.at[:, 1 - c], r0, p.step("c", 1))
+    mine = k.local(part.at[:, c], own)
+    yield
+    mine.wait()
+    core.wait_recv()
+
+    @pl.loop(0, 4)
+    def _(zz):
+        @pl.loop(0, TOK, step=16)
+        def _(t):
+            at = pl.ds(pl.multiple_of(t, 16), 16)
+            own[zz, at] = (own[zz, at].astype(F32) + r0[zz, at].astype(F32)).astype(BF16)
+
+    ring = [k.send(own.at[p.pos("z", j)], r1.at[j - 1], p.step("z", j)) for j in (1, 2, 3)]
+    yield
+    for copy in ring:
+        copy.wait_recv()
+
+    @pl.loop(0, TOK, step=16)
+    def _(t):
+        at = pl.ds(pl.multiple_of(t, 16), 16)
+        total = own[z, at].astype(F32)
+        for j in range(3):
+            total = total + r1[j, at].astype(F32)
+        out[at] = (resid[at] + total).astype(BF16)
 
 
 def head_back(raw, grad, cos, sin, gain):
@@ -961,17 +1081,17 @@
     return scale * (scaled - normed * inner), d_head * normed
 
 
-def back(part, x, og, resid, gains, WQ, WO, KV, pt, lse, segc, segq, cos, sin, qgain, kgain):
-    outs = [
+def back(dn, x, og, resid, gains, att, pt, lse, segc, segq, cos, sin, qgain, kgain, WQ, WO, KV, mix, dwg, dwd):
+    w = 2 * KD
+    vmem = [
         sds((TOK, D), F32),
         sds((TOK, QKV), BF16),
-        sds((TOK, D), BF16),
         sds((8, D), F32),
         sds((2, HEAD, TOK), F32),
-    ]
-    w = 2 * KD
-    scratch = row_scratch() + [
-        pltpu.VMEM((2, 4, 2, 4, 2, 16, 2048), BF16),
+        sds((TOK, D), BF16),
+    ]
+    hbm = [sds((16, 2 * FF), F32), sds((80, 1024), F32), sds((2, 16, 640), F32)]
+    scratch = [
         pltpu.VMEM((2, 4, 2, 4, 2, 16, QD), BF16),
         pltpu.VMEM((2, 2, 4, 2, ROWS, w), BF16),
         pltpu.VMEM((2, SEQ, 256), F32),
@@ -985,25 +1105,119 @@
         pltpu.VMEM((TOK, D), F32),
         pltpu.VMEM((2, 2, 4, 2, ROWS, w), BF16),
         pltpu.VMEM((2, 2, 4, ROWS, w), BF16),
-        pltpu.VMEM((2, 2, 4, ROWS, w), BF16),
         pltpu.VMEM((3, 2, 2, ROWS, w), BF16),
         pltpu.VMEM((2, 2, ROWS, w), BF16),
         pltpu.VMEM((2, ROWS, w), BF16),
         pltpu.VMEM((TOK, w), F32),
-        pltpu.SemaphoreType.DMA((20,)),
-        pltpu.SemaphoreType.DMA((20,)),
+        pltpu.VMEM((2, 2, 4, 2, 16, 2048), BF16),
+        pltpu.VMEM((2, TOK, D), BF16),
+        pltpu.VMEM((2, TOK, QD), BF16),
+        pltpu.VMEM((2, 4, 2, 4, 32, 640), BF16),
+    ]
+    for shapes in PLANE_SHAPES + [O_SHAPES]:
+        scratch += staged_scratch(shapes)
+    scratch += [
+        pltpu.VMEM((4, TOK, D), BF16),
+        pltpu.VMEM((4, TOK, D), BF16),
+        pltpu.VMEM((3, TOK, D), BF16),
+        pltpu.SemaphoreType.DMA((100,)),
+        pltpu.SemaphoreType.DMA((100,)),
     ]
     return pl.pallas_call(
         back_body,
-        out_shape=outs,
-        in_specs=[ANY] + [VMEM] * 4 + [ANY] * 3 + [VMEM] * 8,
-        out_specs=[VMEM] * len(outs),
+        out_shape=vmem + hbm,
+        in_specs=[VMEM] * 14 + [ANY] * 6,
+        out_specs=[VMEM] * len(vmem) + [ANY] * len(hbm),
         scratch_shapes=scratch,
         name="back",
         compiler_params=pltpu.CompilerParams(
-            collective_id=4, has_side_effects=True, vmem_limit_bytes=56 << 20
+            collective_id=2, has_side_effects=True, vmem_limit_bytes=60 << 20
         ),
-    )(part, x, og, resid, gains, WQ, WO, KV, pt, lse, segc, segq, cos, sin, qgain, kgain)
+    )(dn, x, og, resid, gains, att, pt, lse, segc, segq, cos, sin, qgain, kgain, WQ, WO, KV, mix, dwg, dwd)
+
+
+def tail_body(normed, packed, small, GQ, SMALL, *scr):
+    normed2, packed2, dq = scr[:3]
+    scr = list(scr[3:])
+    parts = []
+    for shapes in Q_SHAPES:
+        n = 2 * len(shapes)
+        parts.append(scr[:n])
+        scr = scr[n:]
+    vec, recv, ssem, rsem = scr
+    p = Place()
+    k = Links(ssem, rsem)
+    c = p.c
+    sib = p.step("c", 1)
+    greet([p.step(a, j) for a in "xyz" for j in (1, 2, 3)] + [sib])
+    pair = [k.send(packed, packed2.at[1], sib), k.send(normed, normed2.at[1], sib)]
+    own = [k.local(packed, packed2.at[0]), k.local(normed, normed2.at[0])]
+    sums = small_reduce(p, k, small, vec, recv)
+    next(sums)
+    for copy in own:
+        copy.wait()
+    for copy in pair:
+        copy.wait_recv()
+    flows = []
+    for part, (start, width) in enumerate(((0, 384), (384, 384), (768, 256))):
+        cols = pl.ds(pl.multiple_of(c * 896 + start, 128), width)
+
+        @pl.loop(0, 8)
+        def _(t):
+            rows = pl.ds(pl.multiple_of(t * 256, 256), 256)
+            left = normed2[:, :, rows].reshape(2 * TOK, 256)
+            right = packed2[:, :, cols].reshape(2 * TOK, width)
+            total = dot_rows(left, right).astype(BF16).reshape(2, 4, 32, width)
+            dq[t // 4, t % 4, :, :, :, pl.ds(start, width)] = total
+
+        flow = staged_reduce(p, k, dq, q_stages(part), parts[part], 16)
+        next(flow)
+        flows.append(flow)
+        next(sums, None)
+    alive = list(flows)
+    while alive:
+        alive = [f for f in alive if next(f, alive) is not alive]
+        next(sums, None)
+    next(sums, None)
+    last, local = [], []
+    for part, (start, width) in enumerate(((0, 384), (384, 384), (768, 256))):
+        total = parts[part][-1]
+        dst = GQ.at[c, :, pl.ds(start, width)]
+        local.append(k.local(total.at[pl.ds(pl.multiple_of(c * 16, 16), 16)], dst))
+        last.append(k.send(total.at[pl.ds(pl.multiple_of((1 - c) * 16, 16), 16)], dst, sib))
+    SMALL[...] = vec[4]
+    for copy in local:
+        copy.wait()
+    for copy in last:
+        copy.wait_recv()
+    k.drain()
+
+
+def tail(normed, packed, small):
+    scratch = [
+        pltpu.VMEM((2, TOK, D), BF16),
+        pltpu.VMEM((2, TOK, QKV), BF16),
+        pltpu.VMEM((2, 4, 2, 4, 32, 1024), BF16),
+    ]
+    for shapes in Q_SHAPES:
+        scratch += staged_scratch(shapes)
+    scratch += [
+        pltpu.VMEM((5, 40, 128), F32),
+        pltpu.VMEM((4, 3, 40, 128), F32),
+        pltpu.SemaphoreType.DMA((60,)),
+        pltpu.SemaphoreType.DMA((60,)),
+    ]
+    return pl.pallas_call(
+        tail_body,
+        out_shape=[sds((2, 16, 1024), F32), sds((40, 128), F32)],
+        in_specs=[VMEM] * 3,
+        out_specs=[ANY, VMEM],
+        scratch_shapes=scratch,
+        name="tail",
+        compiler_params=pltpu.CompilerParams(
+            collective_id=3, has_side_effects=True, vmem_limit_bytes=40 << 20
+        ),
+    )(normed, packed, small)
 
 
 def rope_tables(start):
@@ -1042,55 +1256,20 @@
     query_ids = lax.dynamic_slice_in_dim(segment_ids, start, ROWS, axis=1)
     segq = jnp.tile(jnp.where(query_ids >= 0, query_ids, -2), (1, GROUP))
     cos, sin = rope_tables(start)
-    (WQ, WO, WG, WD, OG, RG, KV, pt, lse, attended, resid, normed, gain_rows) = front(
-        x_in, wq_in, w_out.T, w_gate_up, w_down.reshape(80, 1024), og_in,
-        segc, segq, cos, sin, qgain, kgain,
+    wd_in = jnp.concatenate([w_down[:, :1024], w_down[:, 1024:]], axis=0)
+    (WQ, WO, WG, WD, OG, KV, pt, lse, attended, resid, normed, gain_rows, n2) = front(
+        x_in, wq_in, w_out.T, w_gate_up, wd_in, og_in, segc, segq, cos, sin, qgain, kgain
     )
-    WG = WG.reshape(D, 2 * FS)
-    WD = WD.reshape(FS, D)
-    OG = OG.reshape(8 * TOK, D)
-    rows = RG.reshape(8 * TOK, D)
-
-    gate_up = dot(rows, WG)
-    gate = gate_up[:, :FS]
-    upper = gate_up[:, FS:]
-    sigmoid_gate = jax.nn.sigmoid(gate)
-    active = gate * sigmoid_gate
-    inner = (active * upper).astype(BF16)
-    mixed_part = dot(inner, WD).astype(BF16)
-    d_inner = dot_last(OG, WD)
-    d_gate = d_inner * upper * sigmoid_gate * (1.0 + gate * (1.0 - sigmoid_gate))
-    d_upper = d_inner * active
-    d_gate_up = jnp.concatenate([d_gate, d_upper], axis=1).astype(BF16)
-    d_rows_part = dot_last(d_gate_up, WG).astype(BF16)
-    grad_gate_up = dot_rows(rows, d_gate_up).astype(BF16)
-    grad_down = dot_rows(inner, OG).astype(BF16)
-
-    input_grad, d_packed, resid_low, terms, head_terms = back(
-        d_rows_part.reshape(4, 2, TOK, D), x_in, og_in, resid, gain_rows, WQ, WO, KV, pt, lse,
-        segc, segq, cos, sin, qgain, kgain,
+    d_normed, mix_part, dwg, dwd = ffn(n2, OG, WG, WD)
+    input_grad, d_packed, terms, head_terms, result, gwg, gwd, go = back(
+        d_normed, x_in, og_in, resid, gain_rows, attended, pt, lse, segc, segq, cos, sin, qgain, kgain,
+        WQ, WO, KV, mix_part, dwg, dwd,
     )
-
-    pair = pair_exchange(normed, d_packed, attended, resid_low)
-    normed_2, packed_2, attended_2, low_2 = [a.reshape(2 * TOK, -1) for a in pair]
-    packed_cols = lax.dynamic_slice_in_dim(packed_2, c * 896, 1024, axis=1)
-    attended_cols = lax.dynamic_slice_in_dim(attended_2, c * 640, 640, axis=1)
-    grad_q = dot_rows(normed_2, packed_cols).astype(BF16)
-    grad_o = dot_rows(low_2, attended_cols).astype(BF16)
-
     head_sums = jnp.sum(head_terms, axis=2).reshape(1, 128)
     small = jnp.concatenate(
         [terms[:2].reshape(32, 128), jnp.pad(head_sums, ((0, 7), (0, 0)))], axis=0
     )
-    gwg, gwd, gq, go, mix, sums = reduce_grads(
-        grad_gate_up.reshape(2, 4, 2, 128, 2 * FS),
-        grad_down.reshape(2, 4, 2, 80, 1024),
-        grad_q.reshape(2, 4, 2, 4, 32, 1024),
-        grad_o.reshape(2, 4, 2, 4, 32, 640),
-        mixed_part.reshape(4, 2, TOK, D),
-        small,
-    )
-    result = (resid + mix).astype(BF16)
+    gq, sums = tail(normed, d_packed, small)
     w_qkv_grad = jnp.concatenate([gq[0], gq[1][:, 128:]], axis=1)
     w_out_grad = jnp.concatenate([go[0], go[1]], axis=1).T
     at = (g * 16 + s) * 16
@@ -1102,7 +1281,7 @@
         w_qkv_grad,
         w_out_grad,
         gwg,
-        gwd.reshape(40, D),
+        jnp.concatenate([gwd[:40], gwd[40:]], axis=1),
         attn_sum,
         ffn_sum,
         sums[32, :HEAD],

time: 425 us -> 370 us (0.87)
  matrix products: 55.2 us -> 0 us
  Pallas kernels: 338 us -> 346 us
  local copies, waits for them, and re-layouts: 20.2 us -> 14.1 us
    dot_general x8 -> x0, matrix products: 55.2 us -> none  [the longest x4 19.7 us: dot_rows(): lax.dot_general(left, right, (((0,), (0,)), ((), ())), preferred_element_...]
    pallas_call x3, Pallas kernels: 205 us -> 228 us  [the longest x1 116 us: back(): pl.pallas_call(back_body, out_shape=vmem + hbm, in_specs=[VMEM] * 14 + [A...]
    pallas_call x1, Pallas kernels: 133 us -> 117 us  [front(): pl.pallas_call(front_body, out_shape=hbm + vmem, in_specs=[VMEM] + [ANY]...]
    reshape x4 -> x0, local copies, waits for them, and re-layouts: 9.08 us -> none  [the longest x1 3.68 us: per_device(): WD = WD.reshape(FS, D)]
where the time goes in v3:
time: 370 us; the launch traced here: 369 us
  Pallas kernels  346 us (94%)
  local copies, waits for them, and re-layouts  14.1 us (4%)
  other arithmetic  8.67 us (2%)
    pallas_call x1, Pallas kernels, front(): pl.pallas_call(front_body, out_shape=hbm + vmem, in_specs=[VMEM] + [ANY]...  117 us
    pallas_call x1, Pallas kernels, back(): pl.pallas_call(back_body, out_shape=vmem + hbm, in_specs=[VMEM] * 14 + [A...  116 us
    pallas_call x1, Pallas kernels, ffn(): pl.pallas_call(ffn_body, out_shape=outs, in_specs=[VMEM] + [ANY] * 3, out...  69.1 us
    pallas_call x1, Pallas kernels, tail(): pl.pallas_call(tail_body, out_shape=[sds((2, 16, 1024), F32), sds((40, 12...  42.9 us

profile of v3, /device:TPU:1, one launch (start us, length us, event | category | flops | bytes accessed | tf_op | source)
XLA Modules:
  0.0 369.3 jit_solution(1322709147719058292)
XLA Ops:
  0.7 0.7 pad_maximum_fusion.4
  1.3 0.7 bitcast_convert_fusion.1
  2.7 0.8 compare_select_fusion
  3.4 0.7 tile.10.refs_7_.refs_9_
  4.3 0.7 copy.31.refs_11_.refs_13_
  5.0 0.7 copy.30.refs_10_.refs_12_
  5.7 0.7 fusion.2
  6.4 1.5 fusion.1.refs_1_
  7.8 0.9 fusion.7
  8.8 0.7 pad_maximum_fusion.1.refs_4_
  9.4 1.7 copy.29
  11.2 117.5 %front.1 = (bf16[2,4,2,4,2,16,2048]{6,5,4,3,2,1,0:T(8,128)(2,1)}, bf16[2,4,2,4,2,16,1280]{6,5,4,3,2,1,0:T(8,128)(2,1)}, bf16[2,4,2,8,16,1280]{5,4,3,2,1,0:T(8,12...) custom-call(bf16[128,2048]{1,0:T(8,128)(2,1)} %bitcast.34, ...), custom_call_target="tpu_custom_call" | custom-call | tf_op jit(solution)/shard_map/front/pallas_call | solution.py:622
  128.7 69.1 %ffn.1 = (f32[128,2048]{1,0:T(8,128)}, bf16[4,2,128,2048]{3,2,1,0:T(8,128)(2,1)}, bf16[2,4,2,128,1280]{4,3,2,1,0:T(8,128)(2,1)}, bf16[2,4,2,80,1024]{4,3,2,1,0:T(8,128)(2,1)}) custom-call(bf16[128,2048]{1,0:T(8,128)(2,1)} %get-tuple-element.37.n2, bf16[4,2,128,2048]{3,2,1,0:T(8,128)(2,1)} %get-tuple-element.38.OG, ...), custom_call_target="tpu_custom_call" | custom-call | tf_op jit(solution)/shard_map/ffn/pallas_call | solution.py:807
  197.7 116.3 %back.1 = (f32[128,2048]{1,0:T(8,128)}, bf16[128,1920]{1,0:T(8,128)(2,1)}, f32[8,2048]{1,0:T(8,128)}, f32[2,64,128]{2,1,0:T(8,128)}, bf16[128,2048]{1,0:T(8,128)...) custom-call(f32[128,2048]{1,0:T(8,128)} %get-tuple-element.41.refs_0_, ...), custom_call_target="tpu_custom_call" | custom-call | tf_op jit(solution)/shard_map/back/pallas_call | solution.py:1126
  314.1 0.9 reduce_sum.9
  315.1 0.8 slice.44
  316.0 1.0 copy-done.1
  317.0 42.9 %tail.1 = (f32[2,16,1024]{2,1,0:T(8,128)S(1)}, f32[40,128]{1,0:T(8,128)S(1)}) custom-call(bf16[128,2048]{1,0:T(8,128)(2,1)S(1)} %copy-done, bf16[128,1920]{1,0:T(8,128)(2,1)S(1)} %copy-done.1, f32[40,128]{1,0:T(8,128)S(1)} %select_maximum_fusion.small), custom_call_target="tpu_custom_call" | custom-call | tf_op jit(solution)/shard_map/tail/pallas_call | solution.py:1210
  362.4 0.8 slice_bitcast_fusion.3
  363.9 1.0 fusion.6
  364.9 0.7 pad_maximum_fusion
  365.6 1.9 copy.37
  367.5 1.0 copy.38
  368.5 0.8 copy.39
  (24 shorter events, 4.0 us)
Async XLA Ops:
  197.7 118.3 %copy-start = (bf16[128,2048]{1,0:T(8,128)(2,1)S(1)}, bf16[128,2048]{1,0:T(8,128)(2,1)}, u32[]{:S(2)}) copy-start(bf16[128,2048]{1,0:T(8,128)(2,1)} %get-tuple-element.55.normed) | copy-start | bytes 1572868
  316.0 1.0 copy-start.1
  317.0 50.5 %copy-start.2 = (f32[128,2048]{1,0:T(8,128)S(1)}, f32[128,2048]{1,0:T(8,128)}, u32[]{:S(2)}) copy-start(f32[128,2048]{1,0:T(8,128)} %get-tuple-element.54) | copy-start | bytes 3145732
  317.0 51.4 %copy-start.3 = (f32[16,10240]{1,0:T(8,128)S(1)}, f32[16,10240]{1,0:T(8,128)}, u32[]{:S(2)}) copy-start(f32[16,10240]{1,0:T(8,128)} %get-tuple-element.92) | copy-start | bytes 1966084

commit v4 on v3

v4 whole, which is shorter than its diff:
```python
import jax
import jax.numpy as jnp
from jax import lax
from jax.experimental import pallas as pl
from jax.experimental.pallas import tpu as pltpu
from jax.sharding import PartitionSpec as P

Q_HEADS = 20
KV_HEADS = 5
GROUP = 4
HEAD = 64
D = 2048
FF = 5120
QD = 1280
KD = 320
QKV = 1920
SEQ = 1024
MICRO = 2
ROWS = 64
TOK = 128
FS = 640
EPS = 1e-06
MESH = pl.DeviceIdType.MESH
F32 = jnp.float32
BF16 = jnp.bfloat16
ANY = pl.BlockSpec(memory_space=pl.ANY)


class Place:
    def __init__(self):
        g = lax.axis_index("grp")
        s = lax.axis_index("seq")
        self.g, self.s = g, s
        self.yh, self.x = g // 4, g % 4
        self.yl, self.z, self.c = s // 8, (s // 2) % 4, s % 2
        self.y = self.yh * 2 + self.yl

    def at(self, x=None, y=None, z=None, c=None):
        x = self.x if x is None else x
        y = self.y if y is None else y
        z = self.z if z is None else z
        c = self.c if c is None else c
        return ((y // 2) * 4 + x, (y % 2) * 8 + z * 2 + c)

    def step(self, axis, k):
        if axis == "x":
            return self.at(x=(self.x + k) % 4)
        if axis == "y":
            return self.at(y=(self.y + k) % 4)
        if axis == "z":
            return self.at(z=(self.z + k) % 4)
        return self.at(c=1 - self.c)

    def pos(self, axis, k):
        return (getattr(self, axis) + k) % 4


class Links:
    def __init__(self, send_sems, recv_sems):
        self.send_sems, self.recv_sems = send_sems, recv_sems
        self.used = 0
        self.sent = []

    def plan(self, src, dst, to):
        i = self.used
        self.used += 1
        copy = pltpu.make_async_remote_copy(
            src_ref=src,
            dst_ref=dst,
            send_sem=self.send_sems.at[i],
            recv_sem=self.recv_sems.at[i],
            device_id=to,
            device_id_type=MESH,
        )
        self.sent.append(copy)
        return copy

    def send(self, src, dst, to):
        copy = self.plan(src, dst, to)
        copy.start()
        return copy

    def local(self, src, dst):
        i = self.used
        self.used += 1
        copy = pltpu.make_async_copy(src, dst, self.recv_sems.at[i])
        copy.start()
        return copy

    def drain(self):
        for copy in self.sent:
            copy.wait_send()


def greet(partners):
    barrier = pltpu.get_barrier_semaphore()
    for to in partners:
        pl.semaphore_signal(barrier, inc=1, device_id=to, device_id_type=MESH)
    pl.semaphore_wait(barrier, len(partners))


def sds(shape, dtype):
    return jax.ShapeDtypeStruct(shape, dtype)


def rms_scale(values):
    return lax.rsqrt(jnp.mean(values * values, axis=-1, keepdims=True) + EPS)


def norm_back(upstream, normed, scale, gain):
    scaled = upstream * gain
    inner = jnp.mean(scaled * normed, axis=-1, keepdims=True)
    return scale * (scaled - normed * inner)


def dot(left, right):
    return jnp.dot(left, right, preferred_element_type=F32)


def dot_last(left, right):
    return lax.dot_general(left, right, (((1,), (1,)), ((), ())), preferred_element_type=F32)


def dot_rows(left, right):
    return lax.dot_general(left, right, (((0,), (0,)), ((), ())), preferred_element_type=F32)


def slab_target(p):
    to = p.at(x=p.z, y=p.c * 2 + p.yl, z=p.g // 2, c=p.g % 2)
    return to


def slab_source(p):
    m = p.z * 2 + p.c
    return p.at(x=m % 4, y=(m // 4) * 2 + p.yl, z=p.x, c=p.yh)


def same(p, to):
    return (to[0] == p.g) & (to[1] == p.s)


def greet_plane(p, partners, slab_to, slab_from, own_slab):
    barrier = pltpu.get_barrier_semaphore()
    for to in partners:
        pl.semaphore_signal(barrier, inc=1, device_id=to, device_id_type=MESH)

    @pl.when(jnp.logical_not(own_slab))
    def _():
        pl.semaphore_signal(barrier, inc=1, device_id=slab_to, device_id_type=MESH)
        pl.semaphore_signal(barrier, inc=1, device_id=slab_from, device_id_type=MESH)
        pl.semaphore_wait(barrier, len(partners) + 2)

    @pl.when(own_slab)
    def _():
        pl.semaphore_wait(barrier, len(partners))


def slab_copy(src, dst, ssem, rsem, i, to):
    return pltpu.make_async_remote_copy(
        src_ref=src,
        dst_ref=dst,
        send_sem=ssem.at[i],
        recv_sem=rsem.at[i],
        device_id=to,
        device_id_type=MESH,
    )


def add_blocks(dst, own, recv, chunk):
    lead, rows = dst.shape[:-2], dst.shape[-2]
    count = 1
    for n in lead:
        count *= n

    @pl.loop(0, count)
    def _(i):
        at = []
        rest = i
        for n in reversed(lead):
            at.insert(0, rest % n)
            rest = rest // n

        @pl.loop(0, rows, step=chunk)
        def _(t):
            here = (*at, pl.ds(pl.multiple_of(t, chunk), chunk))
            total = own[here].astype(F32)
            for j in range(3):
                total = total + recv[(j, *here)].astype(F32)
            dst[here] = total.astype(dst.dtype)


def staged_reduce(p, k, src, stages, scr, chunk):
    own = scr[0]
    cur = src
    for n, (axis, pick) in enumerate(stages):
        recv = scr[1] if n == 0 else scr[2 * n]
        if n == 0:
            mine = k.local(pick(src, p.pos(axis, 0)), own)
        ring = [k.send(pick(cur, p.pos(axis, j)), recv.at[j - 1], p.step(axis, j)) for j in (1, 2, 3)]
        yield
        if n == 0:
            mine.wait()
        for copy in ring:
            copy.wait_recv()
        total = own if n == 0 else scr[2 * n + 1]
        add_blocks(total, own if n == 0 else pick(cur, p.pos(axis, 0)), recv, chunk)
        cur = total


def staged_scratch(shapes):
    out = [pltpu.VMEM(shapes[0], BF16), pltpu.VMEM((3, *shapes[0]), BF16)]
    for n, shape in enumerate(shapes[1:]):
        out.append(pltpu.VMEM((3, *shape), BF16))
        out.append(pltpu.VMEM(shape, BF16))
    return out


EVERY = slice(None)


def wg_stages(half):
    cols = pl.ds(half * FS, FS)
    if half == 0:
        return [
            ("y", lambda r, i: r.at[i // 2, :, i % 2, :, cols]),
            ("x", lambda r, i: r.at[i]),
        ]
    return [
        ("x", lambda r, i: r.at[:, i, :, :, cols]),
        ("y", lambda r, i: r.at[i // 2, i % 2]),
    ]


def wd_stages(half):
    cols = pl.ds(half * 512, 512)
    if half == 0:
        return [
            ("y", lambda r, i: r.at[i % 2, :, i // 2, :, cols]),
            ("x", lambda r, i: r.at[i]),
        ]
    return [
        ("x", lambda r, i: r.at[:, i, :, :, cols]),
        ("y", lambda r, i: r.at[i % 2, i // 2]),
    ]


def q_stages(half):
    cols = pl.ds(half * 128, 128)
    if half == 0:
        return [
            ("y", lambda r, i: r.at[i // 2, :, i % 2, :, cols]),
            ("x", lambda r, i: r.at[i]),
        ]
    return [
        ("x", lambda r, i: r.at[:, i, :, :, cols]),
        ("y", lambda r, i: r.at[i // 2, i % 2]),
    ]


def o_stages(part):
    cols = pl.ds((0, 256, 512)[part], (256, 256, 128)[part])
    if part == 0:
        return [
            ("x", lambda r, i: r.at[:, i, :, :, :, cols]),
            ("z", lambda r, i: r.at[:, :, i]),
            ("y", lambda r, i: r.at[i // 2, i % 2]),
        ]
    if part == 1:
        return [
            ("y", lambda r, i: r.at[i // 2, :, i % 2, :, :, cols]),
            ("x", lambda r, i: r.at[i]),
            ("z", lambda r, i: r.at[i]),
        ]
    return [
        ("z", lambda r, i: r.at[:, :, :, i, :, cols]),
        ("y", lambda r, i: r.at[i // 2, :, i % 2]),
        ("x", lambda r, i: r.at[i]),
    ]


O_PARTS = ((0, 256), (256, 256), (512, 128))
PLANE_SHAPES = [
    [(4, 128, FS), (128, FS)],
    [(2, 2, 128, FS), (128, FS)],
    [(4, 80, 512), (80, 512)],
    [(2, 2, 80, 512), (80, 512)],
    [(4, 128, 128), (128, 128)],
    [(2, 2, 128, 128), (128, 128)],
]
O_SHAPES = [
    [(2, 2, 4, 32, 256), (2, 2, 32, 256), (32, 256)],
    [(4, 4, 32, 256), (4, 32, 256), (32, 256)],
    [(2, 4, 2, 32, 128), (4, 32, 128), (32, 128)],
]


def small_reduce(p, k, vec, recv):
    for n, axis in enumerate("xyzc"):
        steps = (1,) if axis == "c" else (1, 2, 3)
        ring = [k.send(vec.at[n], recv.at[n, j - 1], p.step(axis, j)) for j in steps]
        yield
        for copy in ring:
            copy.wait_recv()
        total = vec[n]
        for j in range(len(steps)):
            total = total + recv[n, j]
        vec[n + 1] = total


def swap(a, b):
    left = lax.broadcasted_iota(jnp.int32, a.shape, 1) < ROWS
    return jnp.where(left, a, pltpu.roll(b, ROWS, 1)), jnp.where(left, pltpu.roll(a, ROWS, 1), b)


def head_scale(v):
    return lax.rsqrt(jnp.mean(v * v, axis=-2, keepdims=True) + EPS)


def half_turn(v):
    half = HEAD // 2
    return jnp.concatenate([-v[..., half:, :], v[..., :half, :]], axis=-2)


def half_back(v):
    half = HEAD // 2
    return jnp.concatenate([v[..., half:, :], -v[..., :half, :]], axis=-2)


def low(v):
    return v.astype(BF16).astype(F32)


def query_units(packed_t, g, cos, sin, gain):
    raw = packed_t[pl.ds(pl.multiple_of(g * 256, 256), 256)].reshape(GROUP, HEAD, TOK)
    head = raw * head_scale(raw) * gain
    turned = low(head * cos + half_turn(head) * sin) * (HEAD ** -0.5)
    a0, a1 = swap(turned[0], turned[1])
    b0, b1 = swap(turned[2], turned[3])
    none = jnp.zeros((HEAD, 256), F32)
    return [
        jnp.concatenate([jnp.concatenate([a, b], axis=1), none], axis=0) for a, b in ((a0, b0), (a1, b1))
    ]


def fill_bias(bias, segc, segq, start):
    @pl.loop(0, SEQ, step=128)
    def _(t):
        at = pl.ds(pl.multiple_of(t, 128), 128)
        key = lax.broadcasted_iota(jnp.int32, (128, 128), 0) + t
        query = lax.broadcasted_iota(jnp.int32, (128, 128), 1) % ROWS + start
        for m in range(MICRO):
            ok = (key <= query) & (segc[at, m : m + 1] == segq[m : m + 1, :])
            ok = ok | (key == query)
            bias[m, at] = jnp.where(ok, 3e38, -1e30)


def unit_bias(bias, m):
    half = bias[m]
    return jnp.concatenate([half, half], axis=1)


def unit_kv(KV, m, g):
    cols = pl.ds(pl.multiple_of(g * 128, 128), 128)
    return KV[m, :, :, :, :, cols].reshape(SEQ, 128)


def front_body(*refs):
    (x_in, wq, wo, wg, wd, og, segc, segq, cos_ref, sin_ref, qgain, kgain) = refs[:12]
    (WO, WG, WD, OG, NA, KV, PT, LSE, ATT, RESID, N2, gains_out) = refs[12:24]
    (xs, na, wqm, wos, pks, pk, pt, lse, att, resid, n2, kvl, kvs, bias, qts, ots, ssem, rsem) = refs[24:]
    p = Place()
    k = Links(ssem, rsem)
    yh, x, yl, z, c = p.yh, p.x, p.yl, p.z, p.c
    m = z * 2 + c
    sib = p.step("c", 1)
    yl_partner = p.at(y=p.yh * 2 + 1 - yl)
    partners = [p.step(a, j) for a in "xyz" for j in (1, 2, 3)]
    partners += [p.at(z=(z + j) % 4, c=1 - c) for j in range(4)]
    slab_to, slab_from = slab_target(p), slab_source(p)
    own_slab = same(p, slab_to)
    greet_plane(p, partners, slab_to, slab_from, own_slab)

    def spread(src_of, dst_of):
        far, near = [], None
        for dz in range(4):
            for dc in range(2):
                zz, cc = (z + dz) % 4, (c + dc) % 2
                src, dst = src_of(zz * 2 + cc), dst_of(m)
                if dz == 0 and dc == 0:
                    near = k.local(src, dst)
                else:
                    far.append(k.send(src, dst, p.at(z=zz, c=cc)))
        return near, far

    q0 = spread(
        lambda i: wq.at[:, pl.ds(pl.multiple_of(i * 256, 256), 256)], lambda i: wqm.at[yh, x, yl, i]
    )
    own_x = k.local(x_in, xs.at[z, c])
    xcore = {0: k.send(x_in, xs.at[z, c], sib)}
    own_wo = k.local(wo, wos.at[yh, x, yl, z, c])

    def wo_at(part, *at):
        return wos.at[(*at, EVERY, pl.ds((0, 512, 1024)[part], (512, 512, 256)[part]))]

    def wo_own(part):
        return wo.at[:, pl.ds((0, 512, 1024)[part], (512, 512, 256)[part])]

    o1 = []
    for j in (1, 2, 3):
        for part, axis in ((0, "z"), (1, "z"), (2, "x")):
            o1.append(k.send(wo_own(part), wo_at(part, yh, x, yl, z, c), p.step(axis, j)))
    g0 = [
        spread(
            lambda i: wg.at[:, pl.ds(pl.multiple_of(half * FF + i * FS, 128), FS)],
            lambda i: WG.at[yh, x, yl, i, :, pl.ds(half * FS, FS)],
        )
        for half in range(2)
    ]
    slab_dst = WD.at[yl, z, c]
    i = k.used
    k.used += 1
    slab = slab_copy(wd, slab_dst, ssem, rsem, i, slab_to)

    @pl.when(own_slab)
    def _():
        pltpu.make_async_copy(wd, slab_dst, rsem.at[i]).start()

    @pl.when(jnp.logical_not(own_slab))
    def _():
        slab.start()

    xring = {j: k.send(x_in, xs.at[z, c], p.step("z", j)) for j in (1, 3, 2)}

    def to_plane(blocks):
        return [k.send(b, b, p.step(axis, j)) for j in (1, 2, 3) for b, axis in blocks]

    ql, qh = pl.ds(0, 128), pl.ds(128, 128)
    lo, hi = pl.ds(0, FS), pl.ds(FS, FS)
    dlo, dhi = pl.ds(0, 512), pl.ds(512, 512)
    q0[0].wait()
    for copy in q0[1]:
        copy.wait_recv()
    q1 = to_plane(((wqm.at[yh, x, yl, :, :, ql], "x"), (wqm.at[yh, x, yl, :, :, qh], "y")))
    fill_bias(bias, segc, segq, p.s * ROWS)
    for copy in q1:
        copy.wait_recv()
    q2 = to_plane(((wqm.at[yh, :, yl, :, :, ql], "y"), (wqm.at[:, x, :, :, :, qh], "x")))
    for near, far in g0:
        near.wait()
        for copy in far:
            copy.wait_recv()

    @pl.when(own_slab)
    def _():
        pltpu.make_async_copy(wd, slab_dst, rsem.at[i]).wait()

    @pl.when(jnp.logical_not(own_slab))
    def _():
        slab.wait_recv()

    plane = to_plane(
        (
            (WG.at[yh, x, yl, :, :, lo], "x"),
            (WG.at[yh, x, yl, :, :, hi], "y"),
            (WD.at[yl, x, yh, :, dlo], "x"),
            (WD.at[yl, x, yh, :, dhi], "y"),
        ),
    )
    for copy in q2:
        copy.wait_recv()
    own_x.wait()
    own_wo.wait()
    pick = jnp.where(
        lax.broadcasted_iota(jnp.int32, (8, 128), 0) + 112 == lax.broadcasted_iota(jnp.int32, (8, 128), 1), 1.0, 0.0
    ).astype(BF16)
    gains_out[...] = dot_last(pick, wqm[:, :, :, :, :, pl.ds(128, 128)].reshape(D, 128))
    packs = []
    plane2 = []
    for o in (0, 1, 3, 2):
        zz = (z + o) % 4
        if o:
            xring[(4 - o) % 4].wait_recv()
            xcore[o] = k.send(xs.at[zz, c], xs.at[zz, c], sib)
        xcore[o].wait_recv()
        rows = xs[zz].reshape(256, D).astype(F32)
        normed = (rows * rms_scale(rows) * gains_out[0:1, :]).astype(BF16)
        na[zz] = normed.reshape(2, TOK, D)
        pks[zz] = dot(normed, wqm[...].reshape(D, 256)).astype(BF16).reshape(2, TOK, 256)
        if o:
            packs.append(k.send(pks.at[zz, c], pk.at[m], p.at(z=zz)))
        else:
            own_pk = k.local(pks.at[z, c], pk.at[m])
        packs.append(k.send(pks.at[zz, 1 - c], pk.at[m], p.at(z=zz, c=1 - c)))
        if o == 1:
            for copy in o1:
                copy.wait_recv()
            o2 = to_plane(
                (
                    (wo_at(0, yh, x, yl, EVERY, c), "y"),
                    (wo_at(1, yh, x, yl, EVERY, c), "x"),
                    (wo_at(2, yh, EVERY, yl, z, c), "y"),
                ),
            )
        if o == 3:
            for copy in plane:
                copy.wait_recv()
            plane2 = to_plane(
                (
                    (WG.at[:, x, :, :, :, hi], "x"),
                    (WD.at[yl, :, yh, :, dlo], "y"),
                    (WD.at[:, x, :, :, dhi], "x"),
                ),
            )
    keep = [k.local(na, NA)]
    own_pk.wait()
    for copy in packs:
        copy.wait_recv()
    for i8 in range(8):
        pt[i8 * 240 : (i8 + 1) * 240] = pk[i8].astype(F32).T[:240]
    cos, sin = cos_ref[...], sin_ref[...]

    @pl.loop(0, KV_HEADS)
    def _(g):
        raw = pt[pl.ds(pl.multiple_of(QD + g * HEAD, HEAD), HEAD)]
        head = raw * head_scale(raw) * kgain[...]
        key = head * cos + half_turn(head) * sin
        value = pt[pl.ds(pl.multiple_of(QD + KD + g * HEAD, HEAD), HEAD)]
        both = jnp.concatenate([key, value], axis=0).T.astype(BF16)
        cols = pl.ds(pl.multiple_of(g * 128, 128), 128)
        for mm in range(MICRO):
            kvl[mm, :, cols] = both[mm * ROWS : (mm + 1) * ROWS]

    own_kv = k.local(kvl, kvs.at[:, yl, z, c])
    across = k.send(kvl, kvs.at[:, yl, z, c], yl_partner)
    ring = [k.send(kvl, kvs.at[:, yl, z, c], p.step("z", j)) for j in (1, 2, 3)]
    keep.append(k.local(pt, PT))

    @pl.loop(0, KV_HEADS)
    def _(g):
        for mm, unit in enumerate(query_units(pt, g, cos, sin, qgain[...])):
            qts[g, mm] = unit.astype(BF16)

    across.wait_recv()
    src = kvs.at[:, 1 - yl, z, c]
    ring += [k.send(src, src, p.step("z", j)) for j in (1, 2, 3)]
    plane2 += to_plane(((WG.at[yh, :, yl, :, :, lo], "y"),))
    own_kv.wait()
    for copy in o2:
        copy.wait_recv()
    o3 = []
    for j in (1, 2, 3):
        xx, yy, zz = p.pos("x", -j), p.pos("y", -j), p.pos("z", -j)
        src = wo_at(0, EVERY, x, EVERY, EVERY, c)
        o3.append((k.send(src, src, p.step("x", j)), wo_at(0, EVERY, xx, EVERY, EVERY, c)))
        src = wo_at(1, yh, EVERY, yl, EVERY, c)
        o3.append((k.send(src, src, p.step("y", j)), wo_at(1, yy // 2, EVERY, yy % 2, EVERY, c)))
        src = wo_at(2, EVERY, EVERY, EVERY, z, c)
        o3.append((k.send(src, src, p.step("z", j)), wo_at(2, EVERY, EVERY, EVERY, zz, c)))
    oc = []
    for src in (
        wo_at(0, EVERY, x, EVERY, EVERY, c),
        wo_at(1, yh, EVERY, yl, EVERY, c),
        wo_at(2, EVERY, EVERY, EVERY, z, c),
    ):
        oc.append(k.send(src, src, sib))
    keep.append(k.local(og, OG.at[z, c]))
    rows = [k.send(og, OG.at[z, c], p.step("z", j)) for j in (1, 2, 3)]
    last = [k.send(og, OG.at[z, c], sib)]
    for copy in ring:
        copy.wait_recv()
    src = kvs.at[:, :, :, c]
    kvc = k.send(src, src, sib)
    kvc.wait_recv()
    keep.append(k.local(kvs, KV))

    @pl.loop(0, 2 * KV_HEADS)
    def _(u):
        g, mm = u // 2, u % 2
        kv = unit_kv(kvs, mm, g)
        score = jnp.minimum(dot(kv, qts[g, mm]), unit_bias(bias, mm))
        peak = jnp.max(score, axis=0, keepdims=True)
        raised = jnp.exp(score - peak)
        total = jnp.sum(raised, axis=0, keepdims=True)
        probs = (raised * (1.0 / total)).astype(BF16)
        ots[g, mm] = dot_rows(kv, probs)[HEAD:]
        lse[u] = jnp.broadcast_to(peak + jnp.log(total), (8, 256))

    for g in range(KV_HEADS):
        for t in range(2):
            cols = slice(t * 128, (t + 1) * 128)
            a, b = swap(ots[g, 0, :, cols], ots[g, 1, :, cols])
            at = (g * GROUP + 2 * t) * HEAD
            att[:, at : at + 128] = jnp.concatenate([a, b], axis=0).T.astype(BF16)
    keep += [k.local(lse, LSE), k.local(att, ATT)]
    for copy, src in o3:
        copy.wait_recv()
        oc.append(k.send(src, src, sib))
    for copy in oc:
        copy.wait_recv()
    keep.append(k.local(wos, WO))

    @pl.loop(0, 8)
    def _(t):
        w = wos[t // 4, t % 4].reshape(256, QD)
        cols = pl.ds(pl.multiple_of(t * 256, 256), 256)
        resid[:, cols] = xs[z, c, :, cols].astype(F32) + dot_last(att[...], w)

    value = resid[...]
    n2[...] = (value * rms_scale(value) * gains_out[1:2, :]).astype(BF16)
    keep += [k.local(resid, RESID), k.local(n2, N2)]
    for j, copy in zip((1, 2, 3), rows):
        copy.wait_recv()
        src = OG.at[p.pos("z", -j), c]
        last.append(k.send(src, src, sib))
    for copy in plane2 + last:
        copy.wait_recv()
    for copy in keep:
        copy.wait()
    k.drain()

    @pl.when(jnp.logical_not(own_slab))
    def _():
        slab.wait_send()


VMEM = pl.BlockSpec(memory_space=pltpu.VMEM)


def front(x, wq, wo, wg, wd, og, segc, segq, cos, sin, qgain, kgain):
    hbm = [
        sds((2, 4, 2, 4, 2, 16, QD), BF16),
        sds((2, 4, 2, 8, 16, 2 * FS), BF16),
        sds((2, 4, 2, 80, 1024), BF16),
        sds((4, 2, TOK, D), BF16),
        sds((4, 2, TOK, D), BF16),
        sds((2, 2, 4, 2, ROWS, 2 * KD), BF16),
        sds((QKV, TOK), F32),
        sds((2 * KV_HEADS, 8, 256), F32),
        sds((TOK, QD), BF16),
        sds((TOK, D), F32),
        sds((TOK, D), BF16),
    ]
    vmem = [sds((8, D), F32)]
    scratch = [
        pltpu.VMEM((4, 2, TOK, D), BF16),
        pltpu.VMEM((4, 2, TOK, D), BF16),
        pltpu.VMEM((2, 4, 2, 8, 16, 256), BF16),
        pltpu.VMEM((2, 4, 2, 4, 2, 16, QD), BF16),
        pltpu.VMEM((4, 2, TOK, 256), BF16),
        pltpu.VMEM((8, TOK, 256), BF16),
        pltpu.VMEM((QKV, TOK), F32),
        pltpu.VMEM((2 * KV_HEADS, 8, 256), F32),
        pltpu.VMEM((TOK, QD), BF16),
        pltpu.VMEM((TOK, D), F32),
        pltpu.VMEM((TOK, D), BF16),
        pltpu.VMEM((2, ROWS, 2 * KD), BF16),
        pltpu.VMEM((2, 2, 4, 2, ROWS, 2 * KD), BF16),
        pltpu.VMEM((2, SEQ, 128), F32),
        pltpu.VMEM((KV_HEADS, 2, 128, 256), BF16),
        pltpu.VMEM((KV_HEADS, 2, HEAD, 256), F32),
        pltpu.SemaphoreType.DMA((170,)),
        pltpu.SemaphoreType.DMA((170,)),
    ]
    return pl.pallas_call(
        front_body,
        out_shape=hbm + vmem,
        in_specs=[ANY] * 6 + [VMEM] * 6,
        out_specs=[ANY] * len(hbm) + [VMEM] * len(vmem),
        scratch_shapes=scratch,
        name="front",
        compiler_params=pltpu.CompilerParams(
            collective_id=0, has_side_effects=True, vmem_limit_bytes=56 << 20
        ),
    )(x, wq, wo, wg, wd, og, segc, segq, cos, sin, qgain, kgain)


def ffn_body(n2, OG, WG, WD, wq, d_out, mix_out, dwg_out, dwd_out, WQ, *scr):
    (rows, ogs, wgs, wd80, wds, dgu, inn, din, part, mixs, r0, s0, r1, m0, dwg, dwd32, dwd) = scr[:17]
    (dn, ssem, rsem, lsem, wsem, vsem) = scr[17:]
    p = Place()
    k = Links(wsem, vsem)
    yh, x, yl, z, c = p.yh, p.x, p.yl, p.z, p.c
    sib = p.step("c", 1)
    greet([p.step(a, j) for a in "xyz" for j in (1, 2, 3)] + [sib])

    def remote(src, dst, i, to):
        return pltpu.make_async_remote_copy(
            src_ref=src,
            dst_ref=dst,
            send_sem=ssem.at[i],
            recv_sem=rsem.at[i],
            device_id=to,
            device_id_type=MESH,
        )

    def local(src, dst, i):
        copy = pltpu.make_async_copy(src, dst, lsem.at[i])
        copy.start()
        return copy

    def half_of(half, *at):
        return WQ.at[(*at, EVERY, pl.ds(half * 1024, 1024))]

    whole = (EVERY, EVERY, EVERY, EVERY, c)
    own_wq = k.local(wq, WQ.at[yh, x, yl, z, c])
    q1 = [k.plan(wq, WQ.at[yh, x, yl, z, c], p.step("z", j)) for j in (1, 2, 3)]
    q2, q3 = [], []
    for j in (1, 2, 3):
        for half, axis in ((0, "y"), (1, "x")):
            src = half_of(half, yh, x, yl, EVERY, c)
            q2.append(k.plan(src, src, p.step(axis, j)))
    for j in (1, 2, 3):
        src = half_of(0, EVERY, x, EVERY, EVERY, c)
        q3.append(k.plan(src, src, p.step("x", j)))
        src = half_of(1, yh, EVERY, yl, EVERY, c)
        q3.append(k.plan(src, src, p.step("y", j)))
    q4 = k.plan(WQ.at[whole], WQ.at[whole], sib)

    sent = []
    for copy in q1:
        copy.start()
    for j in (1, 3, 2):
        copy = remote(n2, rows.at[z, c], j, p.step("z", j))
        copy.start()
        sent.append(copy)
    remote(n2, rows.at[z, c], 4, sib).start()
    own = local(n2, rows.at[z, c], 0)
    get_wd = local(WD, wd80, 1)
    get_wg = local(WG, wgs, 2)
    get_og = local(OG, ogs, 3)
    get_wd.wait()

    @pl.loop(0, 8)
    def _(i):
        yl, x = i // 4, i % 4
        a, b = wd80[yl, x, 0].astype(F32), wd80[yl, x, 1].astype(F32)
        at = pl.ds(pl.multiple_of(i * 80, 80), 80)
        wds[at, :1024] = jnp.concatenate([a[:40], b[:40]], axis=0).astype(BF16)
        wds[at, 1024:] = jnp.concatenate([a[40:], b[40:]], axis=0).astype(BF16)

    own.wait()
    get_wg.wait()
    get_og.wait()
    own_wq.wait()

    @pl.loop(0, 4)
    def _(j):
        o = jnp.where(j == 2, 3, jnp.where(j == 3, 2, j))
        zz = (z + o) % 4
        at = pl.ds(pl.multiple_of(zz * 256, 256), 256)

        @pl.when(o > 0)
        def _():
            remote(n2, rows.at[zz, c], (4 - o) % 4, sib).wait_recv()
            remote(rows.at[zz, c], rows.at[zz, c], 4 + o, sib).start()

        remote(rows.at[zz, c], rows.at[zz, 1 - c], 4 + o, sib).wait_recv()
        r = rows[zz].reshape(256, D)
        din[...] = dot_last(ogs[zz].reshape(256, D), wds[...])
        for t in range(5):
            lo, hi = slice(t * 128, (t + 1) * 128), slice(FS + t * 128, FS + (t + 1) * 128)
            w = jnp.concatenate(
                [wgs[:, :, :, :, :, lo].reshape(D, 128), wgs[:, :, :, :, :, hi].reshape(D, 128)], axis=1
            )
            both = dot(r, w)
            gate, upper = both[:, :128], both[:, 128:]
            sig = jax.nn.sigmoid(gate)
            active = gate * sig
            d_inner = din[:, lo]
            inn[at, lo] = (active * upper).astype(BF16)
            dgu[at, lo] = (d_inner * upper * sig * (1.0 + gate * (1.0 - sig))).astype(BF16)
            dgu[at, hi] = (d_inner * active).astype(BF16)

        @pl.loop(0, 8)
        def _(t):
            w = wgs[t // 4, t % 4].reshape(256, 2 * FS)
            cols = pl.ds(pl.multiple_of(t * 256, 256), 256)
            part[zz, :, :, cols] = dot_last(dgu[at], w).astype(BF16).reshape(2, TOK, 256)

        remote(part.at[zz, 1 - c], r0.at[zz], 8 + o, sib).start()

        @pl.loop(0, 4)
        def _(t):
            cols = pl.ds(pl.multiple_of(t * 512, 512), 512)
            mixs[zz, :, :, cols] = dot(inn[at], wds[:, cols]).astype(BF16).reshape(2, TOK, 512)

        remote(mixs.at[zz, 1 - c], m0.at[zz], 16 + o, sib).start()
        remote(part.at[zz, 1 - c], r0.at[zz], 8 + o, sib).wait_recv()

        @pl.loop(0, TOK, step=16)
        def _(t):
            here = pl.ds(pl.multiple_of(t, 16), 16)
            s0[zz, here] = (part[zz, c, here].astype(F32) + r0[zz, here].astype(F32)).astype(BF16)

        @pl.when(o > 0)
        def _():
            remote(s0.at[zz], r1.at[o - 1], 12 + o, p.at(z=zz)).start()

        @pl.when(j == 0)
        def _():
            for copy in q1:
                copy.wait_recv()
            for copy in q2:
                copy.start()

        @pl.when(j == 1)
        def _():
            for copy in q2:
                copy.wait_recv()
            for copy in q3:
                copy.start()

    for o in range(4):
        remote(mixs.at[0, 0], m0.at[0], 16 + o, sib).wait_recv()

    @pl.loop(0, 4)
    def _(zz):
        @pl.loop(0, TOK, step=16)
        def _(t):
            here = pl.ds(pl.multiple_of(t, 16), 16)
            m0[zz, here] = (mixs[zz, c, here].astype(F32) + m0[zz, here].astype(F32)).astype(BF16)

    out_mix = local(m0, mix_out, 4)

    @pl.loop(0, 8)
    def _(t):
        cols = pl.ds(pl.multiple_of(t * 256, 256), 256)
        left = rows[:, :, :, cols].reshape(8 * TOK, 256)
        dwg[t // 4, t % 4] = dot_rows(left, dgu[...]).astype(BF16).reshape(2, TOK, 2 * FS)

    out_wg = local(dwg, dwg_out, 5)
    for copy in q3:
        copy.wait_recv()
    q4.start()

    @pl.loop(0, 5)
    def _(t):
        units = pl.ds(pl.multiple_of(t * 128, 128), 128)
        dwd32[units] = dot_rows(inn[:, units], ogs[...].reshape(8 * TOK, D))

    @pl.loop(0, 8)
    def _(i):
        yl, x = i // 4, i % 4
        at = pl.ds(pl.multiple_of(i * 80, 80), 80)
        lo, hi = dwd32[at, :1024], dwd32[at, 1024:]
        dwd[yl, x, 0] = jnp.concatenate([lo[:40], hi[:40]], axis=0).astype(BF16)
        dwd[yl, x, 1] = jnp.concatenate([lo[40:], hi[40:]], axis=0).astype(BF16)

    out_wd = local(dwd, dwd_out, 6)
    for o in (1, 2, 3):
        remote(s0.at[0], r1.at[o - 1], 12 + o, sib).wait_recv()

    @pl.loop(0, TOK, step=16)
    def _(t):
        here = pl.ds(pl.multiple_of(t, 16), 16)
        total = s0[z, here].astype(F32)
        for j in range(3):
            total = total + r1[j, here].astype(F32)
        dn[here] = total

    out_dn = local(dn, d_out, 7)
    q4.wait_recv()
    k.drain()
    for copy in sent:
        copy.wait_send()
    for o in range(4):
        remote(rows.at[0, 0], rows.at[0, 0], 4 + o, sib).wait_send()
        remote(part.at[0, 0], r0.at[0], 8 + o, sib).wait_send()
        remote(mixs.at[0, 0], m0.at[0], 16 + o, sib).wait_send()
    for o in (1, 2, 3):
        remote(s0.at[0], r1.at[o - 1], 12 + o, sib).wait_send()
    for copy in (out_mix, out_wg, out_wd, out_dn):
        copy.wait()


def ffn(n2, OG, WG, WD, wq):
    outs = [
        sds((TOK, D), F32),
        sds((4, TOK, D), BF16),
        sds((2, 4, 2, TOK, 2 * FS), BF16),
        sds((2, 4, 2, 80, 1024), BF16),
        sds((2, 4, 2, 4, 2, 16, 2048), BF16),
    ]
    scratch = [
        pltpu.VMEM((4, 2, TOK, D), BF16),
        pltpu.VMEM((4, 2, TOK, D), BF16),
        pltpu.VMEM((2, 4, 2, 8, 16, 2 * FS), BF16),
        pltpu.VMEM((2, 4, 2, 80, 1024), BF16),
        pltpu.VMEM((FS, D), BF16),
        pltpu.VMEM((8 * TOK, 2 * FS), BF16),
        pltpu.VMEM((8 * TOK, FS), BF16),
        pltpu.VMEM((256, FS), F32),
        pltpu.VMEM((4, 2, TOK, D), BF16),
        pltpu.VMEM((4, 2, TOK, D), BF16),
        pltpu.VMEM((4, TOK, D), BF16),
        pltpu.VMEM((4, TOK, D), BF16),
        pltpu.VMEM((3, TOK, D), BF16),
        pltpu.VMEM((4, TOK, D), BF16),
        pltpu.VMEM((2, 4, 2, TOK, 2 * FS), BF16),
        pltpu.VMEM((FS, D), F32),
        pltpu.VMEM((2, 4, 2, 80, 1024), BF16),
        pltpu.VMEM((TOK, D), F32),
        pltpu.SemaphoreType.DMA((20,)),
        pltpu.SemaphoreType.DMA((20,)),
        pltpu.SemaphoreType.DMA((8,)),
        pltpu.SemaphoreType.DMA((20,)),
        pltpu.SemaphoreType.DMA((20,)),
    ]
    return pl.pallas_call(
        ffn_body,
        out_shape=outs,
        in_specs=[ANY] * 5,
        out_specs=[ANY] * 5,
        scratch_shapes=scratch,
        name="ffn",
        compiler_params=pltpu.CompilerParams(
            collective_id=1, has_side_effects=True, vmem_limit_bytes=60 << 20
        ),
    )(n2, OG, WG, WD, wq)


def back_body(*refs):
    (DN, X_IN, OG_IN, RESID, ATT, PT, LSE, WQ, WO, KV, mix_part, dwg, dwd, NA) = refs[:14]
    (gains, segc, segq, cos_ref, sin_ref, qgain, kgain) = refs[14:21]
    (IN_GRAD, MIXED, GWG, GWD, GQ, GO, SMALL) = refs[21:28]
    (dn, xv, ogv, resid, pt, lse, in_grad, mixed, kvs, bias, qts, qns, dts, dns, dqt, dpt, datt, dres) = refs[28:46]
    (kpart, k0, k1, ks1, k2, kres, w2, wo2, low2, att2, do, dp, dpm, na2, dqm, mix1) = refs[46:62]
    scr = list(refs[62:])
    parts = []
    for shapes in PLANE_SHAPES + O_SHAPES:
        n = 2 * len(shapes)
        parts.append(scr[:n])
        scr = scr[n:]
    vec, vrecv, ssem, rsem = scr
    p = Place()
    k = Links(ssem, rsem)
    yl, z, c = p.yl, p.z, p.c
    m = z * 2 + c
    sib = p.step("c", 1)
    yl_partner = p.at(y=p.yh * 2 + 1 - yl)
    get = {
        "dn": k.local(DN, dn),
        "x": k.local(X_IN, xv),
        "og": k.local(OG_IN, ogv),
        "resid": k.local(RESID, resid),
        "att": k.local(ATT, att2.at[0]),
        "pt": k.local(PT, pt),
        "lse": k.local(LSE, lse),
        "kv": k.local(KV, kvs),
        "mix": k.local(mix_part.at[z], mix1.at[3]),
    }
    partners = [p.step(a, j) for a in "xyz" for j in (1, 2, 3)]
    partners += [p.at(z=(z + j) % 4, c=1 - c) for j in range(4)]
    slab_to, slab_from = slab_target(p), slab_source(p)
    own_slab = same(p, slab_to)
    greet_plane(p, partners, slab_to, slab_from, own_slab)
    plane = [
        staged_reduce(p, k, dwg, wg_stages(0), parts[0], 16),
        staged_reduce(p, k, dwg, wg_stages(1), parts[1], 16),
        staged_reduce(p, k, dwd, wd_stages(0), parts[2], 16),
        staged_reduce(p, k, dwd, wd_stages(1), parts[3], 16),
    ]
    for i in (0, 1, 3):
        next(plane[i])
    pair_att = k.send(ATT, att2.at[1], sib)
    mixing = [k.send(mix_part.at[p.pos("z", j)], mix1.at[j - 1], p.step("z", j)) for j in (1, 2, 3)]
    get_w = [k.local(WO.at[0, t], wo2.at[t]) for t in range(2)]
    fill_bias(bias, segc, segq, p.s * ROWS)
    cos, sin = cos_ref[...], sin_ref[...]
    get["pt"].wait()

    @pl.loop(0, KV_HEADS)
    def _(g):
        for mm, unit in enumerate(query_units(pt, g, cos, sin, qgain[...])):
            qts[g, mm] = unit.astype(BF16)
            qns[g, mm] = unit.T.astype(BF16)

    for name in ("dn", "og", "resid"):
        get[name].wait()
    value = resid[...]
    scale_two = rms_scale(value)
    norm_two = value * scale_two
    d_resid = ogv[...].astype(F32) + norm_back(dn[...], norm_two, scale_two, gains[1:2, :])
    dres[...] = d_resid
    low2[0] = d_resid.astype(BF16)
    pair_low = k.send(low2.at[0], low2.at[1], sib)
    for t in range(8):
        get_w[t].wait()
        term = dot(low2[0, :, t * 256 : (t + 1) * 256], wo2[t % 2].reshape(256, QD))
        datt[...] = term if t == 0 else datt[...] + term
        if t < 6:
            get_w.append(k.local(WO.at[(t + 2) // 4, (t + 2) % 4], wo2.at[t % 2]))
    for g in range(KV_HEADS):
        tiles = []
        for t in range(2):
            at = (g * GROUP + 2 * t) * HEAD
            both = low(datt[:, at : at + 128]).T
            tiles.append(swap(both[:HEAD], both[HEAD:]))
        for mm in range(MICRO):
            none = jnp.zeros((HEAD, 256), F32)
            unit = jnp.concatenate([none, jnp.concatenate([tiles[0][mm], tiles[1][mm]], axis=1)], axis=0)
            dts[g, mm] = unit.astype(BF16)
            dns[g, mm] = unit.T.astype(BF16)
    get["kv"].wait()
    get["lse"].wait()

    @pl.loop(0, 2 * KV_HEADS)
    def _(u):
        g, mm = u // 2, u % 2
        kv = unit_kv(kvs, mm, g)
        score = jnp.minimum(dot(kv, qts[g, mm]), unit_bias(bias, mm))
        again = jnp.exp(score - lse[u, 0:1, :])
        d_probs = dot(kv, dts[g, mm])
        inner = jnp.sum(again * d_probs, axis=0, keepdims=True)
        d_scores = (again * (d_probs - inner)).astype(BF16)
        d_kv = dot(d_scores, qns[g, mm]) + dot(again.astype(BF16), dns[g, mm])
        cols = pl.ds(pl.multiple_of(g * 128, 128), 128)
        kpart[mm, :, :, :, :, cols] = d_kv.astype(BF16).reshape(2, 4, 2, ROWS, 128)
        dqt[g, mm] = dot_rows(kv, d_scores)[:HEAD] * (HEAD ** -0.5)

    core = k.send(kpart.at[:, :, :, 1 - c], k0, sib)
    core.wait_recv()

    @pl.loop(0, 4)
    def _(zz):
        for a in range(2):
            for b in range(2):
                k0[a, b, zz] = (kpart[a, b, zz, c].astype(F32) + k0[a, b, zz].astype(F32)).astype(BF16)

    ring = [k.send(k0.at[:, :, p.pos("z", j)], k1.at[j - 1], p.step("z", j)) for j in (1, 2, 3)]

    get["att"].wait()
    pair_att.wait_recv()
    pair_low.wait_recv()
    att_cols = pl.ds(pl.multiple_of(c * 640, 128), 640)

    @pl.loop(0, 8)
    def _(t):
        cols = pl.ds(pl.multiple_of(t * 256, 256), 256)
        left = low2[:, :, cols].reshape(2 * TOK, 256)
        right = att2[:, :, att_cols].reshape(2 * TOK, 640)
        do[t // 4, t % 4] = dot_rows(left, right).astype(BF16).reshape(2, 4, 32, 640)

    outward = [staged_reduce(p, k, do, o_stages(i), parts[6 + i], 16) for i in range(3)]
    for step in outward:
        next(step)

    query_sum = jnp.zeros((HEAD, TOK), F32)
    for g in range(KV_HEADS):
        heads = []
        for t in range(2):
            cols = slice(t * 128, (t + 1) * 128)
            heads += list(swap(dqt[g, 0, :, cols], dqt[g, 1, :, cols]))
        for h in range(GROUP):
            at = (g * GROUP + h) * HEAD
            d_raw, term = head_back(pt[at : at + HEAD], heads[h], cos, sin, qgain[...])
            query_sum = query_sum + term
            dpt[at : at + HEAD] = d_raw

    for copy in ring:
        copy.wait_recv()
    for a in range(2):
        for b in range(2):
            total = k0[a, b, z].astype(F32)
            for j in range(3):
                total = total + k1[j, a, b].astype(F32)
            ks1[a, b] = total.astype(BF16)
    across = k.send(ks1.at[:, 1 - yl], k2, yl_partner)
    across.wait_recv()
    next(plane[2])
    for a in range(2):
        kres[pl.ds(a * ROWS, ROWS)] = ks1[a, yl].astype(F32) + k2[a].astype(F32)
    key_sum = jnp.zeros((HEAD, TOK), F32)
    for g in range(KV_HEADS):
        both = kres[:, g * 128 : (g + 1) * 128].T
        at = QD + g * HEAD
        d_raw, term = head_back(pt[at : at + HEAD], both[:HEAD], cos, sin, kgain[...])
        key_sum = key_sum + term
        dpt[at : at + HEAD] = d_raw
        dpt[at + KD : at + KD + HEAD] = both[HEAD:]
    get_q = [k.local(WQ.at[0, t], w2.at[t]) for t in range(2)]
    get_n = [k.local(NA.at[:, :, :, pl.ds(t * 256, 256)], na2.at[t]) for t in range(2)]
    for t in range(8):
        block = jnp.concatenate([dpt[t * 240 : (t + 1) * 240], jnp.zeros((16, TOK), F32)], axis=0)
        dp[t] = block.T.astype(BF16)
    members = []
    for dz in range(4):
        for dc in range(2):
            zz, cc = (z + dz) % 4, (c + dc) % 2
            src = dp.at[zz * 2 + cc]
            if dz == 0 and dc == 0:
                own_dp = k.local(src, dpm.at[z, c])
            else:
                members.append(k.send(src, dpm.at[z, c], p.at(z=zz, c=cc)))
    sums = jnp.concatenate(
        [jnp.sum(query_sum.T, axis=0, keepdims=True), jnp.sum(key_sum.T, axis=0, keepdims=True)], axis=1
    )
    vec[0] = jnp.broadcast_to(sums, (8, 128))
    small = small_reduce(p, k, vec, vrecv)
    next(small)
    for i in (0, 1, 3):
        next(plane[i])
    own_dp.wait()
    for copy in members:
        copy.wait_recv()
    for t in range(8):
        get_n[t].wait()
        total = dot_rows(na2[t % 2].reshape(8 * TOK, 256), dpm[...].reshape(8 * TOK, 256))
        dqm[t // 4, t % 4] = total.astype(BF16).reshape(2, TOK, 256)
        if t < 6:
            get_n.append(k.local(NA.at[:, :, :, pl.ds((t + 2) * 256, 256)], na2.at[t % 2]))
    inward = [staged_reduce(p, k, dqm, q_stages(i), parts[4 + i], 16) for i in range(2)]
    for step in inward:
        next(step)
    for step in outward:
        next(step)
    next(small)
    for t in range(8):
        get_q[t].wait()
        w = w2[t % 2].reshape(256, 2048)
        left = jnp.concatenate([dp[i] for i in range(8)], axis=1)
        in_grad[:, t * 256 : (t + 1) * 256] = dot_last(left, w)
        if t < 6:
            get_q.append(k.local(WQ.at[(t + 2) // 4, (t + 2) % 4], w2.at[t % 2]))
    next(plane[2])
    for step in inward:
        next(step)
    next(small)
    for step in outward:
        next(step)
    get["x"].wait()
    hidden = xv[...].astype(F32)
    scale_one = rms_scale(hidden)
    in_grad[...] = dres[...] + norm_back(in_grad[...], hidden * scale_one, scale_one, gains[0:1, :])
    keep = [k.local(in_grad, IN_GRAD)]
    for step in plane:
        next(step, None)
    next(small)

    last = []

    def to_owners(total, dst):
        for dz in range(4):
            for dc in range(2):
                zz, cc = (z + dz) % 4, (c + dc) % 2
                src = total.at[pl.ds(pl.multiple_of((zz * 2 + cc) * 16, 16), 16)]
                if dz == 0 and dc == 0:
                    keep.append(k.local(src, dst))
                else:
                    last.append(k.send(src, dst, p.at(z=zz, c=cc)))

    for half in range(2):
        to_owners(parts[half][-1], GWG.at[:, pl.ds(pl.multiple_of(half * FF + m * FS, 128), FS)])
    slabs = []
    for half in range(2):
        i = k.used
        k.used += 1
        src, dst = parts[2 + half][-1], GWD.at[:, pl.ds(half * 512, 512)]
        slabs.append((src, dst, i))

        @pl.when(own_slab)
        def _(src=src, dst=dst, i=i):
            pltpu.make_async_copy(src, dst, rsem.at[i]).start()

        @pl.when(jnp.logical_not(own_slab))
        def _(src=src, dst=dst, i=i):
            slab_copy(src, dst, ssem, rsem, i, slab_from).start()

    get["mix"].wait()
    for copy in mixing:
        copy.wait_recv()

    @pl.loop(0, TOK, step=16)
    def _(t):
        at = pl.ds(pl.multiple_of(t, 16), 16)
        total = resid[at]
        for j in range(4):
            total = total + mix1[j, at].astype(F32)
        mixed[at] = total.astype(BF16)

    keep.append(k.local(mixed, MIXED))
    for step in inward:
        next(step, None)
    for half in range(2):
        to_owners(parts[4 + half][-1], GQ.at[:, pl.ds(pl.multiple_of(m * 256 + half * 128, 128), 128)])
    for i, step in enumerate(outward):
        next(step, None)
        total = parts[6 + i][-1]
        dst = GO.at[c, :, pl.ds(*O_PARTS[i])]
        keep.append(k.local(total.at[pl.ds(pl.multiple_of(c * 16, 16), 16)], dst))
        last.append(k.send(total.at[pl.ds(pl.multiple_of((1 - c) * 16, 16), 16)], dst, sib))
    next(small, None)
    SMALL[...] = vec[4]
    for copy in keep:
        copy.wait()
    for copy in last:
        copy.wait_recv()
    for src, dst, i in slabs:

        @pl.when(own_slab)
        def _(src=src, dst=dst, i=i):
            pltpu.make_async_copy(src, dst, rsem.at[i]).wait()

        @pl.when(jnp.logical_not(own_slab))
        def _(src=src, dst=dst, i=i):
            slab_copy(src, dst, ssem, rsem, i, slab_from).wait()

    k.drain()


def head_back(raw, grad, cos, sin, gain):
    scale = head_scale(raw)
    normed = raw * scale
    d_head = grad * cos + half_back(grad * sin)
    scaled = d_head * gain
    inner = jnp.mean(scaled * normed, axis=0, keepdims=True)
    return scale * (scaled - normed * inner), d_head * normed


def back(dn, x, og, resid, att, pt, lse, WQ, WO, KV, mix, dwg, dwd, NA, gains, segc, segq, cos, sin, qgain, kgain):
    w = 2 * KD
    outs = [
        sds((TOK, D), F32),
        sds((TOK, D), BF16),
        sds((16, 2 * FF), BF16),
        sds((80, 1024), BF16),
        sds((16, 2048), BF16),
        sds((2, 16, 640), BF16),
        sds((8, 128), F32),
    ]
    scratch = [
        pltpu.VMEM((TOK, D), F32),
        pltpu.VMEM((TOK, D), BF16),
        pltpu.VMEM((TOK, D), BF16),
        pltpu.VMEM((TOK, D), F32),
        pltpu.VMEM((QKV, TOK), F32),
        pltpu.VMEM((2 * KV_HEADS, 8, 256), F32),
        pltpu.VMEM((TOK, D), F32),
        pltpu.VMEM((TOK, D), BF16),
        pltpu.VMEM((2, 2, 4, 2, ROWS, w), BF16),
        pltpu.VMEM((2, SEQ, 128), F32),
        pltpu.VMEM((KV_HEADS, 2, 128, 256), BF16),
        pltpu.VMEM((KV_HEADS, 2, 256, 128), BF16),
        pltpu.VMEM((KV_HEADS, 2, 128, 256), BF16),
        pltpu.VMEM((KV_HEADS, 2, 256, 128), BF16),
        pltpu.VMEM((KV_HEADS, 2, HEAD, 256), F32),
        pltpu.VMEM((QKV, TOK), F32),
        pltpu.VMEM((TOK, QD), F32),
        pltpu.VMEM((TOK, D), F32),
        pltpu.VMEM((2, 2, 4, 2, ROWS, w), BF16),
        pltpu.VMEM((2, 2, 4, ROWS, w), BF16),
        pltpu.VMEM((3, 2, 2, ROWS, w), BF16),
        pltpu.VMEM((2, 2, ROWS, w), BF16),
        pltpu.VMEM((2, ROWS, w), BF16),
        pltpu.VMEM((TOK, w), F32),
        pltpu.VMEM((2, 2, 4, 2, 16, 2048), BF16),
        pltpu.VMEM((2, 2, 4, 2, 16, QD), BF16),
        pltpu.VMEM((2, TOK, D), BF16),
        pltpu.VMEM((2, TOK, QD), BF16),
        pltpu.VMEM((2, 4, 2, 4, 32, 640), BF16),
        pltpu.VMEM((8, TOK, 256), BF16),
        pltpu.VMEM((4, 2, TOK, 256), BF16),
        pltpu.VMEM((2, 4, 2, TOK, 256), BF16),
        pltpu.VMEM((2, 4, 2, TOK, 256), BF16),
        pltpu.VMEM((4, TOK, D), BF16),
    ]
    for shapes in PLANE_SHAPES + O_SHAPES:
        scratch += staged_scratch(shapes)
    scratch += [
        pltpu.VMEM((5, 8, 128), F32),
        pltpu.VMEM((4, 3, 8, 128), F32),
        pltpu.SemaphoreType.DMA((180,)),
        pltpu.SemaphoreType.DMA((180,)),
    ]
    return pl.pallas_call(
        back_body,
        out_shape=outs,
        in_specs=[ANY] * 14 + [VMEM] * 7,
        out_specs=[ANY] * 6 + [VMEM],
        scratch_shapes=scratch,
        name="back",
        compiler_params=pltpu.CompilerParams(
            collective_id=2, has_side_effects=True, vmem_limit_bytes=60 << 20
        ),
    )(dn, x, og, resid, att, pt, lse, WQ, WO, KV, mix, dwg, dwd, NA, gains, segc, segq, cos, sin, qgain, kgain)


def rope_tables(start):
    half = HEAD // 2
    inverse = 10000.0 ** (-jnp.arange(half, dtype=F32) / half)
    positions = (start + jnp.arange(TOK) % ROWS).astype(F32)
    angles = inverse[:, None] * positions[None, :]
    angles = jnp.concatenate([angles, angles], axis=0)
    return jnp.cos(angles), jnp.sin(angles)


def per_device(
    tokens,
    segment_ids,
    w_qkv,
    w_out,
    w_gate_up,
    w_down,
    attn_gain,
    ffn_gain,
    query_gain,
    key_gain,
    out_grad,
):
    start = lax.axis_index("seq") * ROWS
    qgain = query_gain.astype(F32)[:, None]
    kgain = key_gain.astype(F32)[:, None]
    spare = jnp.stack([attn_gain, ffn_gain] + [jnp.zeros_like(attn_gain)] * 14, axis=1)
    spare = jnp.broadcast_to(spare[:, None, :], (16, 8, 16))
    wq_in = jnp.concatenate([w_qkv.reshape(16, 8, 240), spare], axis=2).reshape(16, 2048)
    wd_in = jnp.concatenate([w_down[:, :1024], w_down[:, 1024:]], axis=0)
    og_in = out_grad.reshape(TOK, D)
    x_in = tokens.reshape(TOK, D)
    segc = segment_ids.T
    query_ids = lax.dynamic_slice_in_dim(segment_ids, start, ROWS, axis=1)
    segq = jnp.tile(jnp.where(query_ids >= 0, query_ids, -2), (1, 2))
    cos, sin = rope_tables(start)
    (WO, WG, WD, OG, NA, KV, pt, lse, attended, resid, n2, gains) = front(
        x_in, wq_in, w_out.T, w_gate_up, wd_in, og_in, segc, segq, cos, sin, qgain, kgain
    )
    d_normed, mix_part, dwg, dwd, WQ = ffn(n2, OG, WG, WD, wq_in)
    input_grad, result, gwg, gwd, gq, go, sums = back(
        d_normed, x_in, og_in, resid, attended, pt, lse, WQ, WO, KV, mix_part, dwg, dwd, NA,
        gains, segc, segq, cos, sin, qgain, kgain,
    )
    w_qkv_grad = gq.reshape(16, 8, 256)[:, :, :240].reshape(16, QKV).astype(F32)
    w_out_grad = jnp.concatenate([go[0], go[1]], axis=1).T.astype(F32)
    w_gate_up_grad = gwg.astype(F32)
    attn_sum = jnp.sum(w_qkv.astype(F32) * w_qkv_grad, axis=1) / attn_gain.astype(F32)
    ffn_sum = jnp.sum(w_gate_up.astype(F32) * w_gate_up_grad, axis=1) / ffn_gain.astype(F32)
    return (
        result.reshape(MICRO, ROWS, D),
        input_grad.reshape(MICRO, ROWS, D),
        w_qkv_grad,
        w_out_grad,
        w_gate_up_grad,
        jnp.concatenate([gwd[:40], gwd[40:]], axis=1).astype(F32),
        attn_sum,
        ffn_sum,
        sums[0, :HEAD],
        sums[0, HEAD:],
    )


def solution(mesh):
    return jax.shard_map(
        per_device,
        mesh=mesh,
        in_specs=(
            P(None, ("grp", "seq"), None),
            P(None, "grp"),
            P(("grp", "seq"), None),
            P(None, ("grp", "seq")),
            P(("grp", "seq"), None),
            P(("grp", "seq"), None),
            P(("grp", "seq")),
            P(("grp", "seq")),
            P(),
            P(),
            P(None, ("grp", "seq"), None),
        ),
        out_specs=(
            P(None, ("grp", "seq"), None),
            P(None, ("grp", "seq"), None),
            P(("grp", "seq"), None),
            P(None, ("grp", "seq")),
            P(("grp", "seq"), None),
            P(("grp", "seq"), None),
            P(("grp", "seq")),
            P(("grp", "seq")),
            P(),
            P(),
        ),
        check_vma=False,
    )
```

time: 370 us -> 316 us (0.85)
  Pallas kernels: 346 us -> 291 us
    pallas_call x4 -> x3, Pallas kernels: 346 us -> 291 us  [the longest x1 117 us: front(): pl.pallas_call(front_body, out_shape=hbm + vmem, in_specs=[ANY] * 6 + [VM...]
where the time goes in v4:
time: 316 us; the launch traced here: 314 us
  Pallas kernels  291 us (92%)
  local copies, waits for them, and re-layouts  14.8 us (5%)
  other arithmetic  7.69 us (2%)
    pallas_call x1, Pallas kernels, front(): pl.pallas_call(front_body, out_shape=hbm + vmem, in_specs=[ANY] * 6 + [VM...  117 us
    pallas_call x1, Pallas kernels, back(): pl.pallas_call(back_body, out_shape=outs, in_specs=[ANY] * 14 + [VMEM] *...  103 us
    pallas_call x1, Pallas kernels, ffn(): pl.pallas_call(ffn_body, out_shape=outs, in_specs=[ANY] * 5, out_specs=[A...  70.8 us

profile of v4, /device:TPU:1, one launch (start us, length us, event | category | flops | bytes accessed | tf_op | source)
XLA Modules:
  0.0 314.4 jit_solution(17559211093044296346)
XLA Ops:
  0.7 0.7 bitcast_convert_fusion.1
  1.3 0.7 bitcast_convert_fusion
  2.0 0.8 compare_select_fusion
  2.7 0.6 tile.10.refs_7_.refs_16_
  3.4 0.7 copy.22
  4.1 0.7 copy.21
  5.1 0.7 copy.25.refs_11_.refs_20_
  5.8 0.7 copy.24.refs_10_.refs_19_
  6.5 0.7 fusion
  7.2 1.0 reshape.67
  8.9 0.9 fusion.5
  9.8 0.7 pad_maximum_fusion.refs_4_
  10.5 1.7 copy.23
  12.2 116.9 %front.1 = (bf16[2,4,2,4,2,16,1280]{6,5,4,3,2,1,0:T(8,128)(2,1)}, bf16[2,4,2,8,16,1280]{5,4,3,2,1,0:T(8,128)(2,1)}, bf16[2,4,2,80,1024]{4,3,2,1,0:T(8,128)(2,1)}...) custom-call(bf16[128,2048]{1,0:T(8,128)(2,1)} %bitcast.30, ...), custom_call_target="tpu_custom_call" | custom-call | tf_op jit(solution)/shard_map/front/pallas_call | solution.py:664
  129.1 70.8 %ffn.1 = (f32[128,2048]{1,0:T(8,128)}, bf16[4,128,2048]{2,1,0:T(8,128)(2,1)}, bf16[2,4,2,128,1280]{4,3,2,1,0:T(8,128)(2,1)}, bf16[2,4,2,80,1024]{4,3,2,1,0:T(8,128)(2,1)}, bf16[2,4,2,4,2,16,2048]{6,5,4,3,2,1,0:T(8,128)(2,1)}) custom-call(bf16[128,2048]{1,0:T(8,128)(2,1)} %get-tuple-element.34.n2, bf16[4,2,128,2048]{3,2,1,0:T(8,128)(2,1)} %get-tuple-element.35.OG, ...), custom_call_target="tpu_custom_call" | custom-call | tf_op jit(solution)/shard_map/ffn/pallas_call | solution.py:909
  200.0 103.4 %back.1 = (f32[128,2048]{1,0:T(8,128)}, bf16[128,2048]{1,0:T(8,128)(2,1)}, bf16[16,10240]{1,0:T(8,128)(2,1)}, bf16[80,1024]{1,0:T(8,128)(2,1)}, bf16[16,2048]{1,...) custom-call(f32[128,2048]{1,0:T(8,128)} %get-tuple-element.38.refs_0_, bf16[128,2048]{1,0:T(8,128)(2,1)} %bitcast.31, ...), custom_call_target="tpu_custom_call" | custom-call | tf_op jit(solution)/shard_map/back/pallas_call | solution.py:1275
  303.4 1.4 slice_bitcast_fusion.2
  304.8 0.7 slice_bitcast_fusion.1
  306.2 0.9 copy.29
  307.3 0.9 fusion.4
  308.2 0.7 maximum_convert_fusion
  309.0 2.0 multiply_reduce_fusion
  311.5 1.9 copy.32
  313.4 1.0 copy.33
  (28 shorter events, 2.4 us)
Async XLA Ops:
  199.9 107.2 %copy-start.3 = (bf16[16,1920]{1,0:T(8,128)(2,1)S(1)}, bf16[16,1920]{1,0:T(8,128)(2,1)}, u32[]{:S(2)}) copy-start(bf16[16,1920]{1,0:T(8,128)(2,1)} %param.13) | copy-start | bytes 184324
  199.9 109.1 %copy-start = (bf16[16,10240]{1,0:T(8,128)(2,1)S(1)}, bf16[16,10240]{1,0:T(8,128)(2,1)}, u32[]{:S(2)}) copy-start(bf16[16,10240]{1,0:T(8,128)(2,1)} %refs_3_.1) | copy-start | bytes 983044
  199.9 111.1 %copy-start.4 = (bf16[16]{0:T(256)(128)(2,1)S(1)}, bf16[16]{0:T(256)(128)(2,1)}, u32[]{:S(2)}) copy-start(bf16[16]{0:T(256)(128)(2,1)} %param.17) | copy-start | bytes 100
  200.0 111.0 %copy-start.5 = (bf16[16]{0:T(256)(128)(2,1)S(1)}, bf16[16]{0:T(256)(128)(2,1)}, u32[]{:S(2)}) copy-start(bf16[16]{0:T(256)(128)(2,1)} %param.18) | copy-start | bytes 100
  303.4 10.0 %copy-start.1 = (f32[128,2048]{1,0:T(8,128)S(1)}, f32[128,2048]{1,0:T(8,128)}, u32[]{:S(2)}) copy-start(f32[128,2048]{1,0:T(8,128)} %get-tuple-element.52) | copy-start | bytes 3145732
  307.1 7.2 %copy-start.2 = (f32[16,1920]{1,0:T(8,128)}, f32[16,1920]{1,0:T(8,128)S(1)}, u32[]{:S(2)}) copy-start(f32[16,1920]{1,0:T(8,128)S(1)} %reshape.75) | copy-start | bytes 368644

commit v5 on v4

--- a/solution.py
+++ b/solution.py
@@ -1,5 +1,6 @@
 import jax
 import jax.numpy as jnp
+import numpy as np
 from jax import lax
 from jax.experimental import pallas as pl
 from jax.experimental.pallas import tpu as pltpu
@@ -56,23 +57,25 @@
 
 
 class Links:
-    def __init__(self, send_sems, recv_sems):
-        self.send_sems, self.recv_sems = send_sems, recv_sems
-        self.used = 0
-        self.sent = []
+    def __init__(self, send_sems, recv_sems, local_sems):
+        self.send_sems, self.recv_sems, self.local_sems = send_sems, recv_sems, local_sems
+        self.received = 0
+        self.free = {"send": list(range(send_sems.shape[0]))[::-1], "local": list(range(local_sems.shape[0]))[::-1]}
+        self.sent = {}
 
     def plan(self, src, dst, to):
-        i = self.used
-        self.used += 1
+        i = self.received
+        self.received += 1
+        slot = self.free["send"].pop()
         copy = pltpu.make_async_remote_copy(
             src_ref=src,
             dst_ref=dst,
-            send_sem=self.send_sems.at[i],
+            send_sem=self.send_sems.at[slot],
             recv_sem=self.recv_sems.at[i],
             device_id=to,
             device_id_type=MESH,
         )
-        self.sent.append(copy)
+        self.sent[id(copy)] = (copy, slot)
         return copy
 
     def send(self, src, dst, to):
@@ -81,15 +84,28 @@
         return copy
 
     def local(self, src, dst):
-        i = self.used
-        self.used += 1
-        copy = pltpu.make_async_copy(src, dst, self.recv_sems.at[i])
+        slot = self.free["local"].pop()
+        copy = pltpu.make_async_copy(src, dst, self.local_sems.at[slot])
         copy.start()
-        return copy
+        return Local(self, copy, slot)
+
+    def settle(self, copies):
+        for copy in copies:
+            copy, slot = self.sent.pop(id(copy))
+            copy.wait_send()
+            self.free["send"].append(slot)
 
     def drain(self):
-        for copy in self.sent:
-            copy.wait_send()
+        self.settle([copy for copy, _ in list(self.sent.values())])
+
+
+class Local:
+    def __init__(self, links, copy, slot):
+        self.links, self.copy, self.slot = links, copy, slot
+
+    def wait(self):
+        self.copy.wait()
+        self.links.free["local"].append(self.slot)
 
 
 def greet(partners):
@@ -155,15 +171,35 @@
         pl.semaphore_wait(barrier, len(partners))
 
 
-def slab_copy(src, dst, ssem, rsem, i, to):
-    return pltpu.make_async_remote_copy(
-        src_ref=src,
-        dst_ref=dst,
-        send_sem=ssem.at[i],
-        recv_sem=rsem.at[i],
-        device_id=to,
-        device_id_type=MESH,
-    )
+class Slab:
+    def __init__(self, k, src, dst, to, own):
+        self.own, self.src, self.dst = own, src, dst
+        self.far = k.plan(src, dst, to)
+        k.sent.pop(id(self.far))
+        self.near = pltpu.make_async_copy(src, dst, k.recv_sems.at[k.received - 1])
+
+    def start(self):
+        @pl.when(self.own)
+        def _():
+            self.near.start()
+
+        @pl.when(jnp.logical_not(self.own))
+        def _():
+            self.far.start()
+
+    def wait_recv(self):
+        @pl.when(self.own)
+        def _():
+            self.near.wait()
+
+        @pl.when(jnp.logical_not(self.own))
+        def _():
+            self.far.wait_recv()
+
+    def wait_send(self):
+        @pl.when(jnp.logical_not(self.own))
+        def _():
+            self.far.wait_send()
 
 
 def add_blocks(dst, own, recv, chunk):
@@ -342,16 +378,43 @@
     ]
 
 
-def fill_bias(bias, segc, segq, start):
-    @pl.loop(0, SEQ, step=128)
-    def _(t):
-        at = pl.ds(pl.multiple_of(t, 128), 128)
-        key = lax.broadcasted_iota(jnp.int32, (128, 128), 0) + t
-        query = lax.broadcasted_iota(jnp.int32, (128, 128), 1) % ROWS + start
-        for m in range(MICRO):
-            ok = (key <= query) & (segc[at, m : m + 1] == segq[m : m + 1, :])
-            ok = ok | (key == query)
+def fill_bias(bias, seg, s):
+    lane = lax.broadcasted_iota(jnp.int32, (128, 128), 1)
+    query = lane % ROWS + s * ROWS
+    around = pl.ds(pl.multiple_of((s // 2) * 128, 128), 128)
+    for m in range(MICRO):
+        ids = jnp.broadcast_to(seg[m : m + 1, around].astype(F32), (128, 128))
+        turned = pltpu.roll(ids, ROWS, 1)
+        ids = jnp.where((lane < ROWS) == (s % 2 == 0), ids, turned)
+        ids = jnp.where(ids >= 0, ids, -2.0)
+
+        @pl.loop(0, SEQ, step=128)
+        def _(t):
+            at = pl.ds(pl.multiple_of(t, 128), 128)
+            key = lax.broadcasted_iota(jnp.int32, (128, 128), 0) + t
+            keys = jnp.broadcast_to(seg[m : m + 1, at].astype(F32), (128, 128)).T
+            ok = ((key <= query) & (keys == ids)) | (key == query)
             bias[m, at] = jnp.where(ok, 3e38, -1e30)
+
+
+def rope_parts():
+    inverse = 10000.0 ** (-(np.arange(HEAD) % (HEAD // 2)) / (HEAD // 2))
+    begin = inverse[:, None] * (np.arange(128)[None, :] % 16 * ROWS)
+    inside = inverse[:, None] * (np.arange(128)[None, :] % ROWS)
+    return np.stack([np.cos(begin), np.sin(begin), np.cos(inside), np.sin(inside)]).astype(np.float32)
+
+
+def rope_tables(parts, s):
+    here = lax.broadcasted_iota(jnp.int32, (HEAD, 128), 1) == s
+    c0 = jnp.sum(jnp.where(here, parts[0], 0.0), axis=1, keepdims=True)
+    s0 = jnp.sum(jnp.where(here, parts[1], 0.0), axis=1, keepdims=True)
+    return c0 * parts[2] - s0 * parts[3], s0 * parts[2] + c0 * parts[3]
+
+
+def column(row):
+    n = row.shape[1]
+    place = lax.broadcasted_iota(jnp.int32, (n, n), 0) == lax.broadcasted_iota(jnp.int32, (n, n), 1)
+    return jnp.sum(jnp.where(place, jnp.broadcast_to(row, (n, n)), 0.0), axis=1, keepdims=True)
 
 
 def unit_bias(bias, m):
@@ -365,11 +428,13 @@
 
 
 def front_body(*refs):
-    (x_in, wq, wo, wg, wd, og, segc, segq, cos_ref, sin_ref, qgain, kgain) = refs[:12]
-    (WO, WG, WD, OG, NA, KV, PT, LSE, ATT, RESID, N2, gains_out) = refs[12:24]
-    (xs, na, wqm, wos, pks, pk, pt, lse, att, resid, n2, kvl, kvs, bias, qts, ots, ssem, rsem) = refs[24:]
+    (x_in, w_qkv, wo, wg, w_down, og, seg, g1, g2, g3, g4, parts) = refs[:12]
+    (WO, WG, WD, OG, NA, KV, PT, LSE, ATT, RESID, N2, WQIN, BIAS, ROPE, GAINS, QKGAIN) = refs[12:28]
+    (wq, wd, ogv, gains_out, rope, qkgain) = refs[28:34]
+    (xs, na, wqm, wos, pks, pk, pt, lse, att, resid, n2, kvl, kvs, bias, qts, ots) = refs[34:50]
+    ssem, rsem, lsem = refs[50:]
     p = Place()
-    k = Links(ssem, rsem)
+    k = Links(ssem, rsem, lsem)
     yh, x, yl, z, c = p.yh, p.x, p.yl, p.z, p.c
     m = z * 2 + c
     sib = p.step("c", 1)
@@ -378,6 +443,16 @@
     partners += [p.at(z=(z + j) % 4, c=1 - c) for j in range(4)]
     slab_to, slab_from = slab_target(p), slab_source(p)
     own_slab = same(p, slab_to)
+
+    spare = [column(row[...].astype(F32)) for row in (g1, g2)]
+    wide = w_qkv[...].astype(F32)
+    lane = lax.broadcasted_iota(jnp.int32, (16, 256), 1)
+    rest = jnp.where(lane == 240, spare[0], jnp.where(lane == 241, spare[1], 0.0))
+    for i in range(8):
+        turned = pltpu.roll(wide, (QKV - 240 * i) % QKV, 1)[:, :256]
+        wq[:, i * 256 : (i + 1) * 256] = jnp.where(lane < 240, turned, rest).astype(BF16)
+    slab_rows = w_down[...].astype(F32)
+    wd[...] = jnp.concatenate([slab_rows[:, :1024], slab_rows[:, 1024:]], axis=0).astype(BF16)
     greet_plane(p, partners, slab_to, slab_from, own_slab)
 
     def spread(src_of, dst_of):
@@ -396,6 +471,7 @@
         lambda i: wq.at[:, pl.ds(pl.multiple_of(i * 256, 256), 256)], lambda i: wqm.at[yh, x, yl, i]
     )
     own_x = k.local(x_in, xs.at[z, c])
+    get_og = k.local(og, ogv)
     xcore = {0: k.send(x_in, xs.at[z, c], sib)}
     own_wo = k.local(wo, wos.at[yh, x, yl, z, c])
 
@@ -417,17 +493,8 @@
         for half in range(2)
     ]
     slab_dst = WD.at[yl, z, c]
-    i = k.used
-    k.used += 1
-    slab = slab_copy(wd, slab_dst, ssem, rsem, i, slab_to)
-
-    @pl.when(own_slab)
-    def _():
-        pltpu.make_async_copy(wd, slab_dst, rsem.at[i]).start()
-
-    @pl.when(jnp.logical_not(own_slab))
-    def _():
-        slab.start()
+    slab = Slab(k, wd, slab_dst, slab_to, own_slab)
+    slab.start()
 
     xring = {j: k.send(x_in, xs.at[z, c], p.step("z", j)) for j in (1, 3, 2)}
 
@@ -441,7 +508,11 @@
     for copy in q0[1]:
         copy.wait_recv()
     q1 = to_plane(((wqm.at[yh, x, yl, :, :, ql], "x"), (wqm.at[yh, x, yl, :, :, qh], "y")))
-    fill_bias(bias, segc, segq, p.s * ROWS)
+    fill_bias(bias, seg, p.s)
+    cos, sin = rope_tables(parts, p.s)
+    rope[0], rope[1] = cos, sin
+    qgain, kgain = column(g3[...].astype(F32)), column(g4[...].astype(F32))
+    qkgain[...] = jnp.concatenate([jnp.broadcast_to(qgain, (HEAD, 128)), jnp.broadcast_to(kgain, (HEAD, 128))], axis=0)
     for copy in q1:
         copy.wait_recv()
     q2 = to_plane(((wqm.at[yh, :, yl, :, :, ql], "y"), (wqm.at[:, x, :, :, :, qh], "x")))
@@ -450,14 +521,7 @@
         for copy in far:
             copy.wait_recv()
 
-    @pl.when(own_slab)
-    def _():
-        pltpu.make_async_copy(wd, slab_dst, rsem.at[i]).wait()
-
-    @pl.when(jnp.logical_not(own_slab))
-    def _():
-        slab.wait_recv()
-
+    slab.wait_recv()
     plane = to_plane(
         (
             (WG.at[yh, x, yl, :, :, lo], "x"),
@@ -474,6 +538,8 @@
         lax.broadcasted_iota(jnp.int32, (8, 128), 0) + 112 == lax.broadcasted_iota(jnp.int32, (8, 128), 1), 1.0, 0.0
     ).astype(BF16)
     gains_out[...] = dot_last(pick, wqm[:, :, :, :, :, pl.ds(128, 128)].reshape(D, 128))
+    keep = [k.local(wq, WQIN), k.local(bias, BIAS), k.local(rope, ROPE), k.local(gains_out, GAINS), k.local(qkgain, QKGAIN)]
+    k.settle(q0[1] + q1)
     packs = []
     plane2 = []
     for o in (0, 1, 3, 2):
@@ -511,18 +577,18 @@
                     (WD.at[:, x, :, :, dhi], "x"),
                 ),
             )
-    keep = [k.local(na, NA)]
+    keep.append(k.local(na, NA))
+    k.settle(q2 + o1 + [copy for _, far in g0 for copy in far])
     own_pk.wait()
     for copy in packs:
         copy.wait_recv()
     for i8 in range(8):
         pt[i8 * 240 : (i8 + 1) * 240] = pk[i8].astype(F32).T[:240]
-    cos, sin = cos_ref[...], sin_ref[...]
 
     @pl.loop(0, KV_HEADS)
     def _(g):
         raw = pt[pl.ds(pl.multiple_of(QD + g * HEAD, HEAD), HEAD)]
-        head = raw * head_scale(raw) * kgain[...]
+        head = raw * head_scale(raw) * kgain
         key = head * cos + half_turn(head) * sin
         value = pt[pl.ds(pl.multiple_of(QD + KD + g * HEAD, HEAD), HEAD)]
         both = jnp.concatenate([key, value], axis=0).T.astype(BF16)
@@ -537,25 +603,32 @@
 
     @pl.loop(0, KV_HEADS)
     def _(g):
-        for mm, unit in enumerate(query_units(pt, g, cos, sin, qgain[...])):
+        for mm, unit in enumerate(query_units(pt, g, cos, sin, qgain)):
             qts[g, mm] = unit.astype(BF16)
 
     across.wait_recv()
     src = kvs.at[:, 1 - yl, z, c]
     ring += [k.send(src, src, p.step("z", j)) for j in (1, 2, 3)]
-    plane2 += to_plane(((WG.at[yh, :, yl, :, :, lo], "y"),))
-    own_kv.wait()
     for copy in o2:
         copy.wait_recv()
-    o3 = []
-    for j in (1, 2, 3):
-        xx, yy, zz = p.pos("x", -j), p.pos("y", -j), p.pos("z", -j)
-        src = wo_at(0, EVERY, x, EVERY, EVERY, c)
-        o3.append((k.send(src, src, p.step("x", j)), wo_at(0, EVERY, xx, EVERY, EVERY, c)))
-        src = wo_at(1, yh, EVERY, yl, EVERY, c)
-        o3.append((k.send(src, src, p.step("y", j)), wo_at(1, yy // 2, EVERY, yy % 2, EVERY, c)))
-        src = wo_at(2, EVERY, EVERY, EVERY, z, c)
-        o3.append((k.send(src, src, p.step("z", j)), wo_at(2, EVERY, EVERY, EVERY, zz, c)))
+    own_kv.wait()
+    k.settle(packs + plane)
+
+    def wo_third(part):
+        out = []
+        for j in (1, 2, 3):
+            if part == 0:
+                src, got = wo_at(0, EVERY, x, EVERY, EVERY, c), wo_at(0, EVERY, p.pos("x", -j), EVERY, EVERY, c)
+            elif part == 1:
+                yy = p.pos("y", -j)
+                src, got = wo_at(1, yh, EVERY, yl, EVERY, c), wo_at(1, yy // 2, EVERY, yy % 2, EVERY, c)
+            else:
+                src, got = wo_at(2, EVERY, EVERY, EVERY, z, c), wo_at(2, EVERY, EVERY, EVERY, p.pos("z", -j), c)
+            out.append((k.send(src, src, p.step("xyz"[part], j)), got))
+        return out
+
+    o3 = wo_third(0) + wo_third(1)
+    plane2 += to_plane(((WG.at[yh, :, yl, :, :, lo], "y"),))
     oc = []
     for src in (
         wo_at(0, EVERY, x, EVERY, EVERY, c),
@@ -563,13 +636,16 @@
         wo_at(2, EVERY, EVERY, EVERY, z, c),
     ):
         oc.append(k.send(src, src, sib))
-    keep.append(k.local(og, OG.at[z, c]))
-    rows = [k.send(og, OG.at[z, c], p.step("z", j)) for j in (1, 2, 3)]
-    last = [k.send(og, OG.at[z, c], sib)]
     for copy in ring:
         copy.wait_recv()
     src = kvs.at[:, :, :, c]
     kvc = k.send(src, src, sib)
+    o3 += wo_third(2)
+    get_og.wait()
+    keep.append(k.local(ogv, OG.at[z, c]))
+    rows = [k.send(ogv, OG.at[z, c], p.step("z", j)) for j in (1, 3, 2)]
+    last = [k.send(ogv, OG.at[z, c], sib)]
+    k.settle(o2 + list(xring.values()) + list(xcore.values()))
     kvc.wait_recv()
     keep.append(k.local(kvs, KV))
 
@@ -608,7 +684,7 @@
     value = resid[...]
     n2[...] = (value * rms_scale(value) * gains_out[1:2, :]).astype(BF16)
     keep += [k.local(resid, RESID), k.local(n2, N2)]
-    for j, copy in zip((1, 2, 3), rows):
+    for j, copy in zip((1, 3, 2), rows):
         copy.wait_recv()
         src = OG.at[p.pos("z", -j), c]
         last.append(k.send(src, src, sib))
@@ -616,17 +692,14 @@
         copy.wait_recv()
     for copy in keep:
         copy.wait()
+    slab.wait_send()
     k.drain()
 
-    @pl.when(jnp.logical_not(own_slab))
-    def _():
-        slab.wait_send()
-
 
 VMEM = pl.BlockSpec(memory_space=pltpu.VMEM)
 
 
-def front(x, wq, wo, wg, wd, og, segc, segq, cos, sin, qgain, kgain):
+def front(*args):
     hbm = [
         sds((2, 4, 2, 4, 2, 16, QD), BF16),
         sds((2, 4, 2, 8, 16, 2 * FS), BF16),
@@ -639,9 +712,19 @@
         sds((TOK, QD), BF16),
         sds((TOK, D), F32),
         sds((TOK, D), BF16),
+        sds((16, 2048), BF16),
+        sds((2, SEQ, 128), F32),
+        sds((2, HEAD, TOK), F32),
+        sds((8, D), F32),
+        sds((2 * HEAD, 128), F32),
     ]
-    vmem = [sds((8, D), F32)]
     scratch = [
+        pltpu.VMEM((16, 2048), BF16),
+        pltpu.VMEM((80, 1024), BF16),
+        pltpu.VMEM((TOK, D), BF16),
+        pltpu.VMEM((8, D), F32),
+        pltpu.VMEM((2, HEAD, TOK), F32),
+        pltpu.VMEM((2 * HEAD, 128), F32),
         pltpu.VMEM((4, 2, TOK, D), BF16),
         pltpu.VMEM((4, 2, TOK, D), BF16),
         pltpu.VMEM((2, 4, 2, 8, 16, 256), BF16),
@@ -658,27 +741,28 @@
         pltpu.VMEM((2, SEQ, 128), F32),
         pltpu.VMEM((KV_HEADS, 2, 128, 256), BF16),
         pltpu.VMEM((KV_HEADS, 2, HEAD, 256), F32),
-        pltpu.SemaphoreType.DMA((170,)),
-        pltpu.SemaphoreType.DMA((170,)),
+        pltpu.SemaphoreType.DMA((80,)),
+        pltpu.SemaphoreType.DMA((126,)),
+        pltpu.SemaphoreType.DMA((26,)),
     ]
     return pl.pallas_call(
         front_body,
-        out_shape=hbm + vmem,
-        in_specs=[ANY] * 6 + [VMEM] * 6,
-        out_specs=[ANY] * len(hbm) + [VMEM] * len(vmem),
+        out_shape=hbm,
+        in_specs=[ANY, VMEM, VMEM, ANY, VMEM, ANY] + [VMEM] * 6,
+        out_specs=[ANY] * len(hbm),
         scratch_shapes=scratch,
         name="front",
         compiler_params=pltpu.CompilerParams(
             collective_id=0, has_side_effects=True, vmem_limit_bytes=56 << 20
         ),
-    )(x, wq, wo, wg, wd, og, segc, segq, cos, sin, qgain, kgain)
+    )(*args)
 
 
 def ffn_body(n2, OG, WG, WD, wq, d_out, mix_out, dwg_out, dwd_out, WQ, *scr):
     (rows, ogs, wgs, wd80, wds, dgu, inn, din, part, mixs, r0, s0, r1, m0, dwg, dwd32, dwd) = scr[:17]
-    (dn, ssem, rsem, lsem, wsem, vsem) = scr[17:]
+    (dn, wqv, ssem, rsem, lsem, wsem, vsem, wlsem) = scr[17:]
     p = Place()
-    k = Links(wsem, vsem)
+    k = Links(wsem, vsem, wlsem)
     yh, x, yl, z, c = p.yh, p.x, p.yl, p.z, p.c
     sib = p.step("c", 1)
     greet([p.step(a, j) for a in "xyz" for j in (1, 2, 3)] + [sib])
@@ -702,7 +786,7 @@
         return WQ.at[(*at, EVERY, pl.ds(half * 1024, 1024))]
 
     whole = (EVERY, EVERY, EVERY, EVERY, c)
-    own_wq = k.local(wq, WQ.at[yh, x, yl, z, c])
+    get_wq = k.local(wq, wqv)
     q1 = [k.plan(wq, WQ.at[yh, x, yl, z, c], p.step("z", j)) for j in (1, 2, 3)]
     q2, q3 = [], []
     for j in (1, 2, 3):
@@ -741,7 +825,8 @@
     own.wait()
     get_wg.wait()
     get_og.wait()
-    own_wq.wait()
+    get_wq.wait()
+    own_wq = k.local(wqv, WQ.at[yh, x, yl, z, c])
 
     @pl.loop(0, 4)
     def _(j):
@@ -798,6 +883,7 @@
 
         @pl.when(j == 0)
         def _():
+            own_wq.wait()
             for copy in q1:
                 copy.wait_recv()
             for copy in q2:
@@ -900,11 +986,13 @@
         pltpu.VMEM((FS, D), F32),
         pltpu.VMEM((2, 4, 2, 80, 1024), BF16),
         pltpu.VMEM((TOK, D), F32),
+        pltpu.VMEM((16, 2048), BF16),
         pltpu.SemaphoreType.DMA((20,)),
         pltpu.SemaphoreType.DMA((20,)),
         pltpu.SemaphoreType.DMA((8,)),
-        pltpu.SemaphoreType.DMA((20,)),
-        pltpu.SemaphoreType.DMA((20,)),
+        pltpu.SemaphoreType.DMA((16,)),
+        pltpu.SemaphoreType.DMA((16,)),
+        pltpu.SemaphoreType.DMA((1,)),
     ]
     return pl.pallas_call(
         ffn_body,
@@ -921,19 +1009,20 @@
 
 def back_body(*refs):
     (DN, X_IN, OG_IN, RESID, ATT, PT, LSE, WQ, WO, KV, mix_part, dwg, dwd, NA) = refs[:14]
-    (gains, segc, segq, cos_ref, sin_ref, qgain, kgain) = refs[14:21]
-    (IN_GRAD, MIXED, GWG, GWD, GQ, GO, SMALL) = refs[21:28]
-    (dn, xv, ogv, resid, pt, lse, in_grad, mixed, kvs, bias, qts, qns, dts, dns, dqt, dpt, datt, dres) = refs[28:46]
-    (kpart, k0, k1, ks1, k2, kres, w2, wo2, low2, att2, do, dp, dpm, na2, dqm, mix1) = refs[46:62]
+    (BIAS, ROPE, GAINS, QKGAIN) = refs[14:18]
+    (IN_GRAD, MIXED, GWG, GWD, GQ, GO, SMALL) = refs[18:25]
+    (dn, xv, ogv, resid, pt, lse, in_grad, mixed, kvs, bias, qts, qns, dts, dns, dqt, dpt, datt, dres) = refs[25:43]
+    (kpart, k0, k1, ks1, k2, kres, w2, wo2, low2, att2, do, dp, dpm, na2, dqm, mix1) = refs[43:59]
+    (rope, gains, qkgain) = refs[59:62]
     scr = list(refs[62:])
     parts = []
     for shapes in PLANE_SHAPES + O_SHAPES:
         n = 2 * len(shapes)
         parts.append(scr[:n])
         scr = scr[n:]
-    vec, vrecv, ssem, rsem = scr
+    vec, vrecv, ssem, rsem, lsem = scr
     p = Place()
-    k = Links(ssem, rsem)
+    k = Links(ssem, rsem, lsem)
     yl, z, c = p.yl, p.z, p.c
     m = z * 2 + c
     sib = p.step("c", 1)
@@ -948,6 +1037,10 @@
         "lse": k.local(LSE, lse),
         "kv": k.local(KV, kvs),
         "mix": k.local(mix_part.at[z], mix1.at[3]),
+        "bias": k.local(BIAS, bias),
+        "rope": k.local(ROPE, rope),
+        "gains": k.local(GAINS, gains),
+        "qkgain": k.local(QKGAIN, qkgain),
     }
     partners = [p.step(a, j) for a in "xyz" for j in (1, 2, 3)]
     partners += [p.at(z=(z + j) % 4, c=1 - c) for j in range(4)]
@@ -965,17 +1058,18 @@
     pair_att = k.send(ATT, att2.at[1], sib)
     mixing = [k.send(mix_part.at[p.pos("z", j)], mix1.at[j - 1], p.step("z", j)) for j in (1, 2, 3)]
     get_w = [k.local(WO.at[0, t], wo2.at[t]) for t in range(2)]
-    fill_bias(bias, segc, segq, p.s * ROWS)
-    cos, sin = cos_ref[...], sin_ref[...]
-    get["pt"].wait()
+    for name in ("pt", "rope", "qkgain"):
+        get[name].wait()
+    cos, sin = rope[0], rope[1]
+    qgain, kgain = qkgain[:HEAD], qkgain[HEAD:]
 
     @pl.loop(0, KV_HEADS)
     def _(g):
-        for mm, unit in enumerate(query_units(pt, g, cos, sin, qgain[...])):
+        for mm, unit in enumerate(query_units(pt, g, cos, sin, qgain)):
             qts[g, mm] = unit.astype(BF16)
             qns[g, mm] = unit.T.astype(BF16)
 
-    for name in ("dn", "og", "resid"):
+    for name in ("dn", "og", "resid", "gains"):
         get[name].wait()
     value = resid[...]
     scale_two = rms_scale(value)
@@ -1003,6 +1097,7 @@
             dns[g, mm] = unit.T.astype(BF16)
     get["kv"].wait()
     get["lse"].wait()
+    get["bias"].wait()
 
     @pl.loop(0, 2 * KV_HEADS)
     def _(u):
@@ -1042,8 +1137,7 @@
         do[t // 4, t % 4] = dot_rows(left, right).astype(BF16).reshape(2, 4, 32, 640)
 
     outward = [staged_reduce(p, k, do, o_stages(i), parts[6 + i], 16) for i in range(3)]
-    for step in outward:
-        next(step)
+    next(outward[0])
 
     query_sum = jnp.zeros((HEAD, TOK), F32)
     for g in range(KV_HEADS):
@@ -1053,7 +1147,7 @@
             heads += list(swap(dqt[g, 0, :, cols], dqt[g, 1, :, cols]))
         for h in range(GROUP):
             at = (g * GROUP + h) * HEAD
-            d_raw, term = head_back(pt[at : at + HEAD], heads[h], cos, sin, qgain[...])
+            d_raw, term = head_back(pt[at : at + HEAD], heads[h], cos, sin, qgain)
             query_sum = query_sum + term
             dpt[at : at + HEAD] = d_raw
 
@@ -1074,7 +1168,7 @@
     for g in range(KV_HEADS):
         both = kres[:, g * 128 : (g + 1) * 128].T
         at = QD + g * HEAD
-        d_raw, term = head_back(pt[at : at + HEAD], both[:HEAD], cos, sin, kgain[...])
+        d_raw, term = head_back(pt[at : at + HEAD], both[:HEAD], cos, sin, kgain)
         key_sum = key_sum + term
         dpt[at : at + HEAD] = d_raw
         dpt[at + KD : at + KD + HEAD] = both[HEAD:]
@@ -1098,6 +1192,8 @@
     vec[0] = jnp.broadcast_to(sums, (8, 128))
     small = small_reduce(p, k, vec, vrecv)
     next(small)
+    next(outward[1])
+    next(outward[2])
     for i in (0, 1, 3):
         next(plane[i])
     own_dp.wait()
@@ -1151,20 +1247,11 @@
 
     for half in range(2):
         to_owners(parts[half][-1], GWG.at[:, pl.ds(pl.multiple_of(half * FF + m * FS, 128), FS)])
-    slabs = []
-    for half in range(2):
-        i = k.used
-        k.used += 1
-        src, dst = parts[2 + half][-1], GWD.at[:, pl.ds(half * 512, 512)]
-        slabs.append((src, dst, i))
-
-        @pl.when(own_slab)
-        def _(src=src, dst=dst, i=i):
-            pltpu.make_async_copy(src, dst, rsem.at[i]).start()
-
-        @pl.when(jnp.logical_not(own_slab))
-        def _(src=src, dst=dst, i=i):
-            slab_copy(src, dst, ssem, rsem, i, slab_from).start()
+    slabs = [
+        Slab(k, parts[2 + half][-1], GWD.at[:, pl.ds(half * 512, 512)], slab_from, own_slab) for half in range(2)
+    ]
+    for slab in slabs:
+        slab.start()
 
     get["mix"].wait()
     for copy in mixing:
@@ -1190,21 +1277,14 @@
         keep.append(k.local(total.at[pl.ds(pl.multiple_of(c * 16, 16), 16)], dst))
         last.append(k.send(total.at[pl.ds(pl.multiple_of((1 - c) * 16, 16), 16)], dst, sib))
     next(small, None)
-    SMALL[...] = vec[4]
+    keep.append(k.local(vec.at[4], SMALL))
     for copy in keep:
         copy.wait()
     for copy in last:
         copy.wait_recv()
-    for src, dst, i in slabs:
-
-        @pl.when(own_slab)
-        def _(src=src, dst=dst, i=i):
-            pltpu.make_async_copy(src, dst, rsem.at[i]).wait()
-
-        @pl.when(jnp.logical_not(own_slab))
-        def _(src=src, dst=dst, i=i):
-            slab_copy(src, dst, ssem, rsem, i, slab_from).wait()
-
+    for slab in slabs:
+        slab.wait_recv()
+        slab.wait_send()
     k.drain()
 
 
@@ -1217,7 +1297,7 @@
     return scale * (scaled - normed * inner), d_head * normed
 
 
-def back(dn, x, og, resid, att, pt, lse, WQ, WO, KV, mix, dwg, dwd, NA, gains, segc, segq, cos, sin, qgain, kgain):
+def back(*args):
     w = 2 * KD
     outs = [
         sds((TOK, D), F32),
@@ -1263,35 +1343,113 @@
         pltpu.VMEM((2, 4, 2, TOK, 256), BF16),
         pltpu.VMEM((2, 4, 2, TOK, 256), BF16),
         pltpu.VMEM((4, TOK, D), BF16),
+        pltpu.VMEM((2, HEAD, TOK), F32),
+        pltpu.VMEM((8, D), F32),
+        pltpu.VMEM((2 * HEAD, 128), F32),
     ]
     for shapes in PLANE_SHAPES + O_SHAPES:
         scratch += staged_scratch(shapes)
     scratch += [
         pltpu.VMEM((5, 8, 128), F32),
         pltpu.VMEM((4, 3, 8, 128), F32),
-        pltpu.SemaphoreType.DMA((180,)),
-        pltpu.SemaphoreType.DMA((180,)),
+        pltpu.SemaphoreType.DMA((130,)),
+        pltpu.SemaphoreType.DMA((130,)),
+        pltpu.SemaphoreType.DMA((30,)),
     ]
     return pl.pallas_call(
         back_body,
         out_shape=outs,
-        in_specs=[ANY] * 14 + [VMEM] * 7,
-        out_specs=[ANY] * 6 + [VMEM],
+        in_specs=[ANY] * 18,
+        out_specs=[ANY] * 7,
         scratch_shapes=scratch,
         name="back",
         compiler_params=pltpu.CompilerParams(
             collective_id=2, has_side_effects=True, vmem_limit_bytes=60 << 20
         ),
-    )(dn, x, og, resid, att, pt, lse, WQ, WO, KV, mix, dwg, dwd, NA, gains, segc, segq, cos, sin, qgain, kgain)
-
-
-def rope_tables(start):
-    half = HEAD // 2
-    inverse = 10000.0 ** (-jnp.arange(half, dtype=F32) / half)
-    positions = (start + jnp.arange(TOK) % ROWS).astype(F32)
-    angles = inverse[:, None] * positions[None, :]
-    angles = jnp.concatenate([angles, angles], axis=0)
-    return jnp.cos(angles), jnp.sin(angles)
+    )(*args)
+
+
+def finish_body(*refs):
+    IN_GRAD, MIXED, GWG, GWD, GQ, GO, SUMS, WG, WQ, g1, g2 = refs[:11]
+    in_out, mixed_out, Q, O, G, DOWN, ATTN, FFN, QG, KG = refs[11:21]
+    (gwg, gwd, gq, go, sums, wg, wq, q, o, g, down, attn, ffn_, qg, kg, ing, mix, sem) = refs[21:]
+    used = []
+
+    def copy(src, dst):
+        out = pltpu.make_async_copy(src, dst, sem.at[len(used)])
+        out.start()
+        used.append(out)
+        return out
+
+    rows = [copy(IN_GRAD, ing), copy(MIXED, mix)]
+    through = []
+    got = [copy(a, b) for a, b in ((GQ, gq), (WQ, wq), (GO, go), (SUMS, sums), (GWD, gwd), (GWG, gwg), (WG, wg))]
+    for one in got[:5]:
+        one.wait()
+    for one, (src, dst) in zip(rows, ((ing, in_out), (mix, mixed_out))):
+        one.wait()
+        through.append(copy(src, dst))
+    wide = gq[...].astype(F32)
+    lane = lax.broadcasted_iota(jnp.int32, (16, QKV), 1)
+    total = jnp.zeros((16, QKV), F32)
+    for i in range(8):
+        piece = jnp.concatenate([wide[:, i * 256 : (i + 1) * 256], jnp.zeros((16, QKV - 256), F32)], axis=1)
+        here = (lane >= i * 240) & (lane < (i + 1) * 240)
+        total = jnp.where(here, pltpu.roll(piece, 240 * i, 1) if i else piece, total)
+    q[...] = total
+    through.append(copy(q, Q))
+    o[...] = jnp.concatenate([go[0].astype(F32), go[1].astype(F32)], axis=1)
+    through.append(copy(o, O))
+    slab = gwd[...].astype(F32)
+    down[...] = jnp.concatenate([slab[:40], slab[40:]], axis=1)
+    through.append(copy(down, DOWN))
+    attn[...] = flat(jnp.sum(wq[...].astype(F32) * total, axis=1, keepdims=True)) / g1[...].astype(F32)
+    through.append(copy(attn, ATTN))
+    qg[...] = sums[0:1, :HEAD]
+    kg[...] = pltpu.roll(sums[...], HEAD, 1)[0:1, :HEAD]
+    through += [copy(qg, QG), copy(kg, KG)]
+    for one in got[5:]:
+        one.wait()
+    grown = gwg[...].astype(F32)
+    g[...] = grown
+    through.append(copy(g, G))
+    ffn_[...] = flat(jnp.sum(wg[...].astype(F32) * grown, axis=1, keepdims=True)) / g2[...].astype(F32)
+    through.append(copy(ffn_, FFN))
+    for one in through:
+        one.wait()
+
+
+def flat(col):
+    n = col.shape[0]
+    place = lax.broadcasted_iota(jnp.int32, (n, n), 0) == lax.broadcasted_iota(jnp.int32, (n, n), 1)
+    return jnp.sum(jnp.where(place, jnp.broadcast_to(col, (n, n)), 0.0), axis=0, keepdims=True)
+
+
+def finish(*args):
+    outs = [
+        sds((TOK, D), F32),
+        sds((TOK, D), BF16),
+        sds((16, QKV), F32),
+        sds((16, QD), F32),
+        sds((16, 2 * FF), F32),
+        sds((40, D), F32),
+        sds((1, 16), F32),
+        sds((1, 16), F32),
+        sds((1, HEAD), F32),
+        sds((1, HEAD), F32),
+    ]
+    ins = [(16, 2 * FF), (80, 1024), (16, 2048), (2, 16, 640), (8, 128), (16, 2 * FF), (16, QKV)]
+    scratch = [pltpu.VMEM(a, F32 if a == (8, 128) else BF16) for a in ins]
+    scratch += [pltpu.VMEM(a.shape, a.dtype) for a in outs[2:] + outs[:2]]
+    return pl.pallas_call(
+        finish_body,
+        out_shape=outs,
+        in_specs=[ANY] * 9 + [VMEM] * 2,
+        out_specs=[ANY] * 10,
+        scratch_shapes=scratch + [pltpu.SemaphoreType.DMA((19,))],
+        name="finish",
+        compiler_params=pltpu.CompilerParams(vmem_limit_bytes=60 << 20),
+    )(*args)
 
 
 def per_device(
@@ -1307,43 +1465,29 @@
     key_gain,
     out_grad,
 ):
-    start = lax.axis_index("seq") * ROWS
-    qgain = query_gain.astype(F32)[:, None]
-    kgain = key_gain.astype(F32)[:, None]
-    spare = jnp.stack([attn_gain, ffn_gain] + [jnp.zeros_like(attn_gain)] * 14, axis=1)
-    spare = jnp.broadcast_to(spare[:, None, :], (16, 8, 16))
-    wq_in = jnp.concatenate([w_qkv.reshape(16, 8, 240), spare], axis=2).reshape(16, 2048)
-    wd_in = jnp.concatenate([w_down[:, :1024], w_down[:, 1024:]], axis=0)
+    g1, g2, g3, g4 = [a.reshape(1, -1) for a in (attn_gain, ffn_gain, query_gain, key_gain)]
     og_in = out_grad.reshape(TOK, D)
     x_in = tokens.reshape(TOK, D)
-    segc = segment_ids.T
-    query_ids = lax.dynamic_slice_in_dim(segment_ids, start, ROWS, axis=1)
-    segq = jnp.tile(jnp.where(query_ids >= 0, query_ids, -2), (1, 2))
-    cos, sin = rope_tables(start)
-    (WO, WG, WD, OG, NA, KV, pt, lse, attended, resid, n2, gains) = front(
-        x_in, wq_in, w_out.T, w_gate_up, wd_in, og_in, segc, segq, cos, sin, qgain, kgain
+    (WO, WG, WD, OG, NA, KV, pt, lse, attended, resid, n2, wq_in, bias, rope, gain_rows, head_gains) = front(
+        x_in, w_qkv, w_out.T, w_gate_up, w_down, og_in, segment_ids, g1, g2, g3, g4, rope_parts()
     )
     d_normed, mix_part, dwg, dwd, WQ = ffn(n2, OG, WG, WD, wq_in)
-    input_grad, result, gwg, gwd, gq, go, sums = back(
+    in_grad, mixed, gwg, gwd, gq, go, sums = back(
         d_normed, x_in, og_in, resid, attended, pt, lse, WQ, WO, KV, mix_part, dwg, dwd, NA,
-        gains, segc, segq, cos, sin, qgain, kgain,
+        bias, rope, gain_rows, head_gains,
     )
-    w_qkv_grad = gq.reshape(16, 8, 256)[:, :, :240].reshape(16, QKV).astype(F32)
-    w_out_grad = jnp.concatenate([go[0], go[1]], axis=1).T.astype(F32)
-    w_gate_up_grad = gwg.astype(F32)
-    attn_sum = jnp.sum(w_qkv.astype(F32) * w_qkv_grad, axis=1) / attn_gain.astype(F32)
-    ffn_sum = jnp.sum(w_gate_up.astype(F32) * w_gate_up_grad, axis=1) / ffn_gain.astype(F32)
+    outs = finish(in_grad, mixed, gwg, gwd, gq, go, sums, w_gate_up, w_qkv, g1, g2)
     return (
-        result.reshape(MICRO, ROWS, D),
-        input_grad.reshape(MICRO, ROWS, D),
-        w_qkv_grad,
-        w_out_grad,
-        w_gate_up_grad,
-        jnp.concatenate([gwd[:40], gwd[40:]], axis=1).astype(F32),
-        attn_sum,
-        ffn_sum,
-        sums[0, :HEAD],
-        sums[0, HEAD:],
+        outs[1].reshape(MICRO, ROWS, D),
+        outs[0].reshape(MICRO, ROWS, D),
+        outs[2],
+        outs[3].T,
+        outs[4],
+        outs[5],
+        outs[6].reshape(16),
+        outs[7].reshape(16),
+        outs[8].reshape(HEAD),
+        outs[9].reshape(HEAD),
     )
 
 

time: 316 us -> 298 us (0.943)
  local copies, waits for them, and re-layouts: 14.8 us -> 0 us
  other arithmetic: 7.69 us -> 0 us
  Pallas kernels: 291 us -> 295 us
    pallas_call x2 -> x3, Pallas kernels: 220 us -> 227 us  [the longest x1 115 us: front(): pl.pallas_call(front_body, out_shape=hbm, in_specs=[ANY, VMEM, VMEM, ANY,...]
    unnamed x17 -> x0, local copies, waits for them, and re-layouts: 6.1 us -> none
where the time goes in v5:
time: 298 us; the launch traced here: 295 us
  Pallas kernels  295 us (99%)
    pallas_call x1, Pallas kernels, front(): pl.pallas_call(front_body, out_shape=hbm, in_specs=[ANY, VMEM, VMEM, ANY,...  115 us
    pallas_call x1, Pallas kernels, back(): pl.pallas_call(back_body, out_shape=outs, in_specs=[ANY] * 18, out_specs=...  108 us
    pallas_call x1, Pallas kernels, ffn(): pl.pallas_call(ffn_body, out_shape=outs, in_specs=[ANY] * 5, out_specs=[A...  67.8 us

profile of v5, /device:TPU:1, one launch (start us, length us, event | category | flops | bytes accessed | tf_op | source)
XLA Modules:
  0.0 295.4 jit_solution(3467341236648073755)
XLA Ops:
  0.6 114.7 %front.1 = (bf16[2,4,2,4,2,16,1280]{6,5,4,3,2,1,0:T(8,128)(2,1)}, bf16[2,4,2,8,16,1280]{5,4,3,2,1,0:T(8,128)(2,1)}, bf16[2,4,2,80,1024]{4,3,2,1,0:T(8,128)(2,1)}...) custom-call(bf16[128,2048]{1,0:T(8,128)(2,1)} %bitcast.14, ...), custom_call_target="tpu_custom_call" | custom-call | tf_op jit(solution)/shard_map/front/pallas_call | solution.py:748
  115.3 67.8 %ffn.1 = (f32[128,2048]{1,0:T(8,128)}, bf16[4,128,2048]{2,1,0:T(8,128)(2,1)}, bf16[2,4,2,128,1280]{4,3,2,1,0:T(8,128)(2,1)}, bf16[2,4,2,80,1024]{4,3,2,1,0:T(8,128)(2,1)}, bf16[2,4,2,4,2,16,2048]{6,5,4,3,2,1,0:T(8,128)(2,1)}) custom-call(bf16[128,2048]{1,0:T(8,128)(2,1)} %get-tuple-element.48.n2, bf16[4,2,128,2048]{3,2,1,0:T(8,128)(2,1)} %get-tuple-element.49.OG, ...), custom_call_target="tpu_custom_call" | custom-call | tf_op jit(solution)/shard_map/ffn/pallas_call | solution.py:997
  183.1 108.3 %back.1 = (f32[128,2048]{1,0:T(8,128)}, bf16[128,2048]{1,0:T(8,128)(2,1)}, bf16[16,10240]{1,0:T(8,128)(2,1)}, bf16[80,1024]{1,0:T(8,128)(2,1)}, bf16[16,2048]{1,...) custom-call(f32[128,2048]{1,0:T(8,128)} %get-tuple-element.53.refs_0_, bf16[128,2048]{1,0:T(8,128)(2,1)} %bitcast.15, ...), custom_call_target="tpu_custom_call" | custom-call | tf_op jit(solution)/shard_map/back/pallas_call | solution.py:1359
  291.4 3.8 %finish.1 = (f32[128,2048]{1,0:T(8,128)}, bf16[128,2048]{1,0:T(8,128)(2,1)}, f32[16,1920]{1,0:T(8,128)}, f32[16,1280]{1,0:T(8,128)}, f32[16,10240]{1,0:T(8,128)}...) custom-call(f32[128,2048]{1,0:T(8,128)} %get-tuple-element.69.refs_0_, ...), custom_call_target="tpu_custom_call" | custom-call | tf_op jit(solution)/shard_map/finish/pallas_call | solution.py:1444

commit v6 on v5

--- a/solution.py
+++ b/solution.py
@@ -66,6 +66,7 @@
     def plan(self, src, dst, to):
         i = self.received
         self.received += 1
+        assert i < self.recv_sems.shape[0], i
         slot = self.free["send"].pop()
         copy = pltpu.make_async_remote_copy(
             src_ref=src,
@@ -108,6 +109,41 @@
         self.links.free["local"].append(self.slot)
 
 
+def halves(ref):
+    n = ref.shape[0] // 2
+    return ref.at[pl.ds(0, n)], ref.at[pl.ds(n, n)]
+
+
+class RingGather:
+    def __init__(self, p, k, axis, block, src=None):
+        self.p, self.k, self.axis, self.block = p, k, axis, block
+        dst = block(p.pos(axis, 0))
+        src = dst if src is None else src
+        self.right = k.send(src, dst, p.step(axis, 1))
+        self.left = k.send(src, dst, p.step(axis, 3))
+
+    def from_before(self):
+        self.right.wait_recv()
+        half = halves(self.block(self.p.pos(self.axis, 3)))[0]
+        self.far_right = self.k.send(half, half, self.p.step(self.axis, 1))
+
+    def from_after(self):
+        self.left.wait_recv()
+        half = halves(self.block(self.p.pos(self.axis, 1)))[1]
+        self.far_left = self.k.send(half, half, self.p.step(self.axis, 3))
+
+    def hand_on(self):
+        self.from_before()
+        self.from_after()
+
+    def wait(self):
+        self.far_right.wait_recv()
+        self.far_left.wait_recv()
+
+    def copies(self):
+        return [self.right, self.left, self.far_right, self.far_left]
+
+
 def greet(partners):
     barrier = pltpu.get_barrier_semaphore()
     for to in partners:
@@ -142,13 +178,19 @@
 
 
 def slab_target(p):
-    to = p.at(x=p.z, y=p.c * 2 + p.yl, z=p.g // 2, c=p.g % 2)
-    return to
+    return p.at(x=(p.z + p.x) % 4, y=(p.c + p.yh) % 2 * 2 + p.yl, z=p.g // 2, c=p.g % 2)
+
+
+def slab_place(p, x=None, y=None):
+    m = p.z * 2 + p.c
+    if x is not None:
+        return (x + 4 - m % 4) % 4
+    return (y // 2 + 2 - m // 4) % 2
 
 
 def slab_source(p):
     m = p.z * 2 + p.c
-    return p.at(x=m % 4, y=(m // 4) * 2 + p.yl, z=p.x, c=p.yh)
+    return p.at(x=m % 4, y=(m // 4) * 2 + p.yl, z=slab_place(p, x=p.x), c=slab_place(p, y=p.y))
 
 
 def same(p, to):
@@ -202,7 +244,7 @@
             self.far.wait_send()
 
 
-def add_blocks(dst, own, recv, chunk):
+def add_blocks(dst, terms, chunk):
     lead, rows = dst.shape[:-2], dst.shape[-2]
     count = 1
     for n in lead:
@@ -219,9 +261,9 @@
         @pl.loop(0, rows, step=chunk)
         def _(t):
             here = (*at, pl.ds(pl.multiple_of(t, chunk), chunk))
-            total = own[here].astype(F32)
-            for j in range(3):
-                total = total + recv[(j, *here)].astype(F32)
+            total = terms[0][here].astype(F32)
+            for term in terms[1:]:
+                total = total + term[here].astype(F32)
             dst[here] = total.astype(dst.dtype)
 
 
@@ -239,12 +281,47 @@
         for copy in ring:
             copy.wait_recv()
         total = own if n == 0 else scr[2 * n + 1]
-        add_blocks(total, own if n == 0 else pick(cur, p.pos(axis, 0)), recv, chunk)
+        add_blocks(total, [own if n == 0 else pick(cur, p.pos(axis, 0))] + [recv.at[j] for j in range(3)], chunk)
         cur = total
 
 
-def staged_scratch(shapes):
+def ring_reduce(p, k, src, stages, scr, chunk):
+    own, recv, held, recv2, total = scr
+    axis, pick = stages[0]
+    before, after, far = recv.at[0], recv.at[1], recv.at[2]
+    far_a, far_b = halves(pick(src, p.pos(axis, 2)))
+    right_a, right_b = halves(pick(src, p.pos(axis, 1)))
+    left_a, left_b = halves(pick(src, p.pos(axis, 3)))
+    right, left = p.step(axis, 1), p.step(axis, 3)
+    on_right = k.send(far_a, halves(far)[0], right)
+    on_left = k.send(far_b, halves(far)[1], left)
+    get = [k.local(right_a, halves(held)[0]), k.local(left_b, halves(held)[1])]
+    mine = k.local(pick(src, p.pos(axis, 0)), own)
+    yield
+    near = [k.send(right_b, halves(before)[1], right), k.send(left_a, halves(after)[0], left)]
+    for i, (copy, to, dst) in enumerate(((on_right, right, before), (on_left, left, after))):
+        get[i].wait()
+        copy.wait_recv()
+        here = halves(held)[i]
+        add_blocks(here, [here, halves(far)[i]], chunk)
+        near.append(k.send(here, halves(dst)[i], to))
+    yield
+    mine.wait()
+    for copy in near:
+        copy.wait_recv()
+    add_blocks(own, [own, before, after], chunk)
+    axis, pick = stages[1]
+    ring = [k.send(pick(own, p.pos(axis, j)), recv2.at[j - 1], p.step(axis, j)) for j in (1, 2, 3)]
+    yield
+    for copy in ring:
+        copy.wait_recv()
+    add_blocks(total, [pick(own, p.pos(axis, 0))] + [recv2.at[j] for j in range(3)], chunk)
+
+
+def staged_scratch(shapes, held=False):
     out = [pltpu.VMEM(shapes[0], BF16), pltpu.VMEM((3, *shapes[0]), BF16)]
+    if held:
+        out.append(pltpu.VMEM(shapes[0], BF16))
     for n, shape in enumerate(shapes[1:]):
         out.append(pltpu.VMEM((3, *shape), BF16))
         out.append(pltpu.VMEM(shape, BF16))
@@ -267,16 +344,16 @@
     ]
 
 
-def wd_stages(half):
+def wd_stages(p, half):
     cols = pl.ds(half * 512, 512)
     if half == 0:
         return [
-            ("y", lambda r, i: r.at[i % 2, :, i // 2, :, cols]),
-            ("x", lambda r, i: r.at[i]),
+            ("y", lambda r, i: r.at[i % 2, :, slab_place(p, y=i), :, cols]),
+            ("x", lambda r, i: r.at[slab_place(p, x=i)]),
         ]
     return [
-        ("x", lambda r, i: r.at[:, i, :, :, cols]),
-        ("y", lambda r, i: r.at[i % 2, i // 2]),
+        ("x", lambda r, i: r.at[:, slab_place(p, x=i), :, :, cols]),
+        ("y", lambda r, i: r.at[i % 2, slab_place(p, y=i)]),
     ]
 
 
@@ -294,7 +371,7 @@
 
 
 def o_stages(part):
-    cols = pl.ds((0, 256, 512)[part], (256, 256, 128)[part])
+    cols = pl.ds(*O_PARTS[part])
     if part == 0:
         return [
             ("x", lambda r, i: r.at[:, i, :, :, :, cols]),
@@ -314,7 +391,7 @@
     ]
 
 
-O_PARTS = ((0, 256), (256, 256), (512, 128))
+O_PARTS = ((0, 256), (256, 128), (384, 256))
 PLANE_SHAPES = [
     [(4, 128, FS), (128, FS)],
     [(2, 2, 128, FS), (128, FS)],
@@ -325,8 +402,8 @@
 ]
 O_SHAPES = [
     [(2, 2, 4, 32, 256), (2, 2, 32, 256), (32, 256)],
-    [(4, 4, 32, 256), (4, 32, 256), (32, 256)],
-    [(2, 4, 2, 32, 128), (4, 32, 128), (32, 128)],
+    [(4, 4, 32, 128), (4, 32, 128), (32, 128)],
+    [(2, 4, 2, 32, 256), (4, 32, 256), (32, 256)],
 ]
 
 
@@ -451,8 +528,6 @@
     for i in range(8):
         turned = pltpu.roll(wide, (QKV - 240 * i) % QKV, 1)[:, :256]
         wq[:, i * 256 : (i + 1) * 256] = jnp.where(lane < 240, turned, rest).astype(BF16)
-    slab_rows = w_down[...].astype(F32)
-    wd[...] = jnp.concatenate([slab_rows[:, :1024], slab_rows[:, 1024:]], axis=0).astype(BF16)
     greet_plane(p, partners, slab_to, slab_from, own_slab)
 
     def spread(src_of, dst_of):
@@ -492,11 +567,7 @@
         )
         for half in range(2)
     ]
-    slab_dst = WD.at[yl, z, c]
-    slab = Slab(k, wd, slab_dst, slab_to, own_slab)
-    slab.start()
-
-    xring = {j: k.send(x_in, xs.at[z, c], p.step("z", j)) for j in (1, 3, 2)}
+    xring = RingGather(p, k, "z", lambda i: xs.at[i, c], x_in)
 
     def to_plane(blocks):
         return [k.send(b, b, p.step(axis, j)) for j in (1, 2, 3) for b, axis in blocks]
@@ -520,16 +591,11 @@
         near.wait()
         for copy in far:
             copy.wait_recv()
-
-    slab.wait_recv()
-    plane = to_plane(
-        (
-            (WG.at[yh, x, yl, :, :, lo], "x"),
-            (WG.at[yh, x, yl, :, :, hi], "y"),
-            (WD.at[yl, x, yh, :, dlo], "x"),
-            (WD.at[yl, x, yh, :, dhi], "y"),
-        ),
-    )
+    plane = to_plane(((WG.at[yh, x, yl, :, :, lo], "x"), (WG.at[yh, x, yl, :, :, hi], "y")))
+    slab_rows = w_down[...].astype(F32)
+    wd[...] = jnp.concatenate([slab_rows[:, :1024], slab_rows[:, 1024:]], axis=0).astype(BF16)
+    slab = Slab(k, wd, WD.at[yl, z, c], slab_to, own_slab)
+    slab.start()
     for copy in q2:
         copy.wait_recv()
     own_x.wait()
@@ -540,12 +606,15 @@
     gains_out[...] = dot_last(pick, wqm[:, :, :, :, :, pl.ds(128, 128)].reshape(D, 128))
     keep = [k.local(wq, WQIN), k.local(bias, BIAS), k.local(rope, ROPE), k.local(gains_out, GAINS), k.local(qkgain, QKGAIN)]
     k.settle(q0[1] + q1)
+    xring.hand_on()
+    for o in (1, 3):
+        src = xs.at[(z + o) % 4, c]
+        xcore[o] = k.send(src, src, sib)
     packs = []
-    plane2 = []
     for o in (0, 1, 3, 2):
         zz = (z + o) % 4
-        if o:
-            xring[(4 - o) % 4].wait_recv()
+        if o == 2:
+            xring.wait()
             xcore[o] = k.send(xs.at[zz, c], xs.at[zz, c], sib)
         xcore[o].wait_recv()
         rows = xs[zz].reshape(256, D).astype(F32)
@@ -567,16 +636,15 @@
                     (wo_at(2, yh, EVERY, yl, z, c), "y"),
                 ),
             )
-        if o == 3:
-            for copy in plane:
-                copy.wait_recv()
-            plane2 = to_plane(
-                (
-                    (WG.at[:, x, :, :, :, hi], "x"),
-                    (WD.at[yl, :, yh, :, dlo], "y"),
-                    (WD.at[:, x, :, :, dhi], "x"),
-                ),
-            )
+    slab.wait_recv()
+    held = WD.at[yl, slab_place(p, x=x), slab_place(p, y=p.y)]
+    plane += to_plane(((held.at[:, dlo], "x"), (held.at[:, dhi], "y")))
+    for copy in o2:
+        copy.wait_recv()
+    o3 = [
+        RingGather(p, k, "x", lambda i: wo_at(0, EVERY, i, EVERY, EVERY, c)),
+        RingGather(p, k, "y", lambda i: wo_at(1, i // 2, EVERY, i % 2, EVERY, c)),
+    ]
     keep.append(k.local(na, NA))
     k.settle(q2 + o1 + [copy for _, far in g0 for copy in far])
     own_pk.wait()
@@ -609,26 +677,18 @@
     across.wait_recv()
     src = kvs.at[:, 1 - yl, z, c]
     ring += [k.send(src, src, p.step("z", j)) for j in (1, 2, 3)]
-    for copy in o2:
+    own_kv.wait()
+    for ring4 in o3:
+        ring4.hand_on()
+    for copy in plane:
         copy.wait_recv()
-    own_kv.wait()
     k.settle(packs + plane)
-
-    def wo_third(part):
-        out = []
-        for j in (1, 2, 3):
-            if part == 0:
-                src, got = wo_at(0, EVERY, x, EVERY, EVERY, c), wo_at(0, EVERY, p.pos("x", -j), EVERY, EVERY, c)
-            elif part == 1:
-                yy = p.pos("y", -j)
-                src, got = wo_at(1, yh, EVERY, yl, EVERY, c), wo_at(1, yy // 2, EVERY, yy % 2, EVERY, c)
-            else:
-                src, got = wo_at(2, EVERY, EVERY, EVERY, z, c), wo_at(2, EVERY, EVERY, EVERY, p.pos("z", -j), c)
-            out.append((k.send(src, src, p.step("xyz"[part], j)), got))
-        return out
-
-    o3 = wo_third(0) + wo_third(1)
-    plane2 += to_plane(((WG.at[yh, :, yl, :, :, lo], "y"),))
+    plane2 = [
+        RingGather(p, k, "x", lambda i: WG.at[:, i, :, :, :, hi]),
+        RingGather(p, k, "y", lambda i: WD.at[i % 2, :, slab_place(p, y=i), :, dlo]),
+        RingGather(p, k, "x", lambda i: WD.at[:, slab_place(p, x=i), :, :, dhi]),
+        RingGather(p, k, "y", lambda i: WG.at[i // 2, :, i % 2, :, :, lo]),
+    ]
     oc = []
     for src in (
         wo_at(0, EVERY, x, EVERY, EVERY, c),
@@ -640,12 +700,12 @@
         copy.wait_recv()
     src = kvs.at[:, :, :, c]
     kvc = k.send(src, src, sib)
-    o3 += wo_third(2)
+    o3.append(RingGather(p, k, "z", lambda i: wo_at(2, EVERY, EVERY, EVERY, i, c)))
     get_og.wait()
     keep.append(k.local(ogv, OG.at[z, c]))
-    rows = [k.send(ogv, OG.at[z, c], p.step("z", j)) for j in (1, 3, 2)]
+    rows = RingGather(p, k, "z", lambda i: OG.at[i, c], ogv)
     last = [k.send(ogv, OG.at[z, c], sib)]
-    k.settle(o2 + list(xring.values()) + list(xcore.values()))
+    k.settle(o2 + xring.copies() + list(xcore.values()))
     kvc.wait_recv()
     keep.append(k.local(kvs, KV))
 
@@ -668,9 +728,15 @@
             at = (g * GROUP + 2 * t) * HEAD
             att[:, at : at + 128] = jnp.concatenate([a, b], axis=0).T.astype(BF16)
     keep += [k.local(lse, LSE), k.local(att, ATT)]
-    for copy, src in o3:
-        copy.wait_recv()
-        oc.append(k.send(src, src, sib))
+    plane2[0].hand_on()
+    plane2[1].hand_on()
+    o3[2].hand_on()
+    for axis, ring4 in zip("xyz", o3):
+        ring4.wait()
+        for j in (1, 2, 3):
+            src = ring4.block(p.pos(axis, j))
+            oc.append(k.send(src, src, sib))
+    rows.hand_on()
     for copy in oc:
         copy.wait_recv()
     keep.append(k.local(wos, WO))
@@ -681,14 +747,18 @@
         cols = pl.ds(pl.multiple_of(t * 256, 256), 256)
         resid[:, cols] = xs[z, c, :, cols].astype(F32) + dot_last(att[...], w)
 
+    plane2[2].hand_on()
+    plane2[3].hand_on()
     value = resid[...]
     n2[...] = (value * rms_scale(value) * gains_out[1:2, :]).astype(BF16)
     keep += [k.local(resid, RESID), k.local(n2, N2)]
-    for j, copy in zip((1, 3, 2), rows):
-        copy.wait_recv()
-        src = OG.at[p.pos("z", -j), c]
+    rows.wait()
+    for j in (1, 2, 3):
+        src = OG.at[p.pos("z", j), c]
         last.append(k.send(src, src, sib))
-    for copy in plane2 + last:
+    for ring4 in plane2:
+        ring4.wait()
+    for copy in last:
         copy.wait_recv()
     for copy in keep:
         copy.wait()
@@ -741,8 +811,8 @@
         pltpu.VMEM((2, SEQ, 128), F32),
         pltpu.VMEM((KV_HEADS, 2, 128, 256), BF16),
         pltpu.VMEM((KV_HEADS, 2, HEAD, 256), F32),
-        pltpu.SemaphoreType.DMA((80,)),
-        pltpu.SemaphoreType.DMA((126,)),
+        pltpu.SemaphoreType.DMA((84,)),
+        pltpu.SemaphoreType.DMA((136,)),
         pltpu.SemaphoreType.DMA((26,)),
     ]
     return pl.pallas_call(
@@ -803,10 +873,14 @@
     sent = []
     for copy in q1:
         copy.start()
-    for j in (1, 3, 2):
+    for j in (1, 3):
         copy = remote(n2, rows.at[z, c], j, p.step("z", j))
         copy.start()
         sent.append(copy)
+    half = halves(rows.at[p.pos("z", 1), c])[1], halves(rows.at[p.pos("z", 3), c])[0]
+    on_left = remote(half[0], half[0], 0, p.step("z", 3))
+    on_right = remote(half[1], half[1], 2, p.step("z", 1))
+    sent += [on_left, on_right]
     remote(n2, rows.at[z, c], 4, sib).start()
     own = local(n2, rows.at[z, c], 0)
     get_wd = local(WD, wd80, 1)
@@ -834,9 +908,20 @@
         zz = (z + o) % 4
         at = pl.ds(pl.multiple_of(zz * 256, 256), 256)
 
+        @pl.when(j == 1)
+        def _():
+            remote(n2, rows.at[z, c], 3, sib).wait_recv()
+            on_left.start()
+            remote(n2, rows.at[z, c], 1, sib).wait_recv()
+            on_right.start()
+
+        @pl.when(j == 3)
+        def _():
+            on_left.wait_recv()
+            on_right.wait_recv()
+
         @pl.when(o > 0)
         def _():
-            remote(n2, rows.at[zz, c], (4 - o) % 4, sib).wait_recv()
             remote(rows.at[zz, c], rows.at[zz, c], 4 + o, sib).start()
 
         remote(rows.at[zz, c], rows.at[zz, 1 - c], 4 + o, sib).wait_recv()
@@ -1016,8 +1101,8 @@
     (rope, gains, qkgain) = refs[59:62]
     scr = list(refs[62:])
     parts = []
-    for shapes in PLANE_SHAPES + O_SHAPES:
-        n = 2 * len(shapes)
+    for i, shapes in enumerate(PLANE_SHAPES + O_SHAPES):
+        n = 2 * len(shapes) + (i < 4)
         parts.append(scr[:n])
         scr = scr[n:]
     vec, vrecv, ssem, rsem, lsem = scr
@@ -1048,13 +1133,13 @@
     own_slab = same(p, slab_to)
     greet_plane(p, partners, slab_to, slab_from, own_slab)
     plane = [
-        staged_reduce(p, k, dwg, wg_stages(0), parts[0], 16),
-        staged_reduce(p, k, dwg, wg_stages(1), parts[1], 16),
-        staged_reduce(p, k, dwd, wd_stages(0), parts[2], 16),
-        staged_reduce(p, k, dwd, wd_stages(1), parts[3], 16),
+        ring_reduce(p, k, dwg, wg_stages(0), parts[0], 16),
+        ring_reduce(p, k, dwg, wg_stages(1), parts[1], 16),
+        ring_reduce(p, k, dwd, wd_stages(p, 0), parts[2], 16),
+        ring_reduce(p, k, dwd, wd_stages(p, 1), parts[3], 16),
     ]
-    for i in (0, 1, 3):
-        next(plane[i])
+    for step in plane:
+        next(step)
     pair_att = k.send(ATT, att2.at[1], sib)
     mixing = [k.send(mix_part.at[p.pos("z", j)], mix1.at[j - 1], p.step("z", j)) for j in (1, 2, 3)]
     get_w = [k.local(WO.at[0, t], wo2.at[t]) for t in range(2)]
@@ -1099,8 +1184,7 @@
     get["lse"].wait()
     get["bias"].wait()
 
-    @pl.loop(0, 2 * KV_HEADS)
-    def _(u):
+    def unit(u):
         g, mm = u // 2, u % 2
         kv = unit_kv(kvs, mm, g)
         score = jnp.minimum(dot(kv, qts[g, mm]), unit_bias(bias, mm))
@@ -1113,6 +1197,11 @@
         kpart[mm, :, :, :, :, cols] = d_kv.astype(BF16).reshape(2, 4, 2, ROWS, 128)
         dqt[g, mm] = dot_rows(kv, d_scores)[:HEAD] * (HEAD ** -0.5)
 
+    pl.loop(0, KV_HEADS)(unit)
+    for step in plane:
+        next(step)
+    pl.loop(KV_HEADS, 2 * KV_HEADS)(unit)
+
     core = k.send(kpart.at[:, :, :, 1 - c], k0, sib)
     core.wait_recv()
 
@@ -1161,7 +1250,8 @@
             ks1[a, b] = total.astype(BF16)
     across = k.send(ks1.at[:, 1 - yl], k2, yl_partner)
     across.wait_recv()
-    next(plane[2])
+    for step in plane:
+        next(step)
     for a in range(2):
         kres[pl.ds(a * ROWS, ROWS)] = ks1[a, yl].astype(F32) + k2[a].astype(F32)
     key_sum = jnp.zeros((HEAD, TOK), F32)
@@ -1192,10 +1282,24 @@
     vec[0] = jnp.broadcast_to(sums, (8, 128))
     small = small_reduce(p, k, vec, vrecv)
     next(small)
-    next(outward[1])
-    next(outward[2])
-    for i in (0, 1, 3):
-        next(plane[i])
+
+    last, keep = [], []
+
+    def to_owners(total, dst):
+        for dz in range(4):
+            for dc in range(2):
+                zz, cc = (z + dz) % 4, (c + dc) % 2
+                src = total.at[pl.ds(pl.multiple_of((zz * 2 + cc) * 16, 16), 16)]
+                if dz == 0 and dc == 0:
+                    keep.append(k.local(src, dst))
+                else:
+                    last.append(k.send(src, dst, p.at(z=zz, c=cc)))
+
+    def slab_home(half):
+        slab = Slab(k, parts[2 + half][-1], GWD.at[:, pl.ds(half * 512, 512)], slab_from, own_slab)
+        slab.start()
+        return slab
+
     own_dp.wait()
     for copy in members:
         copy.wait_recv()
@@ -1208,9 +1312,29 @@
     inward = [staged_reduce(p, k, dqm, q_stages(i), parts[4 + i], 16) for i in range(2)]
     for step in inward:
         next(step)
-    for step in outward:
-        next(step)
     next(small)
+    next(outward[1])
+    next(outward[2])
+    for half in range(2):
+        next(plane[half], None)
+        to_owners(parts[half][-1], GWG.at[:, pl.ds(pl.multiple_of(half * FF + m * FS, 128), FS)])
+    slabs = []
+    for half in range(2):
+        next(plane[2 + half], None)
+        slabs.append(slab_home(half))
+    get["mix"].wait()
+    for copy in mixing:
+        copy.wait_recv()
+
+    @pl.loop(0, TOK, step=16)
+    def _(t):
+        at = pl.ds(pl.multiple_of(t, 16), 16)
+        total = resid[at]
+        for j in range(4):
+            total = total + mix1[j, at].astype(F32)
+        mixed[at] = total.astype(BF16)
+
+    keep.append(k.local(mixed, MIXED))
     for t in range(8):
         get_q[t].wait()
         w = w2[t % 2].reshape(256, 2048)
@@ -1218,7 +1342,6 @@
         in_grad[:, t * 256 : (t + 1) * 256] = dot_last(left, w)
         if t < 6:
             get_q.append(k.local(WQ.at[(t + 2) // 4, (t + 2) % 4], w2.at[t % 2]))
-    next(plane[2])
     for step in inward:
         next(step)
     next(small)
@@ -1228,56 +1351,21 @@
     hidden = xv[...].astype(F32)
     scale_one = rms_scale(hidden)
     in_grad[...] = dres[...] + norm_back(in_grad[...], hidden * scale_one, scale_one, gains[0:1, :])
-    keep = [k.local(in_grad, IN_GRAD)]
-    for step in plane:
+    keep.append(k.local(in_grad, IN_GRAD))
+    next(small)
+    for half, step in enumerate(inward):
         next(step, None)
-    next(small)
-
-    last = []
-
-    def to_owners(total, dst):
-        for dz in range(4):
-            for dc in range(2):
-                zz, cc = (z + dz) % 4, (c + dc) % 2
-                src = total.at[pl.ds(pl.multiple_of((zz * 2 + cc) * 16, 16), 16)]
-                if dz == 0 and dc == 0:
-                    keep.append(k.local(src, dst))
-                else:
-                    last.append(k.send(src, dst, p.at(z=zz, c=cc)))
-
-    for half in range(2):
-        to_owners(parts[half][-1], GWG.at[:, pl.ds(pl.multiple_of(half * FF + m * FS, 128), FS)])
-    slabs = [
-        Slab(k, parts[2 + half][-1], GWD.at[:, pl.ds(half * 512, 512)], slab_from, own_slab) for half in range(2)
-    ]
-    for slab in slabs:
-        slab.start()
-
-    get["mix"].wait()
-    for copy in mixing:
-        copy.wait_recv()
-
-    @pl.loop(0, TOK, step=16)
-    def _(t):
-        at = pl.ds(pl.multiple_of(t, 16), 16)
-        total = resid[at]
-        for j in range(4):
-            total = total + mix1[j, at].astype(F32)
-        mixed[at] = total.astype(BF16)
-
-    keep.append(k.local(mixed, MIXED))
-    for step in inward:
-        next(step, None)
-    for half in range(2):
         to_owners(parts[4 + half][-1], GQ.at[:, pl.ds(pl.multiple_of(m * 256 + half * 128, 128), 128)])
+    for step in outward:
+        next(step)
+    next(small, None)
+    keep.append(k.local(vec.at[4], SMALL))
     for i, step in enumerate(outward):
         next(step, None)
         total = parts[6 + i][-1]
         dst = GO.at[c, :, pl.ds(*O_PARTS[i])]
         keep.append(k.local(total.at[pl.ds(pl.multiple_of(c * 16, 16), 16)], dst))
         last.append(k.send(total.at[pl.ds(pl.multiple_of((1 - c) * 16, 16), 16)], dst, sib))
-    next(small, None)
-    keep.append(k.local(vec.at[4], SMALL))
     for copy in keep:
         copy.wait()
     for copy in last:
@@ -1347,14 +1435,14 @@
         pltpu.VMEM((8, D), F32),
         pltpu.VMEM((2 * HEAD, 128), F32),
     ]
-    for shapes in PLANE_SHAPES + O_SHAPES:
-        scratch += staged_scratch(shapes)
+    for i, shapes in enumerate(PLANE_SHAPES + O_SHAPES):
+        scratch += staged_scratch(shapes, i < 4)
     scratch += [
         pltpu.VMEM((5, 8, 128), F32),
         pltpu.VMEM((4, 3, 8, 128), F32),
-        pltpu.SemaphoreType.DMA((130,)),
-        pltpu.SemaphoreType.DMA((130,)),
-        pltpu.SemaphoreType.DMA((30,)),
+        pltpu.SemaphoreType.DMA((150,)),
+        pltpu.SemaphoreType.DMA((150,)),
+        pltpu.SemaphoreType.DMA((36,)),
     ]
     return pl.pallas_call(
         back_body,

time: 298 us -> 269 us (0.903)
  Pallas kernels: 295 us -> 268 us
    pallas_call x1, Pallas kernels: 115 us -> 98.6 us  [front(): pl.pallas_call(front_body, out_shape=hbm, in_specs=[ANY, VMEM, VMEM, ANY,...]
    pallas_call x1, Pallas kernels: 108 us -> 101 us  [back(): pl.pallas_call(back_body, out_shape=outs, in_specs=[ANY] * 18, out_specs=...]
    pallas_call x1, Pallas kernels: 67.8 us -> 64.6 us  [ffn(): pl.pallas_call(ffn_body, out_shape=outs, in_specs=[ANY] * 5, out_specs=[A...]
where the time goes in v6:
time: 269 us
  Pallas kernels  268 us (100%)
    pallas_call x1, Pallas kernels, back(): pl.pallas_call(back_body, out_shape=outs, in_specs=[ANY] * 18, out_specs=...  101 us
    pallas_call x1, Pallas kernels, front(): pl.pallas_call(front_body, out_shape=hbm, in_specs=[ANY, VMEM, VMEM, ANY,...  98.6 us
    pallas_call x1, Pallas kernels, ffn(): pl.pallas_call(ffn_body, out_shape=outs, in_specs=[ANY] * 5, out_specs=[A...  64.6 us

profile of v6, /device:TPU:1, one launch (start us, length us, event | category | flops | bytes accessed | tf_op | source)
XLA Modules:
  0.0 269.0 jit_solution(5311210793169687931)
XLA Ops:
  0.6 98.6 %front.1 = (bf16[2,4,2,4,2,16,1280]{6,5,4,3,2,1,0:T(8,128)(2,1)}, bf16[2,4,2,8,16,1280]{5,4,3,2,1,0:T(8,128)(2,1)}, bf16[2,4,2,80,1024]{4,3,2,1,0:T(8,128)(2,1)}...) custom-call(bf16[128,2048]{1,0:T(8,128)(2,1)} %bitcast.14, ...), custom_call_target="tpu_custom_call" | custom-call | tf_op jit(solution)/shard_map/front/pallas_call | solution.py:818
  99.3 64.6 %ffn.1 = (f32[128,2048]{1,0:T(8,128)}, bf16[4,128,2048]{2,1,0:T(8,128)(2,1)}, bf16[2,4,2,128,1280]{4,3,2,1,0:T(8,128)(2,1)}, bf16[2,4,2,80,1024]{4,3,2,1,0:T(8,128)(2,1)}, bf16[2,4,2,4,2,16,2048]{6,5,4,3,2,1,0:T(8,128)(2,1)}) custom-call(bf16[128,2048]{1,0:T(8,128)(2,1)} %get-tuple-element.48.n2, bf16[4,2,128,2048]{3,2,1,0:T(8,128)(2,1)} %get-tuple-element.49.OG, ...), custom_call_target="tpu_custom_call" | custom-call | tf_op jit(solution)/shard_map/ffn/pallas_call | solution.py:1082
  163.9 101.1 %back.1 = (f32[128,2048]{1,0:T(8,128)}, bf16[128,2048]{1,0:T(8,128)(2,1)}, bf16[16,10240]{1,0:T(8,128)(2,1)}, bf16[80,1024]{1,0:T(8,128)(2,1)}, bf16[16,2048]{1,...) custom-call(f32[128,2048]{1,0:T(8,128)} %get-tuple-element.53.refs_0_, bf16[128,2048]{1,0:T(8,128)(2,1)} %bitcast.15, ...), custom_call_target="tpu_custom_call" | custom-call | tf_op jit(solution)/shard_map/back/pallas_call | solution.py:1447
  265.0 3.8 %finish.1 = (f32[128,2048]{1,0:T(8,128)}, bf16[128,2048]{1,0:T(8,128)(2,1)}, f32[16,1920]{1,0:T(8,128)}, f32[16,1280]{1,0:T(8,128)}, f32[16,10240]{1,0:T(8,128)}...) custom-call(f32[128,2048]{1,0:T(8,128)} %get-tuple-element.69.refs_0_, ...), custom_call_target="tpu_custom_call" | custom-call | tf_op jit(solution)/shard_map/finish/pallas_call | solution.py:1532

commit v7 on v6

--- a/solution.py
+++ b/solution.py
@@ -299,6 +299,7 @@
     mine = k.local(pick(src, p.pos(axis, 0)), own)
     yield
     near = [k.send(right_b, halves(before)[1], right), k.send(left_a, halves(after)[0], left)]
+    yield
     for i, (copy, to, dst) in enumerate(((on_right, right, before), (on_left, left, after))):
         get[i].wait()
         copy.wait_recv()
@@ -391,7 +392,7 @@
     ]
 
 
-O_PARTS = ((0, 256), (256, 128), (384, 256))
+O_PARTS = ((0, 384), (384, 128), (512, 128))
 PLANE_SHAPES = [
     [(4, 128, FS), (128, FS)],
     [(2, 2, 128, FS), (128, FS)],
@@ -401,14 +402,14 @@
     [(2, 2, 128, 128), (128, 128)],
 ]
 O_SHAPES = [
-    [(2, 2, 4, 32, 256), (2, 2, 32, 256), (32, 256)],
+    [(2, 2, 4, 32, 384), (2, 2, 32, 384), (32, 384)],
     [(4, 4, 32, 128), (4, 32, 128), (32, 128)],
-    [(2, 4, 2, 32, 256), (4, 32, 256), (32, 256)],
+    [(2, 4, 2, 32, 128), (4, 32, 128), (32, 128)],
 ]
 
 
 def small_reduce(p, k, vec, recv):
-    for n, axis in enumerate("xyzc"):
+    for n, axis in enumerate("zyxc"):
         steps = (1,) if axis == "c" else (1, 2, 3)
         ring = [k.send(vec.at[n], recv.at[n, j - 1], p.step(axis, j)) for j in steps]
         yield
@@ -492,6 +493,9 @@
     n = row.shape[1]
     place = lax.broadcasted_iota(jnp.int32, (n, n), 0) == lax.broadcasted_iota(jnp.int32, (n, n), 1)
     return jnp.sum(jnp.where(place, jnp.broadcast_to(row, (n, n)), 0.0), axis=1, keepdims=True)
+
+
+KV_PARTS = (pl.ds(0, 384), pl.ds(384, 256))
 
 
 def unit_bias(bias, m):
@@ -551,15 +555,9 @@
     own_wo = k.local(wo, wos.at[yh, x, yl, z, c])
 
     def wo_at(part, *at):
-        return wos.at[(*at, EVERY, pl.ds((0, 512, 1024)[part], (512, 512, 256)[part]))]
-
-    def wo_own(part):
-        return wo.at[:, pl.ds((0, 512, 1024)[part], (512, 512, 256)[part])]
-
-    o1 = []
-    for j in (1, 2, 3):
-        for part, axis in ((0, "z"), (1, "z"), (2, "x")):
-            o1.append(k.send(wo_own(part), wo_at(part, yh, x, yl, z, c), p.step(axis, j)))
+        return wos.at[(*at, EVERY, pl.ds(part * 640, 640))]
+
+    o1 = [k.send(wo, wos.at[yh, x, yl, z, c], p.step("z", j)) for j in (1, 2, 3)]
     g0 = [
         spread(
             lambda i: wg.at[:, pl.ds(pl.multiple_of(half * FF + i * FS, 128), FS)],
@@ -574,7 +572,7 @@
 
     ql, qh = pl.ds(0, 128), pl.ds(128, 128)
     lo, hi = pl.ds(0, FS), pl.ds(FS, FS)
-    dlo, dhi = pl.ds(0, 512), pl.ds(512, 512)
+    dlo, dhi = pl.ds(0, 384), pl.ds(384, 640)
     q0[0].wait()
     for copy in q0[1]:
         copy.wait_recv()
@@ -633,18 +631,21 @@
                 (
                     (wo_at(0, yh, x, yl, EVERY, c), "y"),
                     (wo_at(1, yh, x, yl, EVERY, c), "x"),
-                    (wo_at(2, yh, EVERY, yl, z, c), "y"),
                 ),
             )
+        if o == 3:
+            for copy in plane:
+                copy.wait_recv()
+            plane2 = [
+                RingGather(p, k, "x", lambda i: WG.at[:, i, :, :, :, hi]),
+                RingGather(p, k, "y", lambda i: WG.at[i // 2, :, i % 2, pl.ds(0, 4), :, lo]),
+            ]
     slab.wait_recv()
     held = WD.at[yl, slab_place(p, x=x), slab_place(p, y=p.y)]
-    plane += to_plane(((held.at[:, dlo], "x"), (held.at[:, dhi], "y")))
+    plane_d = to_plane(((held.at[:, dlo], "x"), (held.at[:, dhi], "y")))
     for copy in o2:
         copy.wait_recv()
-    o3 = [
-        RingGather(p, k, "x", lambda i: wo_at(0, EVERY, i, EVERY, EVERY, c)),
-        RingGather(p, k, "y", lambda i: wo_at(1, i // 2, EVERY, i % 2, EVERY, c)),
-    ]
+    o3 = [RingGather(p, k, "x", lambda i: wo_at(0, EVERY, i, EVERY, EVERY, c))]
     keep.append(k.local(na, NA))
     k.settle(q2 + o1 + [copy for _, far in g0 for copy in far])
     own_pk.wait()
@@ -665,8 +666,10 @@
             kvl[mm, :, cols] = both[mm * ROWS : (mm + 1) * ROWS]
 
     own_kv = k.local(kvl, kvs.at[:, yl, z, c])
-    across = k.send(kvl, kvs.at[:, yl, z, c], yl_partner)
-    ring = [k.send(kvl, kvs.at[:, yl, z, c], p.step("z", j)) for j in (1, 2, 3)]
+    across, ring = [], []
+    for cols in KV_PARTS:
+        across.append(k.send(kvl.at[:, :, cols], kvs.at[:, yl, z, c, :, cols], yl_partner))
+        ring.append([k.send(kvl.at[:, :, cols], kvs.at[:, yl, z, c, :, cols], p.step("z", j)) for j in (1, 2, 3)])
     keep.append(k.local(pt, PT))
 
     @pl.loop(0, KV_HEADS)
@@ -674,43 +677,44 @@
         for mm, unit in enumerate(query_units(pt, g, cos, sin, qgain)):
             qts[g, mm] = unit.astype(BF16)
 
-    across.wait_recv()
-    src = kvs.at[:, 1 - yl, z, c]
-    ring += [k.send(src, src, p.step("z", j)) for j in (1, 2, 3)]
+    for copy, group, cols in zip(across, ring, KV_PARTS):
+        copy.wait_recv()
+        src = kvs.at[:, 1 - yl, z, c, :, cols]
+        group += [k.send(src, src, p.step("z", j)) for j in (1, 2, 3)]
+    get_og.wait()
+    keep.append(k.local(ogv, OG.at[z, c]))
+    rows = RingGather(p, k, "z", lambda i: OG.at[i, c], ogv)
+    last = [k.send(ogv, OG.at[z, c], sib)]
     own_kv.wait()
-    for ring4 in o3:
+    o3.append(RingGather(p, k, "y", lambda i: wo_at(1, i // 2, EVERY, i % 2, EVERY, c)))
+    for ring4 in plane2:
         ring4.hand_on()
-    for copy in plane:
-        copy.wait_recv()
-    k.settle(packs + plane)
-    plane2 = [
-        RingGather(p, k, "x", lambda i: WG.at[:, i, :, :, :, hi]),
-        RingGather(p, k, "y", lambda i: WD.at[i % 2, :, slab_place(p, y=i), :, dlo]),
-        RingGather(p, k, "x", lambda i: WD.at[:, slab_place(p, x=i), :, :, dhi]),
-        RingGather(p, k, "y", lambda i: WG.at[i // 2, :, i % 2, :, :, lo]),
-    ]
     oc = []
     for src in (
         wo_at(0, EVERY, x, EVERY, EVERY, c),
         wo_at(1, yh, EVERY, yl, EVERY, c),
-        wo_at(2, EVERY, EVERY, EVERY, z, c),
     ):
         oc.append(k.send(src, src, sib))
-    for copy in ring:
-        copy.wait_recv()
-    src = kvs.at[:, :, :, c]
-    kvc = k.send(src, src, sib)
-    o3.append(RingGather(p, k, "z", lambda i: wo_at(2, EVERY, EVERY, EVERY, i, c)))
-    get_og.wait()
-    keep.append(k.local(ogv, OG.at[z, c]))
-    rows = RingGather(p, k, "z", lambda i: OG.at[i, c], ogv)
-    last = [k.send(ogv, OG.at[z, c], sib)]
-    k.settle(o2 + xring.copies() + list(xcore.values()))
-    kvc.wait_recv()
-    keep.append(k.local(kvs, KV))
-
-    @pl.loop(0, 2 * KV_HEADS)
-    def _(u):
+    for copy in ring[0]:
+        copy.wait_recv()
+    src = kvs.at[:, :, :, c, :, KV_PARTS[0]]
+    kvc = [k.send(src, src, sib)]
+    o3[0].hand_on()
+    o3[1].hand_on()
+    for copy in plane_d:
+        copy.wait_recv()
+    plane2.append(RingGather(p, k, "x", lambda i: WD.at[:, slab_place(p, x=i), :, :, dhi]))
+    plane2 += [
+        RingGather(p, k, "y", lambda i: WD.at[i % 2, :, slab_place(p, y=i), :, dlo]),
+        RingGather(p, k, "y", lambda i: WG.at[i // 2, :, i % 2, pl.ds(4, 4), :, lo]),
+    ]
+    for axis, ring4 in zip("xy", o3):
+        for j in (1, 3):
+            src = ring4.block(p.pos(axis, j))
+            oc.append(k.send(src, src, sib))
+    kvc[0].wait_recv()
+
+    def unit(u):
         g, mm = u // 2, u % 2
         kv = unit_kv(kvs, mm, g)
         score = jnp.minimum(dot(kv, qts[g, mm]), unit_bias(bias, mm))
@@ -721,6 +725,20 @@
         ots[g, mm] = dot_rows(kv, probs)[HEAD:]
         lse[u] = jnp.broadcast_to(peak + jnp.log(total), (8, 256))
 
+    k.settle(packs + plane + plane_d)
+    pl.loop(0, 6)(unit)
+    for copy in ring[1]:
+        copy.wait_recv()
+    src = kvs.at[:, :, :, c, :, KV_PARTS[1]]
+    kvc.append(k.send(src, src, sib))
+    k.settle(o2 + xring.copies() + list(xcore.values()))
+    kvc[1].wait_recv()
+    keep.append(k.local(kvs, KV))
+    for axis, ring4 in zip("xy", o3):
+        ring4.wait()
+        src = ring4.block(p.pos(axis, 2))
+        oc.append(k.send(src, src, sib))
+    pl.loop(6, 2 * KV_HEADS)(unit)
     for g in range(KV_HEADS):
         for t in range(2):
             cols = slice(t * 128, (t + 1) * 128)
@@ -728,15 +746,10 @@
             at = (g * GROUP + 2 * t) * HEAD
             att[:, at : at + 128] = jnp.concatenate([a, b], axis=0).T.astype(BF16)
     keep += [k.local(lse, LSE), k.local(att, ATT)]
-    plane2[0].hand_on()
-    plane2[1].hand_on()
-    o3[2].hand_on()
-    for axis, ring4 in zip("xyz", o3):
-        ring4.wait()
-        for j in (1, 2, 3):
-            src = ring4.block(p.pos(axis, j))
-            oc.append(k.send(src, src, sib))
     rows.hand_on()
+    for j in (1, 3):
+        src = OG.at[p.pos("z", j), c]
+        last.append(k.send(src, src, sib))
     for copy in oc:
         copy.wait_recv()
     keep.append(k.local(wos, WO))
@@ -749,13 +762,13 @@
 
     plane2[2].hand_on()
     plane2[3].hand_on()
+    plane2[4].hand_on()
     value = resid[...]
     n2[...] = (value * rms_scale(value) * gains_out[1:2, :]).astype(BF16)
     keep += [k.local(resid, RESID), k.local(n2, N2)]
     rows.wait()
-    for j in (1, 2, 3):
-        src = OG.at[p.pos("z", j), c]
-        last.append(k.send(src, src, sib))
+    src = OG.at[p.pos("z", 2), c]
+    last.append(k.send(src, src, sib))
     for ring4 in plane2:
         ring4.wait()
     for copy in last:
@@ -812,7 +825,7 @@
         pltpu.VMEM((KV_HEADS, 2, 128, 256), BF16),
         pltpu.VMEM((KV_HEADS, 2, HEAD, 256), F32),
         pltpu.SemaphoreType.DMA((84,)),
-        pltpu.SemaphoreType.DMA((136,)),
+        pltpu.SemaphoreType.DMA((150,)),
         pltpu.SemaphoreType.DMA((26,)),
     ]
     return pl.pallas_call(
@@ -902,9 +915,17 @@
     get_wq.wait()
     own_wq = k.local(wqv, WQ.at[yh, x, yl, z, c])
 
+    def ring_step(j):
+        return jnp.where(j == 2, 3, jnp.where(j == 3, 2, j))
+
+    def d_inner_of(zz):
+        din[...] = dot_last(ogs[zz].reshape(256, D), wds[...])
+
+    d_inner_of(z)
+
     @pl.loop(0, 4)
     def _(j):
-        o = jnp.where(j == 2, 3, jnp.where(j == 3, 2, j))
+        o = ring_step(j)
         zz = (z + o) % 4
         at = pl.ds(pl.multiple_of(zz * 256, 256), 256)
 
@@ -926,7 +947,6 @@
 
         remote(rows.at[zz, c], rows.at[zz, 1 - c], 4 + o, sib).wait_recv()
         r = rows[zz].reshape(256, D)
-        din[...] = dot_last(ogs[zz].reshape(256, D), wds[...])
         for t in range(5):
             lo, hi = slice(t * 128, (t + 1) * 128), slice(FS + t * 128, FS + (t + 1) * 128)
             w = jnp.concatenate(
@@ -941,25 +961,18 @@
             dgu[at, lo] = (d_inner * upper * sig * (1.0 + gate * (1.0 - sig))).astype(BF16)
             dgu[at, hi] = (d_inner * active).astype(BF16)
 
-        @pl.loop(0, 8)
+        for h in range(2):
+            turned = dot_last(wgs[h].reshape(1024, 2 * FS), dgu[at]).astype(BF16)
+            for cc in range(2):
+                part[zz, cc, h * 1024 : (h + 1) * 1024] = turned[:, cc * TOK : (cc + 1) * TOK]
+
+        remote(part.at[zz, 1 - c], r0.at[zz], 8 + o, sib).start()
+        d_inner_of((z + ring_step((j + 1) % 4)) % 4)
+        remote(part.at[zz, 1 - c], r0.at[zz], 8 + o, sib).wait_recv()
+
+        @pl.loop(0, D, step=128)
         def _(t):
-            w = wgs[t // 4, t % 4].reshape(256, 2 * FS)
-            cols = pl.ds(pl.multiple_of(t * 256, 256), 256)
-            part[zz, :, :, cols] = dot_last(dgu[at], w).astype(BF16).reshape(2, TOK, 256)
-
-        remote(part.at[zz, 1 - c], r0.at[zz], 8 + o, sib).start()
-
-        @pl.loop(0, 4)
-        def _(t):
-            cols = pl.ds(pl.multiple_of(t * 512, 512), 512)
-            mixs[zz, :, :, cols] = dot(inn[at], wds[:, cols]).astype(BF16).reshape(2, TOK, 512)
-
-        remote(mixs.at[zz, 1 - c], m0.at[zz], 16 + o, sib).start()
-        remote(part.at[zz, 1 - c], r0.at[zz], 8 + o, sib).wait_recv()
-
-        @pl.loop(0, TOK, step=16)
-        def _(t):
-            here = pl.ds(pl.multiple_of(t, 16), 16)
+            here = pl.ds(pl.multiple_of(t, 128), 128)
             s0[zz, here] = (part[zz, c, here].astype(F32) + r0[zz, here].astype(F32)).astype(BF16)
 
         @pl.when(o > 0)
@@ -981,8 +994,22 @@
             for copy in q3:
                 copy.start()
 
-    for o in range(4):
-        remote(mixs.at[0, 0], m0.at[0], 16 + o, sib).wait_recv()
+    @pl.loop(0, 4)
+    def _(t):
+        cols = pl.ds(pl.multiple_of(t * 512, 512), 512)
+        mixs[:, :, :, cols] = dot(inn[...], wds[:, cols]).astype(BF16).reshape(4, 2, TOK, 512)
+
+    mix_core = remote(mixs.at[:, 1 - c], m0, 16, sib)
+    mix_core.start()
+
+    @pl.loop(0, 8)
+    def _(t):
+        cols = pl.ds(pl.multiple_of(t * 256, 256), 256)
+        left = rows[:, :, :, cols].reshape(8 * TOK, 256)
+        dwg[t // 4, t % 4] = dot_rows(left, dgu[...]).astype(BF16).reshape(2, TOK, 2 * FS)
+
+    out_wg = local(dwg, dwg_out, 5)
+    mix_core.wait_recv()
 
     @pl.loop(0, 4)
     def _(zz):
@@ -992,14 +1019,6 @@
             m0[zz, here] = (mixs[zz, c, here].astype(F32) + m0[zz, here].astype(F32)).astype(BF16)
 
     out_mix = local(m0, mix_out, 4)
-
-    @pl.loop(0, 8)
-    def _(t):
-        cols = pl.ds(pl.multiple_of(t * 256, 256), 256)
-        left = rows[:, :, :, cols].reshape(8 * TOK, 256)
-        dwg[t // 4, t % 4] = dot_rows(left, dgu[...]).astype(BF16).reshape(2, TOK, 2 * FS)
-
-    out_wg = local(dwg, dwg_out, 5)
     for copy in q3:
         copy.wait_recv()
     q4.start()
@@ -1021,13 +1040,12 @@
     for o in (1, 2, 3):
         remote(s0.at[0], r1.at[o - 1], 12 + o, sib).wait_recv()
 
-    @pl.loop(0, TOK, step=16)
-    def _(t):
-        here = pl.ds(pl.multiple_of(t, 16), 16)
+    for t in range(0, D, 128):
+        here = slice(t, t + 128)
         total = s0[z, here].astype(F32)
         for j in range(3):
             total = total + r1[j, here].astype(F32)
-        dn[here] = total
+        dn[:, here] = total.T
 
     out_dn = local(dn, d_out, 7)
     q4.wait_recv()
@@ -1037,9 +1055,9 @@
     for o in range(4):
         remote(rows.at[0, 0], rows.at[0, 0], 4 + o, sib).wait_send()
         remote(part.at[0, 0], r0.at[0], 8 + o, sib).wait_send()
-        remote(mixs.at[0, 0], m0.at[0], 16 + o, sib).wait_send()
     for o in (1, 2, 3):
         remote(s0.at[0], r1.at[o - 1], 12 + o, sib).wait_send()
+    mix_core.wait_send()
     for copy in (out_mix, out_wg, out_wd, out_dn):
         copy.wait()
 
@@ -1061,23 +1079,23 @@
         pltpu.VMEM((8 * TOK, 2 * FS), BF16),
         pltpu.VMEM((8 * TOK, FS), BF16),
         pltpu.VMEM((256, FS), F32),
+        pltpu.VMEM((4, 2, D, TOK), BF16),
         pltpu.VMEM((4, 2, TOK, D), BF16),
-        pltpu.VMEM((4, 2, TOK, D), BF16),
-        pltpu.VMEM((4, TOK, D), BF16),
-        pltpu.VMEM((4, TOK, D), BF16),
-        pltpu.VMEM((3, TOK, D), BF16),
+        pltpu.VMEM((4, D, TOK), BF16),
+        pltpu.VMEM((4, D, TOK), BF16),
+        pltpu.VMEM((3, D, TOK), BF16),
         pltpu.VMEM((4, TOK, D), BF16),
         pltpu.VMEM((2, 4, 2, TOK, 2 * FS), BF16),
         pltpu.VMEM((FS, D), F32),
         pltpu.VMEM((2, 4, 2, 80, 1024), BF16),
         pltpu.VMEM((TOK, D), F32),
         pltpu.VMEM((16, 2048), BF16),
-        pltpu.SemaphoreType.DMA((20,)),
-        pltpu.SemaphoreType.DMA((20,)),
+        pltpu.SemaphoreType.DMA((17,)),
+        pltpu.SemaphoreType.DMA((17,)),
         pltpu.SemaphoreType.DMA((8,)),
-        pltpu.SemaphoreType.DMA((16,)),
-        pltpu.SemaphoreType.DMA((16,)),
-        pltpu.SemaphoreType.DMA((1,)),
+        pltpu.SemaphoreType.DMA((24,)),
+        pltpu.SemaphoreType.DMA((24,)),
+        pltpu.SemaphoreType.DMA((4,)),
     ]
     return pl.pallas_call(
         ffn_body,
@@ -1112,21 +1130,15 @@
     m = z * 2 + c
     sib = p.step("c", 1)
     yl_partner = p.at(y=p.yh * 2 + 1 - yl)
-    get = {
-        "dn": k.local(DN, dn),
-        "x": k.local(X_IN, xv),
-        "og": k.local(OG_IN, ogv),
-        "resid": k.local(RESID, resid),
-        "att": k.local(ATT, att2.at[0]),
-        "pt": k.local(PT, pt),
-        "lse": k.local(LSE, lse),
-        "kv": k.local(KV, kvs),
-        "mix": k.local(mix_part.at[z], mix1.at[3]),
-        "bias": k.local(BIAS, bias),
-        "rope": k.local(ROPE, rope),
-        "gains": k.local(GAINS, gains),
-        "qkgain": k.local(QKGAIN, qkgain),
-    }
+    get = {}
+
+    def fetch(**pairs):
+        for name, (src, dst) in pairs.items():
+            get[name] = k.local(src, dst)
+
+    fetch(dn=(DN, dn), og=(OG_IN, ogv), resid=(RESID, resid), gains=(GAINS, gains))
+    get_w = [k.local(WO.at[t // 4, t % 4], wo2.at[t]) for t in range(8)]
+    fetch(pt=(PT, pt), rope=(ROPE, rope), qkgain=(QKGAIN, qkgain), att=(ATT, att2.at[0]))
     partners = [p.step(a, j) for a in "xyz" for j in (1, 2, 3)]
     partners += [p.at(z=(z + j) % 4, c=1 - c) for j in range(4)]
     slab_to, slab_from = slab_target(p), slab_source(p)
@@ -1138,22 +1150,15 @@
         ring_reduce(p, k, dwd, wd_stages(p, 0), parts[2], 16),
         ring_reduce(p, k, dwd, wd_stages(p, 1), parts[3], 16),
     ]
-    for step in plane:
+    for step in plane + plane:
         next(step)
     pair_att = k.send(ATT, att2.at[1], sib)
-    mixing = [k.send(mix_part.at[p.pos("z", j)], mix1.at[j - 1], p.step("z", j)) for j in (1, 2, 3)]
-    get_w = [k.local(WO.at[0, t], wo2.at[t]) for t in range(2)]
-    for name in ("pt", "rope", "qkgain"):
-        get[name].wait()
-    cos, sin = rope[0], rope[1]
-    qgain, kgain = qkgain[:HEAD], qkgain[HEAD:]
-
-    @pl.loop(0, KV_HEADS)
-    def _(g):
-        for mm, unit in enumerate(query_units(pt, g, cos, sin, qgain)):
-            qts[g, mm] = unit.astype(BF16)
-            qns[g, mm] = unit.T.astype(BF16)
-
+
+    def mix_send(part):
+        at = pl.ds((0, 80)[part], (80, 48)[part])
+        return [k.send(mix_part.at[p.pos("z", j), at], mix1.at[j - 1, at], p.step("z", j)) for j in (1, 2, 3)]
+
+    mixing = mix_send(0)
     for name in ("dn", "og", "resid", "gains"):
         get[name].wait()
     value = resid[...]
@@ -1163,12 +1168,22 @@
     dres[...] = d_resid
     low2[0] = d_resid.astype(BF16)
     pair_low = k.send(low2.at[0], low2.at[1], sib)
+    fetch(kv=(KV, kvs), lse=(LSE, lse), bias=(BIAS, bias))
+    for name in ("pt", "rope", "qkgain"):
+        get[name].wait()
+    cos, sin = rope[0], rope[1]
+    qgain, kgain = qkgain[:HEAD], qkgain[HEAD:]
+
+    @pl.loop(0, KV_HEADS)
+    def _(g):
+        for mm, unit in enumerate(query_units(pt, g, cos, sin, qgain)):
+            qts[g, mm] = unit.astype(BF16)
+            qns[g, mm] = unit.T.astype(BF16)
+
     for t in range(8):
         get_w[t].wait()
-        term = dot(low2[0, :, t * 256 : (t + 1) * 256], wo2[t % 2].reshape(256, QD))
+        term = dot(low2[0, :, t * 256 : (t + 1) * 256], wo2[t].reshape(256, QD))
         datt[...] = term if t == 0 else datt[...] + term
-        if t < 6:
-            get_w.append(k.local(WO.at[(t + 2) // 4, (t + 2) % 4], wo2.at[t % 2]))
     for g in range(KV_HEADS):
         tiles = []
         for t in range(2):
@@ -1180,6 +1195,7 @@
             unit = jnp.concatenate([none, jnp.concatenate([tiles[0][mm], tiles[1][mm]], axis=1)], axis=0)
             dts[g, mm] = unit.astype(BF16)
             dns[g, mm] = unit.T.astype(BF16)
+    fetch(x=(X_IN, xv), mix=(mix_part.at[z], mix1.at[3]))
     get["kv"].wait()
     get["lse"].wait()
     get["bias"].wait()
@@ -1197,22 +1213,33 @@
         kpart[mm, :, :, :, :, cols] = d_kv.astype(BF16).reshape(2, 4, 2, ROWS, 128)
         dqt[g, mm] = dot_rows(kv, d_scores)[:HEAD] * (HEAD ** -0.5)
 
-    pl.loop(0, KV_HEADS)(unit)
+    def core_send(cols):
+        return k.send(kpart.at[:, :, :, 1 - c, :, cols], k0.at[:, :, :, :, cols], sib)
+
+    def ring_send(core, cols):
+        core.wait_recv()
+
+        @pl.loop(0, 4)
+        def _(zz):
+            for a in range(2):
+                for b in range(2):
+                    here = (a, b, zz, EVERY, cols)
+                    both = kpart[a, b, zz, c, :, cols].astype(F32) + k0[here].astype(F32)
+                    k0[here] = both.astype(BF16)
+
+        return [
+            k.send(k0.at[:, :, p.pos("z", j), :, cols], k1.at[j - 1, :, :, :, cols], p.step("z", j))
+            for j in (1, 2, 3)
+        ]
+
+    pl.loop(0, 6)(unit)
+    core = core_send(KV_PARTS[0])
     for step in plane:
         next(step)
-    pl.loop(KV_HEADS, 2 * KV_HEADS)(unit)
-
-    core = k.send(kpart.at[:, :, :, 1 - c], k0, sib)
-    core.wait_recv()
-
-    @pl.loop(0, 4)
-    def _(zz):
-        for a in range(2):
-            for b in range(2):
-                k0[a, b, zz] = (kpart[a, b, zz, c].astype(F32) + k0[a, b, zz].astype(F32)).astype(BF16)
-
-    ring = [k.send(k0.at[:, :, p.pos("z", j)], k1.at[j - 1], p.step("z", j)) for j in (1, 2, 3)]
-
+    ring = ring_send(core, KV_PARTS[0])
+    pl.loop(6, 2 * KV_HEADS)(unit)
+    core = core_send(KV_PARTS[1])
+    ring += ring_send(core, KV_PARTS[1])
     get["att"].wait()
     pair_att.wait_recv()
     pair_low.wait_recv()
@@ -1249,9 +1276,13 @@
                 total = total + k1[j, a, b].astype(F32)
             ks1[a, b] = total.astype(BF16)
     across = k.send(ks1.at[:, 1 - yl], k2, yl_partner)
+    next(outward[1])
+    next(outward[2])
+    next(plane[0])
+    next(plane[2])
     across.wait_recv()
-    for step in plane:
-        next(step)
+    next(plane[1])
+    next(plane[3])
     for a in range(2):
         kres[pl.ds(a * ROWS, ROWS)] = ks1[a, yl].astype(F32) + k2[a].astype(F32)
     key_sum = jnp.zeros((HEAD, TOK), F32)
@@ -1267,6 +1298,30 @@
     for t in range(8):
         block = jnp.concatenate([dpt[t * 240 : (t + 1) * 240], jnp.zeros((16, TOK), F32)], axis=0)
         dp[t] = block.T.astype(BF16)
+    sums = jnp.concatenate(
+        [jnp.sum(query_sum.T, axis=0, keepdims=True), jnp.sum(key_sum.T, axis=0, keepdims=True)], axis=1
+    )
+    vec[0] = jnp.broadcast_to(sums, (8, 128))
+    small = small_reduce(p, k, vec, vrecv)
+    next(small)
+
+    last, keep = [], []
+
+    def to_owners(total, dst):
+        for dz in range(4):
+            for dc in range(2):
+                zz, cc = (z + dz) % 4, (c + dc) % 2
+                src = total.at[pl.ds(pl.multiple_of((zz * 2 + cc) * 16, 16), 16)]
+                if dz == 0 and dc == 0:
+                    keep.append(k.local(src, dst))
+                else:
+                    last.append(k.send(src, dst, p.at(z=zz, c=cc)))
+
+    def slab_home(half):
+        slab = Slab(k, parts[2 + half][-1], GWD.at[:, pl.ds(half * 512, 512)], slab_from, own_slab)
+        slab.start()
+        return slab
+
     members = []
     for dz in range(4):
         for dc in range(2):
@@ -1276,33 +1331,11 @@
                 own_dp = k.local(src, dpm.at[z, c])
             else:
                 members.append(k.send(src, dpm.at[z, c], p.at(z=zz, c=cc)))
-    sums = jnp.concatenate(
-        [jnp.sum(query_sum.T, axis=0, keepdims=True), jnp.sum(key_sum.T, axis=0, keepdims=True)], axis=1
-    )
-    vec[0] = jnp.broadcast_to(sums, (8, 128))
-    small = small_reduce(p, k, vec, vrecv)
-    next(small)
-
-    last, keep = [], []
-
-    def to_owners(total, dst):
-        for dz in range(4):
-            for dc in range(2):
-                zz, cc = (z + dz) % 4, (c + dc) % 2
-                src = total.at[pl.ds(pl.multiple_of((zz * 2 + cc) * 16, 16), 16)]
-                if dz == 0 and dc == 0:
-                    keep.append(k.local(src, dst))
-                else:
-                    last.append(k.send(src, dst, p.at(z=zz, c=cc)))
-
-    def slab_home(half):
-        slab = Slab(k, parts[2 + half][-1], GWD.at[:, pl.ds(half * 512, 512)], slab_from, own_slab)
-        slab.start()
-        return slab
-
+    mixing += mix_send(1)
     own_dp.wait()
     for copy in members:
         copy.wait_recv()
+    next(small)
     for t in range(8):
         get_n[t].wait()
         total = dot_rows(na2[t % 2].reshape(8 * TOK, 256), dpm[...].reshape(8 * TOK, 256))
@@ -1313,8 +1346,6 @@
     for step in inward:
         next(step)
     next(small)
-    next(outward[1])
-    next(outward[2])
     for half in range(2):
         next(plane[half], None)
         to_owners(parts[half][-1], GWG.at[:, pl.ds(pl.multiple_of(half * FF + m * FS, 128), FS)])
@@ -1322,6 +1353,35 @@
     for half in range(2):
         next(plane[2 + half], None)
         slabs.append(slab_home(half))
+    next(outward[0])
+    next(outward[1])
+    left = jnp.concatenate([dp[i] for i in range(8)], axis=1)
+
+    def d_normed_block(t):
+        get_q[t].wait()
+        w = w2[t % 2].reshape(256, 2048)
+        in_grad[:, t * 256 : (t + 1) * 256] = dot_last(left, w)
+        if t < 6:
+            get_q.append(k.local(WQ.at[(t + 2) // 4, (t + 2) % 4], w2.at[t % 2]))
+
+    for t in range(4):
+        d_normed_block(t)
+    for step in inward:
+        next(step)
+    next(outward[2])
+    next(small)
+    for t in range(4, 8):
+        d_normed_block(t)
+    for half, step in enumerate(inward):
+        next(step, None)
+        to_owners(parts[4 + half][-1], GQ.at[:, pl.ds(pl.multiple_of(m * 256 + half * 128, 128), 128)])
+    get["x"].wait()
+    hidden = xv[...].astype(F32)
+    scale_one = rms_scale(hidden)
+    in_grad[...] = dres[...] + norm_back(in_grad[...], hidden * scale_one, scale_one, gains[0:1, :])
+    keep.append(k.local(in_grad, IN_GRAD))
+    next(small, None)
+    keep.append(k.local(vec.at[4], SMALL))
     get["mix"].wait()
     for copy in mixing:
         copy.wait_recv()
@@ -1335,31 +1395,8 @@
         mixed[at] = total.astype(BF16)
 
     keep.append(k.local(mixed, MIXED))
-    for t in range(8):
-        get_q[t].wait()
-        w = w2[t % 2].reshape(256, 2048)
-        left = jnp.concatenate([dp[i] for i in range(8)], axis=1)
-        in_grad[:, t * 256 : (t + 1) * 256] = dot_last(left, w)
-        if t < 6:
-            get_q.append(k.local(WQ.at[(t + 2) // 4, (t + 2) % 4], w2.at[t % 2]))
-    for step in inward:
-        next(step)
-    next(small)
     for step in outward:
         next(step)
-    get["x"].wait()
-    hidden = xv[...].astype(F32)
-    scale_one = rms_scale(hidden)
-    in_grad[...] = dres[...] + norm_back(in_grad[...], hidden * scale_one, scale_one, gains[0:1, :])
-    keep.append(k.local(in_grad, IN_GRAD))
-    next(small)
-    for half, step in enumerate(inward):
-        next(step, None)
-        to_owners(parts[4 + half][-1], GQ.at[:, pl.ds(pl.multiple_of(m * 256 + half * 128, 128), 128)])
-    for step in outward:
-        next(step)
-    next(small, None)
-    keep.append(k.local(vec.at[4], SMALL))
     for i, step in enumerate(outward):
         next(step, None)
         total = parts[6 + i][-1]
@@ -1422,7 +1459,7 @@
         pltpu.VMEM((2, ROWS, w), BF16),
         pltpu.VMEM((TOK, w), F32),
         pltpu.VMEM((2, 2, 4, 2, 16, 2048), BF16),
-        pltpu.VMEM((2, 2, 4, 2, 16, QD), BF16),
+        pltpu.VMEM((8, 2, 4, 2, 16, QD), BF16),
         pltpu.VMEM((2, TOK, D), BF16),
         pltpu.VMEM((2, TOK, QD), BF16),
         pltpu.VMEM((2, 4, 2, 4, 32, 640), BF16),

time: 269 us -> 246 us (0.914)
  Pallas kernels: 268 us -> 245 us
    pallas_call x1, Pallas kernels: 101 us -> 89.4 us  [back(): pl.pallas_call(back_body, out_shape=outs, in_specs=[ANY] * 18, out_specs=...]
    pallas_call x1, Pallas kernels: 98.6 us -> 90.8 us  [front(): pl.pallas_call(front_body, out_shape=hbm, in_specs=[ANY, VMEM, VMEM, ANY,...]
    pallas_call x1, Pallas kernels: 64.6 us -> 61.1 us  [ffn(): pl.pallas_call(ffn_body, out_shape=outs, in_specs=[ANY] * 5, out_specs=[A...]
where the time goes in v7:
time: 246 us
  Pallas kernels  245 us (100%)
    pallas_call x1, Pallas kernels, front(): pl.pallas_call(front_body, out_shape=hbm, in_specs=[ANY, VMEM, VMEM, ANY,...  90.8 us
    pallas_call x1, Pallas kernels, back(): pl.pallas_call(back_body, out_shape=outs, in_specs=[ANY] * 18, out_specs=...  89.4 us
    pallas_call x1, Pallas kernels, ffn(): pl.pallas_call(ffn_body, out_shape=outs, in_specs=[ANY] * 5, out_specs=[A...  61.1 us

profile of v7, /device:TPU:1, one launch (start us, length us, event | category | flops | bytes accessed | tf_op | source)
XLA Modules:
  0.0 246.0 jit_solution(636160575831894382)
XLA Ops:
  0.6 90.8 %front.1 = (bf16[2,4,2,4,2,16,1280]{6,5,4,3,2,1,0:T(8,128)(2,1)}, bf16[2,4,2,8,16,1280]{5,4,3,2,1,0:T(8,128)(2,1)}, bf16[2,4,2,80,1024]{4,3,2,1,0:T(8,128)(2,1)}...) custom-call(bf16[128,2048]{1,0:T(8,128)(2,1)} %bitcast.14, ...), custom_call_target="tpu_custom_call" | custom-call | tf_op jit(solution)/shard_map/front/pallas_call | solution.py:831
  91.5 61.1 %ffn.1 = (f32[128,2048]{1,0:T(8,128)}, bf16[4,128,2048]{2,1,0:T(8,128)(2,1)}, bf16[2,4,2,128,1280]{4,3,2,1,0:T(8,128)(2,1)}, bf16[2,4,2,80,1024]{4,3,2,1,0:T(8,128)(2,1)}, bf16[2,4,2,4,2,16,2048]{6,5,4,3,2,1,0:T(8,128)(2,1)}) custom-call(bf16[128,2048]{1,0:T(8,128)(2,1)} %get-tuple-element.48.n2, bf16[4,2,128,2048]{3,2,1,0:T(8,128)(2,1)} %get-tuple-element.49.OG, ...), custom_call_target="tpu_custom_call" | custom-call | tf_op jit(solution)/shard_map/ffn/pallas_call | solution.py:1100
  152.6 89.4 %back.1 = (f32[128,2048]{1,0:T(8,128)}, bf16[128,2048]{1,0:T(8,128)(2,1)}, bf16[16,10240]{1,0:T(8,128)(2,1)}, bf16[80,1024]{1,0:T(8,128)(2,1)}, bf16[16,2048]{1,...) custom-call(f32[128,2048]{1,0:T(8,128)} %get-tuple-element.53.refs_0_, bf16[128,2048]{1,0:T(8,128)(2,1)} %bitcast.15, ...), custom_call_target="tpu_custom_call" | custom-call | tf_op jit(solution)/shard_map/back/pallas_call | solution.py:1484
  242.0 3.8 %finish.1 = (f32[128,2048]{1,0:T(8,128)}, bf16[128,2048]{1,0:T(8,128)(2,1)}, f32[16,1920]{1,0:T(8,128)}, f32[16,1280]{1,0:T(8,128)}, f32[16,10240]{1,0:T(8,128)}...) custom-call(f32[128,2048]{1,0:T(8,128)} %get-tuple-element.69.refs_0_, ...), custom_call_target="tpu_custom_call" | custom-call | tf_op jit(solution)/shard_map/finish/pallas_call | solution.py:1569

commit v8 on v7

--- a/solution.py
+++ b/solution.py
@@ -392,7 +392,7 @@
     ]
 
 
-O_PARTS = ((0, 384), (384, 128), (512, 128))
+O_PARTS = ((0, 256), (256, 128), (384, 256))
 PLANE_SHAPES = [
     [(4, 128, FS), (128, FS)],
     [(2, 2, 128, FS), (128, FS)],
@@ -402,9 +402,9 @@
     [(2, 2, 128, 128), (128, 128)],
 ]
 O_SHAPES = [
-    [(2, 2, 4, 32, 384), (2, 2, 32, 384), (32, 384)],
+    [(2, 2, 4, 32, 256), (2, 2, 32, 256), (32, 256)],
     [(4, 4, 32, 128), (4, 32, 128), (32, 128)],
-    [(2, 4, 2, 32, 128), (4, 32, 128), (32, 128)],
+    [(2, 4, 2, 32, 256), (4, 32, 256), (32, 256)],
 ]
 
 
@@ -922,6 +922,22 @@
         din[...] = dot_last(ogs[zz].reshape(256, D), wds[...])
 
     d_inner_of(z)
+    own_wq.wait()
+    for copy in q1:
+        copy.wait_recv()
+    for copy in q2:
+        copy.start()
+
+    top, end = pl.ds(0, D // 2), pl.ds(D // 2, D // 2)
+    right, left = p.step("z", 1), p.step("z", 3)
+    to_right, to_left, to_far = s0.at[p.pos("z", 1)], s0.at[p.pos("z", 3)], s0.at[p.pos("z", 2)]
+    near_right = remote(to_right.at[end], r1.at[0, end], 12, right)
+    near_left = remote(to_left.at[top], r1.at[1, top], 13, left)
+    far_right = remote(to_far.at[top], r1.at[2, top], 14, right)
+    far_left = remote(to_far.at[end], r1.at[2, end], 15, left)
+    sum_right = remote(to_right.at[top], r1.at[0, top], 17, right)
+    sum_left = remote(to_left.at[end], r1.at[1, end], 18, left)
+    ring_sums = [near_right, near_left, far_right, far_left, sum_right, sum_left]
 
     @pl.loop(0, 4)
     def _(j):
@@ -935,15 +951,16 @@
             on_left.start()
             remote(n2, rows.at[z, c], 1, sib).wait_recv()
             on_right.start()
-
-        @pl.when(j == 3)
+            for o_near in (1, 3):
+                near = rows.at[(z + o_near) % 4, c]
+                remote(near, near, 4 + o_near, sib).start()
+
+        @pl.when(j == 2)
         def _():
             on_left.wait_recv()
             on_right.wait_recv()
-
-        @pl.when(o > 0)
-        def _():
-            remote(rows.at[zz, c], rows.at[zz, c], 4 + o, sib).start()
+            far = rows.at[(z + 2) % 4, c]
+            remote(far, far, 4 + 2, sib).start()
 
         remote(rows.at[zz, c], rows.at[zz, 1 - c], 4 + o, sib).wait_recv()
         r = rows[zz].reshape(256, D)
@@ -975,20 +992,24 @@
             here = pl.ds(pl.multiple_of(t, 128), 128)
             s0[zz, here] = (part[zz, c, here].astype(F32) + r0[zz, here].astype(F32)).astype(BF16)
 
-        @pl.when(o > 0)
+        @pl.when(j == 1)
         def _():
-            remote(s0.at[zz], r1.at[o - 1], 12 + o, p.at(z=zz)).start()
+            near_right.start()
+
+        @pl.when(j == 2)
+        def _():
+            near_left.start()
+
+        @pl.when(j == 3)
+        def _():
+            far_right.start()
+            far_left.start()
 
         @pl.when(j == 0)
         def _():
-            own_wq.wait()
-            for copy in q1:
-                copy.wait_recv()
-            for copy in q2:
-                copy.start()
-
-        @pl.when(j == 1)
-        def _():
+            for t in range(8):
+                left = rows[z, :, :, t * 256 : (t + 1) * 256].reshape(256, D // 8)
+                dwg[t // 4, t % 4] = dot_rows(left, dgu[at]).astype(BF16).reshape(2, TOK, 2 * FS)
             for copy in q2:
                 copy.wait_recv()
             for copy in q3:
@@ -1001,24 +1022,27 @@
 
     mix_core = remote(mixs.at[:, 1 - c], m0, 16, sib)
     mix_core.start()
-
-    @pl.loop(0, 8)
-    def _(t):
+    others = [((z + o) % 4, pl.ds(pl.multiple_of((z + o) % 4 * 256, 256), 256)) for o in (1, 2, 3)]
+
+    def gate_up_block(t):
         cols = pl.ds(pl.multiple_of(t * 256, 256), 256)
-        left = rows[:, :, :, cols].reshape(8 * TOK, 256)
-        dwg[t // 4, t % 4] = dot_rows(left, dgu[...]).astype(BF16).reshape(2, TOK, 2 * FS)
-
+        total = dwg[t // 4, t % 4].reshape(256, 2 * FS).astype(F32)
+        for zz, at in others:
+            total = total + dot_rows(rows[zz, :, :, cols].reshape(256, 256), dgu[at])
+        dwg[t // 4, t % 4] = total.astype(BF16).reshape(2, TOK, 2 * FS)
+
+    pl.loop(0, 4)(gate_up_block)
+    for first, over, add, at in ((far_right, sum_right, to_right, 0), (far_left, sum_left, to_left, D // 2)):
+        first.wait_recv()
+
+        @pl.loop(0, D // 2, step=128)
+        def _(t, add=add, at=at):
+            here = pl.ds(pl.multiple_of(t + at, 128), 128)
+            add[here] = (add[here].astype(F32) + r1[2, here].astype(F32)).astype(BF16)
+
+        over.start()
+    pl.loop(4, 8)(gate_up_block)
     out_wg = local(dwg, dwg_out, 5)
-    mix_core.wait_recv()
-
-    @pl.loop(0, 4)
-    def _(zz):
-        @pl.loop(0, TOK, step=16)
-        def _(t):
-            here = pl.ds(pl.multiple_of(t, 16), 16)
-            m0[zz, here] = (mixs[zz, c, here].astype(F32) + m0[zz, here].astype(F32)).astype(BF16)
-
-    out_mix = local(m0, mix_out, 4)
     for copy in q3:
         copy.wait_recv()
     q4.start()
@@ -1037,13 +1061,22 @@
         dwd[yl, x, 1] = jnp.concatenate([lo[40:], hi[40:]], axis=0).astype(BF16)
 
     out_wd = local(dwd, dwd_out, 6)
-    for o in (1, 2, 3):
-        remote(s0.at[0], r1.at[o - 1], 12 + o, sib).wait_recv()
-
+    mix_core.wait_recv()
+
+    @pl.loop(0, 4)
+    def _(zz):
+        @pl.loop(0, TOK, step=16)
+        def _(t):
+            here = pl.ds(pl.multiple_of(t, 16), 16)
+            m0[zz, here] = (mixs[zz, c, here].astype(F32) + m0[zz, here].astype(F32)).astype(BF16)
+
+    out_mix = local(m0, mix_out, 4)
+    for copy in (near_right, near_left, sum_right, sum_left):
+        copy.wait_recv()
     for t in range(0, D, 128):
         here = slice(t, t + 128)
         total = s0[z, here].astype(F32)
-        for j in range(3):
+        for j in range(2):
             total = total + r1[j, here].astype(F32)
         dn[:, here] = total.T
 
@@ -1055,8 +1088,8 @@
     for o in range(4):
         remote(rows.at[0, 0], rows.at[0, 0], 4 + o, sib).wait_send()
         remote(part.at[0, 0], r0.at[0], 8 + o, sib).wait_send()
-    for o in (1, 2, 3):
-        remote(s0.at[0], r1.at[o - 1], 12 + o, sib).wait_send()
+    for copy in ring_sums:
+        copy.wait_send()
     mix_core.wait_send()
     for copy in (out_mix, out_wg, out_wd, out_dn):
         copy.wait()
@@ -1090,8 +1123,8 @@
         pltpu.VMEM((2, 4, 2, 80, 1024), BF16),
         pltpu.VMEM((TOK, D), F32),
         pltpu.VMEM((16, 2048), BF16),
-        pltpu.SemaphoreType.DMA((17,)),
-        pltpu.SemaphoreType.DMA((17,)),
+        pltpu.SemaphoreType.DMA((19,)),
+        pltpu.SemaphoreType.DMA((19,)),
         pltpu.SemaphoreType.DMA((8,)),
         pltpu.SemaphoreType.DMA((24,)),
         pltpu.SemaphoreType.DMA((24,)),
@@ -1277,12 +1310,9 @@
             ks1[a, b] = total.astype(BF16)
     across = k.send(ks1.at[:, 1 - yl], k2, yl_partner)
     next(outward[1])
-    next(outward[2])
     next(plane[0])
     next(plane[2])
     across.wait_recv()
-    next(plane[1])
-    next(plane[3])
     for a in range(2):
         kres[pl.ds(a * ROWS, ROWS)] = ks1[a, yl].astype(F32) + k2[a].astype(F32)
     key_sum = jnp.zeros((HEAD, TOK), F32)
@@ -1331,7 +1361,9 @@
                 own_dp = k.local(src, dpm.at[z, c])
             else:
                 members.append(k.send(src, dpm.at[z, c], p.at(z=zz, c=cc)))
-    mixing += mix_send(1)
+    next(plane[1])
+    next(plane[3])
+    next(outward[2])
     own_dp.wait()
     for copy in members:
         copy.wait_recv()
@@ -1345,6 +1377,19 @@
     inward = [staged_reduce(p, k, dqm, q_stages(i), parts[4 + i], 16) for i in range(2)]
     for step in inward:
         next(step)
+    next(outward[0])
+    next(outward[1])
+    left = jnp.concatenate([dp[i] for i in range(8)], axis=1)
+
+    def d_normed_block(t):
+        get_q[t].wait()
+        w = w2[t % 2].reshape(256, 2048)
+        in_grad[:, t * 256 : (t + 1) * 256] = dot_last(left, w)
+        if t < 6:
+            get_q.append(k.local(WQ.at[(t + 2) // 4, (t + 2) % 4], w2.at[t % 2]))
+
+    for t in range(4):
+        d_normed_block(t)
     next(small)
     for half in range(2):
         next(plane[half], None)
@@ -1353,25 +1398,15 @@
     for half in range(2):
         next(plane[2 + half], None)
         slabs.append(slab_home(half))
-    next(outward[0])
-    next(outward[1])
-    left = jnp.concatenate([dp[i] for i in range(8)], axis=1)
-
-    def d_normed_block(t):
-        get_q[t].wait()
-        w = w2[t % 2].reshape(256, 2048)
-        in_grad[:, t * 256 : (t + 1) * 256] = dot_last(left, w)
-        if t < 6:
-            get_q.append(k.local(WQ.at[(t + 2) // 4, (t + 2) % 4], w2.at[t % 2]))
-
-    for t in range(4):
-        d_normed_block(t)
+    mixing += mix_send(1)
     for step in inward:
         next(step)
-    next(outward[2])
-    next(small)
     for t in range(4, 8):
         d_normed_block(t)
+    next(small)
+    next(outward[2])
+    for step in outward:
+        next(step)
     for half, step in enumerate(inward):
         next(step, None)
         to_owners(parts[4 + half][-1], GQ.at[:, pl.ds(pl.multiple_of(m * 256 + half * 128, 128), 128)])
@@ -1395,8 +1430,6 @@
         mixed[at] = total.astype(BF16)
 
     keep.append(k.local(mixed, MIXED))
-    for step in outward:
-        next(step)
     for i, step in enumerate(outward):
         next(step, None)
         total = parts[6 + i][-1]

time: 246 us -> 239 us (0.972)
  Pallas kernels: 245 us -> 236 us
    pallas_call x1, Pallas kernels: 89.4 us -> 84 us  [back(): pl.pallas_call(back_body, out_shape=outs, in_specs=[ANY] * 18, out_specs=...]
    pallas_call x1, Pallas kernels: 61.1 us -> 57.7 us  [ffn(): pl.pallas_call(ffn_body, out_shape=outs, in_specs=[ANY] * 5, out_specs=[A...]
where the time goes in v8:
time: 239 us; the launch traced here: 237 us
  Pallas kernels  236 us (99%)
    pallas_call x1, Pallas kernels, front(): pl.pallas_call(front_body, out_shape=hbm, in_specs=[ANY, VMEM, VMEM, ANY,...  90.8 us
    pallas_call x1, Pallas kernels, back(): pl.pallas_call(back_body, out_shape=outs, in_specs=[ANY] * 18, out_specs=...  84 us
    pallas_call x1, Pallas kernels, ffn(): pl.pallas_call(ffn_body, out_shape=outs, in_specs=[ANY] * 5, out_specs=[A...  57.7 us

profile of v8, /device:TPU:1, one launch (start us, length us, event | category | flops | bytes accessed | tf_op | source)
XLA Modules:
  0.0 237.2 jit_solution(3134966804086352672)
XLA Ops:
  0.6 90.8 %front.1 = (bf16[2,4,2,4,2,16,1280]{6,5,4,3,2,1,0:T(8,128)(2,1)}, bf16[2,4,2,8,16,1280]{5,4,3,2,1,0:T(8,128)(2,1)}, bf16[2,4,2,80,1024]{4,3,2,1,0:T(8,128)(2,1)}...) custom-call(bf16[128,2048]{1,0:T(8,128)(2,1)} %bitcast.14, ...), custom_call_target="tpu_custom_call" | custom-call | tf_op jit(solution)/shard_map/front/pallas_call | solution.py:831
  91.5 57.7 %ffn.1 = (f32[128,2048]{1,0:T(8,128)}, bf16[4,128,2048]{2,1,0:T(8,128)(2,1)}, bf16[2,4,2,128,1280]{4,3,2,1,0:T(8,128)(2,1)}, bf16[2,4,2,80,1024]{4,3,2,1,0:T(8,128)(2,1)}, bf16[2,4,2,4,2,16,2048]{6,5,4,3,2,1,0:T(8,128)(2,1)}) custom-call(bf16[128,2048]{1,0:T(8,128)(2,1)} %get-tuple-element.48.n2, bf16[4,2,128,2048]{3,2,1,0:T(8,128)(2,1)} %get-tuple-element.49.OG, ...), custom_call_target="tpu_custom_call" | custom-call | tf_op jit(solution)/shard_map/ffn/pallas_call | solution.py:1133
  149.1 84.0 %back.1 = (f32[128,2048]{1,0:T(8,128)}, bf16[128,2048]{1,0:T(8,128)(2,1)}, bf16[16,10240]{1,0:T(8,128)(2,1)}, bf16[80,1024]{1,0:T(8,128)(2,1)}, bf16[16,2048]{1,...) custom-call(f32[128,2048]{1,0:T(8,128)} %get-tuple-element.53.refs_0_, bf16[128,2048]{1,0:T(8,128)(2,1)} %bitcast.15, ...), custom_call_target="tpu_custom_call" | custom-call | tf_op jit(solution)/shard_map/back/pallas_call | solution.py:1517
  233.1 3.8 %finish.1 = (f32[128,2048]{1,0:T(8,128)}, bf16[128,2048]{1,0:T(8,128)(2,1)}, f32[16,1920]{1,0:T(8,128)}, f32[16,1280]{1,0:T(8,128)}, f32[16,10240]{1,0:T(8,128)}...) custom-call(f32[128,2048]{1,0:T(8,128)} %get-tuple-element.69.refs_0_, ...), custom_call_target="tpu_custom_call" | custom-call | tf_op jit(solution)/shard_map/finish/pallas_call | solution.py:1602

commit v9 on v8

--- a/solution.py
+++ b/solution.py
@@ -197,7 +197,7 @@
     return (to[0] == p.g) & (to[1] == p.s)
 
 
-def greet_plane(p, partners, slab_to, slab_from, own_slab):
+def greet_plane(partners, slab_to, slab_from, own_slab):
     barrier = pltpu.get_barrier_semaphore()
     for to in partners:
         pl.semaphore_signal(barrier, inc=1, device_id=to, device_id_type=MESH)
@@ -206,11 +206,17 @@
     def _():
         pl.semaphore_signal(barrier, inc=1, device_id=slab_to, device_id_type=MESH)
         pl.semaphore_signal(barrier, inc=1, device_id=slab_from, device_id_type=MESH)
-        pl.semaphore_wait(barrier, len(partners) + 2)
-
-    @pl.when(own_slab)
-    def _():
-        pl.semaphore_wait(barrier, len(partners))
+
+    def wait():
+        @pl.when(jnp.logical_not(own_slab))
+        def _():
+            pl.semaphore_wait(barrier, len(partners) + 2)
+
+        @pl.when(own_slab)
+        def _():
+            pl.semaphore_wait(barrier, len(partners))
+
+    return wait
 
 
 class Slab:
@@ -317,6 +323,27 @@
     for copy in ring:
         copy.wait_recv()
     add_blocks(total, [pick(own, p.pos(axis, 0))] + [recv2.at[j] for j in range(3)], chunk)
+
+
+def mix_reduce(p, k, part, bufs, held):
+    right, left = p.step("z", 1), p.step("z", 3)
+    far_a, far_b = halves(part.at[p.pos("z", 2)])
+    right_a, right_b = halves(part.at[p.pos("z", 1)])
+    left_a, left_b = halves(part.at[p.pos("z", 3)])
+    far = halves(bufs.at[2])
+    first = [k.send(far_a, far[0], right), k.send(far_b, far[1], left)]
+    near = [k.send(right_b, halves(bufs.at[0])[1], right), k.send(left_a, halves(bufs.at[1])[0], left)]
+    get = [k.local(right_a, halves(held)[0]), k.local(left_b, halves(held)[1])]
+    yield
+    for i, to in enumerate((right, left)):
+        get[i].wait()
+        first[i].wait_recv()
+        here = halves(held)[i]
+        add_blocks(here, [here, far[i]], 16)
+        near.append(k.send(here, halves(bufs.at[i])[i], to))
+    yield
+    for copy in near:
+        copy.wait_recv()
 
 
 def staged_scratch(shapes, held=False):
@@ -525,6 +552,9 @@
     slab_to, slab_from = slab_target(p), slab_source(p)
     own_slab = same(p, slab_to)
 
+    met = greet_plane(partners, slab_to, slab_from, own_slab)
+    own_x = k.local(x_in, xs.at[z, c])
+    get_og = k.local(og, ogv)
     spare = [column(row[...].astype(F32)) for row in (g1, g2)]
     wide = w_qkv[...].astype(F32)
     lane = lax.broadcasted_iota(jnp.int32, (16, 256), 1)
@@ -532,7 +562,7 @@
     for i in range(8):
         turned = pltpu.roll(wide, (QKV - 240 * i) % QKV, 1)[:, :256]
         wq[:, i * 256 : (i + 1) * 256] = jnp.where(lane < 240, turned, rest).astype(BF16)
-    greet_plane(p, partners, slab_to, slab_from, own_slab)
+    met()
 
     def spread(src_of, dst_of):
         far, near = [], None
@@ -549,8 +579,6 @@
     q0 = spread(
         lambda i: wq.at[:, pl.ds(pl.multiple_of(i * 256, 256), 256)], lambda i: wqm.at[yh, x, yl, i]
     )
-    own_x = k.local(x_in, xs.at[z, c])
-    get_og = k.local(og, ogv)
     xcore = {0: k.send(x_in, xs.at[z, c], sib)}
     own_wo = k.local(wo, wos.at[yh, x, yl, z, c])
 
@@ -594,6 +622,10 @@
     wd[...] = jnp.concatenate([slab_rows[:, :1024], slab_rows[:, 1024:]], axis=0).astype(BF16)
     slab = Slab(k, wd, WD.at[yl, z, c], slab_to, own_slab)
     slab.start()
+    xring.hand_on()
+    for o in (1, 3):
+        src = xs.at[(z + o) % 4, c]
+        xcore[o] = k.send(src, src, sib)
     for copy in q2:
         copy.wait_recv()
     own_x.wait()
@@ -604,10 +636,6 @@
     gains_out[...] = dot_last(pick, wqm[:, :, :, :, :, pl.ds(128, 128)].reshape(D, 128))
     keep = [k.local(wq, WQIN), k.local(bias, BIAS), k.local(rope, ROPE), k.local(gains_out, GAINS), k.local(qkgain, QKGAIN)]
     k.settle(q0[1] + q1)
-    xring.hand_on()
-    for o in (1, 3):
-        src = xs.at[(z + o) % 4, c]
-        xcore[o] = k.send(src, src, sib)
     packs = []
     for o in (0, 1, 3, 2):
         zz = (z + o) % 4
@@ -824,9 +852,9 @@
         pltpu.VMEM((2, SEQ, 128), F32),
         pltpu.VMEM((KV_HEADS, 2, 128, 256), BF16),
         pltpu.VMEM((KV_HEADS, 2, HEAD, 256), F32),
-        pltpu.SemaphoreType.DMA((84,)),
-        pltpu.SemaphoreType.DMA((150,)),
-        pltpu.SemaphoreType.DMA((26,)),
+        pltpu.SemaphoreType.DMA((80,)),
+        pltpu.SemaphoreType.DMA((130,)),
+        pltpu.SemaphoreType.DMA((14,)),
     ]
     return pl.pallas_call(
         front_body,
@@ -1126,9 +1154,9 @@
         pltpu.SemaphoreType.DMA((19,)),
         pltpu.SemaphoreType.DMA((19,)),
         pltpu.SemaphoreType.DMA((8,)),
-        pltpu.SemaphoreType.DMA((24,)),
-        pltpu.SemaphoreType.DMA((24,)),
-        pltpu.SemaphoreType.DMA((4,)),
+        pltpu.SemaphoreType.DMA((16,)),
+        pltpu.SemaphoreType.DMA((16,)),
+        pltpu.SemaphoreType.DMA((1,)),
     ]
     return pl.pallas_call(
         ffn_body,
@@ -1149,8 +1177,8 @@
     (IN_GRAD, MIXED, GWG, GWD, GQ, GO, SMALL) = refs[18:25]
     (dn, xv, ogv, resid, pt, lse, in_grad, mixed, kvs, bias, qts, qns, dts, dns, dqt, dpt, datt, dres) = refs[25:43]
     (kpart, k0, k1, ks1, k2, kres, w2, wo2, low2, att2, do, dp, dpm, na2, dqm, mix1) = refs[43:59]
-    (rope, gains, qkgain) = refs[59:62]
-    scr = list(refs[62:])
+    (rope, gains, qkgain, mix_held) = refs[59:63]
+    scr = list(refs[63:])
     parts = []
     for i, shapes in enumerate(PLANE_SHAPES + O_SHAPES):
         n = 2 * len(shapes) + (i < 4)
@@ -1163,20 +1191,21 @@
     m = z * 2 + c
     sib = p.step("c", 1)
     yl_partner = p.at(y=p.yh * 2 + 1 - yl)
-    get = {}
-
-    def fetch(**pairs):
-        for name, (src, dst) in pairs.items():
-            get[name] = k.local(src, dst)
-
-    fetch(dn=(DN, dn), og=(OG_IN, ogv), resid=(RESID, resid), gains=(GAINS, gains))
-    get_w = [k.local(WO.at[t // 4, t % 4], wo2.at[t]) for t in range(8)]
-    fetch(pt=(PT, pt), rope=(ROPE, rope), qkgain=(QKGAIN, qkgain), att=(ATT, att2.at[0]))
     partners = [p.step(a, j) for a in "xyz" for j in (1, 2, 3)]
     partners += [p.at(z=(z + j) % 4, c=1 - c) for j in range(4)]
     slab_to, slab_from = slab_target(p), slab_source(p)
     own_slab = same(p, slab_to)
-    greet_plane(p, partners, slab_to, slab_from, own_slab)
+    met = greet_plane(partners, slab_to, slab_from, own_slab)
+    get = {}
+
+    def fetch(**pairs):
+        for name, (src, dst) in pairs.items():
+            get[name] = k.local(src, dst)
+
+    fetch(dn=(DN, dn), og=(OG_IN, ogv), resid=(RESID, resid), gains=(GAINS, gains))
+    get_w = [k.local(WO.at[t // 4, t % 4], wo2.at[t]) for t in range(8)]
+    fetch(pt=(PT, pt), rope=(ROPE, rope), qkgain=(QKGAIN, qkgain), att=(ATT, att2.at[0]))
+    met()
     plane = [
         ring_reduce(p, k, dwg, wg_stages(0), parts[0], 16),
         ring_reduce(p, k, dwg, wg_stages(1), parts[1], 16),
@@ -1187,11 +1216,8 @@
         next(step)
     pair_att = k.send(ATT, att2.at[1], sib)
 
-    def mix_send(part):
-        at = pl.ds((0, 80)[part], (80, 48)[part])
-        return [k.send(mix_part.at[p.pos("z", j), at], mix1.at[j - 1, at], p.step("z", j)) for j in (1, 2, 3)]
-
-    mixing = mix_send(0)
+    mixing = mix_reduce(p, k, mix_part, mix1, mix_held)
+    next(mixing)
     for name in ("dn", "og", "resid", "gains"):
         get[name].wait()
     value = resid[...]
@@ -1270,9 +1296,11 @@
     for step in plane:
         next(step)
     ring = ring_send(core, KV_PARTS[0])
+    early = [copy for copy, _ in k.sent.values()]
     pl.loop(6, 2 * KV_HEADS)(unit)
     core = core_send(KV_PARTS[1])
     ring += ring_send(core, KV_PARTS[1])
+    next(mixing)
     get["att"].wait()
     pair_att.wait_recv()
     pair_low.wait_recv()
@@ -1361,9 +1389,10 @@
                 own_dp = k.local(src, dpm.at[z, c])
             else:
                 members.append(k.send(src, dpm.at[z, c], p.at(z=zz, c=cc)))
+    next(outward[2])
     next(plane[1])
     next(plane[3])
-    next(outward[2])
+    k.settle(early)
     own_dp.wait()
     for copy in members:
         copy.wait_recv()
@@ -1377,20 +1406,20 @@
     inward = [staged_reduce(p, k, dqm, q_stages(i), parts[4 + i], 16) for i in range(2)]
     for step in inward:
         next(step)
+    get["mix"].wait()
+    next(mixing, None)
+
+    @pl.loop(0, TOK, step=16)
+    def _(t):
+        at = pl.ds(pl.multiple_of(t, 16), 16)
+        total = resid[at]
+        for j in (3, 0, 1):
+            total = total + mix1[j, at].astype(F32)
+        mixed[at] = total.astype(BF16)
+
+    keep.append(k.local(mixed, MIXED))
     next(outward[0])
     next(outward[1])
-    left = jnp.concatenate([dp[i] for i in range(8)], axis=1)
-
-    def d_normed_block(t):
-        get_q[t].wait()
-        w = w2[t % 2].reshape(256, 2048)
-        in_grad[:, t * 256 : (t + 1) * 256] = dot_last(left, w)
-        if t < 6:
-            get_q.append(k.local(WQ.at[(t + 2) // 4, (t + 2) % 4], w2.at[t % 2]))
-
-    for t in range(4):
-        d_normed_block(t)
-    next(small)
     for half in range(2):
         next(plane[half], None)
         to_owners(parts[half][-1], GWG.at[:, pl.ds(pl.multiple_of(half * FF + m * FS, 128), FS)])
@@ -1398,13 +1427,24 @@
     for half in range(2):
         next(plane[2 + half], None)
         slabs.append(slab_home(half))
-    mixing += mix_send(1)
+    left = jnp.concatenate([dp[i] for i in range(8)], axis=1)
+
+    def d_normed_block(t):
+        get_q[t].wait()
+        w = w2[t % 2].reshape(256, 2048)
+        in_grad[:, t * 256 : (t + 1) * 256] = dot_last(left, w)
+        if t < 6:
+            get_q.append(k.local(WQ.at[(t + 2) // 4, (t + 2) % 4], w2.at[t % 2]))
+
+    for t in range(4):
+        d_normed_block(t)
+    next(small)
     for step in inward:
         next(step)
+    next(outward[2])
     for t in range(4, 8):
         d_normed_block(t)
     next(small)
-    next(outward[2])
     for step in outward:
         next(step)
     for half, step in enumerate(inward):
@@ -1417,19 +1457,6 @@
     keep.append(k.local(in_grad, IN_GRAD))
     next(small, None)
     keep.append(k.local(vec.at[4], SMALL))
-    get["mix"].wait()
-    for copy in mixing:
-        copy.wait_recv()
-
-    @pl.loop(0, TOK, step=16)
-    def _(t):
-        at = pl.ds(pl.multiple_of(t, 16), 16)
-        total = resid[at]
-        for j in range(4):
-            total = total + mix1[j, at].astype(F32)
-        mixed[at] = total.astype(BF16)
-
-    keep.append(k.local(mixed, MIXED))
     for i, step in enumerate(outward):
         next(step, None)
         total = parts[6 + i][-1]
@@ -1504,15 +1531,16 @@
         pltpu.VMEM((2, HEAD, TOK), F32),
         pltpu.VMEM((8, D), F32),
         pltpu.VMEM((2 * HEAD, 128), F32),
+        pltpu.VMEM((TOK, D), BF16),
     ]
     for i, shapes in enumerate(PLANE_SHAPES + O_SHAPES):
         scratch += staged_scratch(shapes, i < 4)
     scratch += [
         pltpu.VMEM((5, 8, 128), F32),
         pltpu.VMEM((4, 3, 8, 128), F32),
-        pltpu.SemaphoreType.DMA((150,)),
-        pltpu.SemaphoreType.DMA((150,)),
-        pltpu.SemaphoreType.DMA((36,)),
+        pltpu.SemaphoreType.DMA((108,)),
+        pltpu.SemaphoreType.DMA((142,)),
+        pltpu.SemaphoreType.DMA((30,)),
     ]
     return pl.pallas_call(
         back_body,

time: 239 us -> 236 us (0.987)
  no operation moved by 1% of the time
where the time goes in v9:
time: 236 us; the launch traced here: 235 us
  Pallas kernels  234 us (99%)
    pallas_call x1, Pallas kernels, front(): pl.pallas_call(front_body, out_shape=hbm, in_specs=[ANY, VMEM, VMEM, ANY,...  90.1 us
    pallas_call x1, Pallas kernels, back(): pl.pallas_call(back_body, out_shape=outs, in_specs=[ANY] * 18, out_specs=...  82.8 us
    pallas_call x1, Pallas kernels, ffn(): pl.pallas_call(ffn_body, out_shape=outs, in_specs=[ANY] * 5, out_specs=[A...  57.7 us

profile of v9, /device:TPU:1, one launch (start us, length us, event | category | flops | bytes accessed | tf_op | source)
XLA Modules:
  0.0 235.3 jit_solution(16430401609693103798)
XLA Ops:
  0.6 90.1 %front.1 = (bf16[2,4,2,4,2,16,1280]{6,5,4,3,2,1,0:T(8,128)(2,1)}, bf16[2,4,2,8,16,1280]{5,4,3,2,1,0:T(8,128)(2,1)}, bf16[2,4,2,80,1024]{4,3,2,1,0:T(8,128)(2,1)}...) custom-call(bf16[128,2048]{1,0:T(8,128)(2,1)} %bitcast.14, ...), custom_call_target="tpu_custom_call" | custom-call | tf_op jit(solution)/shard_map/front/pallas_call | solution.py:859
  90.7 57.7 %ffn.1 = (f32[128,2048]{1,0:T(8,128)}, bf16[4,128,2048]{2,1,0:T(8,128)(2,1)}, bf16[2,4,2,128,1280]{4,3,2,1,0:T(8,128)(2,1)}, bf16[2,4,2,80,1024]{4,3,2,1,0:T(8,128)(2,1)}, bf16[2,4,2,4,2,16,2048]{6,5,4,3,2,1,0:T(8,128)(2,1)}) custom-call(bf16[128,2048]{1,0:T(8,128)(2,1)} %get-tuple-element.48.n2, bf16[4,2,128,2048]{3,2,1,0:T(8,128)(2,1)} %get-tuple-element.49.OG, ...), custom_call_target="tpu_custom_call" | custom-call | tf_op jit(solution)/shard_map/ffn/pallas_call | solution.py:1161
  148.5 82.8 %back.1 = (f32[128,2048]{1,0:T(8,128)}, bf16[128,2048]{1,0:T(8,128)(2,1)}, bf16[16,10240]{1,0:T(8,128)(2,1)}, bf16[80,1024]{1,0:T(8,128)(2,1)}, bf16[16,2048]{1,...) custom-call(f32[128,2048]{1,0:T(8,128)} %get-tuple-element.53.refs_0_, bf16[128,2048]{1,0:T(8,128)(2,1)} %bitcast.15, ...), custom_call_target="tpu_custom_call" | custom-call | tf_op jit(solution)/shard_map/back/pallas_call | solution.py:1545
  231.3 3.8 %finish.1 = (f32[128,2048]{1,0:T(8,128)}, bf16[128,2048]{1,0:T(8,128)(2,1)}, f32[16,1920]{1,0:T(8,128)}, f32[16,1280]{1,0:T(8,128)}, f32[16,10240]{1,0:T(8,128)}...) custom-call(f32[128,2048]{1,0:T(8,128)} %get-tuple-element.69.refs_0_, ...), custom_call_target="tpu_custom_call" | custom-call | tf_op jit(solution)/shard_map/finish/pallas_call | solution.py:1630

commit v10 on v9

--- a/solution.py
+++ b/solution.py
@@ -84,6 +84,23 @@
         copy.start()
         return copy
 
+    def together(self, copies, region):
+        i = self.received
+        self.received += 1
+        slot = self.free["send"].pop()
+        for src, dst, to in copies:
+            pltpu.make_async_remote_copy(
+                src_ref=src,
+                dst_ref=dst,
+                send_sem=self.send_sems.at[slot],
+                recv_sem=self.recv_sems.at[i],
+                device_id=to,
+                device_id_type=MESH,
+            ).start()
+        group = Group(self.send_sems.at[slot], self.recv_sems.at[i], region)
+        self.sent[id(group)] = (group, slot)
+        return group
+
     def local(self, src, dst):
         slot = self.free["local"].pop()
         copy = pltpu.make_async_copy(src, dst, self.local_sems.at[slot])
@@ -98,6 +115,17 @@
 
     def drain(self):
         self.settle([copy for copy, _ in list(self.sent.values())])
+
+
+class Group:
+    def __init__(self, send_sem, recv_sem, region):
+        self.send_sem, self.recv_sem, self.region = send_sem, recv_sem, region
+
+    def wait_recv(self):
+        pltpu.make_async_copy(self.region, self.region, self.recv_sem).wait()
+
+    def wait_send(self):
+        pltpu.make_async_copy(self.region, self.region, self.send_sem).wait()
 
 
 class Local:
@@ -280,12 +308,13 @@
         recv = scr[1] if n == 0 else scr[2 * n]
         if n == 0:
             mine = k.local(pick(src, p.pos(axis, 0)), own)
-        ring = [k.send(pick(cur, p.pos(axis, j)), recv.at[j - 1], p.step(axis, j)) for j in (1, 2, 3)]
+        ring = k.together(
+            [(pick(cur, p.pos(axis, j)), recv.at[j - 1], p.step(axis, j)) for j in (1, 2, 3)], recv
+        )
         yield
         if n == 0:
             mine.wait()
-        for copy in ring:
-            copy.wait_recv()
+        ring.wait_recv()
         total = own if n == 0 else scr[2 * n + 1]
         add_blocks(total, [own if n == 0 else pick(cur, p.pos(axis, 0))] + [recv.at[j] for j in range(3)], chunk)
         cur = total
@@ -318,10 +347,9 @@
         copy.wait_recv()
     add_blocks(own, [own, before, after], chunk)
     axis, pick = stages[1]
-    ring = [k.send(pick(own, p.pos(axis, j)), recv2.at[j - 1], p.step(axis, j)) for j in (1, 2, 3)]
+    ring = k.together([(pick(own, p.pos(axis, j)), recv2.at[j - 1], p.step(axis, j)) for j in (1, 2, 3)], recv2)
     yield
-    for copy in ring:
-        copy.wait_recv()
+    ring.wait_recv()
     add_blocks(total, [pick(own, p.pos(axis, 0))] + [recv2.at[j] for j in range(3)], chunk)
 
 
@@ -438,10 +466,10 @@
 def small_reduce(p, k, vec, recv):
     for n, axis in enumerate("zyxc"):
         steps = (1,) if axis == "c" else (1, 2, 3)
-        ring = [k.send(vec.at[n], recv.at[n, j - 1], p.step(axis, j)) for j in steps]
+        here = recv.at[n, pl.ds(0, len(steps))]
+        ring = k.together([(vec.at[n], recv.at[n, j - 1], p.step(axis, j)) for j in steps], here)
         yield
-        for copy in ring:
-            copy.wait_recv()
+        ring.wait_recv()
         total = vec[n]
         for j in range(len(steps)):
             total = total + recv[n, j]
@@ -537,10 +565,10 @@
 
 def front_body(*refs):
     (x_in, w_qkv, wo, wg, w_down, og, seg, g1, g2, g3, g4, parts) = refs[:12]
-    (WO, WG, WD, OG, NA, KV, PT, LSE, ATT, RESID, N2, WQIN, BIAS, ROPE, GAINS, QKGAIN) = refs[12:28]
-    (wq, wd, ogv, gains_out, rope, qkgain) = refs[28:34]
-    (xs, na, wqm, wos, pks, pk, pt, lse, att, resid, n2, kvl, kvs, bias, qts, ots) = refs[34:50]
-    ssem, rsem, lsem = refs[50:]
+    (WO, WG, WD, OG, NA, KV, PT, PROBS, ATT, RESID, N2, WQIN, ROPE, GAINS, QKGAIN) = refs[12:27]
+    (wq, wd, ogv, gains_out, rope, qkgain) = refs[27:33]
+    (xs, na, wqm, wos, pks, pk, pt, kept, att, resid, n2, kvl, kvs, bias, qts, ots) = refs[33:49]
+    ssem, rsem, lsem = refs[49:]
     p = Place()
     k = Links(ssem, rsem, lsem)
     yh, x, yl, z, c = p.yh, p.x, p.yl, p.z, p.c
@@ -634,7 +662,7 @@
         lax.broadcasted_iota(jnp.int32, (8, 128), 0) + 112 == lax.broadcasted_iota(jnp.int32, (8, 128), 1), 1.0, 0.0
     ).astype(BF16)
     gains_out[...] = dot_last(pick, wqm[:, :, :, :, :, pl.ds(128, 128)].reshape(D, 128))
-    keep = [k.local(wq, WQIN), k.local(bias, BIAS), k.local(rope, ROPE), k.local(gains_out, GAINS), k.local(qkgain, QKGAIN)]
+    keep = [k.local(wq, WQIN), k.local(rope, ROPE), k.local(gains_out, GAINS), k.local(qkgain, QKGAIN)]
     k.settle(q0[1] + q1)
     packs = []
     for o in (0, 1, 3, 2):
@@ -751,7 +779,7 @@
         total = jnp.sum(raised, axis=0, keepdims=True)
         probs = (raised * (1.0 / total)).astype(BF16)
         ots[g, mm] = dot_rows(kv, probs)[HEAD:]
-        lse[u] = jnp.broadcast_to(peak + jnp.log(total), (8, 256))
+        kept[u] = probs
 
     k.settle(packs + plane + plane_d)
     pl.loop(0, 6)(unit)
@@ -773,7 +801,7 @@
             a, b = swap(ots[g, 0, :, cols], ots[g, 1, :, cols])
             at = (g * GROUP + 2 * t) * HEAD
             att[:, at : at + 128] = jnp.concatenate([a, b], axis=0).T.astype(BF16)
-    keep += [k.local(lse, LSE), k.local(att, ATT)]
+    keep += [k.local(kept, PROBS), k.local(att, ATT)]
     rows.hand_on()
     for j in (1, 3):
         src = OG.at[p.pos("z", j), c]
@@ -819,12 +847,11 @@
         sds((4, 2, TOK, D), BF16),
         sds((2, 2, 4, 2, ROWS, 2 * KD), BF16),
         sds((QKV, TOK), F32),
-        sds((2 * KV_HEADS, 8, 256), F32),
+        sds((2 * KV_HEADS, SEQ, 256), BF16),
         sds((TOK, QD), BF16),
         sds((TOK, D), F32),
         sds((TOK, D), BF16),
         sds((16, 2048), BF16),
-        sds((2, SEQ, 128), F32),
         sds((2, HEAD, TOK), F32),
         sds((8, D), F32),
         sds((2 * HEAD, 128), F32),
@@ -843,7 +870,7 @@
         pltpu.VMEM((4, 2, TOK, 256), BF16),
         pltpu.VMEM((8, TOK, 256), BF16),
         pltpu.VMEM((QKV, TOK), F32),
-        pltpu.VMEM((2 * KV_HEADS, 8, 256), F32),
+        pltpu.VMEM((2 * KV_HEADS, SEQ, 256), BF16),
         pltpu.VMEM((TOK, QD), BF16),
         pltpu.VMEM((TOK, D), F32),
         pltpu.VMEM((TOK, D), BF16),
@@ -1172,13 +1199,13 @@
 
 
 def back_body(*refs):
-    (DN, X_IN, OG_IN, RESID, ATT, PT, LSE, WQ, WO, KV, mix_part, dwg, dwd, NA) = refs[:14]
-    (BIAS, ROPE, GAINS, QKGAIN) = refs[14:18]
-    (IN_GRAD, MIXED, GWG, GWD, GQ, GO, SMALL) = refs[18:25]
-    (dn, xv, ogv, resid, pt, lse, in_grad, mixed, kvs, bias, qts, qns, dts, dns, dqt, dpt, datt, dres) = refs[25:43]
-    (kpart, k0, k1, ks1, k2, kres, w2, wo2, low2, att2, do, dp, dpm, na2, dqm, mix1) = refs[43:59]
-    (rope, gains, qkgain, mix_held) = refs[59:63]
-    scr = list(refs[63:])
+    (DN, X_IN, OG_IN, RESID, ATT, PT, PROBS, WQ, WO, KV, mix_part, dwg, dwd, NA) = refs[:14]
+    (ROPE, GAINS, QKGAIN) = refs[14:17]
+    (IN_GRAD, MIXED, GWG, GWD, GQ, GO, SMALL) = refs[17:24]
+    (dn, xv, ogv, resid, pt, kept, in_grad, mixed, kvs, qns, dts, dns, dqt, dpt, datt, dres) = refs[24:40]
+    (kpart, k0, k1, ks1, k2, kres, w2, wo2, low2, att2, do, dp, dpm, na2, dqm, mix1) = refs[40:56]
+    (rope, gains, qkgain, mix_held) = refs[56:60]
+    scr = list(refs[60:])
     parts = []
     for i, shapes in enumerate(PLANE_SHAPES + O_SHAPES):
         n = 2 * len(shapes) + (i < 4)
@@ -1227,7 +1254,7 @@
     dres[...] = d_resid
     low2[0] = d_resid.astype(BF16)
     pair_low = k.send(low2.at[0], low2.at[1], sib)
-    fetch(kv=(KV, kvs), lse=(LSE, lse), bias=(BIAS, bias))
+    fetch(kv=(KV, kvs), kept=(PROBS, kept))
     for name in ("pt", "rope", "qkgain"):
         get[name].wait()
     cos, sin = rope[0], rope[1]
@@ -1236,7 +1263,6 @@
     @pl.loop(0, KV_HEADS)
     def _(g):
         for mm, unit in enumerate(query_units(pt, g, cos, sin, qgain)):
-            qts[g, mm] = unit.astype(BF16)
             qns[g, mm] = unit.T.astype(BF16)
 
     for t in range(8):
@@ -1256,18 +1282,17 @@
             dns[g, mm] = unit.T.astype(BF16)
     fetch(x=(X_IN, xv), mix=(mix_part.at[z], mix1.at[3]))
     get["kv"].wait()
-    get["lse"].wait()
-    get["bias"].wait()
+    get["kept"].wait()
 
     def unit(u):
         g, mm = u // 2, u % 2
         kv = unit_kv(kvs, mm, g)
-        score = jnp.minimum(dot(kv, qts[g, mm]), unit_bias(bias, mm))
-        again = jnp.exp(score - lse[u, 0:1, :])
+        low_again = kept[u]
+        again = low_again.astype(F32)
         d_probs = dot(kv, dts[g, mm])
         inner = jnp.sum(again * d_probs, axis=0, keepdims=True)
         d_scores = (again * (d_probs - inner)).astype(BF16)
-        d_kv = dot(d_scores, qns[g, mm]) + dot(again.astype(BF16), dns[g, mm])
+        d_kv = dot(d_scores, qns[g, mm]) + dot(low_again, dns[g, mm])
         cols = pl.ds(pl.multiple_of(g * 128, 128), 128)
         kpart[mm, :, :, :, :, cols] = d_kv.astype(BF16).reshape(2, 4, 2, ROWS, 128)
         dqt[g, mm] = dot_rows(kv, d_scores)[:HEAD] * (HEAD ** -0.5)
@@ -1293,12 +1318,12 @@
 
     pl.loop(0, 6)(unit)
     core = core_send(KV_PARTS[0])
+    ring = ring_send(core, KV_PARTS[0])
+    pl.loop(6, 2 * KV_HEADS)(unit)
+    core = core_send(KV_PARTS[1])
     for step in plane:
         next(step)
-    ring = ring_send(core, KV_PARTS[0])
     early = [copy for copy, _ in k.sent.values()]
-    pl.loop(6, 2 * KV_HEADS)(unit)
-    core = core_send(KV_PARTS[1])
     ring += ring_send(core, KV_PARTS[1])
     next(mixing)
     get["att"].wait()
@@ -1366,6 +1391,7 @@
     last, keep = [], []
 
     def to_owners(total, dst):
+        far = []
         for dz in range(4):
             for dc in range(2):
                 zz, cc = (z + dz) % 4, (c + dc) % 2
@@ -1373,7 +1399,8 @@
                 if dz == 0 and dc == 0:
                     keep.append(k.local(src, dst))
                 else:
-                    last.append(k.send(src, dst, p.at(z=zz, c=cc)))
+                    far.append((src, dst, p.at(z=zz, c=cc)))
+        last.append(k.together(far, total.at[pl.ds(0, 112)]))
 
     def slab_home(half):
         slab = Slab(k, parts[2 + half][-1], GWD.at[:, pl.ds(half * 512, 512)], slab_from, own_slab)
@@ -1499,12 +1526,10 @@
         pltpu.VMEM((TOK, D), BF16),
         pltpu.VMEM((TOK, D), F32),
         pltpu.VMEM((QKV, TOK), F32),
-        pltpu.VMEM((2 * KV_HEADS, 8, 256), F32),
+        pltpu.VMEM((2 * KV_HEADS, SEQ, 256), BF16),
         pltpu.VMEM((TOK, D), F32),
         pltpu.VMEM((TOK, D), BF16),
         pltpu.VMEM((2, 2, 4, 2, ROWS, w), BF16),
-        pltpu.VMEM((2, SEQ, 128), F32),
-        pltpu.VMEM((KV_HEADS, 2, 128, 256), BF16),
         pltpu.VMEM((KV_HEADS, 2, 256, 128), BF16),
         pltpu.VMEM((KV_HEADS, 2, 128, 256), BF16),
         pltpu.VMEM((KV_HEADS, 2, 256, 128), BF16),
@@ -1538,14 +1563,14 @@
     scratch += [
         pltpu.VMEM((5, 8, 128), F32),
         pltpu.VMEM((4, 3, 8, 128), F32),
-        pltpu.SemaphoreType.DMA((108,)),
-        pltpu.SemaphoreType.DMA((142,)),
+        pltpu.SemaphoreType.DMA((56,)),
+        pltpu.SemaphoreType.DMA((78,)),
         pltpu.SemaphoreType.DMA((30,)),
     ]
     return pl.pallas_call(
         back_body,
         out_shape=outs,
-        in_specs=[ANY] * 18,
+        in_specs=[ANY] * 17,
         out_specs=[ANY] * 7,
         scratch_shapes=scratch,
         name="back",
@@ -1654,13 +1679,13 @@
     g1, g2, g3, g4 = [a.reshape(1, -1) for a in (attn_gain, ffn_gain, query_gain, key_gain)]
     og_in = out_grad.reshape(TOK, D)
     x_in = tokens.reshape(TOK, D)
-    (WO, WG, WD, OG, NA, KV, pt, lse, attended, resid, n2, wq_in, bias, rope, gain_rows, head_gains) = front(
+    (WO, WG, WD, OG, NA, KV, pt, probs, attended, resid, n2, wq_in, rope, gain_rows, head_gains) = front(
         x_in, w_qkv, w_out.T, w_gate_up, w_down, og_in, segment_ids, g1, g2, g3, g4, rope_parts()
     )
     d_normed, mix_part, dwg, dwd, WQ = ffn(n2, OG, WG, WD, wq_in)
     in_grad, mixed, gwg, gwd, gq, go, sums = back(
-        d_normed, x_in, og_in, resid, attended, pt, lse, WQ, WO, KV, mix_part, dwg, dwd, NA,
-        bias, rope, gain_rows, head_gains,
+        d_normed, x_in, og_in, resid, attended, pt, probs, WQ, WO, KV, mix_part, dwg, dwd, NA,
+        rope, gain_rows, head_gains,
     )
     outs = finish(in_grad, mixed, gwg, gwd, gq, go, sums, w_gate_up, w_qkv, g1, g2)
     return (

time: 236 us -> 234 us (level)
  no operation moved by 1% of the time
where the time goes in v10:
time: 234 us
  Pallas kernels  233 us (100%)
    pallas_call x1, Pallas kernels, front(): pl.pallas_call(front_body, out_shape=hbm, in_specs=[ANY, VMEM, VMEM, ANY,...  90.1 us
    pallas_call x1, Pallas kernels, back(): pl.pallas_call(back_body, out_shape=outs, in_specs=[ANY] * 17, out_specs=...  81.4 us
    pallas_call x1, Pallas kernels, ffn(): pl.pallas_call(ffn_body, out_shape=outs, in_specs=[ANY] * 5, out_specs=[A...  57.7 us

profile of v10, /device:TPU:1, one launch (start us, length us, event | category | flops | bytes accessed | tf_op | source)
XLA Modules:
  0.0 233.9 jit_solution(6431002430367028101)
XLA Ops:
  0.6 90.1 %front.1 = (bf16[2,4,2,4,2,16,1280]{6,5,4,3,2,1,0:T(8,128)(2,1)}, bf16[2,4,2,8,16,1280]{5,4,3,2,1,0:T(8,128)(2,1)}, bf16[2,4,2,80,1024]{4,3,2,1,0:T(8,128)(2,1)}...) custom-call(bf16[128,2048]{1,0:T(8,128)(2,1)} %bitcast.14, ...), custom_call_target="tpu_custom_call" | custom-call | tf_op jit(solution)/shard_map/front/pallas_call | solution.py:886
  90.7 57.7 %ffn.1 = (f32[128,2048]{1,0:T(8,128)}, bf16[4,128,2048]{2,1,0:T(8,128)(2,1)}, bf16[2,4,2,128,1280]{4,3,2,1,0:T(8,128)(2,1)}, bf16[2,4,2,80,1024]{4,3,2,1,0:T(8,128)(2,1)}, bf16[2,4,2,4,2,16,2048]{6,5,4,3,2,1,0:T(8,128)(2,1)}) custom-call(bf16[128,2048]{1,0:T(8,128)(2,1)} %get-tuple-element.47.n2, bf16[4,2,128,2048]{3,2,1,0:T(8,128)(2,1)} %get-tuple-element.48.OG, ...), custom_call_target="tpu_custom_call" | custom-call | tf_op jit(solution)/shard_map/ffn/pallas_call | solution.py:1188
  148.4 81.4 %back.1 = (f32[128,2048]{1,0:T(8,128)}, bf16[128,2048]{1,0:T(8,128)(2,1)}, bf16[16,10240]{1,0:T(8,128)(2,1)}, bf16[80,1024]{1,0:T(8,128)(2,1)}, bf16[16,2048]{1,...) custom-call(f32[128,2048]{1,0:T(8,128)} %get-tuple-element.52.refs_0_, bf16[128,2048]{1,0:T(8,128)(2,1)} %bitcast.15, ...), custom_call_target="tpu_custom_call" | custom-call | tf_op jit(solution)/shard_map/back/pallas_call | solution.py:1570
  229.9 3.8 %finish.1 = (f32[128,2048]{1,0:T(8,128)}, bf16[128,2048]{1,0:T(8,128)(2,1)}, f32[16,1920]{1,0:T(8,128)}, f32[16,1280]{1,0:T(8,128)}, f32[16,10240]{1,0:T(8,128)}...) custom-call(f32[128,2048]{1,0:T(8,128)} %get-tuple-element.67.refs_0_, ...), custom_call_target="tpu_custom_call" | custom-call | tf_op jit(solution)/shard_map/finish/pallas_call | solution.py:1655

commit v11 on v10

--- a/solution.py
+++ b/solution.py
@@ -592,7 +592,7 @@
         wq[:, i * 256 : (i + 1) * 256] = jnp.where(lane < 240, turned, rest).astype(BF16)
     met()
 
-    def spread(src_of, dst_of):
+    def spread(src_of, dst_of, region):
         far, near = [], None
         for dz in range(4):
             for dc in range(2):
@@ -601,11 +601,12 @@
                 if dz == 0 and dc == 0:
                     near = k.local(src, dst)
                 else:
-                    far.append(k.send(src, dst, p.at(z=zz, c=cc)))
-        return near, far
+                    far.append((src, dst, p.at(z=zz, c=cc)))
+        return near, [k.together(far, region)]
 
     q0 = spread(
-        lambda i: wq.at[:, pl.ds(pl.multiple_of(i * 256, 256), 256)], lambda i: wqm.at[yh, x, yl, i]
+        lambda i: wq.at[:, pl.ds(pl.multiple_of(i * 256, 256), 256)], lambda i: wqm.at[yh, x, yl, i],
+        wqm.at[0, 0, 0, pl.ds(0, 7)],
     )
     xcore = {0: k.send(x_in, xs.at[z, c], sib)}
     own_wo = k.local(wo, wos.at[yh, x, yl, z, c])
@@ -613,18 +614,25 @@
     def wo_at(part, *at):
         return wos.at[(*at, EVERY, pl.ds(part * 640, 640))]
 
-    o1 = [k.send(wo, wos.at[yh, x, yl, z, c], p.step("z", j)) for j in (1, 2, 3)]
+    o1 = [
+        k.together(
+            [(wo, wos.at[yh, x, yl, z, c], p.step("z", j)) for j in (1, 2, 3)], wos.at[0, 0, 0, pl.ds(0, 3), 0]
+        )
+    ]
     g0 = [
         spread(
             lambda i: wg.at[:, pl.ds(pl.multiple_of(half * FF + i * FS, 128), FS)],
             lambda i: WG.at[yh, x, yl, i, :, pl.ds(half * FS, FS)],
+            WG.at[0, 0, 0, pl.ds(0, 7), :, pl.ds(0, FS)],
         )
         for half in range(2)
     ]
     xring = RingGather(p, k, "z", lambda i: xs.at[i, c], x_in)
 
     def to_plane(blocks):
-        return [k.send(b, b, p.step(axis, j)) for j in (1, 2, 3) for b, axis in blocks]
+        return [
+            k.together([(b, b, p.step(axis, j)) for j in (1, 2, 3)], region) for b, axis, region in blocks
+        ]
 
     ql, qh = pl.ds(0, 128), pl.ds(128, 128)
     lo, hi = pl.ds(0, FS), pl.ds(FS, FS)
@@ -632,7 +640,8 @@
     q0[0].wait()
     for copy in q0[1]:
         copy.wait_recv()
-    q1 = to_plane(((wqm.at[yh, x, yl, :, :, ql], "x"), (wqm.at[yh, x, yl, :, :, qh], "y")))
+    one = wqm.at[0, pl.ds(0, 3), 0, :, :, ql]
+    q1 = to_plane(((wqm.at[yh, x, yl, :, :, ql], "x", one), (wqm.at[yh, x, yl, :, :, qh], "y", one)))
     fill_bias(bias, seg, p.s)
     cos, sin = rope_tables(parts, p.s)
     rope[0], rope[1] = cos, sin
@@ -640,12 +649,14 @@
     qkgain[...] = jnp.concatenate([jnp.broadcast_to(qgain, (HEAD, 128)), jnp.broadcast_to(kgain, (HEAD, 128))], axis=0)
     for copy in q1:
         copy.wait_recv()
-    q2 = to_plane(((wqm.at[yh, :, yl, :, :, ql], "y"), (wqm.at[:, x, :, :, :, qh], "x")))
+    four = wqm.at[:, pl.ds(0, 3), :, :, :, ql]
+    q2 = to_plane(((wqm.at[yh, :, yl, :, :, ql], "y", four), (wqm.at[:, x, :, :, :, qh], "x", four)))
     for near, far in g0:
         near.wait()
         for copy in far:
             copy.wait_recv()
-    plane = to_plane(((WG.at[yh, x, yl, :, :, lo], "x"), (WG.at[yh, x, yl, :, :, hi], "y")))
+    one = WG.at[0, pl.ds(0, 3), 0, :, :, lo]
+    plane = to_plane(((WG.at[yh, x, yl, :, :, lo], "x", one), (WG.at[yh, x, yl, :, :, hi], "y", one)))
     slab_rows = w_down[...].astype(F32)
     wd[...] = jnp.concatenate([slab_rows[:, :1024], slab_rows[:, 1024:]], axis=0).astype(BF16)
     slab = Slab(k, wd, WD.at[yl, z, c], slab_to, own_slab)
@@ -683,11 +694,9 @@
         if o == 1:
             for copy in o1:
                 copy.wait_recv()
+            four = wos.at[:, pl.ds(0, 3), :, 0, 0, :, pl.ds(0, 640)]
             o2 = to_plane(
-                (
-                    (wo_at(0, yh, x, yl, EVERY, c), "y"),
-                    (wo_at(1, yh, x, yl, EVERY, c), "x"),
-                ),
+                ((wo_at(0, yh, x, yl, EVERY, c), "y", four), (wo_at(1, yh, x, yl, EVERY, c), "x", four))
             )
         if o == 3:
             for copy in plane:
@@ -698,7 +707,8 @@
             ]
     slab.wait_recv()
     held = WD.at[yl, slab_place(p, x=x), slab_place(p, y=p.y)]
-    plane_d = to_plane(((held.at[:, dlo], "x"), (held.at[:, dhi], "y")))
+    few = WD.at[0, pl.ds(0, 3), 0]
+    plane_d = to_plane(((held.at[:, dlo], "x", few.at[:, :, dlo]), (held.at[:, dhi], "y", few.at[:, :, dhi])))
     for copy in o2:
         copy.wait_recv()
     o3 = [RingGather(p, k, "x", lambda i: wo_at(0, EVERY, i, EVERY, EVERY, c))]
@@ -725,7 +735,9 @@
     across, ring = [], []
     for cols in KV_PARTS:
         across.append(k.send(kvl.at[:, :, cols], kvs.at[:, yl, z, c, :, cols], yl_partner))
-        ring.append([k.send(kvl.at[:, :, cols], kvs.at[:, yl, z, c, :, cols], p.step("z", j)) for j in (1, 2, 3)])
+        three = kvs.at[:, 0, pl.ds(0, 3), 0, :, cols]
+        sends = [(kvl.at[:, :, cols], kvs.at[:, yl, z, c, :, cols], p.step("z", j)) for j in (1, 2, 3)]
+        ring.append([k.together(sends, three)])
     keep.append(k.local(pt, PT))
 
     @pl.loop(0, KV_HEADS)
@@ -736,7 +748,8 @@
     for copy, group, cols in zip(across, ring, KV_PARTS):
         copy.wait_recv()
         src = kvs.at[:, 1 - yl, z, c, :, cols]
-        group += [k.send(src, src, p.step("z", j)) for j in (1, 2, 3)]
+        three = kvs.at[:, 0, pl.ds(0, 3), 0, :, cols]
+        group.append(k.together([(src, src, p.step("z", j)) for j in (1, 2, 3)], three))
     get_og.wait()
     keep.append(k.local(ogv, OG.at[z, c]))
     rows = RingGather(p, k, "z", lambda i: OG.at[i, c], ogv)
@@ -879,8 +892,8 @@
         pltpu.VMEM((2, SEQ, 128), F32),
         pltpu.VMEM((KV_HEADS, 2, 128, 256), BF16),
         pltpu.VMEM((KV_HEADS, 2, HEAD, 256), F32),
-        pltpu.SemaphoreType.DMA((80,)),
-        pltpu.SemaphoreType.DMA((130,)),
+        pltpu.SemaphoreType.DMA((60,)),
+        pltpu.SemaphoreType.DMA((82,)),
         pltpu.SemaphoreType.DMA((14,)),
     ]
     return pl.pallas_call(

time: 234 us -> 234 us (level)
  no operation moved by 1% of the time
where the time goes in v11:
time: 234 us; the launch traced here: 233 us
  Pallas kernels  232 us (99%)
    pallas_call x1, Pallas kernels, front(): pl.pallas_call(front_body, out_shape=hbm, in_specs=[ANY, VMEM, VMEM, ANY,...  89.5 us
    pallas_call x1, Pallas kernels, back(): pl.pallas_call(back_body, out_shape=outs, in_specs=[ANY] * 17, out_specs=...  81.5 us
    pallas_call x1, Pallas kernels, ffn(): pl.pallas_call(ffn_body, out_shape=outs, in_specs=[ANY] * 5, out_specs=[A...  57.7 us

profile of v11, /device:TPU:1, one launch (start us, length us, event | category | flops | bytes accessed | tf_op | source)
XLA Modules:
  0.0 233.3 jit_solution(6361969325135815070)
XLA Ops:
  0.6 89.5 %front.1 = (bf16[2,4,2,4,2,16,1280]{6,5,4,3,2,1,0:T(8,128)(2,1)}, bf16[2,4,2,8,16,1280]{5,4,3,2,1,0:T(8,128)(2,1)}, bf16[2,4,2,80,1024]{4,3,2,1,0:T(8,128)(2,1)}...) custom-call(bf16[128,2048]{1,0:T(8,128)(2,1)} %bitcast.14, ...), custom_call_target="tpu_custom_call" | custom-call | tf_op jit(solution)/shard_map/front/pallas_call | solution.py:899
  90.1 57.7 %ffn.1 = (f32[128,2048]{1,0:T(8,128)}, bf16[4,128,2048]{2,1,0:T(8,128)(2,1)}, bf16[2,4,2,128,1280]{4,3,2,1,0:T(8,128)(2,1)}, bf16[2,4,2,80,1024]{4,3,2,1,0:T(8,128)(2,1)}, bf16[2,4,2,4,2,16,2048]{6,5,4,3,2,1,0:T(8,128)(2,1)}) custom-call(bf16[128,2048]{1,0:T(8,128)(2,1)} %get-tuple-element.47.n2, bf16[4,2,128,2048]{3,2,1,0:T(8,128)(2,1)} %get-tuple-element.48.OG, ...), custom_call_target="tpu_custom_call" | custom-call | tf_op jit(solution)/shard_map/ffn/pallas_call | solution.py:1201
  147.8 81.5 %back.1 = (f32[128,2048]{1,0:T(8,128)}, bf16[128,2048]{1,0:T(8,128)(2,1)}, bf16[16,10240]{1,0:T(8,128)(2,1)}, bf16[80,1024]{1,0:T(8,128)(2,1)}, bf16[16,2048]{1,...) custom-call(f32[128,2048]{1,0:T(8,128)} %get-tuple-element.52.refs_0_, bf16[128,2048]{1,0:T(8,128)(2,1)} %bitcast.15, ...), custom_call_target="tpu_custom_call" | custom-call | tf_op jit(solution)/shard_map/back/pallas_call | solution.py:1583
  229.3 3.8 %finish.1 = (f32[128,2048]{1,0:T(8,128)}, bf16[128,2048]{1,0:T(8,128)(2,1)}, f32[16,1920]{1,0:T(8,128)}, f32[16,1280]{1,0:T(8,128)}, f32[16,10240]{1,0:T(8,128)}...) custom-call(f32[128,2048]{1,0:T(8,128)} %get-tuple-element.67.refs_0_, ...), custom_call_target="tpu_custom_call" | custom-call | tf_op jit(solution)/shard_map/finish/pallas_call | solution.py:1668
